TPU v7x, 512 devices: a whole 4x8x8 slice. The times are simulated.
512 devices in a mesh: attn: 16 (over z, x_hi), exp: 32 (over x_lo, y, core).
Axes of the slice: x: 4 (x_hi: 2, x_lo: 2; x = x_hi * 2 + x_lo), y: 8, z: 8, core: 2. Of those that a mesh axis runs over, the one named last changes fastest.
Arguments:
- residual: bfloat16 [4096, 2880], P(('exp', 'attn')), may hold values from -16 to 16
- queries: bfloat16 [4096, 2048], P(('exp', 'attn')), may hold values from -6 to 6
- window_key_value_cache: bfloat16 [4096, 4, 128, 128], P(('exp', 'attn')), may hold values from -6 to 6
- new_key_value: bfloat16 [4096, 4, 128], P(('exp', 'attn')), may hold values from -5.5 to 5.5
- head_sink_logits: float32 [32], replicated, may hold values from 0 to 5
- out_proj: bfloat16 [2048, 2880], P('attn'), may hold values from -0.125 to 0.125
- norm_gain: float32 [2880], replicated, may hold values from 0.5 to 1.5
- expert_ids: int32 [4096, 4], P('exp'), may hold values from 0 to 31, as said below
- gate_mix: float32 [4096, 4], P('exp'), may hold values from 0.05 to 0.6
- w_gate: bfloat16 [32, 2880, 2880], P('exp', None, 'attn'), may hold values from -0.109375 to 0.109375
- w_up: bfloat16 [32, 2880, 2880], P('exp', None, 'attn'), may hold values from -0.109375 to 0.109375
- w_down: bfloat16 [32, 2880, 2880], P('exp', 'attn'), may hold values from -0.109375 to 0.109375
Outputs:
- layer_out: bfloat16 [4096, 2880], P(('exp', 'attn'))
Inputs may be any that keep to these rules, and one draw needn't show every extreme that they name: `expert_ids`: each row names 4 different experts. Within the rows of one index of exp (aligned blocks of 128 rows) no expert is named more than 32 times, and one expert is named exactly 32 times in every block.
All inputs are finite; a program needn't handle non-finite values.
Results may differ from a plain program's by a relative error of at most 0.02.
Values may be sent and summed in bfloat16 or wider, within the bound.
No kernel may reach another device: no remote copies, remote signals or barrier semaphores. Data moves between devices by JAX's collectives and lax.ppermute only.
A program may use at most 128 MiB of HBM per device.

v0:
```python
import jax
import jax.numpy as jnp
from jax import lax
from jax.sharding import PartitionSpec as P

HEAD_SIZE = 64
QUERY_HEADS = 32
KEY_VALUE_HEADS = 4


def attend(queries, window_key_value_cache, new_key_value, head_sink_logits):
    count_of_rows = queries.shape[0]
    query_groups = QUERY_HEADS // KEY_VALUE_HEADS
    grouped_queries = queries.reshape(count_of_rows, KEY_VALUE_HEADS, query_groups, HEAD_SIZE)
    all_keys = jnp.concatenate(
        [window_key_value_cache[:, :, :, :HEAD_SIZE], new_key_value[:, :, None, :HEAD_SIZE]], axis=2
    )
    all_values = jnp.concatenate(
        [window_key_value_cache[:, :, :, HEAD_SIZE:], new_key_value[:, :, None, HEAD_SIZE:]], axis=2
    )
    scores = jnp.einsum(
        "rkgd,rkjd->rkgj", grouped_queries, all_keys, preferred_element_type=jnp.float32
    ) * HEAD_SIZE ** (-0.5)
    sink_portion = head_sink_logits.reshape(1, KEY_VALUE_HEADS, query_groups, 1)
    highest = jnp.maximum(jnp.max(scores, axis=3, keepdims=True), sink_portion)
    raised = jnp.exp(scores - highest)
    denominator = jnp.sum(raised, axis=3, keepdims=True) + jnp.exp(sink_portion - highest)
    weights = (raised / denominator).astype(jnp.bfloat16)
    combined = jnp.einsum(
        "rkgj,rkjd->rkgd", weights, all_values, preferred_element_type=jnp.float32
    )
    return combined.reshape(count_of_rows, QUERY_HEADS * HEAD_SIZE).astype(jnp.bfloat16)


def run_experts(row_block, w_gate, w_up, w_down):
    sources, slot_count, width = row_block.shape
    local_experts = w_gate.shape[0]
    grouped_queries = row_block.reshape(sources // local_experts, local_experts, slot_count, width)
    gate_proj = jnp.einsum(
        "sjcd,jdf->sjcf", grouped_queries, w_gate, preferred_element_type=jnp.float32
    )
    up_proj = jnp.einsum(
        "sjcd,jdf->sjcf", grouped_queries, w_up, preferred_element_type=jnp.float32
    )
    activated = (gate_proj * jax.nn.sigmoid(1.702 * gate_proj) * (up_proj + 1.0)).astype(
        jnp.bfloat16
    )
    partial_value = jnp.einsum(
        "sjcf,jfd->sjcd", activated, w_down, preferred_element_type=jnp.float32
    ).astype(jnp.bfloat16)
    return partial_value.reshape(sources, slot_count, width)


def local(
    residual,
    queries,
    window_key_value_cache,
    new_key_value,
    head_sink_logits,
    out_proj,
    norm_gain,
    expert_ids,
    gate_mix,
    w_gate,
    w_up,
    w_down,
):
    column_rows, top_count = expert_ids.shape
    expert_total = w_gate.shape[0] * lax.axis_size("exp")
    capacity = 2 * column_rows * top_count // expert_total
    attention_output = attend(queries, window_key_value_cache, new_key_value, head_sink_logits)
    head_slices = lax.all_to_all(attention_output, "attn", split_axis=1, concat_axis=0, tiled=True)
    hidden_state = residual.astype(jnp.float32) + lax.psum_scatter(
        jnp.dot(head_slices, out_proj, preferred_element_type=jnp.float32).astype(jnp.bfloat16),
        "attn",
        scatter_dimension=0,
        tiled=True,
    ).astype(jnp.float32)
    mean_square = jnp.mean(hidden_state * hidden_state, axis=1, keepdims=True)
    normed = (hidden_state * lax.rsqrt(mean_square + 1e-05) * norm_gain).astype(jnp.bfloat16)
    flat_ids = expert_ids.reshape(-1)
    onehot_table = (flat_ids[:, None] == jnp.arange(expert_total, dtype=jnp.int32)[None, :]).astype(
        jnp.int32
    )
    slot_index = jnp.sum((jnp.cumsum(onehot_table, axis=0) - 1) * onehot_table, axis=1)
    places = flat_ids * capacity + slot_index
    row_number = jnp.arange(column_rows * top_count, dtype=jnp.int32) // top_count
    source_rows = (
        jnp.full((expert_total * capacity,), column_rows, jnp.int32).at[places].set(row_number)
    )
    column = lax.all_gather(normed, "attn", axis=0, tiled=True)
    padded = jnp.concatenate([column, jnp.zeros((1, column.shape[1]), jnp.bfloat16)], axis=0)
    outgoing = jnp.take(padded, source_rows, axis=0).reshape(
        expert_total, capacity, column.shape[1]
    )
    partial_value = run_experts(
        lax.all_to_all(outgoing, "exp", split_axis=0, concat_axis=0, tiled=True),
        w_gate,
        w_up,
        w_down,
    )
    returned = lax.all_to_all(partial_value, "exp", split_axis=0, concat_axis=0, tiled=True)
    picked = jnp.take(returned.reshape(expert_total * capacity, returned.shape[2]), places, axis=0)
    weighted = jnp.sum(
        picked.reshape(column_rows, top_count, picked.shape[1]).astype(jnp.float32)
        * gate_mix[:, :, None],
        axis=1,
    )
    combined = lax.psum_scatter(
        weighted.astype(jnp.bfloat16), "attn", scatter_dimension=0, tiled=True
    ).astype(jnp.float32)
    return (hidden_state + combined).astype(jnp.bfloat16)


def solution(mesh):
    in_specs = (
        P(("exp", "attn"), None),
        P(("exp", "attn"), None),
        P(("exp", "attn"), None, None, None),
        P(("exp", "attn"), None, None),
        P(),
        P("attn", None),
        P(),
        P("exp", None),
        P("exp", None),
        P("exp", None, "attn"),
        P("exp", None, "attn"),
        P("exp", "attn", None),
    )
    out_specs = P(("exp", "attn"), None)
    return jax.shard_map(local, mesh=mesh, in_specs=in_specs, out_specs=out_specs, check_vma=False)
```

profile of v0, /device:TPU:6, one launch (start us, length us, event | category | flops | bytes accessed | tf_op | source)
XLA Modules:
  0.0 752.1 jit_solution(5121819863465048144)
XLA Ops:
  6.5 0.9 fusion.42
  7.4 1.1 copy.43
  8.5 2.2 fusion.41
  10.7 1.2 copy.55
  11.9 0.1 reshape.140
  12.0 0.1 max.18
  12.1 0.3 copy.46
  12.4 0.4 copy.57
  12.9 1.6 fusion.43
  14.5 0.2 fusion.24
  14.8 0.4 convolution_convert_fusion.2
  15.2 0.1 convert_element_type.51
  15.3 0.6 copy.47
  15.9 13.3 %all-to-all-start = ((bf16[8,16,128]{2,0,1:T(8,128)(2,1)}), bf16[8,16,128]{2,0,1:T(8,128)(2,1)S(1)}, u32[]{:S(2)}, u32[]{:S(2)}) async-start(bf16[8,16,128]{2,0,1:T(8,128)(2,1)} %copy.47), calls=%async_computation | async-start | bytes 65536 | tf_op jit(solution)/shard_map/all_to_all | solution.py:72
  29.3 0.1 copy.48
  29.4 0.1 eq.26
  29.5 0.1 reshape.141
  29.7 1.2 reduce-window.6
  30.8 0.2 slice_reduce_fusion
  31.1 0.1 copy.53
  31.2 0.1 mul.76
  31.3 0.1 fusion.28
  31.4 5.3 all-to-all-done
  36.7 1.2 convolution_convert_fusion.1
  38.0 2.4 scatter_custom_fusion
  40.4 0.1 broadcast_in_dim.45
  40.5 1.3 dynamic-slice
  42.5 157.1 %all-reduce.6.cloned.1.call-done = bf16[128,2880]{1,0:T(8,128)(2,1)} async-done(((bf16[128,2880]{1,0:T(8,128)(2,1)}), bf16[128,2880]{1,0:T(8,128)(2,1)}) %all-reduce.6.cloned.1.call-update) | async-done | bytes 737296
  199.5 0.9 multiply_reduce_fusion.1
  200.5 0.9 multiply_convert_fusion
  201.4 41.2 %all_gather.3 = bf16[128,2880]{1,0:T(8,128)(2,1)S(1)} all-gather(bf16[8,2880]{1,0:T(8,128)(2,1)S(1)} %multiply_convert_fusion), channel_id=1, replica_groups=mesh['attn'=16,'exp'=32] {'attn'}, dimensions={0}, use_global_device_ids=true | all-gather | bytes 783360 | tf_op jit(solution)/shard_map/all_gather | solution.py:91
  242.6 6.5 gather_fusion
  249.2 3.4 broadcast_select_fusion
  252.6 143.1 %all_to_all.26 = bf16[32,32,2880]{2,1,0:T(8,128)(2,1)S(1)} all-to-all(bf16[32,32,2880]{2,1,0:T(8,128)(2,1)S(1)} %broadcast_select_fusion), channel_id=1, replica_groups=mesh['attn'=16,'exp'=32] {'exp'}, dimensions={0} | all-to-all | bytes 11796480 | tf_op jit(solution)/shard_map/all_to_all | solution.py:97
  395.7 2.6 copy-done.1
  398.3 2.8 convolution_bitcast_fusion
  401.1 12.4 %convolution_convert_fusion = bf16[32,32,2880]{2,1,0:T(8,128)(2,1)} fusion(bf16[32,32,2880]{2,1,0:T(8,128)(2,1)} %copy-done.1, bf16[1,180,2880]{2,1,0:T(8,128)(2,1)S(1)} %copy-done, bf16[1,2880,180]{1,2,0:T(8,128)(2,1)} %param.22, f32[32,1,32,180]{3,2,0,1:T(8,128)} %convolution_bitcast_fusion), kind=kOutput, calls=%fused_computation.5 | convolution fusion | flops 2127790080 | bytes 14607360 | tf_op jit(solution)/shard_map/sjcf,jfd->sjcd/dot_general | solution.py:48
  413.5 5.9 all-to-all-start.2
  419.4 0.3 all-reduce.8.cloned.1.call-start
  419.7 0.1 reduce_sum.42
  419.9 0.1 copy.52
  420.1 0.1 copy.54
  420.2 133.1 %all-to-all-done.2 = bf16[32,32,2880]{2,1,0:T(8,128)(2,1)} async-done(((bf16[32,32,2880]{2,1,0:T(8,128)(2,1)}), bf16[32,32,2880]{2,1,0:T(8,128)(2,1)}, u32[]{:S(2)}, u32[]{:S(2)}) %all-to-all-start.2) | async-done | bytes 5898272 | tf_op jit(solution)/shard_map/all_to_all | solution.py:102
  553.2 10.2 %gather_fusion.1 = bf16[512,2880]{1,0:T(8,128)(2,1)} fusion(bf16[1024,2880]{1,0:T(8,128)(2,1)} %bitcast.24, s32[1024]{0:T(1024)S(1)} %pad_clamp_fusion), kind=kCustom, calls=%fused_computation.1 | custom fusion | bytes 5900288 | tf_op jit(solution)/shard_map/jit(_take)/gather | solution.py:103
  563.4 5.8 gather.15
  569.3 9.3 %multiply_reduce_fusion = bf16[128,2880]{1,0:T(8,128)(2,1)} fusion(f32[128,4]{1,0:T(8,128)S(1)} %copy.54, bf16[128,4,2880]{2,1,0:T(4,128)(2,1)} %gather.15, pred[128,4]{1,0:T(8,128)(4,1)S(1)} %copy.52), kind=kLoop, calls=%fused_computation.3 | loop fusion | flops 5529600 | bytes 3688960 | tf_op jit(solution)/shard_map/reduce_sum | solution.py:104
  578.6 165.2 %all-reduce.8.cloned.1.call-done = bf16[128,2880]{1,0:T(8,128)(2,1)} async-done(((bf16[128,2880]{1,0:T(8,128)(2,1)}), bf16[128,2880]{1,0:T(8,128)(2,1)}) %all-reduce.8.cloned.1.call-update) | async-done | bytes 737296
  743.8 1.5 add_convert_fusion
  (40 shorter events, 0.4 us)
Async XLA Ops:
  6.5 394.6 %copy-start = (bf16[1,180,2880]{2,1,0:T(8,128)(2,1)S(1)}, bf16[1,180,2880]{2,1,0:T(8,128)(2,1)}, u32[]{:S(2)}) copy-start(bf16[1,180,2880]{2,1,0:T(8,128)(2,1)} %param.23) | copy-start | bytes 3110404
  8.5 3.4 copy-start.4
  8.5 3.5 copy-start.8
  12.8 16.4 %copy-start.5 = (s32[128,4]{0,1:T(4,128)S(1)}, s32[128,4]{0,1:T(4,128)}, u32[]{:S(2)}) copy-start(s32[128,4]{0,1:T(4,128)} %param.19) | copy-start | bytes 6148
  12.9 23.8 %copy-start.2 = (bf16[128,2880]{0,1:T(8,128)(2,1)S(1)}, bf16[128,2880]{0,1:T(8,128)(2,1)}, u32[]{:S(2)}) copy-start(bf16[128,2880]{0,1:T(8,128)(2,1)} %param.17) | copy-start | bytes 2211844
  14.7 184.8 %copy-start.3 = (bf16[8,2880]{1,0:T(8,128)(2,1)S(1)}, bf16[8,2880]{1,0:T(8,128)(2,1)}, u32[]{:S(2)}) copy-start(bf16[8,2880]{1,0:T(8,128)(2,1)} %param.12) | copy-start | bytes 138244
  14.8 185.7 %copy-start.6 = (f32[2880]{0:T(1024)S(1)}, f32[2880]{0:T(1024)}, u32[]{:S(2)}) copy-start(f32[2880]{0:T(1024)} %param.18) | copy-start | bytes 34564
  15.9 20.7 %all-to-all-start = ((bf16[8,16,128]{2,0,1:T(8,128)(2,1)}), bf16[8,16,128]{2,0,1:T(8,128)(2,1)S(1)}, u32[]{:S(2)}, u32[]{:S(2)}) async-start(bf16[8,16,128]{2,0,1:T(8,128)(2,1)} %copy.47), calls=%async_computation | async-start | bytes 65536 | tf_op jit(solution)/shard_map/all_to_all | solution.py:72
  29.2 170.3 %all-reduce.6.cloned.1.call-start = ((), (), s32[]{:S(2)}) async-start(), calls=%async_computation.3 | async-start | bytes 1507328
  252.6 145.7 %copy-start.9 = (bf16[1,2880,180]{1,2,0:T(8,128)(2,1)S(1)}, bf16[1,2880,180]{1,2,0:T(8,128)(2,1)}, u32[]{:S(2)}) copy-start(bf16[1,2880,180]{1,2,0:T(8,128)(2,1)} %param.21) | copy-start | bytes 3110404
  395.7 2.6 copy-start.1
  413.5 6.6 copy-start.7
  413.5 139.7 %all-to-all-start.2 = ((bf16[32,32,2880]{2,1,0:T(8,128)(2,1)}), bf16[32,32,2880]{2,1,0:T(8,128)(2,1)}, u32[]{:S(2)}, u32[]{:S(2)}) async-start(bf16[32,32,2880]{2,1,0:T(8,128)(2,1)} %convolution_convert_fusion), calls=%async_computation.2 | async-start | bytes 12058624 | tf_op jit(solution)/shard_map/all_to_all | solution.py:102
  419.4 324.4 %all-reduce.8.cloned.1.call-start = ((), (), s32[]{:S(2)}) async-start(), calls=%async_computation.4 | async-start | bytes 1507328
Sparse Core Ops, SparseCore 0:
  38.1 161.4 all-reduce.5
  578.7 165.0 all-reduce.7
where the time goes:
time: 753 us; the launch traced here: 752 us
  waiting for transfers between devices  461 us (61%)
  blocking collectives  184 us (24%)
  local copies, waits for them, and re-layouts  37.3 us (5%)
  starting transfers between devices  19.5 us (3%)
  matrix products  18.5 us (2%)
  other arithmetic  17.6 us (2%)
  between operations  14.3 us (2%)
    unnamed x4, waiting for transfers between devices  322 us
    all_to_all x1, blocking collectives, local(): lax.all_to_all(outgoing, 'exp', split_axis=0, concat_axis=0, tiled=True)  143 us
    all_to_all x1, waiting for transfers between devices, local(): lax.all_to_all(partial_value, 'exp', split_axis=0, concat_axis=0, tiled=T...  133 us
    all_gather x1, blocking collectives, local(): column = lax.all_gather(normed, 'attn', axis=0, tiled=True)  41.2 us
    gather x2, local copies, waits for them, and re-layouts, local(): jnp.take(returned.reshape(expert_total * capacity, returned.shape[2]), pl...  16 us
  transfers between devices with their start and end apart: 4, of which 4 were waited for; matrix products, arithmetic and copies ran while one was open for 1% of the time, Pallas kernels for 0%

commit v1 on v0

v1 whole, which is shorter than its diff:
```python
import jax
import jax.numpy as jnp
from jax import lax
from jax.experimental import pallas as pl
from jax.experimental.pallas import tpu as pltpu
from jax.sharding import PartitionSpec as P

HEAD_SIZE = 64
QUERY_HEADS = 32
KEY_VALUE_HEADS = 4
D = 2880
FF_LOCAL = 180
N_ATTN = 16
N_EXP = 32
CAP = 32
HALVES = 2
BLOCKS = N_ATTN // HALVES
BLOCK = D // BLOCKS
LANES = 384
FF_LANES = 256
ROW_TILE = 256
F32 = jnp.float32
BF16 = jnp.bfloat16

Z_GROUPS = [[z * HALVES + half for z in range(BLOCKS)] for half in range(HALVES)]


def attend(queries, window_key_value_cache, new_key_value, head_sink_logits):
    count_of_rows = queries.shape[0]
    query_groups = QUERY_HEADS // KEY_VALUE_HEADS
    grouped_queries = queries.reshape(count_of_rows, KEY_VALUE_HEADS, query_groups, HEAD_SIZE)
    all_keys = jnp.concatenate(
        [window_key_value_cache[:, :, :, :HEAD_SIZE], new_key_value[:, :, None, :HEAD_SIZE]], axis=2
    )
    all_values = jnp.concatenate(
        [window_key_value_cache[:, :, :, HEAD_SIZE:], new_key_value[:, :, None, HEAD_SIZE:]], axis=2
    )
    scores = jnp.einsum(
        "rkgd,rkjd->rkgj", grouped_queries, all_keys, preferred_element_type=jnp.float32
    ) * HEAD_SIZE ** (-0.5)
    sink_portion = head_sink_logits.reshape(1, KEY_VALUE_HEADS, query_groups, 1)
    highest = jnp.maximum(jnp.max(scores, axis=3, keepdims=True), sink_portion)
    raised = jnp.exp(scores - highest)
    denominator = jnp.sum(raised, axis=3, keepdims=True) + jnp.exp(sink_portion - highest)
    weights = (raised / denominator).astype(jnp.bfloat16)
    combined = jnp.einsum(
        "rkgj,rkjd->rkgd", weights, all_values, preferred_element_type=jnp.float32
    )
    return combined.reshape(count_of_rows, QUERY_HEADS * HEAD_SIZE).astype(jnp.bfloat16)


def experts_kernel(x_ref, w_in_ref, w_out_ref, y_ref):
    square = jnp.zeros((ROW_TILE, 1), F32)
    both = jnp.zeros((ROW_TILE, 2 * FF_LANES), F32)
    for block in range(BLOCKS):
        x = x_ref[block]
        parts = x[:, LANES - 128 :].astype(F32)
        at = BLOCK - (LANES - 128)
        square = square + parts[:, at : at + 1] + parts[:, at + 1 : at + 2]
        both = both + jnp.dot(x, w_in_ref[block], preferred_element_type=F32)
    both = both * lax.rsqrt(square * (1.0 / D) + 1e-05)
    gate = both[:, :FF_LANES]
    up = both[:, FF_LANES:]
    hidden = (gate * jax.nn.sigmoid(1.702 * gate) * (up + 1.0)).astype(BF16)
    for block in range(BLOCKS):
        y_ref[block] = jnp.dot(hidden, w_out_ref[block], preferred_element_type=F32).astype(BF16)


def run_experts(x, w_in, w_out):
    rows = x.shape[1]
    return pl.pallas_call(
        experts_kernel,
        grid=(rows // ROW_TILE,),
        in_specs=[
            pl.BlockSpec((BLOCKS, ROW_TILE, LANES), lambda i: (0, i, 0)),
            pl.BlockSpec((BLOCKS, LANES, 2 * FF_LANES), lambda i: (0, 0, 0)),
            pl.BlockSpec((BLOCKS, FF_LANES, LANES), lambda i: (0, 0, 0)),
        ],
        out_specs=pl.BlockSpec((BLOCKS, ROW_TILE, LANES), lambda i: (0, i, 0)),
        out_shape=jax.ShapeDtypeStruct((BLOCKS, rows, LANES), BF16),
        compiler_params=pltpu.CompilerParams(vmem_limit_bytes=40 * 2**20),
        cost_estimate=pl.CostEstimate(
            flops=2 * rows * D * 3 * FF_LOCAL, bytes_accessed=18 * 2**20, transcendentals=rows * FF_LOCAL
        ),
    )(x, w_in, w_out)


def to_blocks(array):
    array = array.reshape(array.shape[:-1] + (BLOCKS, BLOCK))
    return jnp.pad(array, [(0, 0)] * (array.ndim - 1) + [(0, LANES - BLOCK)])


def local(
    residual,
    queries,
    window_key_value_cache,
    new_key_value,
    head_sink_logits,
    out_proj,
    norm_gain,
    expert_ids,
    gate_mix,
    w_gate,
    w_up,
    w_down,
):
    own_rows = residual.shape[0]
    column_rows = expert_ids.shape[0]
    attn_index = lax.axis_index("attn")
    z_index = attn_index // HALVES

    other_proj = lax.ppermute(out_proj, "attn", [(i, i ^ 1) for i in range(N_ATTN)])

    attended = attend(queries, window_key_value_cache, new_key_value, head_sink_logits)
    heads = attended.reshape(own_rows, BLOCKS, HALVES, 128).transpose(1, 2, 0, 3)
    residual_blocks = to_blocks(residual).transpose(1, 0, 2)
    residual_blocks = jnp.broadcast_to(residual_blocks[:, None], (BLOCKS, HALVES, own_rows, LANES))
    sent = jnp.concatenate([heads, heads[:, ::-1], residual_blocks], axis=3)
    got = lax.all_to_all(sent.reshape(N_ATTN, own_rows, 256 + LANES), "attn", 0, 0, tiled=True)
    got = got.reshape(column_rows, 256 + LANES)

    proj = to_blocks(jnp.concatenate([out_proj, other_proj], axis=0)).transpose(1, 0, 2)
    partial_sums = jnp.einsum("rk,zkd->zrd", got[:, :256], proj, preferred_element_type=F32).astype(BF16)
    sums = lax.all_to_all(partial_sums, "attn", 0, 0, tiled=True, axis_index_groups=Z_GROUPS)
    hidden_state = got[:, 256:].astype(F32) + jnp.sum(sums.astype(F32), axis=0)

    gain = lax.dynamic_index_in_dim(to_blocks(norm_gain), z_index, 0, keepdims=False)
    square = jnp.sum(hidden_state * hidden_state, axis=1, keepdims=True)
    square_high = lax.reduce_precision(square, 8, 7)
    square_low = square - square_high
    lane = lax.broadcasted_iota(jnp.int32, (column_rows, LANES), 1)
    scaled = hidden_state * gain
    scaled = jnp.where(lane == BLOCK, square_high, jnp.where(lane == BLOCK + 1, square_low, scaled)).astype(BF16)

    names = expert_ids.T[None, :, :] == jnp.arange(N_EXP, dtype=jnp.int32)[:, None, None]
    named = jnp.any(names, axis=1)
    weight = jnp.sum(jnp.where(names, gate_mix.T[None, :, :], 0.0), axis=1)
    row = jnp.arange(column_rows, dtype=jnp.int32)
    earlier = (row[:, None] < row[None, :]).astype(BF16)
    slot = jnp.dot(named.astype(BF16), earlier, preferred_element_type=F32).astype(jnp.int32)
    slot = jnp.where(named, slot, -1)
    taken = slot[:, None, :] == jnp.arange(CAP, dtype=jnp.int32)[None, :, None]
    select = taken.astype(BF16).reshape(N_EXP * CAP, column_rows)
    mix = jnp.where(taken, weight[:, None, :], 0.0).reshape(N_EXP * CAP, column_rows)
    mix_high = lax.reduce_precision(mix, 8, 7)
    mix_low = (mix - mix_high).astype(BF16)
    mix_high = mix_high.astype(BF16)

    outgoing = jnp.dot(select, scaled, preferred_element_type=F32).astype(BF16)
    outgoing = outgoing.reshape(N_EXP, CAP, LANES)
    incoming = lax.all_to_all(outgoing, "exp", 0, 0, tiled=True).reshape(N_EXP * CAP, LANES)
    rows_in = lax.all_gather(incoming, "attn", axis=0, tiled=True, axis_index_groups=Z_GROUPS)

    def padded_in(w):
        w = w.reshape(BLOCKS, BLOCK, FF_LOCAL)
        return jnp.pad(w, ((0, 0), (0, LANES - BLOCK), (0, FF_LANES - FF_LOCAL)))

    w_in = jnp.concatenate([padded_in(w_gate), padded_in(w_up)], axis=2)
    w_out = jnp.pad(to_blocks(w_down[0]).transpose(1, 0, 2), ((0, 0), (0, FF_LANES - FF_LOCAL), (0, 0)))
    rows_out = run_experts(rows_in.reshape(BLOCKS, N_EXP * CAP, LANES), w_in, w_out)

    summed = lax.psum_scatter(
        rows_out.reshape(BLOCKS * N_EXP * CAP, LANES),
        "attn",
        scatter_dimension=0,
        tiled=True,
        axis_index_groups=Z_GROUPS,
    )
    returned = lax.all_to_all(summed.reshape(N_EXP, CAP, LANES), "exp", 0, 0, tiled=True)
    returned = returned.reshape(N_EXP * CAP, LANES)
    over_slots = (((0,), (0,)), ((), ()))
    mixed = lax.dot_general(mix_high, returned, over_slots, preferred_element_type=F32)
    mixed = mixed + lax.dot_general(mix_low, returned, over_slots, preferred_element_type=F32)
    first_half = attn_index % HALVES == 0
    mixed = mixed + jnp.where(first_half, hidden_state, 0.0)

    last = lax.all_to_all(mixed.reshape(N_ATTN, own_rows, LANES), "attn", 0, 0, tiled=True)
    last = jnp.sum(last.reshape(BLOCKS, HALVES, own_rows, LANES), axis=1)
    return last[:, :, :BLOCK].transpose(1, 0, 2).reshape(own_rows, D).astype(BF16)


def solution(mesh):
    in_specs = (
        P(("exp", "attn"), None),
        P(("exp", "attn"), None),
        P(("exp", "attn"), None, None, None),
        P(("exp", "attn"), None, None),
        P(),
        P("attn", None),
        P(),
        P("exp", None),
        P("exp", None),
        P("exp", None, "attn"),
        P("exp", None, "attn"),
        P("exp", "attn", None),
    )
    out_specs = P(("exp", "attn"), None)
    return jax.shard_map(local, mesh=mesh, in_specs=in_specs, out_specs=out_specs, check_vma=False)
```

time: 753 us -> 320 us (0.42)
  waiting for transfers between devices: 461 us -> 190 us
  blocking collectives: 184 us -> 47 us
  local copies, waits for them, and re-layouts: 37.3 us -> 20.6 us
  other arithmetic: 17.6 us -> 2.06 us
  matrix products: 18.5 us -> 4.54 us
  Pallas kernels: 0 us -> 9.62 us
  starting transfers between devices: 19.5 us -> 28.6 us
    unnamed x4 -> x2, waiting for transfers between devices: 322 us -> 0.03 us
    all_to_all x1 -> x2, blocking collectives: 143 us -> 47 us  [the longest x1 31 us: local(): lax.all_to_all(outgoing, 'exp', 0, 0, tiled=True)]
    all_to_all x2 -> x3, waiting for transfers between devices: 138 us -> 51.7 us  [the longest x1 22.3 us: local(): lax.all_to_all(summed.reshape(N_EXP, CAP, LANES), 'exp', 0, 0, tiled=True)]
    reduce_scatter x0 -> x1, waiting for transfers between devices: none -> 76.7 us  [local(): lax.psum_scatter(rows_out.reshape(BLOCKS * N_EXP * CAP, LANES), 'attn', s...]
    all_gather x0 -> x1, waiting for transfers between devices: none -> 61.2 us  [local(): lax.all_gather(incoming, 'attn', axis=0, tiled=True, axis_index_groups=Z_...]
    all_gather x1 -> x0, blocking collectives: 41.2 us -> none  [local(): column = lax.all_gather(normed, 'attn', axis=0, tiled=True)]
    gather x3 -> x0, local copies, waits for them, and re-layouts: 22.6 us -> none  [the longest x2 16 us: local(): jnp.take(returned.reshape(expert_total * capacity, returned.shape[2]), pl...]
    dot_general x3 -> x5, matrix products: 16.4 us -> 2.72 us  [the longest x1 1.45 us: local(): jnp.einsum('rk,zkd->zrd', got[:, :256], proj, preferred_element_type=F32)]
  transfers between devices with their start and end apart: 4 -> 6, of which waited for: 4 -> 5; matrix products, arithmetic and copies ran while one was open for 1% -> 6% of each run, Pallas kernels for 0% -> 0%
where the time goes in v1:
time: 320 us; the launch traced here: 316 us
  waiting for transfers between devices  190 us (59%)
  blocking collectives  47 us (15%)
  starting transfers between devices  28.6 us (9%)
  local copies, waits for them, and re-layouts  20.6 us (6%)
  between operations  13.8 us (4%)
  Pallas kernels  9.62 us (3%)
  matrix products  4.54 us (1%)
    reduce_scatter x1, waiting for transfers between devices, local(): lax.psum_scatter(rows_out.reshape(BLOCKS * N_EXP * CAP, LANES), 'attn', s...  76.7 us
    all_gather x1, waiting for transfers between devices, local(): lax.all_gather(incoming, 'attn', axis=0, tiled=True, axis_index_groups=Z_...  61.2 us
    all_to_all x1, blocking collectives, local(): lax.all_to_all(outgoing, 'exp', 0, 0, tiled=True)  31 us
    all_to_all x1, waiting for transfers between devices, local(): lax.all_to_all(summed.reshape(N_EXP, CAP, LANES), 'exp', 0, 0, tiled=True)  22.3 us
    all_to_all x1, waiting for transfers between devices, local(): lax.all_to_all(partial_sums, 'attn', 0, 0, tiled=True, axis_index_groups=...  20.7 us
    all_to_all x1, blocking collectives, local(): lax.all_to_all(mixed.reshape(N_ATTN, own_rows, LANES), 'attn', 0, 0, tile...  16 us
    all_to_all x1, starting transfers between devices, local(): lax.all_to_all(sent.reshape(N_ATTN, own_rows, 256 + LANES), 'attn', 0, 0,...  13.3 us
    unnamed x36, local copies, waits for them, and re-layouts  10.3 us
  transfers between devices with their start and end apart: 6, of which 5 were waited for; matrix products, arithmetic and copies ran while one was open for 6% of the time, Pallas kernels for 0%

profile of v1, /device:TPU:6, one launch (start us, length us, event | category | flops | bytes accessed | tf_op | source)
XLA Modules:
  0.0 315.9 jit_solution(1422523430956557249)
XLA Ops:
  6.5 3.3 %collective-permute-start = (bf16[128,2880]{0,1:T(8,128)(2,1)}, bf16[128,2880]{0,1:T(8,128)(2,1)S(1)}, u32[]{:S(2)}, u32[]{:S(2)}) collective-permute-start(bf16[128,2880]{0,1:T(8,128)(2,1)} %param.17), channel_id=1, source_target_pairs={{0,32},{32,0},{64,96},{96,64},{128,160},{160,128},{192,224},{224,1... | collective-permute-start | bytes 2211848 | tf_op jit(solution)/shard_map/ppermute | solution.py:112
  9.8 0.8 fusion.48
  10.7 1.1 copy.61
  11.8 2.0 fusion.47
  13.8 0.4 copy.73
  14.2 0.3 copy-done.10
  14.6 0.1 reshape.102
  14.8 1.4 fusion.50
  16.2 0.2 fusion.31
  16.4 0.3 copy.64
  16.7 0.1 copy-done.7
  16.9 0.4 copy.75
  17.3 0.5 copy-done.8
  17.8 0.4 convolution_convert_fusion.1
  18.4 0.2 rev.3
  18.6 0.1 reshape.103
  18.8 0.7 pad_maximum_fusion.1
  19.4 13.3 %all-to-all-start = ((bf16[16,8,640]{2,1,0:T(8,128)(2,1)}), bf16[16,8,640]{2,1,0:T(8,128)(2,1)S(1)}, u32[]{:S(2)}, u32[]{:S(2)}) async-start(bf16[16,8,640]{2,1,0:T(8,128)(2,1)} %bitcast.8), calls=%async_computation | async-start | bytes 327680 | tf_op jit(solution)/shard_map/all_to_all | solution.py:119
  32.7 0.2 pad_maximum_fusion
  32.9 8.6 %all-to-all-done = bf16[16,8,640]{2,1,0:T(8,128)(2,1)S(1)} async-done(((bf16[16,8,640]{2,1,0:T(8,128)(2,1)}), bf16[16,8,640]{2,1,0:T(8,128)(2,1)S(1)}, u32[]{:S(2)}, u32[]{:S(2)}) %all-to-all-start) | async-done | bytes 163872 | tf_op jit(solution)/shard_map/all_to_all | solution.py:119
  41.5 1.4 fusion.9
  43.0 3.5 %all-to-all-start.1 = ((bf16[8,128,384]{1,2,0:T(8,128)(2,1)}), bf16[8,128,384]{1,2,0:T(8,128)(2,1)S(1)}, u32[]{:S(2)}, u32[]{:S(2)}) async-start(bf16[8,128,384]{1,2,0:T(8,128)(2,1)} %fusion.9), calls=%async_computation.1 | async-start | bytes 1572864 | tf_op jit(solution)/shard_map/all_to_all | solution.py:124
  46.8 0.1 fusion.16
  46.9 0.2 bitcast_compare_fusion
  47.2 20.7 %all-to-all-done.1 = bf16[8,128,384]{1,2,0:T(8,128)(2,1)S(1)} async-done(((bf16[8,128,384]{1,2,0:T(8,128)(2,1)}), bf16[8,128,384]{1,2,0:T(8,128)(2,1)S(1)}, u32[]{:S(2)}, u32[]{:S(2)}) %all-to-all-start.1) | async-done | bytes 786464 | tf_op jit(solution)/shard_map/all_to_all | solution.py:124
  68.0 0.1 copy.68
  68.3 0.5 convolution_convert_fusion
  68.8 31.0 %all_to_all.25 = bf16[32,32,384]{2,1,0:T(8,128)(2,1)} all-to-all(bf16[32,32,384]{2,1,0:T(8,128)(2,1)S(1)} %bitcast.73), channel_id=1, replica_groups=mesh['attn'=16,'exp'=32] {'exp'}, dimensions={0} | all-to-all | bytes 1572864 | tf_op jit(solution)/shard_map/all_to_all | solution.py:151
  99.8 1.7 copy.69
  101.5 1.6 copy.70
  103.2 2.8 reshape_squeeze.3
  106.0 0.1 copy.71
  106.1 0.1 pad_bitcast_fusion
  106.3 1.3 pad.33.w_out_ref
  107.6 0.5 copy-done.3
  108.1 0.5 copy-done.2
  108.6 0.5 fusion.2.w_in_ref
  109.1 61.2 %all-gather.2.cloned.1.call-done = bf16[8192,384]{1,0:T(8,128)(2,1)} async-done(((bf16[1024,384]{1,0:T(8,128)(2,1)}), bf16[8192,384]{1,0:T(8,128)(2,1)}) %all-gather.2.cloned.1.call-update) | async-done | bytes 6291472 | tf_op jit(solution)/shard_map/all_gather | solution.py:152
  170.3 1.4 copy-done.1
  171.7 9.6 %shard_map.118 = bf16[8,1024,384]{2,1,0:T(8,128)(2,1)S(1)} custom-call(bf16[8,1024,384]{2,1,0:T(8,128)(2,1)} %bitcast.68, bf16[8,384,512]{2,1,0:T(8,128)(2,1)S(1)} %fusion.2.w_in_ref, bf16[8,256,384]{2,1,0:T(8,128)(2,1)S(1)} %copy-done.1), custom_call_target="tpu_custom_call" | custom-call | flops 3185049600 | bytes 18874368 | tf_op jit(solution)/shard_map/pallas_call | solution.py:71
  181.4 2.6 copy-done
  184.0 76.7 %reduce-scatter.2.cloned.1.call-done = bf16[1024,384]{1,0:T(8,128)(2,1)} async-done(((bf16[8192,384]{1,0:T(8,128)(2,1)}), bf16[1024,384]{1,0:T(8,128)(2,1)}) %reduce-scatter.2.cloned.1.call-update) | async-done | bytes 786448 | tf_op jit(solution)/shard_map/reduce_scatter | solution.py:162
  260.8 8.4 %all-to-all-start.3 = ((bf16[32,32,384]{2,1,0:T(8,128)(2,1)}), bf16[32,32,384]{2,1,0:T(8,128)(2,1)S(1)}, u32[]{:S(2)}, u32[]{:S(2)}) async-start(bf16[32,32,384]{2,1,0:T(8,128)(2,1)} %bitcast.78), calls=%async_computation.4 | async-start | bytes 1572864 | tf_op jit(solution)/shard_map/all_to_all | solution.py:169
  269.2 22.3 %all-to-all-done.3 = bf16[32,32,384]{2,1,0:T(8,128)(2,1)S(1)} async-done(((bf16[32,32,384]{2,1,0:T(8,128)(2,1)}), bf16[32,32,384]{2,1,0:T(8,128)(2,1)S(1)}, u32[]{:S(2)}, u32[]{:S(2)}) %all-to-all-start.3) | async-done | bytes 786464 | tf_op jit(solution)/shard_map/all_to_all | solution.py:169
  291.5 0.3 convolution_bitcast_fusion
  291.9 0.3 fusion.15
  292.2 16.0 %all_to_all.26 = f32[16,8,384]{2,1,0:T(8,128)S(1)} all-to-all(f32[16,8,384]{2,1,0:T(8,128)S(1)} %fusion.15), channel_id=1, replica_groups=mesh['attn'=16,'exp'=32] {'attn'}, dimensions={0} | all-to-all | bytes 393216 | tf_op jit(solution)/shard_map/all_to_all | solution.py:177
  308.3 0.7 convert_element_type.75
  (53 shorter events, 0.9 us)
Async XLA Ops:
  6.5 26.2 %collective-permute-start = (bf16[128,2880]{0,1:T(8,128)(2,1)}, bf16[128,2880]{0,1:T(8,128)(2,1)S(1)}, u32[]{:S(2)}, u32[]{:S(2)}) collective-permute-start(bf16[128,2880]{0,1:T(8,128)(2,1)} %param.17), channel_id=1, source_target_pairs={{0,32},{32,0},{64,96},{96,64},{128,160},{160,128},{192,224},{224,1... | collective-permute-start | bytes 2211848 | tf_op jit(solution)/shard_map/ppermute | solution.py:112
  13.8 0.8 copy-start.10
  13.8 0.9 copy-start.14
  16.2 0.7 copy-start.7
  16.9 0.9 copy-start.8
  17.3 1.3 copy-start.9
  17.8 14.9 %copy-start.6 = (bf16[128,2880]{0,1:T(8,128)(2,1)S(1)}, bf16[128,2880]{0,1:T(8,128)(2,1)}, u32[]{:S(2)}) copy-start(bf16[128,2880]{0,1:T(8,128)(2,1)} %param.17) | copy-start | bytes 2211844
  19.4 22.1 %all-to-all-start = ((bf16[16,8,640]{2,1,0:T(8,128)(2,1)}), bf16[16,8,640]{2,1,0:T(8,128)(2,1)S(1)}, u32[]{:S(2)}, u32[]{:S(2)}) async-start(bf16[16,8,640]{2,1,0:T(8,128)(2,1)} %bitcast.8), calls=%async_computation | async-start | bytes 327680 | tf_op jit(solution)/shard_map/all_to_all | solution.py:119
  41.5 5.1 %copy-start.11 = (f32[2880]{0:T(1024)S(1)}, f32[2880]{0:T(1024)}, u32[]{:S(2)}) copy-start(f32[2880]{0:T(1024)} %param.18) | copy-start | bytes 34564
  41.5 5.2 %copy-start.12 = (s32[128,4]{0,1:T(4,128)S(1)}, s32[128,4]{0,1:T(4,128)}, u32[]{:S(2)}) copy-start(s32[128,4]{0,1:T(4,128)} %param.19) | copy-start | bytes 6148
  43.0 24.9 %all-to-all-start.1 = ((bf16[8,128,384]{1,2,0:T(8,128)(2,1)}), bf16[8,128,384]{1,2,0:T(8,128)(2,1)S(1)}, u32[]{:S(2)}, u32[]{:S(2)}) async-start(bf16[8,128,384]{1,2,0:T(8,128)(2,1)} %fusion.9), calls=%async_computation.1 | async-start | bytes 1572864 | tf_op jit(solution)/shard_map/all_to_all | solution.py:124
  46.5 123.8 %all-gather.2.cloned.1.call-start = ((), (), s32[]{:S(2)}) async-start(), calls=%async_computation.6 | async-start | bytes 7077888 | tf_op jit(solution)/shard_map/all_gather | solution.py:152
  68.3 31.5 %copy-start.4 = (bf16[1,2880,180]{1,2,0:T(8,128)(2,1)S(1)}, bf16[1,2880,180]{1,2,0:T(8,128)(2,1)}, u32[]{:S(2)}) copy-start(bf16[1,2880,180]{1,2,0:T(8,128)(2,1)} %param.21) | copy-start | bytes 3110404
  99.7 1.8 copy-start.5
  99.7 161.0 %reduce-scatter.2.cloned.1.call-start = ((), (), s32[]{:S(2)}) async-start(), calls=%async_computation.7 | async-start | bytes 7077888 | tf_op jit(solution)/shard_map/reduce_scatter | solution.py:162
  106.1 2.0 copy-start.3
  106.3 2.3 copy-start.2
  170.3 1.4 copy-start.1
  181.3 2.7 copy-start
  184.0 85.1 %copy-start.13 = (f32[128,4]{0,1:T(4,128)S(1)}, f32[128,4]{0,1:T(4,128)}, u32[]{:S(2)}) copy-start(f32[128,4]{0,1:T(4,128)} %param.20) | copy-start | bytes 6148
  260.8 30.7 %all-to-all-start.3 = ((bf16[32,32,384]{2,1,0:T(8,128)(2,1)}), bf16[32,32,384]{2,1,0:T(8,128)(2,1)S(1)}, u32[]{:S(2)}, u32[]{:S(2)}) async-start(bf16[32,32,384]{2,1,0:T(8,128)(2,1)} %bitcast.78), calls=%async_computation.4 | async-start | bytes 1572864 | tf_op jit(solution)/shard_map/all_to_all | solution.py:169
Sparse Core Ops, SparseCore 0:
  99.9 70.4 all-gather.1
  184.1 76.5 reduce-scatter.1

commit v2 on v1

--- a/solution.py
+++ b/solution.py
@@ -1,8 +1,6 @@
 import jax
 import jax.numpy as jnp
 from jax import lax
-from jax.experimental import pallas as pl
-from jax.experimental.pallas import tpu as pltpu
 from jax.sharding import PartitionSpec as P
 
 HEAD_SIZE = 64
@@ -18,7 +16,7 @@
 BLOCK = D // BLOCKS
 LANES = 384
 FF_LANES = 256
-ROW_TILE = 256
+FAR = BLOCKS // 2
 F32 = jnp.float32
 BF16 = jnp.bfloat16
 
@@ -49,40 +47,11 @@
     return combined.reshape(count_of_rows, QUERY_HEADS * HEAD_SIZE).astype(jnp.bfloat16)
 
 
-def experts_kernel(x_ref, w_in_ref, w_out_ref, y_ref):
-    square = jnp.zeros((ROW_TILE, 1), F32)
-    both = jnp.zeros((ROW_TILE, 2 * FF_LANES), F32)
-    for block in range(BLOCKS):
-        x = x_ref[block]
-        parts = x[:, LANES - 128 :].astype(F32)
-        at = BLOCK - (LANES - 128)
-        square = square + parts[:, at : at + 1] + parts[:, at + 1 : at + 2]
-        both = both + jnp.dot(x, w_in_ref[block], preferred_element_type=F32)
-    both = both * lax.rsqrt(square * (1.0 / D) + 1e-05)
-    gate = both[:, :FF_LANES]
-    up = both[:, FF_LANES:]
-    hidden = (gate * jax.nn.sigmoid(1.702 * gate) * (up + 1.0)).astype(BF16)
-    for block in range(BLOCKS):
-        y_ref[block] = jnp.dot(hidden, w_out_ref[block], preferred_element_type=F32).astype(BF16)
-
-
-def run_experts(x, w_in, w_out):
-    rows = x.shape[1]
-    return pl.pallas_call(
-        experts_kernel,
-        grid=(rows // ROW_TILE,),
-        in_specs=[
-            pl.BlockSpec((BLOCKS, ROW_TILE, LANES), lambda i: (0, i, 0)),
-            pl.BlockSpec((BLOCKS, LANES, 2 * FF_LANES), lambda i: (0, 0, 0)),
-            pl.BlockSpec((BLOCKS, FF_LANES, LANES), lambda i: (0, 0, 0)),
-        ],
-        out_specs=pl.BlockSpec((BLOCKS, ROW_TILE, LANES), lambda i: (0, i, 0)),
-        out_shape=jax.ShapeDtypeStruct((BLOCKS, rows, LANES), BF16),
-        compiler_params=pltpu.CompilerParams(vmem_limit_bytes=40 * 2**20),
-        cost_estimate=pl.CostEstimate(
-            flops=2 * rows * D * 3 * FF_LOCAL, bytes_accessed=18 * 2**20, transcendentals=rows * FF_LOCAL
-        ),
-    )(x, w_in, w_out)
+def shift_over_z(array, step):
+    pairs = [
+        (z * HALVES + half, (z + step) % BLOCKS * HALVES + half) for z in range(BLOCKS) for half in range(HALVES)
+    ]
+    return lax.ppermute(array, "attn", pairs)
 
 
 def to_blocks(array):
@@ -146,31 +115,59 @@
     mix_low = (mix - mix_high).astype(BF16)
     mix_high = mix_high.astype(BF16)
 
-    outgoing = jnp.dot(select, scaled, preferred_element_type=F32).astype(BF16)
-    outgoing = outgoing.reshape(N_EXP, CAP, LANES)
-    incoming = lax.all_to_all(outgoing, "exp", 0, 0, tiled=True).reshape(N_EXP * CAP, LANES)
-    rows_in = lax.all_gather(incoming, "attn", axis=0, tiled=True, axis_index_groups=Z_GROUPS)
+    def dispatch(rows):
+        outgoing = jnp.dot(select, rows, preferred_element_type=F32).astype(BF16)
+        incoming = lax.all_to_all(outgoing.reshape(N_EXP, CAP, LANES), "exp", 0, 0, tiled=True)
+        return incoming.reshape(N_EXP * CAP, LANES)
+
+    def collect(partial_value):
+        returned = lax.all_to_all(partial_value.reshape(N_EXP, CAP, LANES), "exp", 0, 0, tiled=True)
+        returned = returned.reshape(N_EXP * CAP, LANES)
+        over_slots = (((0,), (0,)), ((), ()))
+        mixed = lax.dot_general(mix_high, returned, over_slots, preferred_element_type=F32)
+        return mixed + lax.dot_general(mix_low, returned, over_slots, preferred_element_type=F32)
 
     def padded_in(w):
         w = w.reshape(BLOCKS, BLOCK, FF_LOCAL)
         return jnp.pad(w, ((0, 0), (0, LANES - BLOCK), (0, FF_LANES - FF_LOCAL)))
 
+    def own_first(blocks):
+        return lax.dynamic_slice_in_dim(jnp.concatenate([blocks, blocks]), z_index, BLOCKS, 0)
+
     w_in = jnp.concatenate([padded_in(w_gate), padded_in(w_up)], axis=2)
+    in_row = lax.broadcasted_iota(jnp.int32, w_in.shape, 1)
+    in_column = lax.broadcasted_iota(jnp.int32, w_in.shape, 2)
+    w_in = jnp.where((in_column == FF_LOCAL) & (in_row >= BLOCK) & (in_row < BLOCK + 2), jnp.ones((), BF16), w_in)
+    w_in = own_first(w_in)
     w_out = jnp.pad(to_blocks(w_down[0]).transpose(1, 0, 2), ((0, 0), (0, FF_LANES - FF_LOCAL), (0, 0)))
-    rows_out = run_experts(rows_in.reshape(BLOCKS, N_EXP * CAP, LANES), w_in, w_out)
+    w_out = own_first(w_out)
 
-    summed = lax.psum_scatter(
-        rows_out.reshape(BLOCKS * N_EXP * CAP, LANES),
-        "attn",
-        scatter_dimension=0,
-        tiled=True,
-        axis_index_groups=Z_GROUPS,
-    )
-    returned = lax.all_to_all(summed.reshape(N_EXP, CAP, LANES), "exp", 0, 0, tiled=True)
-    returned = returned.reshape(N_EXP * CAP, LANES)
-    over_slots = (((0,), (0,)), ((), ()))
-    mixed = lax.dot_general(mix_high, returned, over_slots, preferred_element_type=F32)
-    mixed = mixed + lax.dot_general(mix_low, returned, over_slots, preferred_element_type=F32)
+    own = dispatch(scaled)
+    far = dispatch(shift_over_z(scaled, FAR))
+    both = jnp.dot(own, w_in[0], preferred_element_type=F32)
+    up_block, down_block = own, own
+    for step in range(1, FAR):
+        up_block, down_block = shift_over_z(up_block, 1), shift_over_z(down_block, -1)
+        both = both + jnp.dot(up_block, w_in[BLOCKS - step], preferred_element_type=F32)
+        both = both + jnp.dot(down_block, w_in[step], preferred_element_type=F32)
+        if step == FAR - 2:
+            both = lax.optimization_barrier(both + jnp.dot(far, w_in[FAR], preferred_element_type=F32))
+    both = both * lax.rsqrt(both[:, FF_LOCAL : FF_LOCAL + 1] * (1.0 / D) + 1e-05)
+    gate = both[:, :FF_LANES]
+    up = both[:, FF_LANES:]
+    expert_hidden = (gate * jax.nn.sigmoid(1.702 * gate) * (up + 1.0)).astype(BF16)
+
+    def output_block(offset):
+        return jnp.dot(expert_hidden, w_out[offset % BLOCKS], preferred_element_type=F32)
+
+    up_sum = shift_over_z(output_block(FAR - 1).astype(BF16), 1)
+    down_sum = shift_over_z(output_block(1 - FAR).astype(BF16), -1)
+    far_sum = collect(output_block(FAR).astype(BF16))
+    for offset in range(FAR - 2, 0, -1):
+        up_sum = shift_over_z((output_block(offset) + up_sum.astype(F32)).astype(BF16), 1)
+        down_sum = shift_over_z((output_block(-offset) + down_sum.astype(F32)).astype(BF16), -1)
+    own_sum = (output_block(0) + up_sum.astype(F32) + down_sum.astype(F32)).astype(BF16)
+    mixed = collect(own_sum) + shift_over_z(far_sum, FAR)
     first_half = attn_index % HALVES == 0
     mixed = mixed + jnp.where(first_half, hidden_state, 0.0)
 

time: 320 us -> 302 us (0.944)
  starting transfers between devices: 28.6 us -> 100 us
  waiting for transfers between devices: 190 us -> 121 us
  blocking collectives: 47 us -> 16.8 us
  matrix products: 4.54 us -> 30.1 us
  between operations: 13.8 us -> 0.79 us
  Pallas kernels: 9.62 us -> 0 us
  other arithmetic: 2.06 us -> 7.4 us
    reduce_scatter x1 -> x0, waiting for transfers between devices: 76.7 us -> none  [local(): lax.psum_scatter(rows_out.reshape(BLOCKS * N_EXP * CAP, LANES), 'attn', s...]
    ppermute x0 -> x14, waiting for transfers between devices: none -> 67.9 us  [shift_over_z(): return lax.ppermute(array, 'attn', pairs)]
    all_gather x1 -> x0, waiting for transfers between devices: 61.2 us -> none  [local(): lax.all_gather(incoming, 'attn', axis=0, tiled=True, axis_index_groups=Z_...]
    ppermute x0 -> x14, starting transfers between devices: none -> 49.3 us  [shift_over_z(): return lax.ppermute(array, 'attn', pairs)]
    all_to_all x1 -> x0, blocking collectives: 31 us -> none  [local(): lax.all_to_all(outgoing, 'exp', 0, 0, tiled=True)]
    dot_general x3 -> x22, matrix products: 1.14 us -> 25.3 us  [the longest x8 8.52 us: output_block(): jnp.dot(expert_hidden, w_out[offset % BLOCKS], preferred_element_type=F32)]
    all_to_all x1 -> x4, starting transfers between devices: 8.36 us -> 31 us  [the longest x2 16.7 us: collect(): lax.all_to_all(partial_value.reshape(N_EXP, CAP, LANES), 'exp', 0, 0, til...]
    pallas_call x1 -> x0, Pallas kernels: 9.62 us -> none  [run_experts(): pl.pallas_call(experts_kernel, grid=(rows // ROW_TILE,), in_specs=[pl.Blo...]
  transfers between devices with their start and end apart: 6 -> 21, of which waited for: 5 -> 14; matrix products, arithmetic and copies ran while one was open for 6% -> 17% of each run, Pallas kernels for 0% -> 0%
where the time goes in v2:
time: 302 us; the launch traced here: 297 us
  waiting for transfers between devices  121 us (40%)
  starting transfers between devices  100 us (33%)
  matrix products  30.1 us (10%)
  local copies, waits for them, and re-layouts  20.4 us (7%)
  blocking collectives  16.8 us (6%)
  other arithmetic  7.4 us (2%)
    ppermute x14, waiting for transfers between devices, shift_over_z(): return lax.ppermute(array, 'attn', pairs)  67.9 us
    ppermute x14, starting transfers between devices, shift_over_z(): return lax.ppermute(array, 'attn', pairs)  49.3 us
    all_to_all x1, waiting for transfers between devices, local(): lax.all_to_all(partial_sums, 'attn', 0, 0, tiled=True, axis_index_groups=...  20.8 us
    all_to_all x2, waiting for transfers between devices, collect(): lax.all_to_all(partial_value.reshape(N_EXP, CAP, LANES), 'exp', 0, 0, til...  18.1 us
    all_to_all x1, blocking collectives, local(): lax.all_to_all(mixed.reshape(N_ATTN, own_rows, LANES), 'attn', 0, 0, tile...  16.8 us
    all_to_all x2, starting transfers between devices, collect(): lax.all_to_all(partial_value.reshape(N_EXP, CAP, LANES), 'exp', 0, 0, til...  16.7 us
    all_to_all x2, starting transfers between devices, dispatch(): lax.all_to_all(outgoing.reshape(N_EXP, CAP, LANES), 'exp', 0, 0, tiled=True)  14.2 us
    all_to_all x1, starting transfers between devices, local(): lax.all_to_all(sent.reshape(N_ATTN, own_rows, 256 + LANES), 'attn', 0, 0,...  13.3 us
  transfers between devices with their start and end apart: 21, of which 14 were waited for; matrix products, arithmetic and copies ran while one was open for 17% of the time, Pallas kernels for 0%

profile of v2, /device:TPU:6, one launch (start us, length us, event | category | flops | bytes accessed | tf_op | source)
XLA Modules:
  0.0 296.9 jit_solution(14267647894647893232)
XLA Ops:
  0.0 3.3 %collective-permute-start = (bf16[128,2880]{0,1:T(8,128)(2,1)}, bf16[128,2880]{0,1:T(8,128)(2,1)S(1)}, u32[]{:S(2)}, u32[]{:S(2)}) collective-permute-start(bf16[128,2880]{0,1:T(8,128)(2,1)} %param.17), channel_id=1, source_target_pairs={{0,32},{32,0},{64,96},{96,64},{128,160},{160,128},{192,224},{224,1... | collective-permute-start | bytes 2211848 | tf_op jit(solution)/shard_map/ppermute | solution.py:81
  5.3 2.1 fusion.94
  12.8 1.7 convolution_convert_fusion.5
  15.7 13.3 %all-to-all-start = ((bf16[16,8,640]{2,1,0:T(8,128)(2,1)}), bf16[16,8,640]{2,1,0:T(8,128)(2,1)S(1)}, u32[]{:S(2)}, u32[]{:S(2)}) async-start(bf16[16,8,640]{2,1,0:T(8,128)(2,1)} %bitcast.8), calls=%async_computation | async-start | bytes 327680 | tf_op jit(solution)/shard_map/all_to_all | solution.py:88
  29.2 8.6 %all-to-all-done = bf16[16,8,640]{2,1,0:T(8,128)(2,1)S(1)} async-done(((bf16[16,8,640]{2,1,0:T(8,128)(2,1)}), bf16[16,8,640]{2,1,0:T(8,128)(2,1)S(1)}, u32[]{:S(2)}, u32[]{:S(2)}) %all-to-all-start) | async-done | bytes 163872 | tf_op jit(solution)/shard_map/all_to_all | solution.py:88
  39.2 3.5 %all-to-all-start.1 = ((bf16[8,128,384]{1,2,0:T(8,128)(2,1)}), bf16[8,128,384]{1,2,0:T(8,128)(2,1)S(1)}, u32[]{:S(2)}, u32[]{:S(2)}) async-start(bf16[8,128,384]{1,2,0:T(8,128)(2,1)} %fusion.11), calls=%async_computation.1 | async-start | bytes 1572864 | tf_op jit(solution)/shard_map/all_to_all | solution.py:93
  43.4 20.8 %all-to-all-done.1 = bf16[8,128,384]{1,2,0:T(8,128)(2,1)S(1)} async-done(((bf16[8,128,384]{1,2,0:T(8,128)(2,1)}), bf16[8,128,384]{1,2,0:T(8,128)(2,1)S(1)}, u32[]{:S(2)}, u32[]{:S(2)}) %all-to-all-start.1) | async-done | bytes 786464 | tf_op jit(solution)/shard_map/all_to_all | solution.py:93
  65.9 8.7 %all-to-all-start.2 = ((bf16[32,32,384]{2,1,0:T(8,128)(2,1)}), bf16[32,32,384]{2,1,0:T(8,128)(2,1)S(1)}, u32[]{:S(2)}, u32[]{:S(2)}) async-start(bf16[32,32,384]{2,1,0:T(8,128)(2,1)} %bitcast.14), calls=%async_computation.2 | async-start | bytes 1572864 | tf_op jit(solution)/shard_map/all_to_all | solution.py:120
  74.6 2.8 reshape_squeeze.3
  77.7 2.4 collective-permute-start.5
  81.3 9.0 %collective-permute-done.5 = bf16[128,384]{1,0:T(8,128)(2,1)S(1)} collective-permute-done((bf16[128,384]{1,0:T(8,128)(2,1)S(1)}, bf16[128,384]{1,0:T(8,128)(2,1)S(1)}, u32[]{:S(2)}, u32[]{:S(2)}) %collective-permute-start.5) | collective-permute-done | bytes 98336 | tf_op jit(solution)/shard_map/ppermute | solution.py:54
  91.5 5.5 %all-to-all-done.2 = bf16[32,32,384]{2,1,0:T(8,128)(2,1)S(1)} async-done(((bf16[32,32,384]{2,1,0:T(8,128)(2,1)}), bf16[32,32,384]{2,1,0:T(8,128)(2,1)S(1)}, u32[]{:S(2)}, u32[]{:S(2)}) %all-to-all-start.2) | async-done | bytes 786464 | tf_op jit(solution)/shard_map/all_to_all | solution.py:120
  97.0 5.5 %all-to-all-start.3 = ((bf16[32,32,384]{2,1,0:T(8,128)(2,1)}), bf16[32,32,384]{2,1,0:T(8,128)(2,1)}, u32[]{:S(2)}, u32[]{:S(2)}) async-start(bf16[32,32,384]{2,1,0:T(8,128)(2,1)} %bitcast.23), calls=%async_computation.3 | async-start | bytes 1572864 | tf_op jit(solution)/shard_map/all_to_all | solution.py:120
  102.5 3.7 %fusion.93 = (bf16[1,256,384]{2,0,1:T(2,128)(2,1)}, bf16[1,256,384]{2,0,1:T(2,128)(2,1)}, bf16[1,256,384]{2,0,1:T(2,128)(2,1)}, bf16[1,256,384]{2,0,1:T(2,128)(2...) fusion(bf16[8,256,384]{2,0,1:T(8,128)(2,1)S(1)} %fusion.4), kind=kLoop, calls=%fused_computation.151 | loop fusion | bytes 3145728 | tf_op jit(solution)/shard_map/slice | solution.py:161
  106.2 1.9 copy.85
  108.1 2.0 copy.86
  110.1 2.4 collective-permute-start.1
  112.5 4.8 %collective-permute-start.2 = (bf16[1024,384]{1,0:T(8,128)(2,1)}, bf16[1024,384]{1,0:T(8,128)(2,1)}, u32[]{:S(2)}, u32[]{:S(2)}) collective-permute-start(bf16[1024,384]{1,0:T(8,128)(2,1)} %bitcast.157), channel_id=1, source_target_pairs={{0,448},{32,480},{64,0},{96,32},{128,64},{160,96},{192,128},{224,1... | collective-permute-start | bytes 2359304 | tf_op jit(solution)/shard_map/ppermute | solution.py:54
  119.5 2.0 fusion.40
  121.5 11.6 %collective-permute-done.1 = bf16[1024,384]{1,0:T(8,128)(2,1)} collective-permute-done((bf16[1024,384]{1,0:T(8,128)(2,1)}, bf16[1024,384]{1,0:T(8,128)(2,1)}, u32[]{:S(2)}, u32[]{:S(2)}) %collective-permute-start.1) | collective-permute-done | bytes 786464 | tf_op jit(solution)/shard_map/ppermute | solution.py:54
  133.1 1.9 collective-permute-start.3
  135.0 5.1 %collective-permute-start.4 = (bf16[1024,384]{1,0:T(8,128)(2,1)}, bf16[1024,384]{1,0:T(8,128)(2,1)}, u32[]{:S(2)}, u32[]{:S(2)}) collective-permute-start(bf16[1024,384]{1,0:T(8,128)(2,1)} %collective-permute-done.2), channel_id=1, source_target_pairs={{0,448},{32,480},{64,0},{96,32},{128,64},{160,96},{192,128},{224,1... | collective-permute-start | bytes 2359304 | tf_op jit(solution)/shard_map/ppermute | solution.py:54
  140.2 1.8 fusion.35
  142.0 1.8 fusion.38
  143.9 1.8 fusion.39
  145.7 9.6 %collective-permute-done.3 = bf16[1024,384]{1,0:T(8,128)(2,1)} collective-permute-done((bf16[1024,384]{1,0:T(8,128)(2,1)}, bf16[1024,384]{1,0:T(8,128)(2,1)}, u32[]{:S(2)}, u32[]{:S(2)}) %collective-permute-start.3) | collective-permute-done | bytes 786464 | tf_op jit(solution)/shard_map/ppermute | solution.py:54
  155.3 1.9 collective-permute-start.6
  157.2 5.1 %collective-permute-start.7 = (bf16[1024,384]{1,0:T(8,128)(2,1)}, bf16[1024,384]{1,0:T(8,128)(2,1)S(1)}, u32[]{:S(2)}, u32[]{:S(2)}) collective-permute-start(bf16[1024,384]{1,0:T(8,128)(2,1)} %collective-permute-done.4), channel_id=1, source_target_pairs={{0,448},{32,480},{64,0},{96,32},{128,64},{160,96},{192,128},{224,1... | collective-permute-start | bytes 2359304 | tf_op jit(solution)/shard_map/ppermute | solution.py:54
  162.4 1.8 fusion.37
  164.2 2.1 add_add_fusion.1
  166.3 10.1 %collective-permute-done.6 = bf16[1024,384]{1,0:T(8,128)(2,1)S(1)} collective-permute-done((bf16[1024,384]{1,0:T(8,128)(2,1)}, bf16[1024,384]{1,0:T(8,128)(2,1)S(1)}, u32[]{:S(2)}, u32[]{:S(2)}) %collective-permute-start.6) | collective-permute-done | bytes 786464 | tf_op jit(solution)/shard_map/ppermute | solution.py:54
  181.4 1.9 collective-permute-start.8
  184.7 5.5 %collective-permute-start.11 = (bf16[1024,384]{1,0:T(8,128)(2,1)}, bf16[1024,384]{1,0:T(8,128)(2,1)}, u32[]{:S(2)}, u32[]{:S(2)}) collective-permute-start(bf16[1024,384]{1,0:T(8,128)(2,1)} %convolution_convert_fusion.1), channel_id=1, source_target_pairs={{0,448},{32,480},{64,0},{96,32},{128,64},{160,96},{192,128},{224,1... | collective-permute-start | bytes 2359304 | tf_op jit(solution)/shard_map/ppermute | solution.py:54
  191.5 8.5 %all-to-all-start.5 = ((bf16[32,32,384]{2,1,0:T(8,128)(2,1)}), bf16[32,32,384]{2,1,0:T(8,128)(2,1)S(1)}, u32[]{:S(2)}, u32[]{:S(2)}) async-start(bf16[32,32,384]{2,1,0:T(8,128)(2,1)} %bitcast.32), calls=%async_computation.5 | async-start | bytes 1572864 | tf_op jit(solution)/shard_map/all_to_all | solution.py:124
  200.0 2.1 collective-permute-done.8
  202.1 1.6 add_convert_fusion.4
  203.7 1.9 collective-permute-start.9
  205.7 1.6 add_convert_fusion.2
  207.3 5.1 %collective-permute-start.12 = (bf16[1024,384]{1,0:T(8,128)(2,1)S(1)}, bf16[1024,384]{1,0:T(8,128)(2,1)S(1)}, u32[]{:S(2)}, u32[]{:S(2)}) collective-permute-start(bf16[1024,384]{1,0:T(8,128)(2,1)S(1)} %add_convert_fusion.2), channel_id=1, source_target_pairs={{0,448},{32,480},{64,0},{96,32},{128,64},{160,96},{192,128},{224,1... | collective-permute-start | bytes 2359304 | tf_op jit(solution)/shard_map/ppermute | solution.py:54
  213.3 11.0 %collective-permute-done.9 = bf16[1024,384]{1,0:T(8,128)(2,1)S(1)} collective-permute-done((bf16[1024,384]{1,0:T(8,128)(2,1)S(1)}, bf16[1024,384]{1,0:T(8,128)(2,1)S(1)}, u32[]{:S(2)}, u32[]{:S(2)}) %collective-permute-start.9) | collective-permute-done | bytes 786464 | tf_op jit(solution)/shard_map/ppermute | solution.py:54
  224.5 2.1 collective-permute-start.10
  227.3 5.6 %collective-permute-start.13 = (bf16[1024,384]{1,0:T(8,128)(2,1)S(1)}, bf16[1024,384]{1,0:T(8,128)(2,1)S(1)}, u32[]{:S(2)}, u32[]{:S(2)}) collective-permute-start(bf16[1024,384]{1,0:T(8,128)(2,1)S(1)} %add_convert_fusion.1), channel_id=1, source_target_pairs={{0,448},{32,480},{64,0},{96,32},{128,64},{160,96},{192,128},{224,1... | collective-permute-start | bytes 2359304 | tf_op jit(solution)/shard_map/ppermute | solution.py:54
  233.4 10.9 %collective-permute-done.10 = bf16[1024,384]{1,0:T(8,128)(2,1)S(1)} collective-permute-done((bf16[1024,384]{1,0:T(8,128)(2,1)S(1)}, bf16[1024,384]{1,0:T(8,128)(2,1)S(1)}, u32[]{:S(2)}, u32[]{:S(2)}) %collective-permute-start.10) | collective-permute-done | bytes 786464 | tf_op jit(solution)/shard_map/ppermute | solution.py:54
  244.3 2.4 collective-permute-done.13
  247.9 8.3 %all-to-all-start.4 = ((bf16[32,32,384]{2,1,0:T(8,128)(2,1)}), bf16[32,32,384]{2,1,0:T(8,128)(2,1)S(1)}, u32[]{:S(2)}, u32[]{:S(2)}) async-start(bf16[32,32,384]{2,1,0:T(8,128)(2,1)} %bitcast.29), calls=%async_computation.4 | async-start | bytes 1572864 | tf_op jit(solution)/shard_map/all_to_all | solution.py:124
  256.9 3.5 %collective-permute-start.14 = (f32[128,384]{1,0:T(8,128)S(1)}, f32[128,384]{1,0:T(8,128)S(1)}, u32[]{:S(2)}, u32[]{:S(2)}) collective-permute-start(f32[128,384]{1,0:T(8,128)S(1)} %fusion.19), channel_id=1, source_target_pairs={{0,256},{32,288},{64,320},{96,352},{128,384},{160,416},{192,448},{... | collective-permute-start | bytes 589832 | tf_op jit(solution)/shard_map/ppermute | solution.py:54
  260.4 18.1 %all-to-all-done.4 = bf16[32,32,384]{2,1,0:T(8,128)(2,1)S(1)} async-done(((bf16[32,32,384]{2,1,0:T(8,128)(2,1)}), bf16[32,32,384]{2,1,0:T(8,128)(2,1)S(1)}, u32[]{:S(2)}, u32[]{:S(2)}) %all-to-all-start.4) | async-done | bytes 786464 | tf_op jit(solution)/shard_map/all_to_all | solution.py:124
  279.3 16.8 %all_to_all.35 = f32[16,8,384]{2,1,0:T(8,128)S(1)} all-to-all(f32[16,8,384]{2,1,0:T(8,128)S(1)} %fusion.18), channel_id=1, replica_groups=mesh['attn'=16,'exp'=32] {'attn'}, dimensions={0} | all-to-all | bytes 393216 | tf_op jit(solution)/shard_map/all_to_all | solution.py:174
  (115 shorter events, 30.4 us)
Async XLA Ops:
  0.0 29.0 %collective-permute-start = (bf16[128,2880]{0,1:T(8,128)(2,1)}, bf16[128,2880]{0,1:T(8,128)(2,1)S(1)}, u32[]{:S(2)}, u32[]{:S(2)}) collective-permute-start(bf16[128,2880]{0,1:T(8,128)(2,1)} %param.17), channel_id=1, source_target_pairs={{0,32},{32,0},{64,96},{96,64},{128,160},{160,128},{192,224},{224,1... | collective-permute-start | bytes 2211848 | tf_op jit(solution)/shard_map/ppermute | solution.py:81
  5.3 3.2 %copy-start.13 = (bf16[8,2048]{1,0:T(8,128)(2,1)S(1)}, bf16[8,2048]{1,0:T(8,128)(2,1)}, u32[]{:S(2)}) copy-start(bf16[8,2048]{1,0:T(8,128)(2,1)} %param.13) | copy-start | bytes 98308
  5.3 3.4 %copy-start.17 = (f32[32]{0:T(128)S(1)}, f32[32]{0:T(128)}, u32[]{:S(2)}) copy-start(f32[32]{0:T(128)} %param.16) | copy-start | bytes 388
  11.6 3.2 %copy-start.12 = (bf16[8,2880]{1,0:T(8,128)(2,1)S(1)}, bf16[8,2880]{1,0:T(8,128)(2,1)}, u32[]{:S(2)}) copy-start(bf16[8,2880]{1,0:T(8,128)(2,1)} %param.12) | copy-start | bytes 138244
  12.7 16.2 %copy-start.11 = (bf16[128,2880]{0,1:T(8,128)(2,1)S(1)}, bf16[128,2880]{0,1:T(8,128)(2,1)}, u32[]{:S(2)}) copy-start(bf16[128,2880]{0,1:T(8,128)(2,1)} %param.17) | copy-start | bytes 2211844
  15.7 22.1 %all-to-all-start = ((bf16[16,8,640]{2,1,0:T(8,128)(2,1)}), bf16[16,8,640]{2,1,0:T(8,128)(2,1)S(1)}, u32[]{:S(2)}, u32[]{:S(2)}) async-start(bf16[16,8,640]{2,1,0:T(8,128)(2,1)} %bitcast.8), calls=%async_computation | async-start | bytes 327680 | tf_op jit(solution)/shard_map/all_to_all | solution.py:88
  29.1 13.7 %copy-start.14 = (f32[2880]{0:T(1024)S(1)}, f32[2880]{0:T(1024)}, u32[]{:S(2)}) copy-start(f32[2880]{0:T(1024)} %param.18) | copy-start | bytes 34564
  29.1 13.8 %copy-start.15 = (s32[128,4]{0,1:T(4,128)S(1)}, s32[128,4]{0,1:T(4,128)}, u32[]{:S(2)}) copy-start(s32[128,4]{0,1:T(4,128)} %param.19) | copy-start | bytes 6148
  39.2 24.9 %all-to-all-start.1 = ((bf16[8,128,384]{1,2,0:T(8,128)(2,1)}), bf16[8,128,384]{1,2,0:T(8,128)(2,1)S(1)}, u32[]{:S(2)}, u32[]{:S(2)}) async-start(bf16[8,128,384]{1,2,0:T(8,128)(2,1)} %fusion.11), calls=%async_computation.1 | async-start | bytes 1572864 | tf_op jit(solution)/shard_map/all_to_all | solution.py:93
  65.9 31.1 %all-to-all-start.2 = ((bf16[32,32,384]{2,1,0:T(8,128)(2,1)}), bf16[32,32,384]{2,1,0:T(8,128)(2,1)S(1)}, u32[]{:S(2)}, u32[]{:S(2)}) async-start(bf16[32,32,384]{2,1,0:T(8,128)(2,1)} %bitcast.14), calls=%async_computation.2 | async-start | bytes 1572864 | tf_op jit(solution)/shard_map/all_to_all | solution.py:120
  77.7 12.6 %collective-permute-start.5 = (bf16[128,384]{1,0:T(8,128)(2,1)S(1)}, bf16[128,384]{1,0:T(8,128)(2,1)S(1)}, u32[]{:S(2)}, u32[]{:S(2)}) collective-permute-start(bf16[128,384]{1,0:T(8,128)(2,1)S(1)} %select_convert_fusion), channel_id=1, source_target_pairs={{0,256},{32,288},{64,320},{96,352},{128,384},{160,416},{192,448},{... | collective-permute-start | bytes 294920 | tf_op jit(solution)/shard_map/ppermute | solution.py:54
  97.0 9.2 %copy-start.1 = (bf16[32,32,384]{2,1,0:T(8,128)(2,1)}, bf16[32,32,384]{2,1,0:T(8,128)(2,1)S(1)}, u32[]{:S(2)}) copy-start(bf16[32,32,384]{2,1,0:T(8,128)(2,1)S(1)} %all-to-all-done.2) | copy-start | bytes 2359300
  97.0 43.2 %all-to-all-start.3 = ((bf16[32,32,384]{2,1,0:T(8,128)(2,1)}), bf16[32,32,384]{2,1,0:T(8,128)(2,1)}, u32[]{:S(2)}, u32[]{:S(2)}) async-start(bf16[32,32,384]{2,1,0:T(8,128)(2,1)} %bitcast.23), calls=%async_computation.3 | async-start | bytes 1572864 | tf_op jit(solution)/shard_map/all_to_all | solution.py:120
  110.1 23.0 %collective-permute-start.1 = (bf16[1024,384]{1,0:T(8,128)(2,1)}, bf16[1024,384]{1,0:T(8,128)(2,1)}, u32[]{:S(2)}, u32[]{:S(2)}) collective-permute-start(bf16[1024,384]{1,0:T(8,128)(2,1)} %bitcast.156), channel_id=1, source_target_pairs={{0,64},{32,96},{64,128},{96,160},{128,192},{160,224},{192,256},{22... | collective-permute-start | bytes 2359304 | tf_op jit(solution)/shard_map/ppermute | solution.py:54
  112.5 22.5 %collective-permute-start.2 = (bf16[1024,384]{1,0:T(8,128)(2,1)}, bf16[1024,384]{1,0:T(8,128)(2,1)}, u32[]{:S(2)}, u32[]{:S(2)}) collective-permute-start(bf16[1024,384]{1,0:T(8,128)(2,1)} %bitcast.157), channel_id=1, source_target_pairs={{0,448},{32,480},{64,0},{96,32},{128,64},{160,96},{192,128},{224,1... | collective-permute-start | bytes 2359304 | tf_op jit(solution)/shard_map/ppermute | solution.py:54
  118.4 1.2 copy-start.2
  133.1 22.2 %collective-permute-start.3 = (bf16[1024,384]{1,0:T(8,128)(2,1)}, bf16[1024,384]{1,0:T(8,128)(2,1)}, u32[]{:S(2)}, u32[]{:S(2)}) collective-permute-start(bf16[1024,384]{1,0:T(8,128)(2,1)} %collective-permute-done.1), channel_id=1, source_target_pairs={{0,64},{32,96},{64,128},{96,160},{128,192},{160,224},{192,256},{22... | collective-permute-start | bytes 2359304 | tf_op jit(solution)/shard_map/ppermute | solution.py:54
  135.0 22.2 %collective-permute-start.4 = (bf16[1024,384]{1,0:T(8,128)(2,1)}, bf16[1024,384]{1,0:T(8,128)(2,1)}, u32[]{:S(2)}, u32[]{:S(2)}) collective-permute-start(bf16[1024,384]{1,0:T(8,128)(2,1)} %collective-permute-done.2), channel_id=1, source_target_pairs={{0,448},{32,480},{64,0},{96,32},{128,64},{160,96},{192,128},{224,1... | collective-permute-start | bytes 2359304 | tf_op jit(solution)/shard_map/ppermute | solution.py:54
  145.7 18.5 %copy-start = (f32[1024,512]{1,0:T(8,128)S(1)}, f32[1024,512]{1,0:T(8,128)}, u32[]{:S(2)}) copy-start(f32[1024,512]{1,0:T(8,128)} %fusion.40) | copy-start | bytes 6291460
  155.3 21.1 %collective-permute-start.6 = (bf16[1024,384]{1,0:T(8,128)(2,1)}, bf16[1024,384]{1,0:T(8,128)(2,1)S(1)}, u32[]{:S(2)}, u32[]{:S(2)}) collective-permute-start(bf16[1024,384]{1,0:T(8,128)(2,1)} %collective-permute-done.3), channel_id=1, source_target_pairs={{0,64},{32,96},{64,128},{96,160},{128,192},{160,224},{192,256},{22... | collective-permute-start | bytes 2359304 | tf_op jit(solution)/shard_map/ppermute | solution.py:54
  157.2 20.5 %collective-permute-start.7 = (bf16[1024,384]{1,0:T(8,128)(2,1)}, bf16[1024,384]{1,0:T(8,128)(2,1)S(1)}, u32[]{:S(2)}, u32[]{:S(2)}) collective-permute-start(bf16[1024,384]{1,0:T(8,128)(2,1)} %collective-permute-done.4), channel_id=1, source_target_pairs={{0,448},{32,480},{64,0},{96,32},{128,64},{160,96},{192,128},{224,1... | collective-permute-start | bytes 2359304 | tf_op jit(solution)/shard_map/ppermute | solution.py:54
  179.1 1.0 copy-start.10
  179.1 4.2 %copy-start.9 = (bf16[1,256,384]{2,0,1:T(2,128)(2,1)S(1)}, bf16[1,256,384]{2,0,1:T(2,128)(2,1)}, u32[]{:S(2)}) copy-start(bf16[1,256,384]{2,0,1:T(2,128)(2,1)} %get-tuple-element.6) | copy-start | bytes 589828
  179.4 10.7 %copy-start.8 = (bf16[1,256,384]{2,0,1:T(2,128)(2,1)S(1)}, bf16[1,256,384]{2,0,1:T(2,128)(2,1)}, u32[]{:S(2)}) copy-start(bf16[1,256,384]{2,0,1:T(2,128)(2,1)} %get-tuple-element.12) | copy-start | bytes 589828
  181.4 20.7 %collective-permute-start.8 = (bf16[1024,384]{1,0:T(8,128)(2,1)}, bf16[1024,384]{1,0:T(8,128)(2,1)}, u32[]{:S(2)}, u32[]{:S(2)}) collective-permute-start(bf16[1024,384]{1,0:T(8,128)(2,1)} %convolution_convert_fusion.2), channel_id=1, source_target_pairs={{0,64},{32,96},{64,128},{96,160},{128,192},{160,224},{192,256},{22... | collective-permute-start | bytes 2359304 | tf_op jit(solution)/shard_map/ppermute | solution.py:54
  183.3 18.8 %copy-start.7 = (bf16[1,256,384]{2,0,1:T(2,128)(2,1)S(1)}, bf16[1,256,384]{2,0,1:T(2,128)(2,1)}, u32[]{:S(2)}) copy-start(bf16[1,256,384]{2,0,1:T(2,128)(2,1)} %get-tuple-element.5) | copy-start | bytes 589828
  184.7 21.0 %collective-permute-start.11 = (bf16[1024,384]{1,0:T(8,128)(2,1)}, bf16[1024,384]{1,0:T(8,128)(2,1)}, u32[]{:S(2)}, u32[]{:S(2)}) collective-permute-start(bf16[1024,384]{1,0:T(8,128)(2,1)} %convolution_convert_fusion.1), channel_id=1, source_target_pairs={{0,448},{32,480},{64,0},{96,32},{128,64},{160,96},{192,128},{224,1... | collective-permute-start | bytes 2359304 | tf_op jit(solution)/shard_map/ppermute | solution.py:54
  191.5 14.2 %copy-start.6 = (bf16[1,256,384]{2,0,1:T(2,128)(2,1)S(1)}, bf16[1,256,384]{2,0,1:T(2,128)(2,1)}, u32[]{:S(2)}) copy-start(bf16[1,256,384]{2,0,1:T(2,128)(2,1)} %get-tuple-element.7) | copy-start | bytes 589828
  191.5 56.4 %all-to-all-start.5 = ((bf16[32,32,384]{2,1,0:T(8,128)(2,1)}), bf16[32,32,384]{2,1,0:T(8,128)(2,1)S(1)}, u32[]{:S(2)}, u32[]{:S(2)}) async-start(bf16[32,32,384]{2,1,0:T(8,128)(2,1)} %bitcast.32), calls=%async_computation.5 | async-start | bytes 1572864 | tf_op jit(solution)/shard_map/all_to_all | solution.py:124
  202.1 10.4 %copy-start.5 = (bf16[1,256,384]{2,0,1:T(2,128)(2,1)S(1)}, bf16[1,256,384]{2,0,1:T(2,128)(2,1)}, u32[]{:S(2)}) copy-start(bf16[1,256,384]{2,0,1:T(2,128)(2,1)} %get-tuple-element.10) | copy-start | bytes 589828
  203.7 20.6 %collective-permute-start.9 = (bf16[1024,384]{1,0:T(8,128)(2,1)S(1)}, bf16[1024,384]{1,0:T(8,128)(2,1)S(1)}, u32[]{:S(2)}, u32[]{:S(2)}) collective-permute-start(bf16[1024,384]{1,0:T(8,128)(2,1)S(1)} %add_convert_fusion.4), channel_id=1, source_target_pairs={{0,64},{32,96},{64,128},{96,160},{128,192},{160,224},{192,256},{22... | collective-permute-start | bytes 2359304 | tf_op jit(solution)/shard_map/ppermute | solution.py:54
  205.7 7.2 %copy-start.4 = (bf16[1,256,384]{2,0,1:T(2,128)(2,1)S(1)}, bf16[1,256,384]{2,0,1:T(2,128)(2,1)}, u32[]{:S(2)}) copy-start(bf16[1,256,384]{2,0,1:T(2,128)(2,1)} %get-tuple-element.8) | copy-start | bytes 589828
  207.3 19.8 %collective-permute-start.12 = (bf16[1024,384]{1,0:T(8,128)(2,1)S(1)}, bf16[1024,384]{1,0:T(8,128)(2,1)S(1)}, u32[]{:S(2)}, u32[]{:S(2)}) collective-permute-start(bf16[1024,384]{1,0:T(8,128)(2,1)S(1)} %add_convert_fusion.2), channel_id=1, source_target_pairs={{0,448},{32,480},{64,0},{96,32},{128,64},{160,96},{192,128},{224,1... | collective-permute-start | bytes 2359304 | tf_op jit(solution)/shard_map/ppermute | solution.py:54
  224.5 8.4 %copy-start.3 = (bf16[1,256,384]{2,0,1:T(2,128)(2,1)S(1)}, bf16[1,256,384]{2,0,1:T(2,128)(2,1)}, u32[]{:S(2)}) copy-start(bf16[1,256,384]{2,0,1:T(2,128)(2,1)} %get-tuple-element.11) | copy-start | bytes 589828
  224.5 19.8 %collective-permute-start.10 = (bf16[1024,384]{1,0:T(8,128)(2,1)S(1)}, bf16[1024,384]{1,0:T(8,128)(2,1)S(1)}, u32[]{:S(2)}, u32[]{:S(2)}) collective-permute-start(bf16[1024,384]{1,0:T(8,128)(2,1)S(1)} %add_convert_fusion.3), channel_id=1, source_target_pairs={{0,64},{32,96},{64,128},{96,160},{128,192},{160,224},{192,256},{22... | collective-permute-start | bytes 2359304 | tf_op jit(solution)/shard_map/ppermute | solution.py:54
  227.3 19.4 %collective-permute-start.13 = (bf16[1024,384]{1,0:T(8,128)(2,1)S(1)}, bf16[1024,384]{1,0:T(8,128)(2,1)S(1)}, u32[]{:S(2)}, u32[]{:S(2)}) collective-permute-start(bf16[1024,384]{1,0:T(8,128)(2,1)S(1)} %add_convert_fusion.1), channel_id=1, source_target_pairs={{0,448},{32,480},{64,0},{96,32},{128,64},{160,96},{192,128},{224,1... | collective-permute-start | bytes 2359304 | tf_op jit(solution)/shard_map/ppermute | solution.py:54
  233.4 22.9 %copy-start.16 = (f32[128,4]{0,1:T(4,128)S(1)}, f32[128,4]{0,1:T(4,128)}, u32[]{:S(2)}) copy-start(f32[128,4]{0,1:T(4,128)} %param.20) | copy-start | bytes 6148
  247.9 30.7 %all-to-all-start.4 = ((bf16[32,32,384]{2,1,0:T(8,128)(2,1)}), bf16[32,32,384]{2,1,0:T(8,128)(2,1)S(1)}, u32[]{:S(2)}, u32[]{:S(2)}) async-start(bf16[32,32,384]{2,1,0:T(8,128)(2,1)} %bitcast.29), calls=%async_computation.4 | async-start | bytes 1572864 | tf_op jit(solution)/shard_map/all_to_all | solution.py:124
  256.9 22.0 %collective-permute-start.14 = (f32[128,384]{1,0:T(8,128)S(1)}, f32[128,384]{1,0:T(8,128)S(1)}, u32[]{:S(2)}, u32[]{:S(2)}) collective-permute-start(f32[128,384]{1,0:T(8,128)S(1)} %fusion.19), channel_id=1, source_target_pairs={{0,256},{32,288},{64,320},{96,352},{128,384},{160,416},{192,448},{... | collective-permute-start | bytes 589832 | tf_op jit(solution)/shard_map/ppermute | solution.py:54

commit v3 on v2

v3 whole, which is shorter than its diff:
```python
import jax
import jax.numpy as jnp
from jax import lax
from jax.sharding import PartitionSpec as P

HEAD_SIZE = 64
QUERY_HEADS = 32
KEY_VALUE_HEADS = 4
D = 2880
FF_LOCAL = 180
N_ATTN = 16
N_EXP = 32
CAP = 32
HALVES = 2
BLOCKS = N_ATTN // HALVES
BLOCK = D // BLOCKS
LANES = 384
FF_LANES = 256
FAR = BLOCKS // 2
F32 = jnp.float32
BF16 = jnp.bfloat16

Z_GROUPS = [[z * HALVES + half for z in range(BLOCKS)] for half in range(HALVES)]


def attend(queries, window_key_value_cache, new_key_value, head_sink_logits):
    count_of_rows = queries.shape[0]
    query_groups = QUERY_HEADS // KEY_VALUE_HEADS
    grouped_queries = queries.reshape(count_of_rows, KEY_VALUE_HEADS, query_groups, HEAD_SIZE)
    all_keys = jnp.concatenate(
        [window_key_value_cache[:, :, :, :HEAD_SIZE], new_key_value[:, :, None, :HEAD_SIZE]], axis=2
    )
    all_values = jnp.concatenate(
        [window_key_value_cache[:, :, :, HEAD_SIZE:], new_key_value[:, :, None, HEAD_SIZE:]], axis=2
    )
    scores = jnp.einsum(
        "rkgd,rkjd->rkgj", grouped_queries, all_keys, preferred_element_type=jnp.float32
    ) * HEAD_SIZE ** (-0.5)
    sink_portion = head_sink_logits.reshape(1, KEY_VALUE_HEADS, query_groups, 1)
    highest = jnp.maximum(jnp.max(scores, axis=3, keepdims=True), sink_portion)
    raised = jnp.exp(scores - highest)
    denominator = jnp.sum(raised, axis=3, keepdims=True) + jnp.exp(sink_portion - highest)
    weights = (raised / denominator).astype(jnp.bfloat16)
    combined = jnp.einsum(
        "rkgj,rkjd->rkgd", weights, all_values, preferred_element_type=jnp.float32
    )
    return combined.reshape(count_of_rows, QUERY_HEADS * HEAD_SIZE).astype(jnp.bfloat16)


def shift_over_z(array, step):
    pairs = [
        (z * HALVES + half, (z + step) % BLOCKS * HALVES + half) for z in range(BLOCKS) for half in range(HALVES)
    ]
    return lax.ppermute(array, "attn", pairs)


def swap_halves(array):
    return lax.ppermute(array, "attn", [(i, i ^ 1) for i in range(N_ATTN)])


def over_z(array):
    return lax.all_to_all(array, "attn", 0, 0, tiled=True, axis_index_groups=Z_GROUPS)


def over_experts(array):
    return lax.all_to_all(array, "exp", 0, 0, tiled=True)


def to_blocks(array):
    array = array.reshape(array.shape[:-1] + (BLOCKS, BLOCK))
    return jnp.pad(array, [(0, 0)] * (array.ndim - 1) + [(0, LANES - BLOCK)])


def local(
    residual,
    queries,
    window_key_value_cache,
    new_key_value,
    head_sink_logits,
    out_proj,
    norm_gain,
    expert_ids,
    gate_mix,
    w_gate,
    w_up,
    w_down,
):
    own_rows = residual.shape[0]
    column_rows = expert_ids.shape[0]
    half_rows = column_rows // HALVES
    half_cap = CAP // HALVES
    half_slots = N_EXP * half_cap
    attn_index = lax.axis_index("attn")
    z_index = lax.shift_right_logical(attn_index, 1)
    half = lax.bitwise_and(attn_index, 1)
    first_half = half == 0

    other_proj = swap_halves(out_proj)
    proj = jnp.concatenate(
        [jnp.where(first_half, out_proj, other_proj), jnp.where(first_half, other_proj, out_proj)], axis=0
    )
    proj = to_blocks(proj).transpose(1, 0, 2)

    attended = attend(queries, window_key_value_cache, new_key_value, head_sink_logits)
    heads = attended.reshape(own_rows, BLOCKS, HALVES * 128)
    sent = jnp.concatenate([heads, to_blocks(residual)], axis=2).transpose(1, 0, 2)
    got = over_z(sent).reshape(half_rows, HALVES * 128 + LANES)
    partial_sums = jnp.einsum("rk,zkd->zrd", got[:, : HALVES * 128], proj, preferred_element_type=F32).astype(BF16)
    hidden_state = got[:, HALVES * 128 :].astype(F32) + jnp.sum(over_z(partial_sums).astype(F32), axis=0)

    gain = lax.dynamic_index_in_dim(to_blocks(norm_gain), z_index, 0, keepdims=False)
    square = jnp.sum(hidden_state * hidden_state, axis=1, keepdims=True)
    square_high = lax.reduce_precision(square, 8, 7)
    square_low = square - square_high
    lane = lax.broadcasted_iota(jnp.int32, (half_rows, LANES), 1)
    scaled = hidden_state * gain
    scaled = jnp.where(lane == BLOCK, square_high, jnp.where(lane == BLOCK + 1, square_low, scaled)).astype(BF16)
    other_scaled = swap_halves(scaled).reshape(BLOCKS, own_rows, LANES)
    scaled = scaled.reshape(BLOCKS, own_rows, LANES)
    scaled = jnp.stack(
        [jnp.where(first_half, scaled, other_scaled), jnp.where(first_half, other_scaled, scaled)], axis=1
    ).reshape(column_rows, LANES)

    names = expert_ids.T[None, :, :] == jnp.arange(N_EXP, dtype=jnp.int32)[:, None, None]
    named = jnp.any(names, axis=1)
    weight = jnp.sum(jnp.where(names, gate_mix.T[None, :, :], 0.0), axis=1)
    row = jnp.arange(column_rows, dtype=jnp.int32)
    earlier = (row[:, None] < row[None, :]).astype(BF16)
    slot = jnp.dot(named.astype(BF16), earlier, preferred_element_type=F32).astype(jnp.int32)
    slot = jnp.where(named, slot, -1)

    def taken_of(own_half):
        base = half_cap * (half if own_half else 1 - half)
        return slot[:, None, :] == base + jnp.arange(half_cap, dtype=jnp.int32)[None, :, None]

    taken_own, taken_other = taken_of(True), taken_of(False)
    taken_both = jnp.concatenate([taken_own, taken_other], axis=1)

    def picked(taken, rows):
        select = taken.astype(BF16).reshape(-1, column_rows)
        return jnp.dot(select, rows, preferred_element_type=F32).astype(BF16).reshape(N_EXP, -1, LANES)

    def mixed_of(taken, partial_value):
        returned = over_experts(partial_value).reshape(-1, LANES)
        mix = jnp.where(taken, weight[:, None, :], 0.0).reshape(-1, column_rows)
        mix_high = lax.reduce_precision(mix, 8, 7)
        mix_low = (mix - mix_high).astype(BF16)
        over_slots = (((0,), (0,)), ((), ()))
        mixed = lax.dot_general(mix_high.astype(BF16), returned, over_slots, preferred_element_type=F32)
        return mixed + lax.dot_general(mix_low, returned, over_slots, preferred_element_type=F32)

    def padded_in(w):
        w = w.reshape(BLOCKS, BLOCK, FF_LOCAL)
        return jnp.pad(w, ((0, 0), (0, LANES - BLOCK), (0, FF_LANES - FF_LOCAL)))

    def own_first(blocks):
        return lax.dynamic_slice_in_dim(jnp.concatenate([blocks, blocks]), z_index, BLOCKS, 0)

    w_in = jnp.concatenate([padded_in(w_gate), padded_in(w_up)], axis=2)
    in_row = lax.broadcasted_iota(jnp.int32, w_in.shape, 1)
    in_column = lax.broadcasted_iota(jnp.int32, w_in.shape, 2)
    w_in = jnp.where((in_column == FF_LOCAL) & (in_row >= BLOCK) & (in_row < BLOCK + 2), jnp.ones((), BF16), w_in)
    w_in = own_first(w_in)
    w_out = jnp.pad(to_blocks(w_down[0]).transpose(1, 0, 2), ((0, 0), (0, FF_LANES - FF_LOCAL), (0, 0)))
    w_out = own_first(w_out)

    far_outgoing = picked(taken_both, shift_over_z(scaled, FAR))
    own = over_experts(picked(taken_own, scaled)).reshape(half_slots, LANES)
    own, w_in, w_out, far_outgoing = lax.optimization_barrier((own, w_in, w_out, far_outgoing))
    chunks = [own, swap_halves(own)]
    ups, downs = [chunks], [chunks]
    for step in range(1, FAR):
        pairs = [(shift_over_z(ups[-1][c], 1), shift_over_z(downs[-1][c], -1)) for c in range(2)]
        ups.append([pair[0] for pair in pairs])
        downs.append([pair[1] for pair in pairs])
        if step == 1:
            far_outgoing = lax.optimization_barrier((far_outgoing, pairs[0][0]))[0]
    far = over_experts(far_outgoing).reshape(N_EXP, 2, half_cap, LANES)

    expert_hidden = []
    for c in range(2):
        both = jnp.dot(chunks[c], w_in[0], preferred_element_type=F32)
        for step in range(1, FAR):
            if step == FAR - 1:
                both = lax.optimization_barrier(both)
            both = both + jnp.dot(ups[step][c], w_in[BLOCKS - step], preferred_element_type=F32)
            both = both + jnp.dot(downs[step][c], w_in[step], preferred_element_type=F32)
        both = both + jnp.dot(far[:, c].reshape(half_slots, LANES), w_in[FAR], preferred_element_type=F32)
        factor = lax.rsqrt(both[:, FF_LOCAL : FF_LOCAL + 1] * (1.0 / D) + 1e-05)
        gate = both[:, :FF_LANES] * factor
        up = both[:, FF_LANES:] * factor
        expert_hidden.append((gate * jax.nn.sigmoid(1.702 * gate) * (up + 1.0)).astype(BF16))

    def output_block(c, offset):
        return jnp.dot(expert_hidden[c], w_out[offset % BLOCKS], preferred_element_type=F32)

    up_sums, down_sums = [None, None], [None, None]
    for offset in range(FAR - 1, 0, -1):
        for c in range(2):
            up_sum, down_sum = output_block(c, offset), output_block(c, -offset)
            if offset < FAR - 1:
                up_sum = up_sum + up_sums[c].astype(F32)
                down_sum = down_sum + down_sums[c].astype(F32)
            up_sums[c] = shift_over_z(up_sum.astype(BF16), 1)
            down_sums[c] = shift_over_z(down_sum.astype(BF16), -1)
        if offset == FAR - 1:
            far_hidden = lax.optimization_barrier((expert_hidden[0], expert_hidden[1], up_sums[0]))[:2]
    far_value = jnp.stack(
        [
            jnp.dot(h, w_out[FAR], preferred_element_type=F32).astype(BF16).reshape(N_EXP, half_cap, LANES)
            for h in far_hidden
        ],
        axis=1,
    )
    far_mixed = shift_over_z(mixed_of(taken_both, far_value.reshape(N_EXP, CAP, LANES)), FAR)
    sums = [output_block(c, 0) + up_sums[c].astype(F32) + down_sums[c].astype(F32) for c in range(2)]
    other_sum = swap_halves(sums[0].astype(BF16))
    whole_sum = (sums[1] + other_sum.astype(F32)).astype(BF16)
    mixed = mixed_of(taken_other, whole_sum.reshape(N_EXP, half_cap, LANES)) + far_mixed

    mixed = mixed.reshape(BLOCKS, HALVES, own_rows, LANES)
    halves = jnp.arange(HALVES, dtype=jnp.int32)[None, :, None, None]
    mixed = mixed + jnp.where(halves == half, hidden_state.reshape(BLOCKS, 1, own_rows, LANES), 0.0)
    last = lax.all_to_all(mixed.reshape(N_ATTN, own_rows, LANES), "attn", 0, 0, tiled=True)
    last = jnp.sum(last.reshape(BLOCKS, HALVES, own_rows, LANES), axis=1)
    return last[:, :, :BLOCK].transpose(1, 0, 2).reshape(own_rows, D).astype(BF16)


def solution(mesh):
    in_specs = (
        P(("exp", "attn"), None),
        P(("exp", "attn"), None),
        P(("exp", "attn"), None, None, None),
        P(("exp", "attn"), None, None),
        P(),
        P("attn", None),
        P(),
        P("exp", None),
        P("exp", None),
        P("exp", None, "attn"),
        P("exp", None, "attn"),
        P("exp", "attn", None),
    )
    out_specs = P(("exp", "attn"), None)
    return jax.shard_map(local, mesh=mesh, in_specs=in_specs, out_specs=out_specs, check_vma=False)
```

time: 302 us -> 324 us (1.073)
  waiting for transfers between devices: 121 us -> 62 us
  starting transfers between devices: 100 us -> 154 us
  matrix products: 30.1 us -> 41.7 us
  other arithmetic: 7.4 us -> 16.5 us
  local copies, waits for them, and re-layouts: 20.4 us -> 28.8 us
    ppermute x14 -> x26, starting transfers between devices: 49.3 us -> 87.7 us  [shift_over_z(): return lax.ppermute(array, 'attn', pairs)]
    all_to_all x6, waiting for transfers between devices: 53 us -> 19.5 us  [the longest x2 10.7 us: over_z(): lax.all_to_all(array, 'attn', 0, 0, tiled=True, axis_index_groups=Z_GROUPS)]
    ppermute x14 -> x26, waiting for transfers between devices: 67.9 us -> 36.8 us  [shift_over_z(): return lax.ppermute(array, 'attn', pairs)]
    dot_general x23 -> x39, matrix products: 26.7 us -> 38.5 us  [the longest x14 12.6 us: output_block(): jnp.dot(expert_hidden[c], w_out[offset % BLOCKS], preferred_element_type=...]
    ppermute x1 -> x4, starting transfers between devices: 3.3 us -> 14.9 us  [swap_halves(): return lax.ppermute(array, 'attn', [(i, i ^ 1) for i in range(N_ATTN)])]
    slice x1, local copies, waits for them, and re-layouts: 3.67 us -> 9.59 us  [output_block(): w_out[offset % BLOCKS]]
    ppermute x1 -> x4, waiting for transfers between devices: 0.01 us -> 5.75 us  [swap_halves(): return lax.ppermute(array, 'attn', [(i, i ^ 1) for i in range(N_ATTN)])]
    unnamed x42 -> x72, local copies, waits for them, and re-layouts: 6.9 us -> 6.01 us
  transfers between devices with their start and end apart: 21 -> 36, of which waited for: 14 -> 14; matrix products, arithmetic and copies ran while one was open for 17% -> 24% of each run, Pallas kernels for 0% -> 0%
where the time goes in v3:
time: 324 us; the launch traced here: 320 us
  starting transfers between devices  154 us (48%)
  waiting for transfers between devices  62 us (19%)
  matrix products  41.7 us (13%)
  local copies, waits for them, and re-layouts  28.8 us (9%)
  other arithmetic  16.5 us (5%)
  blocking collectives  16.3 us (5%)
    ppermute x26, starting transfers between devices, shift_over_z(): return lax.ppermute(array, 'attn', pairs)  87.7 us
    ppermute x26, waiting for transfers between devices, shift_over_z(): return lax.ppermute(array, 'attn', pairs)  36.8 us
    all_to_all x4, starting transfers between devices, over_experts(): return lax.all_to_all(array, 'exp', 0, 0, tiled=True)  33.8 us
    all_to_all x2, starting transfers between devices, over_z(): lax.all_to_all(array, 'attn', 0, 0, tiled=True, axis_index_groups=Z_GROUPS)  17.3 us
    all_to_all x1, blocking collectives, local(): lax.all_to_all(mixed.reshape(N_ATTN, own_rows, LANES), 'attn', 0, 0, tile...  16.3 us
    ppermute x4, starting transfers between devices, swap_halves(): return lax.ppermute(array, 'attn', [(i, i ^ 1) for i in range(N_ATTN)])  14.9 us
    dot_general x14, matrix products, output_block(): jnp.dot(expert_hidden[c], w_out[offset % BLOCKS], preferred_element_type=...  12.6 us
    all_to_all x2, waiting for transfers between devices, over_z(): lax.all_to_all(array, 'attn', 0, 0, tiled=True, axis_index_groups=Z_GROUPS)  10.7 us
  transfers between devices with their start and end apart: 36, of which 14 were waited for; matrix products, arithmetic and copies ran while one was open for 24% of the time, Pallas kernels for 0%

profile of v3, /device:TPU:6, one launch (start us, length us, event | category | flops | bytes accessed | tf_op | source)
XLA Modules:
  0.0 320.0 jit_solution(10467579926670966233)
XLA Ops:
  0.0 3.3 %collective-permute-start = (bf16[128,2880]{0,1:T(8,128)(2,1)}, bf16[128,2880]{0,1:T(8,128)(2,1)}, u32[]{:S(2)}, u32[]{:S(2)}) collective-permute-start(bf16[128,2880]{0,1:T(8,128)(2,1)} %param.17), channel_id=1, source_target_pairs={{0,32},{32,0},{64,96},{96,64},{128,160},{160,128},{192,224},{224,1... | collective-permute-start | bytes 2211848 | tf_op jit(solution)/shard_map/ppermute | solution.py:58
  6.2 2.0 fusion.169
  15.3 10.3 %all-to-all-start = ((bf16[8,8,640]{2,1,0:T(8,128)(2,1)}), bf16[8,8,640]{2,1,0:T(8,128)(2,1)S(1)}, u32[]{:S(2)}, u32[]{:S(2)}) async-start(bf16[8,8,640]{2,1,0:T(8,128)(2,1)} %fusion.140), calls=%async_computation | async-start | bytes 163840 | tf_op jit(solution)/shard_map/all_to_all | solution.py:62
  26.8 2.5 copy.122
  35.3 6.9 %all-to-all-start.1 = ((bf16[8,64,384]{2,1,0:T(8,128)(2,1)}), bf16[8,64,384]{2,1,0:T(8,128)(2,1)S(1)}, u32[]{:S(2)}, u32[]{:S(2)}) async-start(bf16[8,64,384]{2,1,0:T(8,128)(2,1)} %fusion.17), calls=%async_computation.1 | async-start | bytes 786432 | tf_op jit(solution)/shard_map/all_to_all | solution.py:62
  42.2 3.4 %and_select_fusion = bf16[8,384,512]{2,1,0:T(8,128)(2,1)} fusion(bf16[8,360,180]{2,1,0:T(8,128)(2,1)S(1)} %bitcast.218, bf16[8,360,180]{2,1,0:T(8,128)(2,1)} %bitcast.219, pred[384]{0:T(512)(128)(4,1)S(1)} %get-tuple-element.51, pred[512]{0:T(512)(128)(4,1)S(1)} %iota_compare_fusion.8, pred[384]{0:T(512)(128)(4,1)S(1)} %get-tuple-element.52), kind=kLoop, calls=%fused_computation.6 | loop fusion | flops 17301504 | bytes 5220608 | tf_op jit(solution)/shard_map/jit(_where)/select_n | solution.py:162
  45.6 10.5 %all-to-all-done.1 = bf16[8,64,384]{2,1,0:T(8,128)(2,1)S(1)} async-done(((bf16[8,64,384]{2,1,0:T(8,128)(2,1)}), bf16[8,64,384]{2,1,0:T(8,128)(2,1)S(1)}, u32[]{:S(2)}, u32[]{:S(2)}) %all-to-all-start.1) | async-done | bytes 393248 | tf_op jit(solution)/shard_map/all_to_all | solution.py:62
  57.0 4.0 %collective-permute-start.1 = (bf16[64,384]{1,0:T(8,128)(2,1)S(1)}, bf16[64,384]{1,0:T(8,128)(2,1)S(1)}, u32[]{:S(2)}, u32[]{:S(2)}) collective-permute-start(bf16[64,384]{1,0:T(8,128)(2,1)S(1)} %select_convert_fusion), channel_id=1, source_target_pairs={{0,32},{32,0},{64,96},{96,64},{128,160},{160,128},{192,224},{224,1... | collective-permute-start | bytes 147464 | tf_op jit(solution)/shard_map/ppermute | solution.py:58
  66.2 8.7 %all-to-all-start.2 = ((bf16[32,16,384]{2,1,0:T(8,128)(2,1)}), bf16[32,16,384]{2,1,0:T(8,128)(2,1)S(1)}, u32[]{:S(2)}, u32[]{:S(2)}) async-start(bf16[32,16,384]{2,1,0:T(8,128)(2,1)} %bitcast.17), calls=%async_computation.2 | async-start | bytes 786432 | tf_op jit(solution)/shard_map/all_to_all | solution.py:66
  75.2 2.3 fusion.4
  77.6 3.1 fusion.3
  80.6 2.5 collective-permute-start.2
  83.1 8.2 %collective-permute-done.2 = bf16[128,384]{1,0:T(8,128)(2,1)S(1)} collective-permute-done((bf16[128,384]{1,0:T(8,128)(2,1)S(1)}, bf16[128,384]{1,0:T(8,128)(2,1)S(1)}, u32[]{:S(2)}, u32[]{:S(2)}) %collective-permute-start.2) | collective-permute-done | bytes 98336 | tf_op jit(solution)/shard_map/ppermute | solution.py:54
  92.6 4.0 %collective-permute-start.10 = (bf16[512,384]{1,0:T(8,128)(2,1)S(1)}, bf16[512,384]{1,0:T(8,128)(2,1)}, u32[]{:S(2)}, u32[]{:S(2)}) collective-permute-start(bf16[512,384]{1,0:T(8,128)(2,1)S(1)} %bitcast.222), channel_id=1, source_target_pairs={{0,64},{32,96},{64,128},{96,160},{128,192},{160,224},{192,256},{22... | collective-permute-start | bytes 1179656 | tf_op jit(solution)/shard_map/ppermute | solution.py:54
  96.7 3.0 collective-permute-start.17
  99.7 4.2 %collective-permute-start.3 = (bf16[512,384]{1,0:T(8,128)(2,1)S(1)}, bf16[512,384]{1,0:T(8,128)(2,1)}, u32[]{:S(2)}, u32[]{:S(2)}) collective-permute-start(bf16[512,384]{1,0:T(8,128)(2,1)S(1)} %bitcast.224), channel_id=1, source_target_pairs={{0,32},{32,0},{64,96},{96,64},{128,160},{160,128},{192,224},{224,1... | collective-permute-start | bytes 1179656 | tf_op jit(solution)/shard_map/ppermute | solution.py:58
  103.9 9.6 %fusion.168 = (bf16[1,256,384]{2,0,1:T(2,128)(2,1)}, bf16[1,256,384]{2,0,1:T(2,128)(2,1)}, bf16[1,256,384]{2,0,1:T(2,128)(2,1)}, bf16[1,256,384]{2,0,1:T(2,128)(...) fusion(bf16[8,256,384]{2,0,1:T(8,128)(2,1)} %fusion.4), kind=kLoop, calls=%fused_computation.243 | loop fusion | bytes 3145728 | tf_op jit(solution)/shard_map/slice | solution.py:195
  115.0 8.4 %all-to-all-start.3 = ((bf16[32,32,384]{2,1,0:T(8,128)(2,1)}), bf16[32,32,384]{2,1,0:T(8,128)(2,1)}, u32[]{:S(2)}, u32[]{:S(2)}) async-start(bf16[32,32,384]{2,1,0:T(8,128)(2,1)} %bitcast.221), calls=%async_computation.3 | async-start | bytes 1572864 | tf_op jit(solution)/shard_map/all_to_all | solution.py:66
  123.4 2.8 collective-permute-start.18
  126.2 4.2 %collective-permute-start.5 = (bf16[512,384]{1,0:T(8,128)(2,1)}, bf16[512,384]{1,0:T(8,128)(2,1)S(1)}, u32[]{:S(2)}, u32[]{:S(2)}) collective-permute-start(bf16[512,384]{1,0:T(8,128)(2,1)} %collective-permute-done.3), channel_id=1, source_target_pairs={{0,448},{32,480},{64,0},{96,32},{128,64},{160,96},{192,128},{224,1... | collective-permute-start | bytes 1179656 | tf_op jit(solution)/shard_map/ppermute | solution.py:54
  133.8 5.1 %collective-permute-start.19 = (bf16[512,384]{1,0:T(8,128)(2,1)}, bf16[512,384]{1,0:T(8,128)(2,1)S(1)}, u32[]{:S(2)}, u32[]{:S(2)}) collective-permute-start(bf16[512,384]{1,0:T(8,128)(2,1)} %collective-permute-done.17), channel_id=1, source_target_pairs={{0,448},{32,480},{64,0},{96,32},{128,64},{160,96},{192,128},{224,1... | collective-permute-start | bytes 1179656 | tf_op jit(solution)/shard_map/ppermute | solution.py:54
  142.2 5.4 %collective-permute-done.19 = bf16[512,384]{1,0:T(8,128)(2,1)S(1)} collective-permute-done((bf16[512,384]{1,0:T(8,128)(2,1)}, bf16[512,384]{1,0:T(8,128)(2,1)S(1)}, u32[]{:S(2)}, u32[]{:S(2)}) %collective-permute-start.19) | collective-permute-done | bytes 393248 | tf_op jit(solution)/shard_map/ppermute | solution.py:54
  148.1 2.5 fusion.10
  150.5 5.5 %collective-permute-start.21 = (bf16[512,384]{1,0:T(8,128)(2,1)S(1)}, bf16[512,384]{1,0:T(8,128)(2,1)S(1)}, u32[]{:S(2)}, u32[]{:S(2)}) collective-permute-start(bf16[512,384]{1,0:T(8,128)(2,1)S(1)} %collective-permute-done.19), channel_id=1, source_target_pairs={{0,448},{32,480},{64,0},{96,32},{128,64},{160,96},{192,128},{224,1... | collective-permute-start | bytes 1179656 | tf_op jit(solution)/shard_map/ppermute | solution.py:54
  157.9 5.1 %collective-permute-start.7 = (bf16[512,384]{1,0:T(8,128)(2,1)S(1)}, bf16[512,384]{1,0:T(8,128)(2,1)S(1)}, u32[]{:S(2)}, u32[]{:S(2)}) collective-permute-start(bf16[512,384]{1,0:T(8,128)(2,1)S(1)} %collective-permute-done.5), channel_id=1, source_target_pairs={{0,448},{32,480},{64,0},{96,32},{128,64},{160,96},{192,128},{224,1... | collective-permute-start | bytes 1179656 | tf_op jit(solution)/shard_map/ppermute | solution.py:54
  165.9 5.9 %collective-permute-done.7 = bf16[512,384]{1,0:T(8,128)(2,1)S(1)} collective-permute-done((bf16[512,384]{1,0:T(8,128)(2,1)S(1)}, bf16[512,384]{1,0:T(8,128)(2,1)S(1)}, u32[]{:S(2)}, u32[]{:S(2)}) %collective-permute-start.7) | collective-permute-done | bytes 393248 | tf_op jit(solution)/shard_map/ppermute | solution.py:54
  171.8 5.6 %collective-permute-start.9 = (bf16[512,384]{1,0:T(8,128)(2,1)S(1)}, bf16[512,384]{1,0:T(8,128)(2,1)S(1)}, u32[]{:S(2)}, u32[]{:S(2)}) collective-permute-start(bf16[512,384]{1,0:T(8,128)(2,1)S(1)} %collective-permute-done.7), channel_id=1, source_target_pairs={{0,448},{32,480},{64,0},{96,32},{128,64},{160,96},{192,128},{224,1... | collective-permute-start | bytes 1179656 | tf_op jit(solution)/shard_map/ppermute | solution.py:54
  177.8 2.4 fusion.13
  188.8 3.8 %collective-permute-done.8 = bf16[512,384]{1,0:T(8,128)(2,1)} collective-permute-done((bf16[512,384]{1,0:T(8,128)(2,1)}, bf16[512,384]{1,0:T(8,128)(2,1)}, u32[]{:S(2)}, u32[]{:S(2)}) %collective-permute-start.8) | collective-permute-done | bytes 393248 | tf_op jit(solution)/shard_map/ppermute | solution.py:54
  200.6 5.1 %collective-permute-start.25 = (bf16[512,384]{1,0:T(8,128)(2,1)}, bf16[512,384]{1,0:T(8,128)(2,1)}, u32[]{:S(2)}, u32[]{:S(2)}) collective-permute-start(bf16[512,384]{1,0:T(8,128)(2,1)} %convolution_convert_fusion.3), channel_id=1, source_target_pairs={{0,448},{32,480},{64,0},{96,32},{128,64},{160,96},{192,128},{224,1... | collective-permute-start | bytes 1179656 | tf_op jit(solution)/shard_map/ppermute | solution.py:54
  208.9 3.9 %collective-permute-start.11 = (bf16[512,384]{1,0:T(8,128)(2,1)}, bf16[512,384]{1,0:T(8,128)(2,1)}, u32[]{:S(2)}, u32[]{:S(2)}) collective-permute-start(bf16[512,384]{1,0:T(8,128)(2,1)} %convolution_convert_fusion.6), channel_id=1, source_target_pairs={{0,64},{32,96},{64,128},{96,160},{128,192},{160,224},{192,256},{22... | collective-permute-start | bytes 1179656 | tf_op jit(solution)/shard_map/ppermute | solution.py:54
  216.1 8.4 %all-to-all-start.5 = ((bf16[32,32,384]{2,1,0:T(8,128)(2,1)}), bf16[32,32,384]{2,1,0:T(8,128)(2,1)}, u32[]{:S(2)}, u32[]{:S(2)}) async-start(bf16[32,32,384]{2,1,0:T(8,128)(2,1)} %bitcast.40), calls=%async_computation.5 | async-start | bytes 1572864 | tf_op jit(solution)/shard_map/all_to_all | solution.py:66
  226.0 3.1 collective-permute-start.26
  230.6 2.7 collective-permute-start.23
  234.7 4.6 %collective-permute-start.15 = (bf16[512,384]{1,0:T(8,128)(2,1)S(1)}, bf16[512,384]{1,0:T(8,128)(2,1)S(1)}, u32[]{:S(2)}, u32[]{:S(2)}) collective-permute-start(bf16[512,384]{1,0:T(8,128)(2,1)S(1)} %add_convert_fusion.7), channel_id=1, source_target_pairs={{0,448},{32,480},{64,0},{96,32},{128,64},{160,96},{192,128},{224,1... | collective-permute-start | bytes 1179656 | tf_op jit(solution)/shard_map/ppermute | solution.py:54
  240.6 2.1 collective-permute-start.12
  242.8 5.1 %collective-permute-start.27 = (bf16[512,384]{1,0:T(8,128)(2,1)S(1)}, bf16[512,384]{1,0:T(8,128)(2,1)S(1)}, u32[]{:S(2)}, u32[]{:S(2)}) collective-permute-start(bf16[512,384]{1,0:T(8,128)(2,1)S(1)} %add_convert_fusion.2), channel_id=1, source_target_pairs={{0,448},{32,480},{64,0},{96,32},{128,64},{160,96},{192,128},{224,1... | collective-permute-start | bytes 1179656 | tf_op jit(solution)/shard_map/ppermute | solution.py:54
  250.1 5.1 %collective-permute-start.16 = (bf16[512,384]{1,0:T(8,128)(2,1)S(1)}, bf16[512,384]{1,0:T(8,128)(2,1)S(1)}, u32[]{:S(2)}, u32[]{:S(2)}) collective-permute-start(bf16[512,384]{1,0:T(8,128)(2,1)S(1)} %add_convert_fusion.6), channel_id=1, source_target_pairs={{0,448},{32,480},{64,0},{96,32},{128,64},{160,96},{192,128},{224,1... | collective-permute-start | bytes 1179656 | tf_op jit(solution)/shard_map/ppermute | solution.py:54
  256.0 2.1 collective-permute-start.13
  258.0 6.2 %collective-permute-done.24 = bf16[512,384]{1,0:T(8,128)(2,1)S(1)} collective-permute-done((bf16[512,384]{1,0:T(8,128)(2,1)S(1)}, bf16[512,384]{1,0:T(8,128)(2,1)S(1)}, u32[]{:S(2)}, u32[]{:S(2)}) %collective-permute-start.24) | collective-permute-done | bytes 393248 | tf_op jit(solution)/shard_map/ppermute | solution.py:54
  264.4 3.3 %collective-permute-start.28 = (bf16[512,384]{1,0:T(8,128)(2,1)S(1)}, bf16[512,384]{1,0:T(8,128)(2,1)S(1)}, u32[]{:S(2)}, u32[]{:S(2)}) collective-permute-start(bf16[512,384]{1,0:T(8,128)(2,1)S(1)} %add_convert_fusion.1), channel_id=1, source_target_pairs={{0,32},{32,0},{64,96},{96,64},{128,160},{160,128},{192,224},{224,1... | collective-permute-start | bytes 1179656 | tf_op jit(solution)/shard_map/ppermute | solution.py:58
  268.1 3.0 collective-permute-done.13
  271.1 4.6 %collective-permute-done.28 = bf16[512,384]{1,0:T(8,128)(2,1)S(1)} collective-permute-done((bf16[512,384]{1,0:T(8,128)(2,1)S(1)}, bf16[512,384]{1,0:T(8,128)(2,1)S(1)}, u32[]{:S(2)}, u32[]{:S(2)}) %collective-permute-start.28) | collective-permute-done | bytes 393248 | tf_op jit(solution)/shard_map/ppermute | solution.py:58
  276.6 8.3 %all-to-all-start.4 = ((bf16[32,16,384]{2,1,0:T(8,128)(2,1)}), bf16[32,16,384]{2,1,0:T(8,128)(2,1)S(1)}, u32[]{:S(2)}, u32[]{:S(2)}) async-start(bf16[32,16,384]{2,1,0:T(8,128)(2,1)} %bitcast.35), calls=%async_computation.4 | async-start | bytes 786432 | tf_op jit(solution)/shard_map/all_to_all | solution.py:66
  287.9 2.6 collective-permute-start.29
  290.7 8.7 %all-to-all-done.4 = bf16[32,16,384]{2,1,0:T(8,128)(2,1)S(1)} async-done(((bf16[32,16,384]{2,1,0:T(8,128)(2,1)}), bf16[32,16,384]{2,1,0:T(8,128)(2,1)S(1)}, u32[]{:S(2)}, u32[]{:S(2)}) %all-to-all-start.4) | async-done | bytes 393248 | tf_op jit(solution)/shard_map/all_to_all | solution.py:66
  299.8 2.8 collective-permute-done.29
  302.9 16.3 %all_to_all.35 = f32[16,8,384]{2,1,0:T(8,128)S(1)} all-to-all(f32[16,8,384]{2,1,0:T(8,128)S(1)} %fusion.24), channel_id=1, replica_groups=mesh['attn'=16,'exp'=32] {'attn'}, dimensions={0} | all-to-all | bytes 393216 | tf_op jit(solution)/shard_map/all_to_all | solution.py:224
  (201 shorter events, 75.4 us)
Async XLA Ops:
  0.0 29.5 %collective-permute-start = (bf16[128,2880]{0,1:T(8,128)(2,1)}, bf16[128,2880]{0,1:T(8,128)(2,1)}, u32[]{:S(2)}, u32[]{:S(2)}) collective-permute-start(bf16[128,2880]{0,1:T(8,128)(2,1)} %param.17), channel_id=1, source_target_pairs={{0,32},{32,0},{64,96},{96,64},{128,160},{160,128},{192,224},{224,1... | collective-permute-start | bytes 2211848 | tf_op jit(solution)/shard_map/ppermute | solution.py:58
  15.3 18.9 %all-to-all-start = ((bf16[8,8,640]{2,1,0:T(8,128)(2,1)}), bf16[8,8,640]{2,1,0:T(8,128)(2,1)S(1)}, u32[]{:S(2)}, u32[]{:S(2)}) async-start(bf16[8,8,640]{2,1,0:T(8,128)(2,1)} %fusion.140), calls=%async_computation | async-start | bytes 163840 | tf_op jit(solution)/shard_map/all_to_all | solution.py:62
  29.3 31.7 %copy-start.29 = (s32[16]{0:T(128)}, s32[16]{0:T(128)S(1)}, u32[]{:S(2)}) copy-start(s32[16]{0:T(128)S(1)} %get-tuple-element.46) | copy-start | bytes 196
  35.3 20.8 %all-to-all-start.1 = ((bf16[8,64,384]{2,1,0:T(8,128)(2,1)}), bf16[8,64,384]{2,1,0:T(8,128)(2,1)S(1)}, u32[]{:S(2)}, u32[]{:S(2)}) async-start(bf16[8,64,384]{2,1,0:T(8,128)(2,1)} %fusion.17), calls=%async_computation.1 | async-start | bytes 786432 | tf_op jit(solution)/shard_map/all_to_all | solution.py:62
  42.2 19.6 %copy-start.14 = (bf16[1,180,2880]{2,1,0:T(8,128)(2,1)S(1)}, bf16[1,180,2880]{2,1,0:T(8,128)(2,1)}, u32[]{:S(2)}) copy-start(bf16[1,180,2880]{2,1,0:T(8,128)(2,1)} %param.23) | copy-start | bytes 3110404
  57.0 7.5 %collective-permute-start.1 = (bf16[64,384]{1,0:T(8,128)(2,1)S(1)}, bf16[64,384]{1,0:T(8,128)(2,1)S(1)}, u32[]{:S(2)}, u32[]{:S(2)}) collective-permute-start(bf16[64,384]{1,0:T(8,128)(2,1)S(1)} %select_convert_fusion), channel_id=1, source_target_pairs={{0,32},{32,0},{64,96},{96,64},{128,160},{160,128},{192,224},{224,1... | collective-permute-start | bytes 147464 | tf_op jit(solution)/shard_map/ppermute | solution.py:58
  66.2 26.4 %all-to-all-start.2 = ((bf16[32,16,384]{2,1,0:T(8,128)(2,1)}), bf16[32,16,384]{2,1,0:T(8,128)(2,1)S(1)}, u32[]{:S(2)}, u32[]{:S(2)}) async-start(bf16[32,16,384]{2,1,0:T(8,128)(2,1)} %bitcast.17), calls=%async_computation.2 | async-start | bytes 786432 | tf_op jit(solution)/shard_map/all_to_all | solution.py:66
  80.6 10.8 %collective-permute-start.2 = (bf16[128,384]{1,0:T(8,128)(2,1)S(1)}, bf16[128,384]{1,0:T(8,128)(2,1)S(1)}, u32[]{:S(2)}, u32[]{:S(2)}) collective-permute-start(bf16[128,384]{1,0:T(8,128)(2,1)S(1)} %bitcast.236), channel_id=1, source_target_pairs={{0,256},{32,288},{64,320},{96,352},{128,384},{160,416},{192,448},{... | collective-permute-start | bytes 294920 | tf_op jit(solution)/shard_map/ppermute | solution.py:54
  92.6 22.4 %collective-permute-start.10 = (bf16[512,384]{1,0:T(8,128)(2,1)S(1)}, bf16[512,384]{1,0:T(8,128)(2,1)}, u32[]{:S(2)}, u32[]{:S(2)}) collective-permute-start(bf16[512,384]{1,0:T(8,128)(2,1)S(1)} %bitcast.222), channel_id=1, source_target_pairs={{0,64},{32,96},{64,128},{96,160},{128,192},{160,224},{192,256},{22... | collective-permute-start | bytes 1179656 | tf_op jit(solution)/shard_map/ppermute | solution.py:54
  96.7 37.2 %collective-permute-start.17 = (bf16[512,384]{1,0:T(8,128)(2,1)S(1)}, bf16[512,384]{1,0:T(8,128)(2,1)}, u32[]{:S(2)}, u32[]{:S(2)}) collective-permute-start(bf16[512,384]{1,0:T(8,128)(2,1)S(1)} %bitcast.223), channel_id=1, source_target_pairs={{0,448},{32,480},{64,0},{96,32},{128,64},{160,96},{192,128},{224,1... | collective-permute-start | bytes 1179656 | tf_op jit(solution)/shard_map/ppermute | solution.py:54
  99.7 26.5 %collective-permute-start.3 = (bf16[512,384]{1,0:T(8,128)(2,1)S(1)}, bf16[512,384]{1,0:T(8,128)(2,1)}, u32[]{:S(2)}, u32[]{:S(2)}) collective-permute-start(bf16[512,384]{1,0:T(8,128)(2,1)S(1)} %bitcast.224), channel_id=1, source_target_pairs={{0,32},{32,0},{64,96},{96,64},{128,160},{160,128},{192,224},{224,1... | collective-permute-start | bytes 1179656 | tf_op jit(solution)/shard_map/ppermute | solution.py:58
  115.0 70.6 %all-to-all-start.3 = ((bf16[32,32,384]{2,1,0:T(8,128)(2,1)}), bf16[32,32,384]{2,1,0:T(8,128)(2,1)}, u32[]{:S(2)}, u32[]{:S(2)}) async-start(bf16[32,32,384]{2,1,0:T(8,128)(2,1)} %bitcast.221), calls=%async_computation.3 | async-start | bytes 1572864 | tf_op jit(solution)/shard_map/all_to_all | solution.py:66
  123.4 24.7 %collective-permute-start.18 = (bf16[512,384]{1,0:T(8,128)(2,1)}, bf16[512,384]{1,0:T(8,128)(2,1)}, u32[]{:S(2)}, u32[]{:S(2)}) collective-permute-start(bf16[512,384]{1,0:T(8,128)(2,1)} %collective-permute-done.10), channel_id=1, source_target_pairs={{0,64},{32,96},{64,128},{96,160},{128,192},{160,224},{192,256},{22... | collective-permute-start | bytes 1179656 | tf_op jit(solution)/shard_map/ppermute | solution.py:54
  126.2 31.7 %collective-permute-start.5 = (bf16[512,384]{1,0:T(8,128)(2,1)}, bf16[512,384]{1,0:T(8,128)(2,1)S(1)}, u32[]{:S(2)}, u32[]{:S(2)}) collective-permute-start(bf16[512,384]{1,0:T(8,128)(2,1)} %collective-permute-done.3), channel_id=1, source_target_pairs={{0,448},{32,480},{64,0},{96,32},{128,64},{160,96},{192,128},{224,1... | collective-permute-start | bytes 1179656 | tf_op jit(solution)/shard_map/ppermute | solution.py:54
  130.5 32.6 %collective-permute-start.4 = (bf16[512,384]{1,0:T(8,128)(2,1)}, bf16[512,384]{1,0:T(8,128)(2,1)S(1)}, u32[]{:S(2)}, u32[]{:S(2)}) collective-permute-start(bf16[512,384]{1,0:T(8,128)(2,1)} %collective-permute-done.3), channel_id=1, source_target_pairs={{0,64},{32,96},{64,128},{96,160},{128,192},{160,224},{192,256},{22... | collective-permute-start | bytes 1179656 | tf_op jit(solution)/shard_map/ppermute | solution.py:54
  133.8 13.8 %collective-permute-start.19 = (bf16[512,384]{1,0:T(8,128)(2,1)}, bf16[512,384]{1,0:T(8,128)(2,1)S(1)}, u32[]{:S(2)}, u32[]{:S(2)}) collective-permute-start(bf16[512,384]{1,0:T(8,128)(2,1)} %collective-permute-done.17), channel_id=1, source_target_pairs={{0,448},{32,480},{64,0},{96,32},{128,64},{160,96},{192,128},{224,1... | collective-permute-start | bytes 1179656 | tf_op jit(solution)/shard_map/ppermute | solution.py:54
  150.5 31.6 %collective-permute-start.21 = (bf16[512,384]{1,0:T(8,128)(2,1)S(1)}, bf16[512,384]{1,0:T(8,128)(2,1)S(1)}, u32[]{:S(2)}, u32[]{:S(2)}) collective-permute-start(bf16[512,384]{1,0:T(8,128)(2,1)S(1)} %collective-permute-done.19), channel_id=1, source_target_pairs={{0,448},{32,480},{64,0},{96,32},{128,64},{160,96},{192,128},{224,1... | collective-permute-start | bytes 1179656 | tf_op jit(solution)/shard_map/ppermute | solution.py:54
  156.0 31.4 %collective-permute-start.20 = (bf16[512,384]{1,0:T(8,128)(2,1)}, bf16[512,384]{1,0:T(8,128)(2,1)S(1)}, u32[]{:S(2)}, u32[]{:S(2)}) collective-permute-start(bf16[512,384]{1,0:T(8,128)(2,1)} %collective-permute-done.18), channel_id=1, source_target_pairs={{0,64},{32,96},{64,128},{96,160},{128,192},{160,224},{192,256},{22... | collective-permute-start | bytes 1179656 | tf_op jit(solution)/shard_map/ppermute | solution.py:54
  157.9 13.9 %collective-permute-start.7 = (bf16[512,384]{1,0:T(8,128)(2,1)S(1)}, bf16[512,384]{1,0:T(8,128)(2,1)S(1)}, u32[]{:S(2)}, u32[]{:S(2)}) collective-permute-start(bf16[512,384]{1,0:T(8,128)(2,1)S(1)} %collective-permute-done.5), channel_id=1, source_target_pairs={{0,448},{32,480},{64,0},{96,32},{128,64},{160,96},{192,128},{224,1... | collective-permute-start | bytes 1179656 | tf_op jit(solution)/shard_map/ppermute | solution.py:54
  163.1 14.7 %collective-permute-start.6 = (bf16[512,384]{1,0:T(8,128)(2,1)S(1)}, bf16[512,384]{1,0:T(8,128)(2,1)}, u32[]{:S(2)}, u32[]{:S(2)}) collective-permute-start(bf16[512,384]{1,0:T(8,128)(2,1)S(1)} %collective-permute-done.4), channel_id=1, source_target_pairs={{0,64},{32,96},{64,128},{96,160},{128,192},{160,224},{192,256},{22... | collective-permute-start | bytes 1179656 | tf_op jit(solution)/shard_map/ppermute | solution.py:54
  171.8 12.4 %collective-permute-start.9 = (bf16[512,384]{1,0:T(8,128)(2,1)S(1)}, bf16[512,384]{1,0:T(8,128)(2,1)S(1)}, u32[]{:S(2)}, u32[]{:S(2)}) collective-permute-start(bf16[512,384]{1,0:T(8,128)(2,1)S(1)} %collective-permute-done.7), channel_id=1, source_target_pairs={{0,448},{32,480},{64,0},{96,32},{128,64},{160,96},{192,128},{224,1... | collective-permute-start | bytes 1179656 | tf_op jit(solution)/shard_map/ppermute | solution.py:54
  180.2 12.4 %collective-permute-start.8 = (bf16[512,384]{1,0:T(8,128)(2,1)}, bf16[512,384]{1,0:T(8,128)(2,1)}, u32[]{:S(2)}, u32[]{:S(2)}) collective-permute-start(bf16[512,384]{1,0:T(8,128)(2,1)} %collective-permute-done.6), channel_id=1, source_target_pairs={{0,64},{32,96},{64,128},{96,160},{128,192},{160,224},{192,256},{22... | collective-permute-start | bytes 1179656 | tf_op jit(solution)/shard_map/ppermute | solution.py:54
  196.0 17.1 %copy-start.6 = (bf16[1,256,384]{2,0,1:T(2,128)(2,1)S(1)}, bf16[1,256,384]{2,0,1:T(2,128)(2,1)}, u32[]{:S(2)}) copy-start(bf16[1,256,384]{2,0,1:T(2,128)(2,1)} %get-tuple-element.26) | copy-start | bytes 589828
  196.3 18.0 %copy-start.10 = (bf16[1,256,384]{2,0,1:T(2,128)(2,1)S(1)}, bf16[1,256,384]{2,0,1:T(2,128)(2,1)}, u32[]{:S(2)}) copy-start(bf16[1,256,384]{2,0,1:T(2,128)(2,1)} %get-tuple-element.20) | copy-start | bytes 589828
  198.7 15.6 %collective-permute-start.22 = (bf16[512,384]{1,0:T(8,128)(2,1)S(1)}, bf16[512,384]{1,0:T(8,128)(2,1)S(1)}, u32[]{:S(2)}, u32[]{:S(2)}) collective-permute-start(bf16[512,384]{1,0:T(8,128)(2,1)S(1)} %convolution_convert_fusion.4), channel_id=1, source_target_pairs={{0,64},{32,96},{64,128},{96,160},{128,192},{160,224},{192,256},{22... | collective-permute-start | bytes 1179656 | tf_op jit(solution)/shard_map/ppermute | solution.py:54
  200.6 23.9 %collective-permute-start.25 = (bf16[512,384]{1,0:T(8,128)(2,1)}, bf16[512,384]{1,0:T(8,128)(2,1)}, u32[]{:S(2)}, u32[]{:S(2)}) collective-permute-start(bf16[512,384]{1,0:T(8,128)(2,1)} %convolution_convert_fusion.3), channel_id=1, source_target_pairs={{0,448},{32,480},{64,0},{96,32},{128,64},{160,96},{192,128},{224,1... | collective-permute-start | bytes 1179656 | tf_op jit(solution)/shard_map/ppermute | solution.py:54
  207.0 26.3 %collective-permute-start.14 = (bf16[512,384]{1,0:T(8,128)(2,1)}, bf16[512,384]{1,0:T(8,128)(2,1)}, u32[]{:S(2)}, u32[]{:S(2)}) collective-permute-start(bf16[512,384]{1,0:T(8,128)(2,1)} %convolution_convert_fusion.5), channel_id=1, source_target_pairs={{0,448},{32,480},{64,0},{96,32},{128,64},{160,96},{192,128},{224,1... | collective-permute-start | bytes 1179656 | tf_op jit(solution)/shard_map/ppermute | solution.py:54
  208.9 30.4 %collective-permute-start.11 = (bf16[512,384]{1,0:T(8,128)(2,1)}, bf16[512,384]{1,0:T(8,128)(2,1)}, u32[]{:S(2)}, u32[]{:S(2)}) collective-permute-start(bf16[512,384]{1,0:T(8,128)(2,1)} %convolution_convert_fusion.6), channel_id=1, source_target_pairs={{0,64},{32,96},{64,128},{96,160},{128,192},{160,224},{192,256},{22... | collective-permute-start | bytes 1179656 | tf_op jit(solution)/shard_map/ppermute | solution.py:54
  216.1 60.5 %all-to-all-start.5 = ((bf16[32,32,384]{2,1,0:T(8,128)(2,1)}), bf16[32,32,384]{2,1,0:T(8,128)(2,1)}, u32[]{:S(2)}, u32[]{:S(2)}) async-start(bf16[32,32,384]{2,1,0:T(8,128)(2,1)} %bitcast.40), calls=%async_computation.5 | async-start | bytes 1572864 | tf_op jit(solution)/shard_map/all_to_all | solution.py:66
  224.5 23.4 %copy-start.4 = (f32[512,384]{1,0:T(8,128)S(1)}, f32[512,384]{1,0:T(8,128)}, u32[]{:S(2)}) copy-start(f32[512,384]{1,0:T(8,128)} %fusion.119) | copy-start | bytes 2359300
  226.0 16.7 %collective-permute-start.26 = (bf16[512,384]{1,0:T(8,128)(2,1)S(1)}, bf16[512,384]{1,0:T(8,128)(2,1)S(1)}, u32[]{:S(2)}, u32[]{:S(2)}) collective-permute-start(bf16[512,384]{1,0:T(8,128)(2,1)S(1)} %add_convert_fusion.3), channel_id=1, source_target_pairs={{0,448},{32,480},{64,0},{96,32},{128,64},{160,96},{192,128},{224,1... | collective-permute-start | bytes 1179656 | tf_op jit(solution)/shard_map/ppermute | solution.py:54
  230.6 17.3 %collective-permute-start.23 = (bf16[512,384]{1,0:T(8,128)(2,1)S(1)}, bf16[512,384]{1,0:T(8,128)(2,1)S(1)}, u32[]{:S(2)}, u32[]{:S(2)}) collective-permute-start(bf16[512,384]{1,0:T(8,128)(2,1)S(1)} %add_convert_fusion.5), channel_id=1, source_target_pairs={{0,64},{32,96},{64,128},{96,160},{128,192},{160,224},{192,256},{22... | collective-permute-start | bytes 1179656 | tf_op jit(solution)/shard_map/ppermute | solution.py:54
  234.7 15.2 %collective-permute-start.15 = (bf16[512,384]{1,0:T(8,128)(2,1)S(1)}, bf16[512,384]{1,0:T(8,128)(2,1)S(1)}, u32[]{:S(2)}, u32[]{:S(2)}) collective-permute-start(bf16[512,384]{1,0:T(8,128)(2,1)S(1)} %add_convert_fusion.7), channel_id=1, source_target_pairs={{0,448},{32,480},{64,0},{96,32},{128,64},{160,96},{192,128},{224,1... | collective-permute-start | bytes 1179656 | tf_op jit(solution)/shard_map/ppermute | solution.py:54
  240.6 23.7 %copy-start.5 = (f32[512,384]{1,0:T(8,128)S(1)}, f32[512,384]{1,0:T(8,128)}, u32[]{:S(2)}) copy-start(f32[512,384]{1,0:T(8,128)} %fusion.123) | copy-start | bytes 2359300
  240.6 15.2 %collective-permute-start.12 = (bf16[512,384]{1,0:T(8,128)(2,1)S(1)}, bf16[512,384]{1,0:T(8,128)(2,1)S(1)}, u32[]{:S(2)}, u32[]{:S(2)}) collective-permute-start(bf16[512,384]{1,0:T(8,128)(2,1)S(1)} %add_convert_fusion.9), channel_id=1, source_target_pairs={{0,64},{32,96},{64,128},{96,160},{128,192},{160,224},{192,256},{22... | collective-permute-start | bytes 1179656 | tf_op jit(solution)/shard_map/ppermute | solution.py:54
  242.8 15.2 %collective-permute-start.27 = (bf16[512,384]{1,0:T(8,128)(2,1)S(1)}, bf16[512,384]{1,0:T(8,128)(2,1)S(1)}, u32[]{:S(2)}, u32[]{:S(2)}) collective-permute-start(bf16[512,384]{1,0:T(8,128)(2,1)S(1)} %add_convert_fusion.2), channel_id=1, source_target_pairs={{0,448},{32,480},{64,0},{96,32},{128,64},{160,96},{192,128},{224,1... | collective-permute-start | bytes 1179656 | tf_op jit(solution)/shard_map/ppermute | solution.py:54
  248.0 16.2 %collective-permute-start.24 = (bf16[512,384]{1,0:T(8,128)(2,1)S(1)}, bf16[512,384]{1,0:T(8,128)(2,1)S(1)}, u32[]{:S(2)}, u32[]{:S(2)}) collective-permute-start(bf16[512,384]{1,0:T(8,128)(2,1)S(1)} %add_convert_fusion.4), channel_id=1, source_target_pairs={{0,64},{32,96},{64,128},{96,160},{128,192},{160,224},{192,256},{22... | collective-permute-start | bytes 1179656 | tf_op jit(solution)/shard_map/ppermute | solution.py:54
  250.1 18.0 %collective-permute-start.16 = (bf16[512,384]{1,0:T(8,128)(2,1)S(1)}, bf16[512,384]{1,0:T(8,128)(2,1)S(1)}, u32[]{:S(2)}, u32[]{:S(2)}) collective-permute-start(bf16[512,384]{1,0:T(8,128)(2,1)S(1)} %add_convert_fusion.6), channel_id=1, source_target_pairs={{0,448},{32,480},{64,0},{96,32},{128,64},{160,96},{192,128},{224,1... | collective-permute-start | bytes 1179656 | tf_op jit(solution)/shard_map/ppermute | solution.py:54
  255.9 29.0 %copy-start.28 = (s32[128,4]{0,1:T(4,128)S(1)}, s32[128,4]{0,1:T(4,128)}, u32[]{:S(2)}) copy-start(s32[128,4]{0,1:T(4,128)} %param.19) | copy-start | bytes 6148
  255.9 29.0 %copy-start.31 = (f32[128,4]{0,1:T(4,128)S(1)}, f32[128,4]{0,1:T(4,128)}, u32[]{:S(2)}) copy-start(f32[128,4]{0,1:T(4,128)} %param.20) | copy-start | bytes 6148
  256.0 29.0 %copy-start.18 = (pred[32,16,128]{2,1,0:T(8,128)(4,1)S(1)}, pred[32,16,128]{2,1,0:T(8,128)(4,1)}, u32[]{:S(2)}) copy-start(pred[32,16,128]{2,1,0:T(8,128)(4,1)} %copy-done.16) | copy-start | bytes 196612
  256.0 29.0 %copy-start.24 = (pred[32,16,128]{2,1,0:T(8,128)(4,1)S(1)}, pred[32,16,128]{2,1,0:T(8,128)(4,1)}, u32[]{:S(2)}) copy-start(pred[32,16,128]{2,1,0:T(8,128)(4,1)} %get-tuple-element.37) | copy-start | bytes 196612
  256.0 15.1 %collective-permute-start.13 = (bf16[512,384]{1,0:T(8,128)(2,1)S(1)}, bf16[512,384]{1,0:T(8,128)(2,1)S(1)}, u32[]{:S(2)}, u32[]{:S(2)}) collective-permute-start(bf16[512,384]{1,0:T(8,128)(2,1)S(1)} %add_convert_fusion.8), channel_id=1, source_target_pairs={{0,64},{32,96},{64,128},{96,160},{128,192},{160,224},{192,256},{22... | collective-permute-start | bytes 1179656 | tf_op jit(solution)/shard_map/ppermute | solution.py:54
  264.4 11.2 %collective-permute-start.28 = (bf16[512,384]{1,0:T(8,128)(2,1)S(1)}, bf16[512,384]{1,0:T(8,128)(2,1)S(1)}, u32[]{:S(2)}, u32[]{:S(2)}) collective-permute-start(bf16[512,384]{1,0:T(8,128)(2,1)S(1)} %add_convert_fusion.1), channel_id=1, source_target_pairs={{0,32},{32,0},{64,96},{96,64},{128,160},{160,128},{192,224},{224,1... | collective-permute-start | bytes 1179656 | tf_op jit(solution)/shard_map/ppermute | solution.py:58
  268.0 22.6 %copy-start.20 = (f32[8,8,384]{2,1,0:T(8,128)S(1)}, f32[8,8,384]{2,1,0:T(8,128)}, u32[]{:S(2)}) copy-start(f32[8,8,384]{2,1,0:T(8,128)} %get-tuple-element.34) | copy-start | bytes 294916
  268.0 31.4 %copy-start.30 = (s32[16]{0:T(128)S(1)}, s32[16]{0:T(128)}, u32[]{:S(2)}) copy-start(s32[16]{0:T(128)} %copy-done.29) | copy-start | bytes 196
  276.6 22.8 %all-to-all-start.4 = ((bf16[32,16,384]{2,1,0:T(8,128)(2,1)}), bf16[32,16,384]{2,1,0:T(8,128)(2,1)S(1)}, u32[]{:S(2)}, u32[]{:S(2)}) async-start(bf16[32,16,384]{2,1,0:T(8,128)(2,1)} %bitcast.35), calls=%async_computation.4 | async-start | bytes 786432 | tf_op jit(solution)/shard_map/all_to_all | solution.py:66
  287.9 14.7 %collective-permute-start.29 = (f32[128,384]{1,0:T(8,128)S(1)}, f32[128,384]{1,0:T(8,128)S(1)}, u32[]{:S(2)}, u32[]{:S(2)}) collective-permute-start(f32[128,384]{1,0:T(8,128)S(1)} %fusion.25), channel_id=1, source_target_pairs={{0,256},{32,288},{64,320},{96,352},{128,384},{160,416},{192,448},{... | collective-permute-start | bytes 589832 | tf_op jit(solution)/shard_map/ppermute | solution.py:54
  (21 other events, 142.7 us)

commit v4 on v3

--- a/solution.py
+++ b/solution.py
@@ -96,16 +96,16 @@
     first_half = half == 0
 
     other_proj = swap_halves(out_proj)
-    proj = jnp.concatenate(
-        [jnp.where(first_half, out_proj, other_proj), jnp.where(first_half, other_proj, out_proj)], axis=0
-    )
-    proj = to_blocks(proj).transpose(1, 0, 2)
 
     attended = attend(queries, window_key_value_cache, new_key_value, head_sink_logits)
-    heads = attended.reshape(own_rows, BLOCKS, HALVES * 128)
-    sent = jnp.concatenate([heads, to_blocks(residual)], axis=2).transpose(1, 0, 2)
+    heads = attended.reshape(own_rows, BLOCKS, HALVES, 128)
+    own_heads = jnp.where(first_half, heads[:, :, 0], heads[:, :, 1])
+    other_heads = jnp.where(first_half, heads[:, :, 1], heads[:, :, 0])
+    sent = jnp.concatenate([own_heads, other_heads, to_blocks(residual)], axis=2).transpose(1, 0, 2)
     got = over_z(sent).reshape(half_rows, HALVES * 128 + LANES)
-    partial_sums = jnp.einsum("rk,zkd->zrd", got[:, : HALVES * 128], proj, preferred_element_type=F32).astype(BF16)
+    partial_sums = jnp.dot(got[:, :128], out_proj, preferred_element_type=F32)
+    partial_sums = partial_sums + jnp.dot(got[:, 128:256], other_proj, preferred_element_type=F32)
+    partial_sums = to_blocks(lax.optimization_barrier(partial_sums.astype(BF16))).transpose(1, 0, 2)
     hidden_state = got[:, HALVES * 128 :].astype(F32) + jnp.sum(over_z(partial_sums).astype(F32), axis=0)
 
     gain = lax.dynamic_index_in_dim(to_blocks(norm_gain), z_index, 0, keepdims=False)
@@ -153,67 +153,58 @@
         w = w.reshape(BLOCKS, BLOCK, FF_LOCAL)
         return jnp.pad(w, ((0, 0), (0, LANES - BLOCK), (0, FF_LANES - FF_LOCAL)))
 
-    def own_first(blocks):
-        return lax.dynamic_slice_in_dim(jnp.concatenate([blocks, blocks]), z_index, BLOCKS, 0)
-
     w_in = jnp.concatenate([padded_in(w_gate), padded_in(w_up)], axis=2)
     in_row = lax.broadcasted_iota(jnp.int32, w_in.shape, 1)
     in_column = lax.broadcasted_iota(jnp.int32, w_in.shape, 2)
     w_in = jnp.where((in_column == FF_LOCAL) & (in_row >= BLOCK) & (in_row < BLOCK + 2), jnp.ones((), BF16), w_in)
-    w_in = own_first(w_in)
     w_out = jnp.pad(to_blocks(w_down[0]).transpose(1, 0, 2), ((0, 0), (0, FF_LANES - FF_LOCAL), (0, 0)))
-    w_out = own_first(w_out)
+
+    def at_offset(blocks, offset):
+        index = lax.bitwise_and(z_index + offset % BLOCKS, BLOCKS - 1)
+        return lax.dynamic_index_in_dim(blocks, index, 0, keepdims=False)
+
+    def input_term(rows, offset):
+        return jnp.dot(rows, at_offset(w_in, offset), preferred_element_type=F32)
 
     far_outgoing = picked(taken_both, shift_over_z(scaled, FAR))
     own = over_experts(picked(taken_own, scaled)).reshape(half_slots, LANES)
     own, w_in, w_out, far_outgoing = lax.optimization_barrier((own, w_in, w_out, far_outgoing))
-    chunks = [own, swap_halves(own)]
-    ups, downs = [chunks], [chunks]
-    for step in range(1, FAR):
-        pairs = [(shift_over_z(ups[-1][c], 1), shift_over_z(downs[-1][c], -1)) for c in range(2)]
-        ups.append([pair[0] for pair in pairs])
-        downs.append([pair[1] for pair in pairs])
-        if step == 1:
-            far_outgoing = lax.optimization_barrier((far_outgoing, pairs[0][0]))[0]
+    halves_of_own = [own, swap_halves(own)]
+    up_block = jnp.concatenate([shift_over_z(h, 1) for h in halves_of_own])
+    down_block = jnp.concatenate([shift_over_z(h, -1) for h in halves_of_own])
+    both = input_term(jnp.concatenate(halves_of_own), 0) + input_term(up_block, -1)
+    far_outgoing, both = lax.optimization_barrier((far_outgoing, both))
     far = over_experts(far_outgoing).reshape(N_EXP, 2, half_cap, LANES)
-
-    expert_hidden = []
-    for c in range(2):
-        both = jnp.dot(chunks[c], w_in[0], preferred_element_type=F32)
-        for step in range(1, FAR):
-            if step == FAR - 1:
-                both = lax.optimization_barrier(both)
-            both = both + jnp.dot(ups[step][c], w_in[BLOCKS - step], preferred_element_type=F32)
-            both = both + jnp.dot(downs[step][c], w_in[step], preferred_element_type=F32)
-        both = both + jnp.dot(far[:, c].reshape(half_slots, LANES), w_in[FAR], preferred_element_type=F32)
-        factor = lax.rsqrt(both[:, FF_LOCAL : FF_LOCAL + 1] * (1.0 / D) + 1e-05)
-        gate = both[:, :FF_LANES] * factor
-        up = both[:, FF_LANES:] * factor
-        expert_hidden.append((gate * jax.nn.sigmoid(1.702 * gate) * (up + 1.0)).astype(BF16))
-
-    def output_block(c, offset):
-        return jnp.dot(expert_hidden[c], w_out[offset % BLOCKS], preferred_element_type=F32)
-
-    up_sums, down_sums = [None, None], [None, None]
-    for offset in range(FAR - 1, 0, -1):
-        for c in range(2):
-            up_sum, down_sum = output_block(c, offset), output_block(c, -offset)
-            if offset < FAR - 1:
-                up_sum = up_sum + up_sums[c].astype(F32)
-                down_sum = down_sum + down_sums[c].astype(F32)
-            up_sums[c] = shift_over_z(up_sum.astype(BF16), 1)
-            down_sums[c] = shift_over_z(down_sum.astype(BF16), -1)
-        if offset == FAR - 1:
-            far_hidden = lax.optimization_barrier((expert_hidden[0], expert_hidden[1], up_sums[0]))[:2]
-    far_value = jnp.stack(
-        [
-            jnp.dot(h, w_out[FAR], preferred_element_type=F32).astype(BF16).reshape(N_EXP, half_cap, LANES)
-            for h in far_hidden
-        ],
-        axis=1,
-    )
+    both = both + input_term(down_block, 1)
+    for step in range(2, FAR):
+        up_block, down_block = shift_over_z(up_block, 1), shift_over_z(down_block, -1)
+        if step == FAR - 1:
+            both = lax.optimization_barrier(both)
+        both = both + input_term(up_block, -step)
+        both = both + input_term(down_block, step)
+    both = both + input_term(far.transpose(1, 0, 2, 3).reshape(N_EXP * CAP, LANES), FAR)
+    factor = lax.rsqrt(both[:, FF_LOCAL : FF_LOCAL + 1] * (1.0 / D) + 1e-05)
+    gate = both[:, :FF_LANES] * factor
+    up = both[:, FF_LANES:] * factor
+    expert_hidden = (gate * jax.nn.sigmoid(1.702 * gate) * (up + 1.0)).astype(BF16)
+
+    def output_block(offset):
+        return jnp.dot(expert_hidden, at_offset(w_out, offset), preferred_element_type=F32)
+
+    up_sum = shift_over_z(output_block(FAR - 1).astype(BF16), 1)
+    down_sum = shift_over_z(output_block(1 - FAR).astype(BF16), -1)
+    far_value = output_block(FAR).astype(BF16).reshape(2, N_EXP, half_cap, LANES).transpose(1, 0, 2, 3)
     far_mixed = shift_over_z(mixed_of(taken_both, far_value.reshape(N_EXP, CAP, LANES)), FAR)
-    sums = [output_block(c, 0) + up_sums[c].astype(F32) + down_sums[c].astype(F32) for c in range(2)]
+    for offset in range(FAR - 2, 0, -1):
+        up_sum = (output_block(offset) + up_sum.astype(F32)).astype(BF16)
+        down_sum = (output_block(-offset) + down_sum.astype(F32)).astype(BF16)
+        if offset > 1:
+            up_sum, down_sum = shift_over_z(up_sum, 1), shift_over_z(down_sum, -1)
+    own_block = output_block(0)
+    sums = []
+    for rows in (slice(0, half_slots), slice(half_slots, None)):
+        arrived = shift_over_z(up_sum[rows], 1).astype(F32) + shift_over_z(down_sum[rows], -1).astype(F32)
+        sums.append(own_block[rows] + arrived)
     other_sum = swap_halves(sums[0].astype(BF16))
     whole_sum = (sums[1] + other_sum.astype(F32)).astype(BF16)
     mixed = mixed_of(taken_other, whole_sum.reshape(N_EXP, half_cap, LANES)) + far_mixed

time: 324 us -> 294 us (0.907)
  starting transfers between devices: 154 us -> 127 us
  waiting for transfers between devices: 62 us -> 80.8 us
  matrix products: 41.7 us -> 31.8 us
  other arithmetic: 16.5 us -> 7.73 us
  local copies, waits for them, and re-layouts: 28.8 us -> 25.3 us
    ppermute x26 -> x18, starting transfers between devices: 87.7 us -> 65 us  [shift_over_z(): return lax.ppermute(array, 'attn', pairs)]
    slice x2 -> x3, local copies, waits for them, and re-layouts: 10.9 us -> 0.21 us  [the longest x1 0.08 us: local(): down_sum[rows]]
    ppermute x26 -> x18, waiting for transfers between devices: 36.8 us -> 44.5 us  [shift_over_z(): return lax.ppermute(array, 'attn', pairs)]
    all_to_all x2, waiting for transfers between devices: 10.7 us -> 17.9 us  [over_z(): lax.all_to_all(array, 'attn', 0, 0, tiled=True, axis_index_groups=Z_GROUPS)]
    concatenate x3 -> x0, other arithmetic: 6.66 us -> none  [the longest x2 5.37 us: own_first(): jnp.concatenate([blocks, blocks])]
    dot_general x33 -> x18, matrix products: 32.6 us -> 26.2 us  [the longest x8 16.8 us: input_term(): return jnp.dot(rows, at_offset(w_in, offset), preferred_element_type=F32)]
    dynamic_slice x0 -> x1, local copies, waits for them, and re-layouts: none -> 4.23 us  [at_offset(): return lax.dynamic_index_in_dim(blocks, index, 0, keepdims=False)]
    all_to_all x2, starting transfers between devices: 17.3 us -> 13.8 us  [over_z(): lax.all_to_all(array, 'attn', 0, 0, tiled=True, axis_index_groups=Z_GROUPS)]
  transfers between devices with their start and end apart: 36 -> 28, of which waited for: 14 -> 17; matrix products, arithmetic and copies ran while one was open for 24% -> 19% of each run, Pallas kernels for 0% -> 0%
where the time goes in v4:
time: 294 us; the launch traced here: 290 us
  starting transfers between devices  127 us (43%)
  waiting for transfers between devices  80.8 us (27%)
  matrix products  31.8 us (11%)
  local copies, waits for them, and re-layouts  25.3 us (9%)
  blocking collectives  16.8 us (6%)
  other arithmetic  7.73 us (3%)
    ppermute x18, starting transfers between devices, shift_over_z(): return lax.ppermute(array, 'attn', pairs)  65 us
    ppermute x18, waiting for transfers between devices, shift_over_z(): return lax.ppermute(array, 'attn', pairs)  44.5 us
    all_to_all x4, starting transfers between devices, over_experts(): return lax.all_to_all(array, 'exp', 0, 0, tiled=True)  34 us
    all_to_all x2, waiting for transfers between devices, over_z(): lax.all_to_all(array, 'attn', 0, 0, tiled=True, axis_index_groups=Z_GROUPS)  17.9 us
    all_to_all x1, blocking collectives, local(): lax.all_to_all(mixed.reshape(N_ATTN, own_rows, LANES), 'attn', 0, 0, tile...  16.8 us
    dot_general x8, matrix products, input_term(): return jnp.dot(rows, at_offset(w_in, offset), preferred_element_type=F32)  16.8 us
    ppermute x4, starting transfers between devices, swap_halves(): return lax.ppermute(array, 'attn', [(i, i ^ 1) for i in range(N_ATTN)])  14 us
    all_to_all x2, starting transfers between devices, over_z(): lax.all_to_all(array, 'attn', 0, 0, tiled=True, axis_index_groups=Z_GROUPS)  13.8 us
  transfers between devices with their start and end apart: 28, of which 17 were waited for; matrix products, arithmetic and copies ran while one was open for 19% of the time, Pallas kernels for 0%

profile of v4, /device:TPU:6, one launch (start us, length us, event | category | flops | bytes accessed | tf_op | source)
XLA Modules:
  0.0 290.1 jit_solution(4514469450347332046)
XLA Ops:
  0.0 3.3 %collective-permute-start = (bf16[128,2880]{0,1:T(8,128)(2,1)}, bf16[128,2880]{0,1:T(8,128)(2,1)S(1)}, u32[]{:S(2)}, u32[]{:S(2)}) collective-permute-start(bf16[128,2880]{0,1:T(8,128)(2,1)} %param.17), channel_id=1, source_target_pairs={{0,32},{32,0},{64,96},{96,64},{128,160},{160,128},{192,224},{224,1... | collective-permute-start | bytes 2211848 | tf_op jit(solution)/shard_map/ppermute | solution.py:58
  5.3 2.2 fusion.122
  12.0 10.3 %all-to-all-start = ((bf16[8,8,640]{2,1,0:T(8,128)(2,1)}), bf16[8,8,640]{2,1,0:T(8,128)(2,1)S(1)}, u32[]{:S(2)}, u32[]{:S(2)}) async-start(bf16[8,8,640]{2,1,0:T(8,128)(2,1)} %copy.108), calls=%async_computation | async-start | bytes 163840 | tf_op jit(solution)/shard_map/all_to_all | solution.py:62
  24.0 6.9 %all-to-all-done = bf16[8,8,640]{2,1,0:T(8,128)(2,1)S(1)} async-done(((bf16[8,8,640]{2,1,0:T(8,128)(2,1)}), bf16[8,8,640]{2,1,0:T(8,128)(2,1)S(1)}, u32[]{:S(2)}, u32[]{:S(2)}) %all-to-all-start) | async-done | bytes 81952 | tf_op jit(solution)/shard_map/all_to_all | solution.py:62
  34.2 3.5 %all-to-all-start.1 = ((bf16[8,64,384]{2,1,0:T(8,128)(2,1)}), bf16[8,64,384]{2,1,0:T(8,128)(2,1)S(1)}, u32[]{:S(2)}, u32[]{:S(2)}) async-start(bf16[8,64,384]{2,1,0:T(8,128)(2,1)} %pad_bitcast_fusion.1), calls=%async_computation.1 | async-start | bytes 786432 | tf_op jit(solution)/shard_map/all_to_all | solution.py:62
  39.7 11.1 %all-to-all-done.1 = bf16[8,64,384]{2,1,0:T(8,128)(2,1)S(1)} async-done(((bf16[8,64,384]{2,1,0:T(8,128)(2,1)}), bf16[8,64,384]{2,1,0:T(8,128)(2,1)S(1)}, u32[]{:S(2)}, u32[]{:S(2)}) %all-to-all-start.1) | async-done | bytes 393248 | tf_op jit(solution)/shard_map/all_to_all | solution.py:62
  51.7 4.0 %collective-permute-start.1 = (bf16[64,384]{1,0:T(8,128)(2,1)S(1)}, bf16[64,384]{1,0:T(8,128)(2,1)S(1)}, u32[]{:S(2)}, u32[]{:S(2)}) collective-permute-start(bf16[64,384]{1,0:T(8,128)(2,1)S(1)} %select_convert_fusion), channel_id=1, source_target_pairs={{0,32},{32,0},{64,96},{96,64},{128,160},{160,128},{192,224},{224,1... | collective-permute-start | bytes 147464 | tf_op jit(solution)/shard_map/ppermute | solution.py:58
  55.8 2.0 copy.113
  62.0 8.7 %all-to-all-start.2 = ((bf16[32,16,384]{2,1,0:T(8,128)(2,1)}), bf16[32,16,384]{2,1,0:T(8,128)(2,1)S(1)}, u32[]{:S(2)}, u32[]{:S(2)}) async-start(bf16[32,16,384]{2,1,0:T(8,128)(2,1)} %bitcast.16), calls=%async_computation.2 | async-start | bytes 786432 | tf_op jit(solution)/shard_map/all_to_all | solution.py:66
  70.7 3.3 %and_select_fusion = bf16[8,384,512]{2,1,0:T(8,128)(2,1)} fusion(bf16[8,360,180]{2,1,0:T(8,128)(2,1)S(1)} %bitcast.164, bf16[8,360,180]{2,1,0:T(8,128)(2,1)} %bitcast.165, pred[384]{0:T(512)(128)(4,1)S(1)} %get-tuple-element.53, pred[512]{0:T(512)(128)(4,1)S(1)} %iota_compare_fusion.8, pred[384]{0:T(512)(128)(4,1)S(1)} %get-tuple-element.54), kind=kLoop, calls=%fused_computation.4 | loop fusion | flops 17301504 | bytes 5220608 | tf_op jit(solution)/shard_map/jit(_where)/select_n | solution.py:159
  74.0 2.5 collective-permute-start.2
  76.5 8.2 %collective-permute-done.2 = bf16[128,384]{1,0:T(8,128)(2,1)S(1)} collective-permute-done((bf16[128,384]{1,0:T(8,128)(2,1)S(1)}, bf16[128,384]{1,0:T(8,128)(2,1)S(1)}, u32[]{:S(2)}, u32[]{:S(2)}) %collective-permute-start.2) | collective-permute-done | bytes 98336 | tf_op jit(solution)/shard_map/ppermute | solution.py:54
  86.0 3.3 %collective-permute-start.3 = (bf16[512,384]{1,0:T(8,128)(2,1)S(1)}, bf16[512,384]{1,0:T(8,128)(2,1)}, u32[]{:S(2)}, u32[]{:S(2)}) collective-permute-start(bf16[512,384]{1,0:T(8,128)(2,1)S(1)} %bitcast.170), channel_id=1, source_target_pairs={{0,32},{32,0},{64,96},{96,64},{128,160},{160,128},{192,224},{224,1... | collective-permute-start | bytes 1179656 | tf_op jit(solution)/shard_map/ppermute | solution.py:58
  89.3 4.4 %collective-permute-start.4 = (bf16[512,384]{1,0:T(8,128)(2,1)S(1)}, bf16[512,384]{1,0:T(8,128)(2,1)S(1)}, u32[]{:S(2)}, u32[]{:S(2)}) collective-permute-start(bf16[512,384]{1,0:T(8,128)(2,1)S(1)} %bitcast.171), channel_id=1, source_target_pairs={{0,64},{32,96},{64,128},{96,160},{128,192},{160,224},{192,256},{22... | collective-permute-start | bytes 1179656 | tf_op jit(solution)/shard_map/ppermute | solution.py:54
  93.7 2.7 collective-permute-start.6
  96.4 3.5 %collective-permute-done.3 = bf16[512,384]{1,0:T(8,128)(2,1)} collective-permute-done((bf16[512,384]{1,0:T(8,128)(2,1)S(1)}, bf16[512,384]{1,0:T(8,128)(2,1)}, u32[]{:S(2)}, u32[]{:S(2)}) %collective-permute-start.3) | collective-permute-done | bytes 393248 | tf_op jit(solution)/shard_map/ppermute | solution.py:58
  99.9 2.4 collective-permute-start.5
  102.4 4.6 %collective-permute-start.7 = (bf16[512,384]{1,0:T(8,128)(2,1)}, bf16[512,384]{1,0:T(8,128)(2,1)S(1)}, u32[]{:S(2)}, u32[]{:S(2)}) collective-permute-start(bf16[512,384]{1,0:T(8,128)(2,1)} %collective-permute-done.3), channel_id=1, source_target_pairs={{0,448},{32,480},{64,0},{96,32},{128,64},{160,96},{192,128},{224,1... | collective-permute-start | bytes 1179656 | tf_op jit(solution)/shard_map/ppermute | solution.py:54
  110.4 3.6 %collective-permute-done.7 = bf16[512,384]{1,0:T(8,128)(2,1)S(1)} collective-permute-done((bf16[512,384]{1,0:T(8,128)(2,1)}, bf16[512,384]{1,0:T(8,128)(2,1)S(1)}, u32[]{:S(2)}, u32[]{:S(2)}) %collective-permute-start.7) | collective-permute-done | bytes 393248 | tf_op jit(solution)/shard_map/ppermute | solution.py:54
  114.9 5.5 %collective-permute-start.9 = (bf16[1024,384]{1,0:T(8,128)(2,1)}, bf16[1024,384]{1,0:T(8,128)(2,1)}, u32[]{:S(2)}, u32[]{:S(2)}) collective-permute-start(bf16[1024,384]{1,0:T(8,128)(2,1)} %constant_dynamic-update-slice_fusion.2), channel_id=1, source_target_pairs={{0,448},{32,480},{64,0},{96,32},{128,64},{160,96},{192,128},{224,1... | collective-permute-start | bytes 2359304 | tf_op jit(solution)/shard_map/ppermute | solution.py:54
  123.1 3.3 %convolution_add_fusion.1 = f32[1024,512]{1,0:T(8,128)} fusion(f32[1024,512]{1,0:T(8,128)S(1)} %fusion.23, bf16[1024,384]{1,0:T(8,128)(2,1)} %constant_dynamic-update-slice_fusion, bf16[8,384,512]{2,1,0:T(8,128)(2,1)} %and_select_fusion, s32[]{:T(128)S(6)} %select_n.144), kind=kOutput, calls=%fused_computation.10 | convolution fusion | flops 403177472 | bytes 5373956 | tf_op jit(solution)/shard_map/dot_general | solution.py:167
  126.4 8.3 %all-to-all-start.3 = ((bf16[32,32,384]{2,1,0:T(8,128)(2,1)}), bf16[32,32,384]{2,1,0:T(8,128)(2,1)S(1)}, u32[]{:S(2)}, u32[]{:S(2)}) async-start(bf16[32,32,384]{2,1,0:T(8,128)(2,1)} %bitcast.168), calls=%async_computation.3 | async-start | bytes 1572864 | tf_op jit(solution)/shard_map/all_to_all | solution.py:66
  134.7 4.2 %constant_dynamic-slice_fusion.5 = (bf16[1,256,384]{2,0,1:T(2,128)(2,1)}, bf16[1,256,384]{2,0,1:T(2,128)(2,1)}, bf16[1,256,384]{2,0,1:T(2,128)(2,1)}, bf16[1,256...) fusion(bf16[8,256,384]{2,0,1:T(8,128)(2,1)S(1)} %pad.33, ...), kind=kLoop, calls=%fused_computation.167 | loop fusion | bytes 3145760 | tf_op jit(solution)/shard_map/jit(dynamic_index_in_dim)/dynamic_slice | solution.py:164
  138.9 2.1 collective-permute-done.8
  143.0 1.9 fusion.41
  144.9 2.1 fusion.39
  147.0 5.1 %collective-permute-start.11 = (bf16[1024,384]{1,0:T(8,128)(2,1)}, bf16[1024,384]{1,0:T(8,128)(2,1)}, u32[]{:S(2)}, u32[]{:S(2)}) collective-permute-start(bf16[1024,384]{1,0:T(8,128)(2,1)} %collective-permute-done.9), channel_id=1, source_target_pairs={{0,448},{32,480},{64,0},{96,32},{128,64},{160,96},{192,128},{224,1... | collective-permute-start | bytes 2359304 | tf_op jit(solution)/shard_map/ppermute | solution.py:54
  152.2 2.0 add_add_fusion.1
  154.1 2.8 all-to-all-done.3
  158.7 3.5 %collective-permute-done.10 = bf16[1024,384]{1,0:T(8,128)(2,1)} collective-permute-done((bf16[1024,384]{1,0:T(8,128)(2,1)}, bf16[1024,384]{1,0:T(8,128)(2,1)}, u32[]{:S(2)}, u32[]{:S(2)}) %collective-permute-start.10) | collective-permute-done | bytes 786464 | tf_op jit(solution)/shard_map/ppermute | solution.py:54
  164.2 3.3 %collective-permute-done.11 = bf16[1024,384]{1,0:T(8,128)(2,1)} collective-permute-done((bf16[1024,384]{1,0:T(8,128)(2,1)}, bf16[1024,384]{1,0:T(8,128)(2,1)}, u32[]{:S(2)}, u32[]{:S(2)}) %collective-permute-start.11) | collective-permute-done | bytes 786464 | tf_op jit(solution)/shard_map/ppermute | solution.py:54
  167.5 2.1 add_add_fusion
  171.8 5.6 %collective-permute-start.15 = (bf16[1024,384]{1,0:T(8,128)(2,1)}, bf16[1024,384]{1,0:T(8,128)(2,1)}, u32[]{:S(2)}, u32[]{:S(2)}) collective-permute-start(bf16[1024,384]{1,0:T(8,128)(2,1)} %convolution_convert_fusion.1), channel_id=1, source_target_pairs={{0,448},{32,480},{64,0},{96,32},{128,64},{160,96},{192,128},{224,1... | collective-permute-start | bytes 2359304 | tf_op jit(solution)/shard_map/ppermute | solution.py:54
  182.1 8.4 %all-to-all-start.5 = ((bf16[32,32,384]{2,1,0:T(8,128)(2,1)}), bf16[32,32,384]{2,1,0:T(8,128)(2,1)S(1)}, u32[]{:S(2)}, u32[]{:S(2)}) async-start(bf16[32,32,384]{2,1,0:T(8,128)(2,1)} %bitcast.39), calls=%async_computation.5 | async-start | bytes 1572864 | tf_op jit(solution)/shard_map/all_to_all | solution.py:66
  190.6 2.5 collective-permute-done.15
  194.7 4.3 %collective-permute-start.16 = (bf16[1024,384]{1,0:T(8,128)(2,1)S(1)}, bf16[1024,384]{1,0:T(8,128)(2,1)S(1)}, u32[]{:S(2)}, u32[]{:S(2)}) collective-permute-start(bf16[1024,384]{1,0:T(8,128)(2,1)S(1)} %add_convert_fusion.1), channel_id=1, source_target_pairs={{0,448},{32,480},{64,0},{96,32},{128,64},{160,96},{192,128},{224,1... | collective-permute-start | bytes 2359304 | tf_op jit(solution)/shard_map/ppermute | solution.py:54
  203.5 11.3 %collective-permute-done.16 = bf16[1024,384]{1,0:T(8,128)(2,1)S(1)} collective-permute-done((bf16[1024,384]{1,0:T(8,128)(2,1)S(1)}, bf16[1024,384]{1,0:T(8,128)(2,1)S(1)}, u32[]{:S(2)}, u32[]{:S(2)}) %collective-permute-start.16) | collective-permute-done | bytes 786464 | tf_op jit(solution)/shard_map/ppermute | solution.py:54
  215.0 5.3 %collective-permute-start.19 = (bf16[512,384]{1,0:T(8,128)(2,1)S(1)}, bf16[512,384]{1,0:T(8,128)(2,1)S(1)}, u32[]{:S(2)}, u32[]{:S(2)}) collective-permute-start(bf16[512,384]{1,0:T(8,128)(2,1)S(1)} %get-tuple-element.30), channel_id=1, source_target_pairs={{0,448},{32,480},{64,0},{96,32},{128,64},{160,96},{192,128},{224,1... | collective-permute-start | bytes 1179656 | tf_op jit(solution)/shard_map/ppermute | solution.py:54
  224.5 5.1 %collective-permute-start.17 = (bf16[512,384]{1,0:T(8,128)(2,1)S(1)}, bf16[512,384]{1,0:T(8,128)(2,1)S(1)}, u32[]{:S(2)}, u32[]{:S(2)}) collective-permute-start(bf16[512,384]{1,0:T(8,128)(2,1)S(1)} %get-tuple-element.29), channel_id=1, source_target_pairs={{0,448},{32,480},{64,0},{96,32},{128,64},{160,96},{192,128},{224,1... | collective-permute-start | bytes 1179656 | tf_op jit(solution)/shard_map/ppermute | solution.py:54
  229.7 2.1 collective-permute-start.14
  231.8 3.1 %collective-permute-done.18 = bf16[512,384]{1,0:T(8,128)(2,1)S(1)} collective-permute-done((bf16[512,384]{1,0:T(8,128)(2,1)S(1)}, bf16[512,384]{1,0:T(8,128)(2,1)S(1)}, u32[]{:S(2)}, u32[]{:S(2)}) %collective-permute-start.18) | collective-permute-done | bytes 393248 | tf_op jit(solution)/shard_map/ppermute | solution.py:54
  235.0 3.3 %collective-permute-start.20 = (bf16[512,384]{1,0:T(8,128)(2,1)S(1)}, bf16[512,384]{1,0:T(8,128)(2,1)S(1)}, u32[]{:S(2)}, u32[]{:S(2)}) collective-permute-start(bf16[512,384]{1,0:T(8,128)(2,1)S(1)} %fusion.20), channel_id=1, source_target_pairs={{0,32},{32,0},{64,96},{96,64},{128,160},{160,128},{192,224},{224,1... | collective-permute-start | bytes 1179656 | tf_op jit(solution)/shard_map/ppermute | solution.py:58
  238.3 3.7 %collective-permute-done.14 = bf16[512,384]{1,0:T(8,128)(2,1)S(1)} collective-permute-done((bf16[512,384]{1,0:T(8,128)(2,1)S(1)}, bf16[512,384]{1,0:T(8,128)(2,1)S(1)}, u32[]{:S(2)}, u32[]{:S(2)}) %collective-permute-start.14) | collective-permute-done | bytes 393248 | tf_op jit(solution)/shard_map/ppermute | solution.py:54
  242.0 4.2 %collective-permute-done.20 = bf16[512,384]{1,0:T(8,128)(2,1)S(1)} collective-permute-done((bf16[512,384]{1,0:T(8,128)(2,1)S(1)}, bf16[512,384]{1,0:T(8,128)(2,1)S(1)}, u32[]{:S(2)}, u32[]{:S(2)}) %collective-permute-start.20) | collective-permute-done | bytes 393248 | tf_op jit(solution)/shard_map/ppermute | solution.py:58
  247.1 8.5 %all-to-all-start.4 = ((bf16[32,16,384]{2,1,0:T(8,128)(2,1)}), bf16[32,16,384]{2,1,0:T(8,128)(2,1)S(1)}, u32[]{:S(2)}, u32[]{:S(2)}) async-start(bf16[32,16,384]{2,1,0:T(8,128)(2,1)} %bitcast.34), calls=%async_computation.4 | async-start | bytes 786432 | tf_op jit(solution)/shard_map/all_to_all | solution.py:66
  256.3 5.8 %collective-permute-start.21 = (f32[128,384]{1,0:T(8,128)S(1)}, f32[128,384]{1,0:T(8,128)S(1)}, u32[]{:S(2)}, u32[]{:S(2)}) collective-permute-start(f32[128,384]{1,0:T(8,128)S(1)} %fusion.9), channel_id=1, source_target_pairs={{0,256},{32,288},{64,320},{96,352},{128,384},{160,416},{192,448},{... | collective-permute-start | bytes 589832 | tf_op jit(solution)/shard_map/ppermute | solution.py:54
  262.3 7.8 %all-to-all-done.4 = bf16[32,16,384]{2,1,0:T(8,128)(2,1)S(1)} async-done(((bf16[32,16,384]{2,1,0:T(8,128)(2,1)}), bf16[32,16,384]{2,1,0:T(8,128)(2,1)S(1)}, u32[]{:S(2)}, u32[]{:S(2)}) %all-to-all-start.4) | async-done | bytes 393248 | tf_op jit(solution)/shard_map/all_to_all | solution.py:66
  272.5 16.8 %all_to_all.35 = f32[16,8,384]{2,1,0:T(8,128)S(1)} all-to-all(f32[16,8,384]{2,1,0:T(8,128)S(1)} %fusion.8), channel_id=1, replica_groups=mesh['attn'=16,'exp'=32] {'attn'}, dimensions={0} | all-to-all | bytes 393216 | tf_op jit(solution)/shard_map/all_to_all | solution.py:215
  (146 shorter events, 54.8 us)
Async XLA Ops:
  0.0 32.4 %collective-permute-start = (bf16[128,2880]{0,1:T(8,128)(2,1)}, bf16[128,2880]{0,1:T(8,128)(2,1)S(1)}, u32[]{:S(2)}, u32[]{:S(2)}) collective-permute-start(bf16[128,2880]{0,1:T(8,128)(2,1)} %param.17), channel_id=1, source_target_pairs={{0,32},{32,0},{64,96},{96,64},{128,160},{160,128},{192,224},{224,1... | collective-permute-start | bytes 2211848 | tf_op jit(solution)/shard_map/ppermute | solution.py:58
  5.3 2.6 copy-start.16
  7.4 1.3 copy-start.20
  9.1 2.0 copy-start.15
  9.2 13.2 %copy-start.17 = (f32[2880]{0:T(1024)S(1)}, f32[2880]{0:T(1024)}, u32[]{:S(2)}) copy-start(f32[2880]{0:T(1024)} %param.18) | copy-start | bytes 34564
  9.2 13.3 %copy-start.1 = (bf16[1,180,2880]{2,1,0:T(8,128)(2,1)S(1)}, bf16[1,180,2880]{2,1,0:T(8,128)(2,1)}, u32[]{:S(2)}) copy-start(bf16[1,180,2880]{2,1,0:T(8,128)(2,1)} %param.23) | copy-start | bytes 3110404
  11.0 13.0 %copy-start.18 = (s32[128,4]{0,1:T(4,128)S(1)}, s32[128,4]{0,1:T(4,128)}, u32[]{:S(2)}) copy-start(s32[128,4]{0,1:T(4,128)} %param.19) | copy-start | bytes 6148
  12.0 18.9 %all-to-all-start = ((bf16[8,8,640]{2,1,0:T(8,128)(2,1)}), bf16[8,8,640]{2,1,0:T(8,128)(2,1)S(1)}, u32[]{:S(2)}, u32[]{:S(2)}) async-start(bf16[8,8,640]{2,1,0:T(8,128)(2,1)} %copy.108), calls=%async_computation | async-start | bytes 163840 | tf_op jit(solution)/shard_map/all_to_all | solution.py:62
  34.2 16.6 %all-to-all-start.1 = ((bf16[8,64,384]{2,1,0:T(8,128)(2,1)}), bf16[8,64,384]{2,1,0:T(8,128)(2,1)S(1)}, u32[]{:S(2)}, u32[]{:S(2)}) async-start(bf16[8,64,384]{2,1,0:T(8,128)(2,1)} %pad_bitcast_fusion.1), calls=%async_computation.1 | async-start | bytes 786432 | tf_op jit(solution)/shard_map/all_to_all | solution.py:62
  38.8 19.0 %copy-start.2 = (bf16[1,2880,180]{1,2,0:T(8,128)(2,1)S(1)}, bf16[1,2880,180]{1,2,0:T(8,128)(2,1)}, u32[]{:S(2)}) copy-start(bf16[1,2880,180]{1,2,0:T(8,128)(2,1)} %param.21) | copy-start | bytes 3110404
  51.7 9.1 %collective-permute-start.1 = (bf16[64,384]{1,0:T(8,128)(2,1)S(1)}, bf16[64,384]{1,0:T(8,128)(2,1)S(1)}, u32[]{:S(2)}, u32[]{:S(2)}) collective-permute-start(bf16[64,384]{1,0:T(8,128)(2,1)S(1)} %select_convert_fusion), channel_id=1, source_target_pairs={{0,32},{32,0},{64,96},{96,64},{128,160},{160,128},{192,224},{224,1... | collective-permute-start | bytes 147464 | tf_op jit(solution)/shard_map/ppermute | solution.py:58
  60.9 1.0 copy-start.11
  62.0 24.1 %all-to-all-start.2 = ((bf16[32,16,384]{2,1,0:T(8,128)(2,1)}), bf16[32,16,384]{2,1,0:T(8,128)(2,1)S(1)}, u32[]{:S(2)}, u32[]{:S(2)}) async-start(bf16[32,16,384]{2,1,0:T(8,128)(2,1)} %bitcast.16), calls=%async_computation.2 | async-start | bytes 786432 | tf_op jit(solution)/shard_map/all_to_all | solution.py:66
  70.7 3.3 %copy-start.12 = (bf16[8,2,8,384]{3,2,1,0:T(8,128)(2,1)S(1)}, bf16[8,2,8,384]{3,2,1,0:T(8,128)(2,1)}, u32[]{:S(2)}) copy-start(bf16[8,2,8,384]{3,2,1,0:T(8,128)(2,1)} %copy-done.11) | copy-start | bytes 294916
  70.7 5.8 %copy-start.13 = (pred[32,16,128]{2,1,0:T(8,128)(4,1)S(1)}, pred[32,16,128]{2,1,0:T(8,128)(4,1)}, u32[]{:S(2)}) copy-start(pred[32,16,128]{2,1,0:T(8,128)(4,1)} %get-tuple-element.39) | copy-start | bytes 196612
  74.0 10.7 %collective-permute-start.2 = (bf16[128,384]{1,0:T(8,128)(2,1)S(1)}, bf16[128,384]{1,0:T(8,128)(2,1)S(1)}, u32[]{:S(2)}, u32[]{:S(2)}) collective-permute-start(bf16[128,384]{1,0:T(8,128)(2,1)S(1)} %bitcast.181), channel_id=1, source_target_pairs={{0,256},{32,288},{64,320},{96,352},{128,384},{160,416},{192,448},{... | collective-permute-start | bytes 294920 | tf_op jit(solution)/shard_map/ppermute | solution.py:54
  86.0 13.9 %collective-permute-start.3 = (bf16[512,384]{1,0:T(8,128)(2,1)S(1)}, bf16[512,384]{1,0:T(8,128)(2,1)}, u32[]{:S(2)}, u32[]{:S(2)}) collective-permute-start(bf16[512,384]{1,0:T(8,128)(2,1)S(1)} %bitcast.170), channel_id=1, source_target_pairs={{0,32},{32,0},{64,96},{96,64},{128,160},{160,128},{192,224},{224,1... | collective-permute-start | bytes 1179656 | tf_op jit(solution)/shard_map/ppermute | solution.py:58
  89.3 17.7 %collective-permute-start.4 = (bf16[512,384]{1,0:T(8,128)(2,1)S(1)}, bf16[512,384]{1,0:T(8,128)(2,1)S(1)}, u32[]{:S(2)}, u32[]{:S(2)}) collective-permute-start(bf16[512,384]{1,0:T(8,128)(2,1)S(1)} %bitcast.171), channel_id=1, source_target_pairs={{0,64},{32,96},{64,128},{96,160},{128,192},{160,224},{192,256},{22... | collective-permute-start | bytes 1179656 | tf_op jit(solution)/shard_map/ppermute | solution.py:54
  93.7 14.1 %collective-permute-start.6 = (bf16[512,384]{1,0:T(8,128)(2,1)S(1)}, bf16[512,384]{1,0:T(8,128)(2,1)S(1)}, u32[]{:S(2)}, u32[]{:S(2)}) collective-permute-start(bf16[512,384]{1,0:T(8,128)(2,1)S(1)} %bitcast.172), channel_id=1, source_target_pairs={{0,448},{32,480},{64,0},{96,32},{128,64},{160,96},{192,128},{224,1... | collective-permute-start | bytes 1179656 | tf_op jit(solution)/shard_map/ppermute | solution.py:54
  99.9 20.4 %collective-permute-start.5 = (bf16[512,384]{1,0:T(8,128)(2,1)}, bf16[512,384]{1,0:T(8,128)(2,1)S(1)}, u32[]{:S(2)}, u32[]{:S(2)}) collective-permute-start(bf16[512,384]{1,0:T(8,128)(2,1)} %collective-permute-done.3), channel_id=1, source_target_pairs={{0,64},{32,96},{64,128},{96,160},{128,192},{160,224},{192,256},{22... | collective-permute-start | bytes 1179656 | tf_op jit(solution)/shard_map/ppermute | solution.py:54
  102.4 11.7 %collective-permute-start.7 = (bf16[512,384]{1,0:T(8,128)(2,1)}, bf16[512,384]{1,0:T(8,128)(2,1)S(1)}, u32[]{:S(2)}, u32[]{:S(2)}) collective-permute-start(bf16[512,384]{1,0:T(8,128)(2,1)} %collective-permute-done.3), channel_id=1, source_target_pairs={{0,448},{32,480},{64,0},{96,32},{128,64},{160,96},{192,128},{224,1... | collective-permute-start | bytes 1179656 | tf_op jit(solution)/shard_map/ppermute | solution.py:54
  114.9 30.1 %collective-permute-start.9 = (bf16[1024,384]{1,0:T(8,128)(2,1)}, bf16[1024,384]{1,0:T(8,128)(2,1)}, u32[]{:S(2)}, u32[]{:S(2)}) collective-permute-start(bf16[1024,384]{1,0:T(8,128)(2,1)} %constant_dynamic-update-slice_fusion.2), channel_id=1, source_target_pairs={{0,448},{32,480},{64,0},{96,32},{128,64},{160,96},{192,128},{224,1... | collective-permute-start | bytes 2359304 | tf_op jit(solution)/shard_map/ppermute | solution.py:54
  121.2 19.9 %collective-permute-start.8 = (bf16[1024,384]{1,0:T(8,128)(2,1)}, bf16[1024,384]{1,0:T(8,128)(2,1)}, u32[]{:S(2)}, u32[]{:S(2)}) collective-permute-start(bf16[1024,384]{1,0:T(8,128)(2,1)} %constant_dynamic-update-slice_fusion), channel_id=1, source_target_pairs={{0,64},{32,96},{64,128},{96,160},{128,192},{160,224},{192,256},{22... | collective-permute-start | bytes 2359304 | tf_op jit(solution)/shard_map/ppermute | solution.py:54
  126.4 30.6 %all-to-all-start.3 = ((bf16[32,32,384]{2,1,0:T(8,128)(2,1)}), bf16[32,32,384]{2,1,0:T(8,128)(2,1)S(1)}, u32[]{:S(2)}, u32[]{:S(2)}) async-start(bf16[32,32,384]{2,1,0:T(8,128)(2,1)} %bitcast.168), calls=%async_computation.3 | async-start | bytes 1572864 | tf_op jit(solution)/shard_map/all_to_all | solution.py:66
  141.0 21.2 %collective-permute-start.10 = (bf16[1024,384]{1,0:T(8,128)(2,1)}, bf16[1024,384]{1,0:T(8,128)(2,1)}, u32[]{:S(2)}, u32[]{:S(2)}) collective-permute-start(bf16[1024,384]{1,0:T(8,128)(2,1)} %collective-permute-done.8), channel_id=1, source_target_pairs={{0,64},{32,96},{64,128},{96,160},{128,192},{160,224},{192,256},{22... | collective-permute-start | bytes 2359304 | tf_op jit(solution)/shard_map/ppermute | solution.py:54
  144.9 7.3 %copy-start = (f32[1024,512]{1,0:T(8,128)S(1)}, f32[1024,512]{1,0:T(8,128)}, u32[]{:S(2)}) copy-start(f32[1024,512]{1,0:T(8,128)} %convolution_add_fusion.1) | copy-start | bytes 6291460
  147.0 20.5 %collective-permute-start.11 = (bf16[1024,384]{1,0:T(8,128)(2,1)}, bf16[1024,384]{1,0:T(8,128)(2,1)}, u32[]{:S(2)}, u32[]{:S(2)}) collective-permute-start(bf16[1024,384]{1,0:T(8,128)(2,1)} %collective-permute-done.9), channel_id=1, source_target_pairs={{0,448},{32,480},{64,0},{96,32},{128,64},{160,96},{192,128},{224,1... | collective-permute-start | bytes 2359304 | tf_op jit(solution)/shard_map/ppermute | solution.py:54
  169.9 7.5 %copy-start.8 = (bf16[1,256,384]{2,0,1:T(2,128)(2,1)S(1)}, bf16[1,256,384]{2,0,1:T(2,128)(2,1)}, u32[]{:S(2)}) copy-start(bf16[1,256,384]{2,0,1:T(2,128)(2,1)} %get-tuple-element.22) | copy-start | bytes 589828
  170.3 10.3 %copy-start.7 = (bf16[1,256,384]{2,0,1:T(2,128)(2,1)S(1)}, bf16[1,256,384]{2,0,1:T(2,128)(2,1)}, u32[]{:S(2)}) copy-start(bf16[1,256,384]{2,0,1:T(2,128)(2,1)} %get-tuple-element.18) | copy-start | bytes 589828
  171.8 21.2 %collective-permute-start.15 = (bf16[1024,384]{1,0:T(8,128)(2,1)}, bf16[1024,384]{1,0:T(8,128)(2,1)}, u32[]{:S(2)}, u32[]{:S(2)}) collective-permute-start(bf16[1024,384]{1,0:T(8,128)(2,1)} %convolution_convert_fusion.1), channel_id=1, source_target_pairs={{0,448},{32,480},{64,0},{96,32},{128,64},{160,96},{192,128},{224,1... | collective-permute-start | bytes 2359304 | tf_op jit(solution)/shard_map/ppermute | solution.py:54
  178.8 20.7 %collective-permute-start.12 = (bf16[1024,384]{1,0:T(8,128)(2,1)}, bf16[1024,384]{1,0:T(8,128)(2,1)}, u32[]{:S(2)}, u32[]{:S(2)}) collective-permute-start(bf16[1024,384]{1,0:T(8,128)(2,1)} %convolution_convert_fusion.2), channel_id=1, source_target_pairs={{0,64},{32,96},{64,128},{96,160},{128,192},{160,224},{192,256},{22... | collective-permute-start | bytes 2359304 | tf_op jit(solution)/shard_map/ppermute | solution.py:54
  180.7 12.4 %copy-start.6 = (bf16[1,256,384]{2,0,1:T(2,128)(2,1)S(1)}, bf16[1,256,384]{2,0,1:T(2,128)(2,1)}, u32[]{:S(2)}) copy-start(bf16[1,256,384]{2,0,1:T(2,128)(2,1)} %get-tuple-element.20) | copy-start | bytes 589828
  182.1 16.9 %copy-start.5 = (bf16[1,256,384]{2,0,1:T(2,128)(2,1)S(1)}, bf16[1,256,384]{2,0,1:T(2,128)(2,1)}, u32[]{:S(2)}) copy-start(bf16[1,256,384]{2,0,1:T(2,128)(2,1)} %get-tuple-element.21) | copy-start | bytes 589828
  182.1 65.0 %all-to-all-start.5 = ((bf16[32,32,384]{2,1,0:T(8,128)(2,1)}), bf16[32,32,384]{2,1,0:T(8,128)(2,1)S(1)}, u32[]{:S(2)}, u32[]{:S(2)}) async-start(bf16[32,32,384]{2,1,0:T(8,128)(2,1)} %bitcast.39), calls=%async_computation.5 | async-start | bytes 1572864 | tf_op jit(solution)/shard_map/all_to_all | solution.py:66
  193.1 6.4 %copy-start.4 = (bf16[1,256,384]{2,0,1:T(2,128)(2,1)S(1)}, bf16[1,256,384]{2,0,1:T(2,128)(2,1)}, u32[]{:S(2)}) copy-start(bf16[1,256,384]{2,0,1:T(2,128)(2,1)} %get-tuple-element.17) | copy-start | bytes 589828
  194.7 20.0 %collective-permute-start.16 = (bf16[1024,384]{1,0:T(8,128)(2,1)S(1)}, bf16[1024,384]{1,0:T(8,128)(2,1)S(1)}, u32[]{:S(2)}, u32[]{:S(2)}) collective-permute-start(bf16[1024,384]{1,0:T(8,128)(2,1)S(1)} %add_convert_fusion.1), channel_id=1, source_target_pairs={{0,448},{32,480},{64,0},{96,32},{128,64},{160,96},{192,128},{224,1... | collective-permute-start | bytes 2359304 | tf_op jit(solution)/shard_map/ppermute | solution.py:54
  199.1 4.0 %copy-start.3 = (bf16[1,256,384]{2,0,1:T(2,128)(2,1)S(1)}, bf16[1,256,384]{2,0,1:T(2,128)(2,1)}, u32[]{:S(2)}) copy-start(bf16[1,256,384]{2,0,1:T(2,128)(2,1)} %get-tuple-element.23) | copy-start | bytes 589828
  201.1 20.8 %collective-permute-start.13 = (bf16[1024,384]{1,0:T(8,128)(2,1)S(1)}, bf16[1024,384]{1,0:T(8,128)(2,1)S(1)}, u32[]{:S(2)}, u32[]{:S(2)}) collective-permute-start(bf16[1024,384]{1,0:T(8,128)(2,1)S(1)} %add_convert_fusion.3), channel_id=1, source_target_pairs={{0,64},{32,96},{64,128},{96,160},{128,192},{160,224},{192,256},{22... | collective-permute-start | bytes 2359304 | tf_op jit(solution)/shard_map/ppermute | solution.py:54
  215.0 16.8 %collective-permute-start.19 = (bf16[512,384]{1,0:T(8,128)(2,1)S(1)}, bf16[512,384]{1,0:T(8,128)(2,1)S(1)}, u32[]{:S(2)}, u32[]{:S(2)}) collective-permute-start(bf16[512,384]{1,0:T(8,128)(2,1)S(1)} %get-tuple-element.30), channel_id=1, source_target_pairs={{0,448},{32,480},{64,0},{96,32},{128,64},{160,96},{192,128},{224,1... | collective-permute-start | bytes 1179656 | tf_op jit(solution)/shard_map/ppermute | solution.py:54
  222.2 12.7 %collective-permute-start.18 = (bf16[512,384]{1,0:T(8,128)(2,1)S(1)}, bf16[512,384]{1,0:T(8,128)(2,1)S(1)}, u32[]{:S(2)}, u32[]{:S(2)}) collective-permute-start(bf16[512,384]{1,0:T(8,128)(2,1)S(1)} %get-tuple-element.28), channel_id=1, source_target_pairs={{0,64},{32,96},{64,128},{96,160},{128,192},{160,224},{192,256},{22... | collective-permute-start | bytes 1179656 | tf_op jit(solution)/shard_map/ppermute | solution.py:54
  224.5 13.8 %collective-permute-start.17 = (bf16[512,384]{1,0:T(8,128)(2,1)S(1)}, bf16[512,384]{1,0:T(8,128)(2,1)S(1)}, u32[]{:S(2)}, u32[]{:S(2)}) collective-permute-start(bf16[512,384]{1,0:T(8,128)(2,1)S(1)} %get-tuple-element.29), channel_id=1, source_target_pairs={{0,448},{32,480},{64,0},{96,32},{128,64},{160,96},{192,128},{224,1... | collective-permute-start | bytes 1179656 | tf_op jit(solution)/shard_map/ppermute | solution.py:54
  229.7 25.9 %copy-start.19 = (f32[128,4]{0,1:T(4,128)S(1)}, f32[128,4]{0,1:T(4,128)}, u32[]{:S(2)}) copy-start(f32[128,4]{0,1:T(4,128)} %param.20) | copy-start | bytes 6148
  229.7 25.9 %copy-start.14 = (pred[32,16,128]{2,1,0:T(8,128)(4,1)S(1)}, pred[32,16,128]{2,1,0:T(8,128)(4,1)}, u32[]{:S(2)}) copy-start(pred[32,16,128]{2,1,0:T(8,128)(4,1)} %get-tuple-element.39) | copy-start | bytes 196612
  229.7 12.3 %collective-permute-start.14 = (bf16[512,384]{1,0:T(8,128)(2,1)S(1)}, bf16[512,384]{1,0:T(8,128)(2,1)S(1)}, u32[]{:S(2)}, u32[]{:S(2)}) collective-permute-start(bf16[512,384]{1,0:T(8,128)(2,1)S(1)} %get-tuple-element.27), channel_id=1, source_target_pairs={{0,64},{32,96},{64,128},{96,160},{128,192},{160,224},{192,256},{22... | collective-permute-start | bytes 1179656 | tf_op jit(solution)/shard_map/ppermute | solution.py:54
  235.0 11.2 %collective-permute-start.20 = (bf16[512,384]{1,0:T(8,128)(2,1)S(1)}, bf16[512,384]{1,0:T(8,128)(2,1)S(1)}, u32[]{:S(2)}, u32[]{:S(2)}) collective-permute-start(bf16[512,384]{1,0:T(8,128)(2,1)S(1)} %fusion.20), channel_id=1, source_target_pairs={{0,32},{32,0},{64,96},{96,64},{128,160},{160,128},{192,224},{224,1... | collective-permute-start | bytes 1179656 | tf_op jit(solution)/shard_map/ppermute | solution.py:58
  247.1 15.2 %copy-start.10 = (f32[8,8,384]{2,1,0:T(8,128)S(1)}, f32[8,8,384]{2,1,0:T(8,128)}, u32[]{:S(2)}) copy-start(f32[8,8,384]{2,1,0:T(8,128)} %get-tuple-element.32) | copy-start | bytes 294916
  247.1 23.0 %all-to-all-start.4 = ((bf16[32,16,384]{2,1,0:T(8,128)(2,1)}), bf16[32,16,384]{2,1,0:T(8,128)(2,1)S(1)}, u32[]{:S(2)}, u32[]{:S(2)}) async-start(bf16[32,16,384]{2,1,0:T(8,128)(2,1)} %bitcast.34), calls=%async_computation.4 | async-start | bytes 786432 | tf_op jit(solution)/shard_map/all_to_all | solution.py:66
  256.3 15.9 %collective-permute-start.21 = (f32[128,384]{1,0:T(8,128)S(1)}, f32[128,384]{1,0:T(8,128)S(1)}, u32[]{:S(2)}, u32[]{:S(2)}) collective-permute-start(f32[128,384]{1,0:T(8,128)S(1)} %fusion.9), channel_id=1, source_target_pairs={{0,256},{32,288},{64,320},{96,352},{128,384},{160,416},{192,448},{... | collective-permute-start | bytes 589832 | tf_op jit(solution)/shard_map/ppermute | solution.py:54
  (1 other events, 1.0 us)

commit v5 on v4

--- a/solution.py
+++ b/solution.py
@@ -1,6 +1,8 @@
 import jax
 import jax.numpy as jnp
 from jax import lax
+from jax.experimental import pallas as pl
+from jax.experimental.pallas import tpu as pltpu
 from jax.sharding import PartitionSpec as P
 
 HEAD_SIZE = 64
@@ -16,7 +18,9 @@
 BLOCK = D // BLOCKS
 LANES = 384
 FF_LANES = 256
-FAR = BLOCKS // 2
+Z_SLOTS = 24
+Y_SLOTS = CAP - Z_SLOTS
+ROW_TILE = 256
 F32 = jnp.float32
 BF16 = jnp.bfloat16
 
@@ -47,11 +51,59 @@
     return combined.reshape(count_of_rows, QUERY_HEADS * HEAD_SIZE).astype(jnp.bfloat16)
 
 
-def shift_over_z(array, step):
-    pairs = [
-        (z * HALVES + half, (z + step) % BLOCKS * HALVES + half) for z in range(BLOCKS) for half in range(HALVES)
-    ]
-    return lax.ppermute(array, "attn", pairs)
+def activated(both):
+    both = both * lax.rsqrt(both[:, FF_LOCAL : FF_LOCAL + 1] * (1.0 / D) + 1e-05)
+    gate = both[:, :FF_LANES]
+    up = both[:, FF_LANES:]
+    return (gate * jax.nn.sigmoid(1.702 * gate) * (up + 1.0)).astype(BF16)
+
+
+def blocks_kernel(x_ref, w_in_ref, w_out_ref, y_ref):
+    both = jnp.dot(x_ref[0], w_in_ref[0], preferred_element_type=F32)
+    for block in range(1, BLOCKS):
+        both = both + jnp.dot(x_ref[block], w_in_ref[block], preferred_element_type=F32)
+    hidden = activated(both)
+    for block in range(BLOCKS):
+        y_ref[block] = jnp.dot(hidden, w_out_ref[block], preferred_element_type=F32).astype(BF16)
+
+
+def rows_kernel(x_ref, w_in_ref, w_out_ref, y_ref):
+    both = jnp.dot(x_ref[:, :LANES], w_in_ref[0], preferred_element_type=F32)
+    for block in range(1, BLOCKS):
+        x = x_ref[:, block * LANES : (block + 1) * LANES]
+        both = both + jnp.dot(x, w_in_ref[block], preferred_element_type=F32)
+    hidden = activated(both)
+    for block in range(BLOCKS):
+        y = jnp.dot(hidden, w_out_ref[block], preferred_element_type=F32).astype(BF16)
+        y_ref[:, block * LANES : (block + 1) * LANES] = y
+
+
+def run_experts(kernel, x, w_in, w_out, rows, block_shape, index_map):
+    return pl.pallas_call(
+        kernel,
+        grid=(rows // ROW_TILE,),
+        in_specs=[
+            pl.BlockSpec(block_shape, index_map),
+            pl.BlockSpec(w_in.shape, lambda i: (0, 0, 0)),
+            pl.BlockSpec(w_out.shape, lambda i: (0, 0, 0)),
+        ],
+        out_specs=pl.BlockSpec(block_shape, index_map),
+        out_shape=jax.ShapeDtypeStruct(x.shape, BF16),
+        compiler_params=pltpu.CompilerParams(vmem_limit_bytes=60 * 2**20),
+        cost_estimate=pl.CostEstimate(
+            flops=2 * rows * D * 3 * FF_LOCAL,
+            bytes_accessed=4 * rows * D + 5 * 2**20,
+            transcendentals=rows * FF_LOCAL,
+        ),
+    )(x, w_in, w_out)
+
+
+def experts_on_blocks(x, w_in, w_out):
+    return run_experts(blocks_kernel, x, w_in, w_out, x.shape[1], (BLOCKS, ROW_TILE, LANES), lambda i: (0, i, 0))
+
+
+def experts_on_rows(x, w_in, w_out):
+    return run_experts(rows_kernel, x, w_in, w_out, x.shape[0], (ROW_TILE, BLOCKS * LANES), lambda i: (i, 0))
 
 
 def swap_halves(array):
@@ -88,8 +140,6 @@
     own_rows = residual.shape[0]
     column_rows = expert_ids.shape[0]
     half_rows = column_rows // HALVES
-    half_cap = CAP // HALVES
-    half_slots = N_EXP * half_cap
     attn_index = lax.axis_index("attn")
     z_index = lax.shift_right_logical(attn_index, 1)
     half = lax.bitwise_and(attn_index, 1)
@@ -129,19 +179,19 @@
     slot = jnp.dot(named.astype(BF16), earlier, preferred_element_type=F32).astype(jnp.int32)
     slot = jnp.where(named, slot, -1)
 
-    def taken_of(own_half):
-        base = half_cap * (half if own_half else 1 - half)
-        return slot[:, None, :] == base + jnp.arange(half_cap, dtype=jnp.int32)[None, :, None]
-
-    taken_own, taken_other = taken_of(True), taken_of(False)
-    taken_both = jnp.concatenate([taken_own, taken_other], axis=1)
+    def taken_of(first, count):
+        return slot[:, None, :] == first + jnp.arange(count, dtype=jnp.int32)[None, :, None]
+
+    taken_z, taken_y = taken_of(0, Z_SLOTS), taken_of(Z_SLOTS, Y_SLOTS)
 
     def picked(taken, rows):
         select = taken.astype(BF16).reshape(-1, column_rows)
-        return jnp.dot(select, rows, preferred_element_type=F32).astype(BF16).reshape(N_EXP, -1, LANES)
+        rows = jnp.dot(select, rows, preferred_element_type=F32).astype(BF16)
+        return rows.reshape(N_EXP, -1, rows.shape[1])
 
     def mixed_of(taken, partial_value):
-        returned = over_experts(partial_value).reshape(-1, LANES)
+        returned = over_experts(partial_value)
+        returned = returned.reshape(-1, returned.shape[2])
         mix = jnp.where(taken, weight[:, None, :], 0.0).reshape(-1, column_rows)
         mix_high = lax.reduce_precision(mix, 8, 7)
         mix_low = (mix - mix_high).astype(BF16)
@@ -159,55 +209,27 @@
     w_in = jnp.where((in_column == FF_LOCAL) & (in_row >= BLOCK) & (in_row < BLOCK + 2), jnp.ones((), BF16), w_in)
     w_out = jnp.pad(to_blocks(w_down[0]).transpose(1, 0, 2), ((0, 0), (0, FF_LANES - FF_LOCAL), (0, 0)))
 
-    def at_offset(blocks, offset):
-        index = lax.bitwise_and(z_index + offset % BLOCKS, BLOCKS - 1)
-        return lax.dynamic_index_in_dim(blocks, index, 0, keepdims=False)
-
-    def input_term(rows, offset):
-        return jnp.dot(rows, at_offset(w_in, offset), preferred_element_type=F32)
-
-    far_outgoing = picked(taken_both, shift_over_z(scaled, FAR))
-    own = over_experts(picked(taken_own, scaled)).reshape(half_slots, LANES)
-    own, w_in, w_out, far_outgoing = lax.optimization_barrier((own, w_in, w_out, far_outgoing))
-    halves_of_own = [own, swap_halves(own)]
-    up_block = jnp.concatenate([shift_over_z(h, 1) for h in halves_of_own])
-    down_block = jnp.concatenate([shift_over_z(h, -1) for h in halves_of_own])
-    both = input_term(jnp.concatenate(halves_of_own), 0) + input_term(up_block, -1)
-    far_outgoing, both = lax.optimization_barrier((far_outgoing, both))
-    far = over_experts(far_outgoing).reshape(N_EXP, 2, half_cap, LANES)
-    both = both + input_term(down_block, 1)
-    for step in range(2, FAR):
-        up_block, down_block = shift_over_z(up_block, 1), shift_over_z(down_block, -1)
-        if step == FAR - 1:
-            both = lax.optimization_barrier(both)
-        both = both + input_term(up_block, -step)
-        both = both + input_term(down_block, step)
-    both = both + input_term(far.transpose(1, 0, 2, 3).reshape(N_EXP * CAP, LANES), FAR)
-    factor = lax.rsqrt(both[:, FF_LOCAL : FF_LOCAL + 1] * (1.0 / D) + 1e-05)
-    gate = both[:, :FF_LANES] * factor
-    up = both[:, FF_LANES:] * factor
-    expert_hidden = (gate * jax.nn.sigmoid(1.702 * gate) * (up + 1.0)).astype(BF16)
-
-    def output_block(offset):
-        return jnp.dot(expert_hidden, at_offset(w_out, offset), preferred_element_type=F32)
-
-    up_sum = shift_over_z(output_block(FAR - 1).astype(BF16), 1)
-    down_sum = shift_over_z(output_block(1 - FAR).astype(BF16), -1)
-    far_value = output_block(FAR).astype(BF16).reshape(2, N_EXP, half_cap, LANES).transpose(1, 0, 2, 3)
-    far_mixed = shift_over_z(mixed_of(taken_both, far_value.reshape(N_EXP, CAP, LANES)), FAR)
-    for offset in range(FAR - 2, 0, -1):
-        up_sum = (output_block(offset) + up_sum.astype(F32)).astype(BF16)
-        down_sum = (output_block(-offset) + down_sum.astype(F32)).astype(BF16)
-        if offset > 1:
-            up_sum, down_sum = shift_over_z(up_sum, 1), shift_over_z(down_sum, -1)
-    own_block = output_block(0)
-    sums = []
-    for rows in (slice(0, half_slots), slice(half_slots, None)):
-        arrived = shift_over_z(up_sum[rows], 1).astype(F32) + shift_over_z(down_sum[rows], -1).astype(F32)
-        sums.append(own_block[rows] + arrived)
-    other_sum = swap_halves(sums[0].astype(BF16))
-    whole_sum = (sums[1] + other_sum.astype(F32)).astype(BF16)
-    mixed = mixed_of(taken_other, whole_sum.reshape(N_EXP, half_cap, LANES)) + far_mixed
+    own = over_experts(picked(taken_z, scaled)).reshape(N_EXP * Z_SLOTS, LANES)
+    whole = lax.all_gather(scaled, "attn", axis=0, axis_index_groups=Z_GROUPS)
+    own, whole = lax.optimization_barrier((own, whole))
+    rows_z = lax.all_gather(own, "attn", axis=0, tiled=True, axis_index_groups=Z_GROUPS)
+    whole = whole.transpose(1, 0, 2).reshape(column_rows, BLOCKS * LANES)
+    rows_y = over_experts(picked(taken_y, whole)).reshape(N_EXP * Y_SLOTS, BLOCKS * LANES)
+    out_y = experts_on_rows(rows_y, w_in, w_out)
+    rows_z, out_y = lax.optimization_barrier((rows_z, out_y))
+    out_z = experts_on_blocks(rows_z.reshape(BLOCKS, N_EXP * Z_SLOTS, LANES), w_in, w_out)
+
+    sum_z = lax.psum_scatter(
+        out_z.reshape(BLOCKS * N_EXP * Z_SLOTS, LANES),
+        "attn",
+        scatter_dimension=0,
+        tiled=True,
+        axis_index_groups=Z_GROUPS,
+    )
+    mixed_y = mixed_of(taken_y, out_y.reshape(N_EXP, Y_SLOTS, BLOCKS * LANES)).astype(BF16)
+    mixed_y = over_z(mixed_y.reshape(column_rows, BLOCKS, LANES).transpose(1, 0, 2))
+    mixed_y = jnp.sum(mixed_y.astype(F32), axis=0)
+    mixed = mixed_of(taken_z, sum_z.reshape(N_EXP, Z_SLOTS, LANES)) + mixed_y
 
     mixed = mixed.reshape(BLOCKS, HALVES, own_rows, LANES)
     halves = jnp.arange(HALVES, dtype=jnp.int32)[None, :, None, None]

time: 294 us -> 305 us (1.037)
  starting transfers between devices: 127 us -> 44.8 us
  blocking collectives: 16.8 us -> 91.8 us
  matrix products: 31.8 us -> 7.28 us
  waiting for transfers between devices: 80.8 us -> 101 us
  Pallas kernels: 0 us -> 15.9 us
  between operations: 0.96 us -> 13.9 us
  other arithmetic: 7.73 us -> 3.04 us
    all_to_all x4, waiting for transfers between devices: 10.5 us -> 80.2 us  [over_experts(): return lax.all_to_all(array, 'exp', 0, 0, tiled=True)]
    ppermute x18 -> x0, starting transfers between devices: 65 us -> none  [shift_over_z(): return lax.ppermute(array, 'attn', pairs)]
    all_to_all x0 -> x2, blocking collectives: none -> 51.1 us  [over_z(): lax.all_to_all(array, 'attn', 0, 0, tiled=True, axis_index_groups=Z_GROUPS)]
    ppermute x18 -> x0, waiting for transfers between devices: 44.5 us -> none  [shift_over_z(): return lax.ppermute(array, 'attn', pairs)]
    all_gather x0 -> x1, blocking collectives: none -> 26.1 us  [local(): whole = lax.all_gather(scaled, 'attn', axis=0, axis_index_groups=Z_GROUPS)]
    dot_general x18 -> x2, matrix products: 26.6 us -> 2.91 us  [picked(): rows = jnp.dot(select, rows, preferred_element_type=F32).astype(BF16)]
    pallas_call x0 -> x2, Pallas kernels: none -> 15.9 us  [run_experts(): pl.pallas_call(kernel, grid=(rows // ROW_TILE,), in_specs=[pl.BlockSpec(b...]
    all_to_all x2 -> x1, starting transfers between devices: 13.8 us -> 3.45 us  [over_z(): lax.all_to_all(array, 'attn', 0, 0, tiled=True, axis_index_groups=Z_GROUPS)]
  transfers between devices with their start and end apart: 28 -> 9, of which waited for: 17 -> 6; matrix products, arithmetic and copies ran while one was open for 19% -> 9% of each run, Pallas kernels for 0% -> 2%
where the time goes in v5:
time: 305 us; the launch traced here: 301 us
  waiting for transfers between devices  101 us (33%)
  blocking collectives  91.8 us (30%)
  starting transfers between devices  44.8 us (15%)
  local copies, waits for them, and re-layouts  23.8 us (8%)
  Pallas kernels  15.9 us (5%)
  between operations  13.9 us (5%)
  matrix products  7.28 us (2%)
    all_to_all x4, waiting for transfers between devices, over_experts(): return lax.all_to_all(array, 'exp', 0, 0, tiled=True)  80.2 us
    all_to_all x2, blocking collectives, over_z(): lax.all_to_all(array, 'attn', 0, 0, tiled=True, axis_index_groups=Z_GROUPS)  51.1 us
    all_to_all x4, starting transfers between devices, over_experts(): return lax.all_to_all(array, 'exp', 0, 0, tiled=True)  33.8 us
    all_gather x1, blocking collectives, local(): whole = lax.all_gather(scaled, 'attn', axis=0, axis_index_groups=Z_GROUPS)  26.1 us
    pallas_call x2, Pallas kernels, run_experts(): pl.pallas_call(kernel, grid=(rows // ROW_TILE,), in_specs=[pl.BlockSpec(b...  15.9 us
    all_to_all x1, blocking collectives, local(): lax.all_to_all(mixed.reshape(N_ATTN, own_rows, LANES), 'attn', 0, 0, tile...  14.6 us
    all_to_all x1, waiting for transfers between devices, over_z(): lax.all_to_all(array, 'attn', 0, 0, tiled=True, axis_index_groups=Z_GROUPS)  12.9 us
    unnamed x26, local copies, waits for them, and re-layouts  8.22 us
  transfers between devices with their start and end apart: 9, of which 6 were waited for; matrix products, arithmetic and copies ran while one was open for 9% of the time, Pallas kernels for 2%

profile of v5, /device:TPU:6, one launch (start us, length us, event | category | flops | bytes accessed | tf_op | source)
XLA Modules:
  0.0 301.1 jit_solution(12442193054384730363)
XLA Ops:
  6.5 3.3 %collective-permute-start = (bf16[128,2880]{0,1:T(8,128)(2,1)}, bf16[128,2880]{0,1:T(8,128)(2,1)S(1)}, u32[]{:S(2)}, u32[]{:S(2)}) collective-permute-start(bf16[128,2880]{0,1:T(8,128)(2,1)} %param.17), channel_id=1, source_target_pairs={{0,32},{32,0},{64,96},{96,64},{128,160},{160,128},{192,224},{224,1... | collective-permute-start | bytes 2211848 | tf_op jit(solution)/shard_map/ppermute | solution.py:110
  9.8 0.9 reshape.257
  10.8 0.9 fusion.60
  11.6 1.1 copy.95
  12.7 2.1 fusion.58
  14.9 0.4 copy.110
  15.3 0.3 copy-done.5
  15.8 1.1 copy.92
  16.8 0.4 copy.108
  17.3 1.4 fusion.62
  19.1 0.4 convolution_convert_fusion.2
  19.7 18.7 %all_to_all.40 = bf16[8,8,640]{2,1,0:T(8,128)(2,1)S(1)} all-to-all(bf16[8,8,640]{2,1,0:T(8,128)(2,1)S(1)} %copy.98), channel_id=1, replica_groups={{0,64,128,192,256,320,384,448},{32,96,160,224,288,352,416,480},{1,65,12..., dimensions={0} | all-to-all | bytes 163840 | tf_op jit(solution)/shard_map/all_to_all | solution.py:114
  38.4 0.4 fusion.49
  38.8 0.4 fusion.5
  39.2 0.5 reshape.259
  39.8 0.8 pad_bitcast_fusion.1
  40.6 3.5 %all-to-all-start.1 = ((bf16[8,64,384]{2,1,0:T(8,128)(2,1)}), bf16[8,64,384]{2,1,0:T(8,128)(2,1)S(1)}, u32[]{:S(2)}, u32[]{:S(2)}) async-start(bf16[8,64,384]{2,1,0:T(8,128)(2,1)} %pad_bitcast_fusion.1), calls=%async_computation.1 | async-start | bytes 786432 | tf_op jit(solution)/shard_map/all_to_all | solution.py:114
  44.3 12.9 %all-to-all-done.1 = bf16[8,64,384]{2,1,0:T(8,128)(2,1)S(1)} async-done(((bf16[8,64,384]{2,1,0:T(8,128)(2,1)}), bf16[8,64,384]{2,1,0:T(8,128)(2,1)S(1)}, u32[]{:S(2)}, u32[]{:S(2)}) %all-to-all-start.1) | async-done | bytes 393248 | tf_op jit(solution)/shard_map/all_to_all | solution.py:114
  57.5 4.0 %collective-permute-start.1 = (bf16[64,384]{1,0:T(8,128)(2,1)S(1)}, bf16[64,384]{1,0:T(8,128)(2,1)S(1)}, u32[]{:S(2)}, u32[]{:S(2)}) collective-permute-start(bf16[64,384]{1,0:T(8,128)(2,1)S(1)} %select_convert_fusion), channel_id=1, source_target_pairs={{0,32},{32,0},{64,96},{96,64},{128,160},{160,128},{192,224},{224,1... | collective-permute-start | bytes 147464 | tf_op jit(solution)/shard_map/ppermute | solution.py:110
  61.6 3.4 %collective-permute-done.1 = bf16[64,384]{1,0:T(8,128)(2,1)S(1)} collective-permute-done((bf16[64,384]{1,0:T(8,128)(2,1)S(1)}, bf16[64,384]{1,0:T(8,128)(2,1)S(1)}, u32[]{:S(2)}, u32[]{:S(2)}) %collective-permute-start.1) | collective-permute-done | bytes 49184 | tf_op jit(solution)/shard_map/ppermute | solution.py:110
  65.0 1.1 convolution_convert_fusion.1
  66.2 8.7 %all-to-all-start.2 = ((bf16[32,24,384]{2,1,0:T(8,128)(2,1)}), bf16[32,24,384]{2,1,0:T(8,128)(2,1)S(1)}, u32[]{:S(2)}, u32[]{:S(2)}) async-start(bf16[32,24,384]{2,1,0:T(8,128)(2,1)} %bitcast.16), calls=%async_computation.2 | async-start | bytes 1179648 | tf_op jit(solution)/shard_map/all_to_all | solution.py:118
  75.0 26.1 %all_gather.6 = bf16[8,128,384]{2,1,0:T(8,128)(2,1)S(1)} all-gather(bf16[1,128,384]{2,1,0:T(8,128)(2,1)S(1)} %bitcast.116), channel_id=1, replica_groups={{0,64,128,192,256,320,384,448},{32,96,160,224,288,352,416,480},{1,65,12..., dimensions={0}, use_global_device_ids=true | all-gather | bytes 884736 | tf_op jit(solution)/shard_map/all_gather | solution.py:213
  101.0 0.9 copy-done.2
  101.9 0.4 copy.102
  102.3 1.8 fusion.2
  104.1 8.3 %all-to-all-start.3 = ((bf16[32,8,3072]{2,1,0:T(8,128)(2,1)}), bf16[32,8,3072]{2,1,0:T(8,128)(2,1)S(1)}, u32[]{:S(2)}, u32[]{:S(2)}) async-start(bf16[32,8,3072]{2,1,0:T(8,128)(2,1)} %fusion.2), calls=%async_computation.3 | async-start | bytes 3145728 | tf_op jit(solution)/shard_map/all_to_all | solution.py:118
  112.6 2.0 copy.104
  114.6 2.5 copy.103
  117.1 3.5 %reshape_squeeze.3 = bf16[180,8,360]{2,1,0:T(8,128)(2,1)} reshape(bf16[1,180,2880]{2,1,0:T(8,128)(2,1)} %param.23) | data formatting | bytes 2073600 | tf_op jit(solution)/shard_map/reshape;squeeze | solution.py:122
  120.6 1.4 copy.105
  122.1 1.3 pad.33.w_out_ref
  123.5 0.6 copy-done.1
  124.1 2.1 and_select_fusion.w_in_ref
  126.2 24.1 %all-to-all-done.3 = bf16[32,8,3072]{2,1,0:T(8,128)(2,1)S(1)} async-done(((bf16[32,8,3072]{2,1,0:T(8,128)(2,1)}), bf16[32,8,3072]{2,1,0:T(8,128)(2,1)S(1)}, u32[]{:S(2)}, u32[]{:S(2)}) %all-to-all-start.3) | async-done | bytes 1572896 | tf_op jit(solution)/shard_map/all_to_all | solution.py:118
  150.3 1.2 copy-done
  151.5 6.0 %shard_map.118 = bf16[256,3072]{1,0:T(8,128)(2,1)} custom-call(bf16[256,3072]{1,0:T(8,128)(2,1)} %bitcast.107, bf16[8,384,512]{2,1,0:T(8,128)(2,1)} %and_select_fusion.w_in_ref, bf16[8,256,384]{2,1,0:T(8,128)(2,1)} %pad.33.w_out_ref), custom_call_target="tpu_custom_call" | custom-call | flops 796262400 | bytes 8192000 | tf_op jit(solution)/shard_map/pallas_call | solution.py:82
  157.4 4.1 %all-gather.2.cloned.1.call-done = bf16[6144,384]{1,0:T(8,128)(2,1)} async-done(((bf16[768,384]{1,0:T(8,128)(2,1)}), bf16[6144,384]{1,0:T(8,128)(2,1)}) %all-gather.2.cloned.1.call-update) | async-done | bytes 4718608 | tf_op jit(solution)/shard_map/all_gather | solution.py:215
  161.6 9.9 %shard_map.119 = bf16[8,768,384]{2,1,0:T(8,128)(2,1)} custom-call(bf16[8,768,384]{2,1,0:T(8,128)(2,1)} %bitcast.110, bf16[8,384,512]{2,1,0:T(8,128)(2,1)} %and_select_fusion.w_in_ref, bf16[8,256,384]{2,1,0:T(8,128)(2,1)} %pad.33.w_out_ref), custom_call_target="tpu_custom_call" | custom-call | flops 2388787200 | bytes 14090240 | tf_op jit(solution)/shard_map/pallas_call | solution.py:82
  171.5 8.4 %all-to-all-start.5 = ((bf16[32,8,3072]{2,1,0:T(8,128)(2,1)}), bf16[32,8,3072]{2,1,0:T(8,128)(2,1)S(1)}, u32[]{:S(2)}, u32[]{:S(2)}) async-start(bf16[32,8,3072]{2,1,0:T(8,128)(2,1)} %bitcast.32), calls=%async_computation.6 | async-start | bytes 3145728 | tf_op jit(solution)/shard_map/all_to_all | solution.py:118
  179.9 37.9 %all-to-all-done.5 = bf16[32,8,3072]{2,1,0:T(8,128)(2,1)S(1)} async-done(((bf16[32,8,3072]{2,1,0:T(8,128)(2,1)}), bf16[32,8,3072]{2,1,0:T(8,128)(2,1)S(1)}, u32[]{:S(2)}, u32[]{:S(2)}) %all-to-all-start.5) | async-done | bytes 1572896 | tf_op jit(solution)/shard_map/all_to_all | solution.py:118
  217.8 0.5 convolution_bitcast_fusion
  218.3 0.5 fusion.4
  218.9 32.4 %all_to_all.41 = bf16[8,128,384]{2,1,0:T(8,128)(2,1)S(1)} all-to-all(bf16[8,128,384]{2,1,0:T(8,128)(2,1)S(1)} %bitcast.111), channel_id=1, replica_groups={{0,64,128,192,256,320,384,448},{32,96,160,224,288,352,416,480},{1,65,12..., dimensions={0} | all-to-all | bytes 1572864 | tf_op jit(solution)/shard_map/all_to_all | solution.py:114
  251.3 8.4 %all-to-all-start.4 = ((bf16[32,24,384]{2,1,0:T(8,128)(2,1)}), bf16[32,24,384]{2,1,0:T(8,128)(2,1)S(1)}, u32[]{:S(2)}, u32[]{:S(2)}) async-start(bf16[32,24,384]{2,1,0:T(8,128)(2,1)} %bitcast.117), calls=%async_computation.5 | async-start | bytes 1179648 | tf_op jit(solution)/shard_map/all_to_all | solution.py:118
  260.0 18.2 %all-to-all-done.4 = bf16[32,24,384]{2,1,0:T(8,128)(2,1)S(1)} async-done(((bf16[32,24,384]{2,1,0:T(8,128)(2,1)}), bf16[32,24,384]{2,1,0:T(8,128)(2,1)S(1)}, u32[]{:S(2)}, u32[]{:S(2)}) %all-to-all-start.4) | async-done | bytes 589856 | tf_op jit(solution)/shard_map/all_to_all | solution.py:118
  278.8 14.6 %all_to_all.42 = f32[16,8,384]{2,1,0:T(8,128)S(1)} all-to-all(f32[16,8,384]{2,1,0:T(8,128)S(1)} %fusion.11), channel_id=1, replica_groups=mesh['attn'=16,'exp'=32] {'attn'}, dimensions={0} | all-to-all | bytes 393216 | tf_op jit(solution)/shard_map/all_to_all | solution.py:237
  293.5 0.7 convert_element_type.94
  (65 shorter events, 2.8 us)
Async XLA Ops:
  6.5 32.2 %collective-permute-start = (bf16[128,2880]{0,1:T(8,128)(2,1)}, bf16[128,2880]{0,1:T(8,128)(2,1)S(1)}, u32[]{:S(2)}, u32[]{:S(2)}) collective-permute-start(bf16[128,2880]{0,1:T(8,128)(2,1)} %param.17), channel_id=1, source_target_pairs={{0,32},{32,0},{64,96},{96,64},{128,160},{160,128},{192,224},{224,1... | collective-permute-start | bytes 2211848 | tf_op jit(solution)/shard_map/ppermute | solution.py:110
  14.9 0.8 copy-start.5
  14.9 2.3 copy-start.9
  17.2 1.8 copy-start.4
  19.0 19.4 %copy-start.3 = (bf16[128,2880]{0,1:T(8,128)(2,1)S(1)}, bf16[128,2880]{0,1:T(8,128)(2,1)}, u32[]{:S(2)}) copy-start(bf16[128,2880]{0,1:T(8,128)(2,1)} %param.17) | copy-start | bytes 2211844
  39.2 4.9 %copy-start.6 = (f32[2880]{0:T(1024)S(1)}, f32[2880]{0:T(1024)}, u32[]{:S(2)}) copy-start(f32[2880]{0:T(1024)} %param.18) | copy-start | bytes 34564
  39.2 5.0 %copy-start.7 = (s32[128,4]{0,1:T(4,128)S(1)}, s32[128,4]{0,1:T(4,128)}, u32[]{:S(2)}) copy-start(s32[128,4]{0,1:T(4,128)} %param.19) | copy-start | bytes 6148
  40.6 16.6 %all-to-all-start.1 = ((bf16[8,64,384]{2,1,0:T(8,128)(2,1)}), bf16[8,64,384]{2,1,0:T(8,128)(2,1)S(1)}, u32[]{:S(2)}, u32[]{:S(2)}) async-start(bf16[8,64,384]{2,1,0:T(8,128)(2,1)} %pad_bitcast_fusion.1), calls=%async_computation.1 | async-start | bytes 786432 | tf_op jit(solution)/shard_map/all_to_all | solution.py:114
  57.5 7.5 %collective-permute-start.1 = (bf16[64,384]{1,0:T(8,128)(2,1)S(1)}, bf16[64,384]{1,0:T(8,128)(2,1)S(1)}, u32[]{:S(2)}, u32[]{:S(2)}) collective-permute-start(bf16[64,384]{1,0:T(8,128)(2,1)S(1)} %select_convert_fusion), channel_id=1, source_target_pairs={{0,32},{32,0},{64,96},{96,64},{128,160},{160,128},{192,224},{224,1... | collective-permute-start | bytes 147464 | tf_op jit(solution)/shard_map/ppermute | solution.py:110
  66.2 34.8 %all-to-all-start.2 = ((bf16[32,24,384]{2,1,0:T(8,128)(2,1)}), bf16[32,24,384]{2,1,0:T(8,128)(2,1)S(1)}, u32[]{:S(2)}, u32[]{:S(2)}) async-start(bf16[32,24,384]{2,1,0:T(8,128)(2,1)} %bitcast.16), calls=%async_computation.2 | async-start | bytes 1179648 | tf_op jit(solution)/shard_map/all_to_all | solution.py:118
  74.9 86.7 %all-gather.2.cloned.1.call-start = ((), (), s32[]{:S(2)}) async-start(), calls=%async_computation.9 | async-start | bytes 5308416 | tf_op jit(solution)/shard_map/all_gather | solution.py:215
  101.0 0.9 copy-start.2
  104.1 46.2 %all-to-all-start.3 = ((bf16[32,8,3072]{2,1,0:T(8,128)(2,1)}), bf16[32,8,3072]{2,1,0:T(8,128)(2,1)S(1)}, u32[]{:S(2)}, u32[]{:S(2)}) async-start(bf16[32,8,3072]{2,1,0:T(8,128)(2,1)} %fusion.2), calls=%async_computation.3 | async-start | bytes 3145728 | tf_op jit(solution)/shard_map/all_to_all | solution.py:118
  112.4 138.9 %reduce-scatter.2.cloned.1.call-start = ((), (), s32[]{:S(2)}) async-start(), calls=%async_computation.10 | async-start | bytes 5308416 | tf_op jit(solution)/shard_map/reduce_scatter | solution.py:222
  122.1 2.0 copy-start.1
  150.3 1.2 copy-start
  171.5 8.4 %copy-start.8 = (f32[128,4]{0,1:T(4,128)S(1)}, f32[128,4]{0,1:T(4,128)}, u32[]{:S(2)}) copy-start(f32[128,4]{0,1:T(4,128)} %param.20) | copy-start | bytes 6148
  171.5 46.3 %all-to-all-start.5 = ((bf16[32,8,3072]{2,1,0:T(8,128)(2,1)}), bf16[32,8,3072]{2,1,0:T(8,128)(2,1)S(1)}, u32[]{:S(2)}, u32[]{:S(2)}) async-start(bf16[32,8,3072]{2,1,0:T(8,128)(2,1)} %bitcast.32), calls=%async_computation.6 | async-start | bytes 3145728 | tf_op jit(solution)/shard_map/all_to_all | solution.py:118
  251.3 26.9 %all-to-all-start.4 = ((bf16[32,24,384]{2,1,0:T(8,128)(2,1)}), bf16[32,24,384]{2,1,0:T(8,128)(2,1)S(1)}, u32[]{:S(2)}, u32[]{:S(2)}) async-start(bf16[32,24,384]{2,1,0:T(8,128)(2,1)} %bitcast.117), calls=%async_computation.5 | async-start | bytes 1179648 | tf_op jit(solution)/shard_map/all_to_all | solution.py:118
Sparse Core Ops, SparseCore 0:
  102.0 59.4 all-gather.1
  171.6 75.8 reduce-scatter.1

commit v6 on v4

--- a/solution.py
+++ b/solution.py
@@ -88,8 +88,6 @@
     own_rows = residual.shape[0]
     column_rows = expert_ids.shape[0]
     half_rows = column_rows // HALVES
-    half_cap = CAP // HALVES
-    half_slots = N_EXP * half_cap
     attn_index = lax.axis_index("attn")
     z_index = lax.shift_right_logical(attn_index, 1)
     half = lax.bitwise_and(attn_index, 1)
@@ -129,24 +127,20 @@
     slot = jnp.dot(named.astype(BF16), earlier, preferred_element_type=F32).astype(jnp.int32)
     slot = jnp.where(named, slot, -1)
 
-    def taken_of(own_half):
-        base = half_cap * (half if own_half else 1 - half)
-        return slot[:, None, :] == base + jnp.arange(half_cap, dtype=jnp.int32)[None, :, None]
-
-    taken_own, taken_other = taken_of(True), taken_of(False)
-    taken_both = jnp.concatenate([taken_own, taken_other], axis=1)
-
-    def picked(taken, rows):
-        select = taken.astype(BF16).reshape(-1, column_rows)
-        return jnp.dot(select, rows, preferred_element_type=F32).astype(BF16).reshape(N_EXP, -1, LANES)
-
-    def mixed_of(taken, partial_value):
-        returned = over_experts(partial_value).reshape(-1, LANES)
-        mix = jnp.where(taken, weight[:, None, :], 0.0).reshape(-1, column_rows)
-        mix_high = lax.reduce_precision(mix, 8, 7)
-        mix_low = (mix - mix_high).astype(BF16)
+    taken = slot[:, None, :] == jnp.arange(CAP, dtype=jnp.int32)[None, :, None]
+    select = taken.astype(BF16).reshape(N_EXP * CAP, column_rows)
+    mix = jnp.where(taken, weight[:, None, :], 0.0).reshape(N_EXP * CAP, column_rows)
+    mix_high = lax.reduce_precision(mix, 8, 7)
+    mix_low = (mix - mix_high).astype(BF16)
+    mix_high = mix_high.astype(BF16)
+
+    def picked(rows):
+        return jnp.dot(select, rows, preferred_element_type=F32).astype(BF16).reshape(N_EXP, CAP, LANES)
+
+    def mixed_of(partial_value):
+        returned = over_experts(partial_value.reshape(N_EXP, CAP, LANES)).reshape(N_EXP * CAP, LANES)
         over_slots = (((0,), (0,)), ((), ()))
-        mixed = lax.dot_general(mix_high.astype(BF16), returned, over_slots, preferred_element_type=F32)
+        mixed = lax.dot_general(mix_high, returned, over_slots, preferred_element_type=F32)
         return mixed + lax.dot_general(mix_low, returned, over_slots, preferred_element_type=F32)
 
     def padded_in(w):
@@ -166,48 +160,37 @@
     def input_term(rows, offset):
         return jnp.dot(rows, at_offset(w_in, offset), preferred_element_type=F32)
 
-    far_outgoing = picked(taken_both, shift_over_z(scaled, FAR))
-    own = over_experts(picked(taken_own, scaled)).reshape(half_slots, LANES)
-    own, w_in, w_out, far_outgoing = lax.optimization_barrier((own, w_in, w_out, far_outgoing))
-    halves_of_own = [own, swap_halves(own)]
-    up_block = jnp.concatenate([shift_over_z(h, 1) for h in halves_of_own])
-    down_block = jnp.concatenate([shift_over_z(h, -1) for h in halves_of_own])
-    both = input_term(jnp.concatenate(halves_of_own), 0) + input_term(up_block, -1)
-    far_outgoing, both = lax.optimization_barrier((far_outgoing, both))
-    far = over_experts(far_outgoing).reshape(N_EXP, 2, half_cap, LANES)
-    both = both + input_term(down_block, 1)
+    w_out = [at_offset(w_out, offset) for offset in range(BLOCKS)]
+
+    far_outgoing = picked(shift_over_z(scaled, FAR))
+    own = over_experts(picked(scaled)).reshape(N_EXP * CAP, LANES)
+    own, w_in, far_outgoing, *w_out = lax.optimization_barrier((own, w_in, far_outgoing, *w_out))
+    up_block, down_block = shift_over_z(own, 1), shift_over_z(own, -1)
+    far = over_experts(far_outgoing).reshape(N_EXP * CAP, LANES)
+    both = input_term(own, 0) + input_term(up_block, -1) + input_term(down_block, 1)
     for step in range(2, FAR):
         up_block, down_block = shift_over_z(up_block, 1), shift_over_z(down_block, -1)
         if step == FAR - 1:
             both = lax.optimization_barrier(both)
         both = both + input_term(up_block, -step)
         both = both + input_term(down_block, step)
-    both = both + input_term(far.transpose(1, 0, 2, 3).reshape(N_EXP * CAP, LANES), FAR)
+    both = both + input_term(far, FAR)
     factor = lax.rsqrt(both[:, FF_LOCAL : FF_LOCAL + 1] * (1.0 / D) + 1e-05)
     gate = both[:, :FF_LANES] * factor
     up = both[:, FF_LANES:] * factor
     expert_hidden = (gate * jax.nn.sigmoid(1.702 * gate) * (up + 1.0)).astype(BF16)
 
     def output_block(offset):
-        return jnp.dot(expert_hidden, at_offset(w_out, offset), preferred_element_type=F32)
+        return jnp.dot(expert_hidden, w_out[offset % BLOCKS], preferred_element_type=F32)
 
     up_sum = shift_over_z(output_block(FAR - 1).astype(BF16), 1)
     down_sum = shift_over_z(output_block(1 - FAR).astype(BF16), -1)
-    far_value = output_block(FAR).astype(BF16).reshape(2, N_EXP, half_cap, LANES).transpose(1, 0, 2, 3)
-    far_mixed = shift_over_z(mixed_of(taken_both, far_value.reshape(N_EXP, CAP, LANES)), FAR)
+    far_mixed = shift_over_z(mixed_of(output_block(FAR).astype(BF16)), FAR)
     for offset in range(FAR - 2, 0, -1):
-        up_sum = (output_block(offset) + up_sum.astype(F32)).astype(BF16)
-        down_sum = (output_block(-offset) + down_sum.astype(F32)).astype(BF16)
-        if offset > 1:
-            up_sum, down_sum = shift_over_z(up_sum, 1), shift_over_z(down_sum, -1)
-    own_block = output_block(0)
-    sums = []
-    for rows in (slice(0, half_slots), slice(half_slots, None)):
-        arrived = shift_over_z(up_sum[rows], 1).astype(F32) + shift_over_z(down_sum[rows], -1).astype(F32)
-        sums.append(own_block[rows] + arrived)
-    other_sum = swap_halves(sums[0].astype(BF16))
-    whole_sum = (sums[1] + other_sum.astype(F32)).astype(BF16)
-    mixed = mixed_of(taken_other, whole_sum.reshape(N_EXP, half_cap, LANES)) + far_mixed
+        up_sum = shift_over_z((output_block(offset) + up_sum.astype(F32)).astype(BF16), 1)
+        down_sum = shift_over_z((output_block(-offset) + down_sum.astype(F32)).astype(BF16), -1)
+    own_sum = (output_block(0) + up_sum.astype(F32) + down_sum.astype(F32)).astype(BF16)
+    mixed = mixed_of(own_sum) + far_mixed
 
     mixed = mixed.reshape(BLOCKS, HALVES, own_rows, LANES)
     halves = jnp.arange(HALVES, dtype=jnp.int32)[None, :, None, None]

time: 294 us -> 302 us (1.027)
  waiting for transfers between devices: 80.8 us -> 107 us
  starting transfers between devices: 127 us -> 106 us
    ppermute x18 -> x14, waiting for transfers between devices: 44.5 us -> 64.4 us  [shift_over_z(): return lax.ppermute(array, 'attn', pairs)]
    ppermute x18 -> x14, starting transfers between devices: 65 us -> 50.1 us  [shift_over_z(): return lax.ppermute(array, 'attn', pairs)]
    all_to_all x4, waiting for transfers between devices: 10.5 us -> 19.2 us  [over_experts(): return lax.all_to_all(array, 'exp', 0, 0, tiled=True)]
    ppermute x4 -> x2, starting transfers between devices: 14 us -> 6.62 us  [swap_halves(): return lax.ppermute(array, 'attn', [(i, i ^ 1) for i in range(N_ATTN)])]
    all_to_all x2, waiting for transfers between devices: 17.9 us -> 11.4 us  [over_z(): lax.all_to_all(array, 'attn', 0, 0, tiled=True, axis_index_groups=Z_GROUPS)]
    ppermute x4 -> x2, waiting for transfers between devices: 7.72 us -> 11.8 us  [swap_halves(): return lax.ppermute(array, 'attn', [(i, i ^ 1) for i in range(N_ATTN)])]
    all_to_all x2, starting transfers between devices: 13.8 us -> 17.4 us  [over_z(): lax.all_to_all(array, 'attn', 0, 0, tiled=True, axis_index_groups=Z_GROUPS)]
    unnamed x50 -> x70, local copies, waits for them, and re-layouts: 6.28 us -> 7.6 us
  transfers between devices with their start and end apart: 28 -> 22, of which waited for: 17 -> 14; matrix products, arithmetic and copies ran while one was open for 19% -> 16% of each run, Pallas kernels for 0% -> 0%
where the time goes in v6:
time: 302 us; the launch traced here: 297 us
  waiting for transfers between devices  107 us (35%)
  starting transfers between devices  106 us (35%)
  matrix products  33.8 us (11%)
  local copies, waits for them, and re-layouts  24.1 us (8%)
  blocking collectives  16.8 us (6%)
  other arithmetic  8.6 us (3%)
    ppermute x14, waiting for transfers between devices, shift_over_z(): return lax.ppermute(array, 'attn', pairs)  64.4 us
    ppermute x14, starting transfers between devices, shift_over_z(): return lax.ppermute(array, 'attn', pairs)  50.1 us
    all_to_all x4, starting transfers between devices, over_experts(): return lax.all_to_all(array, 'exp', 0, 0, tiled=True)  32 us
    all_to_all x4, waiting for transfers between devices, over_experts(): return lax.all_to_all(array, 'exp', 0, 0, tiled=True)  19.2 us
    all_to_all x2, starting transfers between devices, over_z(): lax.all_to_all(array, 'attn', 0, 0, tiled=True, axis_index_groups=Z_GROUPS)  17.4 us
    all_to_all x1, blocking collectives, local(): lax.all_to_all(mixed.reshape(N_ATTN, own_rows, LANES), 'attn', 0, 0, tile...  16.8 us
    dot_general x8, matrix products, input_term(): return jnp.dot(rows, at_offset(w_in, offset), preferred_element_type=F32)  16.8 us
    ppermute x2, waiting for transfers between devices, swap_halves(): return lax.ppermute(array, 'attn', [(i, i ^ 1) for i in range(N_ATTN)])  11.8 us
  transfers between devices with their start and end apart: 22, of which 14 were waited for; matrix products, arithmetic and copies ran while one was open for 16% of the time, Pallas kernels for 0%

profile of v6, /device:TPU:6, one launch (start us, length us, event | category | flops | bytes accessed | tf_op | source)
XLA Modules:
  0.0 297.1 jit_solution(12190187461396924481)
XLA Ops:
  2.0 2.2 fusion.93
  9.5 10.3 %all-to-all-start = ((bf16[8,8,640]{2,1,0:T(8,128)(2,1)}), bf16[8,8,640]{2,1,0:T(8,128)(2,1)S(1)}, u32[]{:S(2)}, u32[]{:S(2)}) async-start(bf16[8,8,640]{2,1,0:T(8,128)(2,1)} %copy.94), calls=%async_computation | async-start | bytes 163840 | tf_op jit(solution)/shard_map/all_to_all | solution.py:62
  19.8 3.3 %collective-permute-start = (bf16[128,2880]{0,1:T(8,128)(2,1)}, bf16[128,2880]{0,1:T(8,128)(2,1)}, u32[]{:S(2)}, u32[]{:S(2)}) collective-permute-start(bf16[128,2880]{0,1:T(8,128)(2,1)} %param.17), channel_id=1, source_target_pairs={{0,32},{32,0},{64,96},{96,64},{128,160},{160,128},{192,224},{224,1... | collective-permute-start | bytes 2211848 | tf_op jit(solution)/shard_map/ppermute | solution.py:58
  24.8 4.8 %pad_dynamic-slice_fusion = (bf16[1,256,384]{2,0,1:T(2,128)(2,1)S(1)}, bf16[1,256,384]{2,0,1:T(2,128)(2,1)S(1)}, bf16[1,256,384]{2,0,1:T(2,128)(2,1)S(1)}, bf16[...) fusion(s32[]{:T(128)S(6)} %select_n.145, ...), kind=kLoop, calls=%fused_computation.10 | loop fusion | bytes 2678816 | tf_op jit(solution)/shard_map/jit(dynamic_index_in_dim)/dynamic_slice | solution.py:158
  33.7 7.8 %collective-permute-done = bf16[128,2880]{0,1:T(8,128)(2,1)} collective-permute-done((bf16[128,2880]{0,1:T(8,128)(2,1)}, bf16[128,2880]{0,1:T(8,128)(2,1)}, u32[]{:S(2)}, u32[]{:S(2)}) %collective-permute-start) | collective-permute-done | bytes 737312 | tf_op jit(solution)/shard_map/ppermute | solution.py:58
  44.4 7.1 %all-to-all-start.1 = ((bf16[8,64,384]{2,1,0:T(8,128)(2,1)}), bf16[8,64,384]{2,1,0:T(8,128)(2,1)S(1)}, u32[]{:S(2)}, u32[]{:S(2)}) async-start(bf16[8,64,384]{2,1,0:T(8,128)(2,1)} %pad_bitcast_fusion.1), calls=%async_computation.1 | async-start | bytes 786432 | tf_op jit(solution)/shard_map/all_to_all | solution.py:62
  53.2 11.4 %all-to-all-done.1 = bf16[8,64,384]{2,1,0:T(8,128)(2,1)S(1)} async-done(((bf16[8,64,384]{2,1,0:T(8,128)(2,1)}), bf16[8,64,384]{2,1,0:T(8,128)(2,1)S(1)}, u32[]{:S(2)}, u32[]{:S(2)}) %all-to-all-start.1) | async-done | bytes 393248 | tf_op jit(solution)/shard_map/all_to_all | solution.py:62
  65.6 3.3 %collective-permute-start.1 = (bf16[64,384]{1,0:T(8,128)(2,1)S(1)}, bf16[64,384]{1,0:T(8,128)(2,1)S(1)}, u32[]{:S(2)}, u32[]{:S(2)}) collective-permute-start(bf16[64,384]{1,0:T(8,128)(2,1)S(1)} %select_convert_fusion), channel_id=1, source_target_pairs={{0,32},{32,0},{64,96},{96,64},{128,160},{160,128},{192,224},{224,1... | collective-permute-start | bytes 147464 | tf_op jit(solution)/shard_map/ppermute | solution.py:58
  69.0 4.1 %collective-permute-done.1 = bf16[64,384]{1,0:T(8,128)(2,1)S(1)} collective-permute-done((bf16[64,384]{1,0:T(8,128)(2,1)S(1)}, bf16[64,384]{1,0:T(8,128)(2,1)S(1)}, u32[]{:S(2)}, u32[]{:S(2)}) %collective-permute-start.1) | collective-permute-done | bytes 49184 | tf_op jit(solution)/shard_map/ppermute | solution.py:58
  73.8 2.1 convolution_convert_fusion.4
  75.9 8.9 %all-to-all-start.2 = ((bf16[32,32,384]{2,1,0:T(8,128)(2,1)}), bf16[32,32,384]{2,1,0:T(8,128)(2,1)}, u32[]{:S(2)}, u32[]{:S(2)}) async-start(bf16[32,32,384]{2,1,0:T(8,128)(2,1)} %bitcast.16), calls=%async_computation.2 | async-start | bytes 1572864 | tf_op jit(solution)/shard_map/all_to_all | solution.py:66
  85.3 1.6 copy.98
  87.0 1.7 copy.99
  89.5 2.4 and_select_fusion
  91.9 2.5 collective-permute-start.2
  95.5 7.5 %collective-permute-done.2 = bf16[128,384]{1,0:T(8,128)(2,1)} collective-permute-done((bf16[128,384]{1,0:T(8,128)(2,1)}, bf16[128,384]{1,0:T(8,128)(2,1)}, u32[]{:S(2)}, u32[]{:S(2)}) %collective-permute-start.2) | collective-permute-done | bytes 98336 | tf_op jit(solution)/shard_map/ppermute | solution.py:54
  103.0 2.1 convolution_convert_fusion.3
  105.1 2.2 all-to-all-done.2
  107.2 6.2 %all-to-all-start.3 = ((bf16[32,32,384]{2,1,0:T(8,128)(2,1)}), bf16[32,32,384]{2,1,0:T(8,128)(2,1)}, u32[]{:S(2)}, u32[]{:S(2)}) async-start(bf16[32,32,384]{2,1,0:T(8,128)(2,1)} %bitcast.160), calls=%async_computation.3 | async-start | bytes 1572864 | tf_op jit(solution)/shard_map/all_to_all | solution.py:66
  113.4 4.4 %collective-permute-start.3 = (bf16[1024,384]{1,0:T(8,128)(2,1)}, bf16[1024,384]{1,0:T(8,128)(2,1)}, u32[]{:S(2)}, u32[]{:S(2)}) collective-permute-start(bf16[1024,384]{1,0:T(8,128)(2,1)} %bitcast.17), channel_id=1, source_target_pairs={{0,64},{32,96},{64,128},{96,160},{128,192},{160,224},{192,256},{22... | collective-permute-start | bytes 2359304 | tf_op jit(solution)/shard_map/ppermute | solution.py:54
  117.9 2.8 collective-permute-start.4
  120.7 3.2 %fusion.42 = f32[1024,512]{1,0:T(8,128)} fusion(bf16[1024,384]{1,0:T(8,128)(2,1)} %bitcast.17, bf16[8,384,512]{2,1,0:T(8,128)(2,1)S(1)} %and_select_fusion, s32[]{:T(128)S(6)} %select_n.138), kind=kOutput, calls=%fused_computation.78 | convolution fusion | flops 402653184 | bytes 3276804 | tf_op jit(solution)/shard_map/dot_general | solution.py:161
  123.9 12.6 %collective-permute-done.3 = bf16[1024,384]{1,0:T(8,128)(2,1)} collective-permute-done((bf16[1024,384]{1,0:T(8,128)(2,1)}, bf16[1024,384]{1,0:T(8,128)(2,1)}, u32[]{:S(2)}, u32[]{:S(2)}) %collective-permute-start.3) | collective-permute-done | bytes 786464 | tf_op jit(solution)/shard_map/ppermute | solution.py:54
  136.5 3.2 %collective-permute-start.5 = (bf16[1024,384]{1,0:T(8,128)(2,1)}, bf16[1024,384]{1,0:T(8,128)(2,1)}, u32[]{:S(2)}, u32[]{:S(2)}) collective-permute-start(bf16[1024,384]{1,0:T(8,128)(2,1)} %collective-permute-done.3), channel_id=1, source_target_pairs={{0,64},{32,96},{64,128},{96,160},{128,192},{160,224},{192,256},{22... | collective-permute-start | bytes 2359304 | tf_op jit(solution)/shard_map/ppermute | solution.py:54
  139.7 3.8 %collective-permute-start.6 = (bf16[1024,384]{1,0:T(8,128)(2,1)}, bf16[1024,384]{1,0:T(8,128)(2,1)}, u32[]{:S(2)}, u32[]{:S(2)}) collective-permute-start(bf16[1024,384]{1,0:T(8,128)(2,1)} %collective-permute-done.4), channel_id=1, source_target_pairs={{0,448},{32,480},{64,0},{96,32},{128,64},{160,96},{192,128},{224,1... | collective-permute-start | bytes 2359304 | tf_op jit(solution)/shard_map/ppermute | solution.py:54
  143.5 3.2 %fusion.40 = f32[1024,512]{1,0:T(8,128)} fusion(bf16[1024,384]{1,0:T(8,128)(2,1)} %collective-permute-done.3, bf16[8,384,512]{2,1,0:T(8,128)(2,1)S(1)} %and_select_fusion, s32[]{:T(128)S(6)} %select_n.145), kind=kOutput, calls=%fused_computation.76 | convolution fusion | flops 402653184 | bytes 3276804 | tf_op jit(solution)/shard_map/dot_general | solution.py:161
  146.7 3.2 %fusion.38 = f32[1024,512]{1,0:T(8,128)} fusion(bf16[1024,384]{1,0:T(8,128)(2,1)} %collective-permute-done.4, bf16[8,384,512]{2,1,0:T(8,128)(2,1)S(1)} %and_select_fusion, s32[]{:T(128)S(6)} %select_n.139), kind=kOutput, calls=%fused_computation.74 | convolution fusion | flops 402653184 | bytes 3276804 | tf_op jit(solution)/shard_map/dot_general | solution.py:161
  149.9 2.0 fusion.24
  151.9 6.7 %collective-permute-done.5 = bf16[1024,384]{1,0:T(8,128)(2,1)} collective-permute-done((bf16[1024,384]{1,0:T(8,128)(2,1)}, bf16[1024,384]{1,0:T(8,128)(2,1)}, u32[]{:S(2)}, u32[]{:S(2)}) %collective-permute-start.5) | collective-permute-done | bytes 786464 | tf_op jit(solution)/shard_map/ppermute | solution.py:54
  158.6 2.0 collective-permute-start.7
  160.7 5.0 %collective-permute-start.8 = (bf16[1024,384]{1,0:T(8,128)(2,1)}, bf16[1024,384]{1,0:T(8,128)(2,1)S(1)}, u32[]{:S(2)}, u32[]{:S(2)}) collective-permute-start(bf16[1024,384]{1,0:T(8,128)(2,1)} %collective-permute-done.6), channel_id=1, source_target_pairs={{0,448},{32,480},{64,0},{96,32},{128,64},{160,96},{192,128},{224,1... | collective-permute-start | bytes 2359304 | tf_op jit(solution)/shard_map/ppermute | solution.py:54
  165.7 1.8 fusion.36
  167.6 1.9 add_add_fusion.1
  169.5 10.3 %collective-permute-done.7 = bf16[1024,384]{1,0:T(8,128)(2,1)S(1)} collective-permute-done((bf16[1024,384]{1,0:T(8,128)(2,1)}, bf16[1024,384]{1,0:T(8,128)(2,1)S(1)}, u32[]{:S(2)}, u32[]{:S(2)}) %collective-permute-start.7) | collective-permute-done | bytes 786464 | tf_op jit(solution)/shard_map/ppermute | solution.py:54
  184.1 2.2 collective-permute-start.9
  186.7 5.3 %collective-permute-start.12 = (bf16[1024,384]{1,0:T(8,128)(2,1)S(1)}, bf16[1024,384]{1,0:T(8,128)(2,1)S(1)}, u32[]{:S(2)}, u32[]{:S(2)}) collective-permute-start(bf16[1024,384]{1,0:T(8,128)(2,1)S(1)} %convolution_convert_fusion.1), channel_id=1, source_target_pairs={{0,448},{32,480},{64,0},{96,32},{128,64},{160,96},{192,128},{224,1... | collective-permute-start | bytes 2359304 | tf_op jit(solution)/shard_map/ppermute | solution.py:54
  193.4 8.5 %all-to-all-start.5 = ((bf16[32,32,384]{2,1,0:T(8,128)(2,1)}), bf16[32,32,384]{2,1,0:T(8,128)(2,1)S(1)}, u32[]{:S(2)}, u32[]{:S(2)}) async-start(bf16[32,32,384]{2,1,0:T(8,128)(2,1)} %bitcast.35), calls=%async_computation.5 | async-start | bytes 1572864 | tf_op jit(solution)/shard_map/all_to_all | solution.py:66
  201.9 3.0 %collective-permute-done.9 = bf16[1024,384]{1,0:T(8,128)(2,1)} collective-permute-done((bf16[1024,384]{1,0:T(8,128)(2,1)}, bf16[1024,384]{1,0:T(8,128)(2,1)}, u32[]{:S(2)}, u32[]{:S(2)}) %collective-permute-start.9) | collective-permute-done | bytes 786464 | tf_op jit(solution)/shard_map/ppermute | solution.py:54
  206.5 2.1 collective-permute-start.10
  209.0 5.1 %collective-permute-start.13 = (bf16[1024,384]{1,0:T(8,128)(2,1)S(1)}, bf16[1024,384]{1,0:T(8,128)(2,1)S(1)}, u32[]{:S(2)}, u32[]{:S(2)}) collective-permute-start(bf16[1024,384]{1,0:T(8,128)(2,1)S(1)} %add_convert_fusion.2), channel_id=1, source_target_pairs={{0,448},{32,480},{64,0},{96,32},{128,64},{160,96},{192,128},{224,1... | collective-permute-start | bytes 2359304 | tf_op jit(solution)/shard_map/ppermute | solution.py:54
  215.0 11.3 %collective-permute-done.10 = bf16[1024,384]{1,0:T(8,128)(2,1)S(1)} collective-permute-done((bf16[1024,384]{1,0:T(8,128)(2,1)S(1)}, bf16[1024,384]{1,0:T(8,128)(2,1)S(1)}, u32[]{:S(2)}, u32[]{:S(2)}) %collective-permute-start.10) | collective-permute-done | bytes 786464 | tf_op jit(solution)/shard_map/ppermute | solution.py:54
  226.5 2.1 collective-permute-start.11
  228.8 5.1 %collective-permute-start.14 = (bf16[1024,384]{1,0:T(8,128)(2,1)S(1)}, bf16[1024,384]{1,0:T(8,128)(2,1)S(1)}, u32[]{:S(2)}, u32[]{:S(2)}) collective-permute-start(bf16[1024,384]{1,0:T(8,128)(2,1)S(1)} %add_convert_fusion.1), channel_id=1, source_target_pairs={{0,448},{32,480},{64,0},{96,32},{128,64},{160,96},{192,128},{224,1... | collective-permute-start | bytes 2359304 | tf_op jit(solution)/shard_map/ppermute | solution.py:54
  234.4 11.1 %collective-permute-done.11 = bf16[1024,384]{1,0:T(8,128)(2,1)S(1)} collective-permute-done((bf16[1024,384]{1,0:T(8,128)(2,1)S(1)}, bf16[1024,384]{1,0:T(8,128)(2,1)S(1)}, u32[]{:S(2)}, u32[]{:S(2)}) %collective-permute-start.11) | collective-permute-done | bytes 786464 | tf_op jit(solution)/shard_map/ppermute | solution.py:54
  248.0 8.4 %all-to-all-start.4 = ((bf16[32,32,384]{2,1,0:T(8,128)(2,1)}), bf16[32,32,384]{2,1,0:T(8,128)(2,1)S(1)}, u32[]{:S(2)}, u32[]{:S(2)}) async-start(bf16[32,32,384]{2,1,0:T(8,128)(2,1)} %bitcast.32), calls=%async_computation.4 | async-start | bytes 1572864 | tf_op jit(solution)/shard_map/all_to_all | solution.py:66
  257.2 4.4 %collective-permute-start.15 = (f32[128,384]{1,0:T(8,128)S(1)}, f32[128,384]{1,0:T(8,128)S(1)}, u32[]{:S(2)}, u32[]{:S(2)}) collective-permute-start(f32[128,384]{1,0:T(8,128)S(1)} %fusion.8), channel_id=1, source_target_pairs={{0,256},{32,288},{64,320},{96,352},{128,384},{160,416},{192,448},{... | collective-permute-start | bytes 589832 | tf_op jit(solution)/shard_map/ppermute | solution.py:54
  261.8 17.0 %all-to-all-done.4 = bf16[32,32,384]{2,1,0:T(8,128)(2,1)S(1)} async-done(((bf16[32,32,384]{2,1,0:T(8,128)(2,1)}), bf16[32,32,384]{2,1,0:T(8,128)(2,1)S(1)}, u32[]{:S(2)}, u32[]{:S(2)}) %all-to-all-start.4) | async-done | bytes 786464 | tf_op jit(solution)/shard_map/all_to_all | solution.py:66
  279.5 16.8 %all_to_all.35 = f32[16,8,384]{2,1,0:T(8,128)S(1)} all-to-all(f32[16,8,384]{2,1,0:T(8,128)S(1)} %fusion.9), channel_id=1, replica_groups=mesh['attn'=16,'exp'=32] {'attn'}, dimensions={0} | all-to-all | bytes 393216 | tf_op jit(solution)/shard_map/all_to_all | solution.py:198
  (147 shorter events, 36.3 us)
Async XLA Ops:
  2.0 2.6 copy-start.21
  2.0 2.7 copy-start.29
  7.7 15.4 %copy-start.5 = (bf16[1,180,2880]{2,1,0:T(8,128)(2,1)S(1)}, bf16[1,180,2880]{2,1,0:T(8,128)(2,1)}, u32[]{:S(2)}) copy-start(bf16[1,180,2880]{2,1,0:T(8,128)(2,1)} %param.23) | copy-start | bytes 3110404
  9.5 22.7 %all-to-all-start = ((bf16[8,8,640]{2,1,0:T(8,128)(2,1)}), bf16[8,8,640]{2,1,0:T(8,128)(2,1)S(1)}, u32[]{:S(2)}, u32[]{:S(2)}) async-start(bf16[8,8,640]{2,1,0:T(8,128)(2,1)} %copy.94), calls=%async_computation | async-start | bytes 163840 | tf_op jit(solution)/shard_map/all_to_all | solution.py:62
  19.8 21.7 %collective-permute-start = (bf16[128,2880]{0,1:T(8,128)(2,1)}, bf16[128,2880]{0,1:T(8,128)(2,1)}, u32[]{:S(2)}, u32[]{:S(2)}) collective-permute-start(bf16[128,2880]{0,1:T(8,128)(2,1)} %param.17), channel_id=1, source_target_pairs={{0,32},{32,0},{64,96},{96,64},{128,160},{160,128},{192,224},{224,1... | collective-permute-start | bytes 2211848 | tf_op jit(solution)/shard_map/ppermute | solution.py:58
  24.8 6.8 %copy-start.23 = (s32[128,4]{0,1:T(4,128)S(1)}, s32[128,4]{0,1:T(4,128)}, u32[]{:S(2)}) copy-start(s32[128,4]{0,1:T(4,128)} %param.19) | copy-start | bytes 6148
  33.7 17.9 %copy-start.4 = (bf16[1,256,384]{2,0,1:T(2,128)(2,1)S(1)}, bf16[1,256,384]{2,0,1:T(2,128)(2,1)}, u32[]{:S(2)}) copy-start(bf16[1,256,384]{2,0,1:T(2,128)(2,1)} %get-tuple-element.33) | copy-start | bytes 589828
  41.4 10.0 %copy-start.25 = (pred[32,128]{1,0:T(8,128)(4,1)S(1)}, pred[32,128]{1,0:T(8,128)(4,1)}, u32[]{:S(2)}) copy-start(pred[32,128]{1,0:T(8,128)(4,1)} %fusion.72) | copy-start | bytes 12292
  43.6 21.1 %copy-start.17 = (bf16[8,8,640]{2,1,0:T(8,128)(2,1)S(1)}, bf16[8,8,640]{2,1,0:T(8,128)(2,1)}, u32[]{:S(2)}) copy-start(bf16[8,8,640]{2,1,0:T(8,128)(2,1)} %copy-done.16) | copy-start | bytes 245764
  44.4 21.1 %copy-start.22 = (f32[384]{0:T(512)S(1)}, f32[384]{0:T(512)}, u32[]{:S(2)}) copy-start(f32[384]{0:T(512)} %fusion.86) | copy-start | bytes 4612
  44.4 21.1 %copy-start.27 = (pred[384]{0:T(512)(128)(4,1)S(1)}, pred[384]{0:T(512)(128)(4,1)}, u32[]{:S(2)}) copy-start(pred[384]{0:T(512)(128)(4,1)} %get-tuple-element.53) | copy-start | bytes 1156
  44.4 21.1 %copy-start.28 = (pred[384]{0:T(512)(128)(4,1)S(1)}, pred[384]{0:T(512)(128)(4,1)}, u32[]{:S(2)}) copy-start(pred[384]{0:T(512)(128)(4,1)} %get-tuple-element.54) | copy-start | bytes 1156
  44.4 20.3 %all-to-all-start.1 = ((bf16[8,64,384]{2,1,0:T(8,128)(2,1)}), bf16[8,64,384]{2,1,0:T(8,128)(2,1)S(1)}, u32[]{:S(2)}, u32[]{:S(2)}) async-start(bf16[8,64,384]{2,1,0:T(8,128)(2,1)} %pad_bitcast_fusion.1), calls=%async_computation.1 | async-start | bytes 786432 | tf_op jit(solution)/shard_map/all_to_all | solution.py:62
  53.2 32.1 %copy-start.6 = (bf16[1,2880,180]{1,2,0:T(8,128)(2,1)S(1)}, bf16[1,2880,180]{1,2,0:T(8,128)(2,1)}, u32[]{:S(2)}) copy-start(bf16[1,2880,180]{1,2,0:T(8,128)(2,1)} %param.21) | copy-start | bytes 3110404
  65.6 7.5 %collective-permute-start.1 = (bf16[64,384]{1,0:T(8,128)(2,1)S(1)}, bf16[64,384]{1,0:T(8,128)(2,1)S(1)}, u32[]{:S(2)}, u32[]{:S(2)}) collective-permute-start(bf16[64,384]{1,0:T(8,128)(2,1)S(1)} %select_convert_fusion), channel_id=1, source_target_pairs={{0,32},{32,0},{64,96},{96,64},{128,160},{160,128},{192,224},{224,1... | collective-permute-start | bytes 147464 | tf_op jit(solution)/shard_map/ppermute | solution.py:58
  75.9 11.1 %copy-start.7 = (bf16[1,2880,180]{1,2,0:T(8,128)(2,1)S(1)}, bf16[1,2880,180]{1,2,0:T(8,128)(2,1)}, u32[]{:S(2)}) copy-start(bf16[1,2880,180]{1,2,0:T(8,128)(2,1)} %param.22) | copy-start | bytes 3110404
  75.9 31.3 %all-to-all-start.2 = ((bf16[32,32,384]{2,1,0:T(8,128)(2,1)}), bf16[32,32,384]{2,1,0:T(8,128)(2,1)}, u32[]{:S(2)}, u32[]{:S(2)}) async-start(bf16[32,32,384]{2,1,0:T(8,128)(2,1)} %bitcast.16), calls=%async_computation.2 | async-start | bytes 1572864 | tf_op jit(solution)/shard_map/all_to_all | solution.py:66
  89.5 4.9 %copy-start.3 = (bf16[1,256,384]{2,0,1:T(2,128)(2,1)S(1)}, bf16[1,256,384]{2,0,1:T(2,128)(2,1)}, u32[]{:S(2)}) copy-start(bf16[1,256,384]{2,0,1:T(2,128)(2,1)} %get-tuple-element.34) | copy-start | bytes 589828
  91.9 11.1 %collective-permute-start.2 = (bf16[128,384]{1,0:T(8,128)(2,1)}, bf16[128,384]{1,0:T(8,128)(2,1)}, u32[]{:S(2)}, u32[]{:S(2)}) collective-permute-start(bf16[128,384]{1,0:T(8,128)(2,1)} %bitcast.15), channel_id=1, source_target_pairs={{0,256},{32,288},{64,320},{96,352},{128,384},{160,416},{192,448},{... | collective-permute-start | bytes 294920 | tf_op jit(solution)/shard_map/ppermute | solution.py:54
  107.2 42.7 %all-to-all-start.3 = ((bf16[32,32,384]{2,1,0:T(8,128)(2,1)}), bf16[32,32,384]{2,1,0:T(8,128)(2,1)}, u32[]{:S(2)}, u32[]{:S(2)}) async-start(bf16[32,32,384]{2,1,0:T(8,128)(2,1)} %bitcast.160), calls=%async_computation.3 | async-start | bytes 1572864 | tf_op jit(solution)/shard_map/all_to_all | solution.py:66
  113.4 23.0 %collective-permute-start.3 = (bf16[1024,384]{1,0:T(8,128)(2,1)}, bf16[1024,384]{1,0:T(8,128)(2,1)}, u32[]{:S(2)}, u32[]{:S(2)}) collective-permute-start(bf16[1024,384]{1,0:T(8,128)(2,1)} %bitcast.17), channel_id=1, source_target_pairs={{0,64},{32,96},{64,128},{96,160},{128,192},{160,224},{192,256},{22... | collective-permute-start | bytes 2359304 | tf_op jit(solution)/shard_map/ppermute | solution.py:54
  117.9 21.8 %collective-permute-start.4 = (bf16[1024,384]{1,0:T(8,128)(2,1)}, bf16[1024,384]{1,0:T(8,128)(2,1)}, u32[]{:S(2)}, u32[]{:S(2)}) collective-permute-start(bf16[1024,384]{1,0:T(8,128)(2,1)} %bitcast.17), channel_id=1, source_target_pairs={{0,448},{32,480},{64,0},{96,32},{128,64},{160,96},{192,128},{224,1... | collective-permute-start | bytes 2359304 | tf_op jit(solution)/shard_map/ppermute | solution.py:54
  136.5 22.2 %collective-permute-start.5 = (bf16[1024,384]{1,0:T(8,128)(2,1)}, bf16[1024,384]{1,0:T(8,128)(2,1)}, u32[]{:S(2)}, u32[]{:S(2)}) collective-permute-start(bf16[1024,384]{1,0:T(8,128)(2,1)} %collective-permute-done.3), channel_id=1, source_target_pairs={{0,64},{32,96},{64,128},{96,160},{128,192},{160,224},{192,256},{22... | collective-permute-start | bytes 2359304 | tf_op jit(solution)/shard_map/ppermute | solution.py:54
  139.7 21.0 %collective-permute-start.6 = (bf16[1024,384]{1,0:T(8,128)(2,1)}, bf16[1024,384]{1,0:T(8,128)(2,1)}, u32[]{:S(2)}, u32[]{:S(2)}) collective-permute-start(bf16[1024,384]{1,0:T(8,128)(2,1)} %collective-permute-done.4), channel_id=1, source_target_pairs={{0,448},{32,480},{64,0},{96,32},{128,64},{160,96},{192,128},{224,1... | collective-permute-start | bytes 2359304 | tf_op jit(solution)/shard_map/ppermute | solution.py:54
  149.9 17.6 %copy-start.1 = (f32[1024,512]{1,0:T(8,128)S(1)}, f32[1024,512]{1,0:T(8,128)}, u32[]{:S(2)}) copy-start(f32[1024,512]{1,0:T(8,128)} %fusion.40) | copy-start | bytes 6291460
  149.9 17.6 %copy-start.2 = (f32[1024,512]{1,0:T(8,128)S(1)}, f32[1024,512]{1,0:T(8,128)}, u32[]{:S(2)}) copy-start(f32[1024,512]{1,0:T(8,128)} %fusion.38) | copy-start | bytes 6291460
  151.9 15.7 %copy-start = (f32[1024,512]{1,0:T(8,128)S(1)}, f32[1024,512]{1,0:T(8,128)}, u32[]{:S(2)}) copy-start(f32[1024,512]{1,0:T(8,128)} %fusion.42) | copy-start | bytes 6291460
  158.6 21.1 %collective-permute-start.7 = (bf16[1024,384]{1,0:T(8,128)(2,1)}, bf16[1024,384]{1,0:T(8,128)(2,1)S(1)}, u32[]{:S(2)}, u32[]{:S(2)}) collective-permute-start(bf16[1024,384]{1,0:T(8,128)(2,1)} %collective-permute-done.5), channel_id=1, source_target_pairs={{0,64},{32,96},{64,128},{96,160},{128,192},{160,224},{192,256},{22... | collective-permute-start | bytes 2359304 | tf_op jit(solution)/shard_map/ppermute | solution.py:54
  160.7 20.4 %collective-permute-start.8 = (bf16[1024,384]{1,0:T(8,128)(2,1)}, bf16[1024,384]{1,0:T(8,128)(2,1)S(1)}, u32[]{:S(2)}, u32[]{:S(2)}) collective-permute-start(bf16[1024,384]{1,0:T(8,128)(2,1)} %collective-permute-done.6), channel_id=1, source_target_pairs={{0,448},{32,480},{64,0},{96,32},{128,64},{160,96},{192,128},{224,1... | collective-permute-start | bytes 2359304 | tf_op jit(solution)/shard_map/ppermute | solution.py:54
  182.2 4.1 %copy-start.14 = (bf16[256,384]{1,0:T(8,128)(2,1)S(1)}, bf16[256,384]{1,0:T(8,128)(2,1)}, u32[]{:S(2)}) copy-start(bf16[256,384]{1,0:T(8,128)(2,1)} %get-tuple-element.25) | copy-start | bytes 589828
  182.7 9.3 %copy-start.13 = (bf16[256,384]{1,0:T(8,128)(2,1)S(1)}, bf16[256,384]{1,0:T(8,128)(2,1)}, u32[]{:S(2)}) copy-start(bf16[256,384]{1,0:T(8,128)(2,1)} %get-tuple-element.26) | copy-start | bytes 589828
  184.1 20.8 %copy-start.12 = (bf16[256,384]{1,0:T(8,128)(2,1)S(1)}, bf16[256,384]{1,0:T(8,128)(2,1)}, u32[]{:S(2)}) copy-start(bf16[256,384]{1,0:T(8,128)(2,1)} %get-tuple-element.21) | copy-start | bytes 589828
  184.1 20.8 %collective-permute-start.9 = (bf16[1024,384]{1,0:T(8,128)(2,1)}, bf16[1024,384]{1,0:T(8,128)(2,1)}, u32[]{:S(2)}, u32[]{:S(2)}) collective-permute-start(bf16[1024,384]{1,0:T(8,128)(2,1)} %convolution_convert_fusion.2), channel_id=1, source_target_pairs={{0,64},{32,96},{64,128},{96,160},{128,192},{160,224},{192,256},{22... | collective-permute-start | bytes 2359304 | tf_op jit(solution)/shard_map/ppermute | solution.py:54
  186.7 21.8 %collective-permute-start.12 = (bf16[1024,384]{1,0:T(8,128)(2,1)S(1)}, bf16[1024,384]{1,0:T(8,128)(2,1)S(1)}, u32[]{:S(2)}, u32[]{:S(2)}) collective-permute-start(bf16[1024,384]{1,0:T(8,128)(2,1)S(1)} %convolution_convert_fusion.1), channel_id=1, source_target_pairs={{0,448},{32,480},{64,0},{96,32},{128,64},{160,96},{192,128},{224,1... | collective-permute-start | bytes 2359304 | tf_op jit(solution)/shard_map/ppermute | solution.py:54
  193.4 15.1 %copy-start.9 = (bf16[256,384]{1,0:T(8,128)(2,1)S(1)}, bf16[256,384]{1,0:T(8,128)(2,1)}, u32[]{:S(2)}) copy-start(bf16[256,384]{1,0:T(8,128)(2,1)} %get-tuple-element.24) | copy-start | bytes 589828
  193.4 54.6 %all-to-all-start.5 = ((bf16[32,32,384]{2,1,0:T(8,128)(2,1)}), bf16[32,32,384]{2,1,0:T(8,128)(2,1)S(1)}, u32[]{:S(2)}, u32[]{:S(2)}) async-start(bf16[32,32,384]{2,1,0:T(8,128)(2,1)} %bitcast.35), calls=%async_computation.5 | async-start | bytes 1572864 | tf_op jit(solution)/shard_map/all_to_all | solution.py:66
  201.9 12.3 %copy-start.11 = (bf16[256,384]{1,0:T(8,128)(2,1)S(1)}, bf16[256,384]{1,0:T(8,128)(2,1)}, u32[]{:S(2)}) copy-start(bf16[256,384]{1,0:T(8,128)(2,1)} %get-tuple-element.20) | copy-start | bytes 589828
  206.4 8.1 %copy-start.8 = (bf16[256,384]{1,0:T(8,128)(2,1)S(1)}, bf16[256,384]{1,0:T(8,128)(2,1)}, u32[]{:S(2)}) copy-start(bf16[256,384]{1,0:T(8,128)(2,1)} %get-tuple-element.23) | copy-start | bytes 589828
  206.5 19.9 %collective-permute-start.10 = (bf16[1024,384]{1,0:T(8,128)(2,1)S(1)}, bf16[1024,384]{1,0:T(8,128)(2,1)S(1)}, u32[]{:S(2)}, u32[]{:S(2)}) collective-permute-start(bf16[1024,384]{1,0:T(8,128)(2,1)S(1)} %add_convert_fusion.4), channel_id=1, source_target_pairs={{0,64},{32,96},{64,128},{96,160},{128,192},{160,224},{192,256},{22... | collective-permute-start | bytes 2359304 | tf_op jit(solution)/shard_map/ppermute | solution.py:54
  209.0 19.6 %collective-permute-start.13 = (bf16[1024,384]{1,0:T(8,128)(2,1)S(1)}, bf16[1024,384]{1,0:T(8,128)(2,1)S(1)}, u32[]{:S(2)}, u32[]{:S(2)}) collective-permute-start(bf16[1024,384]{1,0:T(8,128)(2,1)S(1)} %add_convert_fusion.2), channel_id=1, source_target_pairs={{0,448},{32,480},{64,0},{96,32},{128,64},{160,96},{192,128},{224,1... | collective-permute-start | bytes 2359304 | tf_op jit(solution)/shard_map/ppermute | solution.py:54
  226.5 7.4 %copy-start.10 = (bf16[256,384]{1,0:T(8,128)(2,1)S(1)}, bf16[256,384]{1,0:T(8,128)(2,1)}, u32[]{:S(2)}) copy-start(bf16[256,384]{1,0:T(8,128)(2,1)} %get-tuple-element.19) | copy-start | bytes 589828
  226.5 19.0 %collective-permute-start.11 = (bf16[1024,384]{1,0:T(8,128)(2,1)S(1)}, bf16[1024,384]{1,0:T(8,128)(2,1)S(1)}, u32[]{:S(2)}, u32[]{:S(2)}) collective-permute-start(bf16[1024,384]{1,0:T(8,128)(2,1)S(1)} %add_convert_fusion.3), channel_id=1, source_target_pairs={{0,64},{32,96},{64,128},{96,160},{128,192},{160,224},{192,256},{22... | collective-permute-start | bytes 2359304 | tf_op jit(solution)/shard_map/ppermute | solution.py:54
  228.8 18.1 %collective-permute-start.14 = (bf16[1024,384]{1,0:T(8,128)(2,1)S(1)}, bf16[1024,384]{1,0:T(8,128)(2,1)S(1)}, u32[]{:S(2)}, u32[]{:S(2)}) collective-permute-start(bf16[1024,384]{1,0:T(8,128)(2,1)S(1)} %add_convert_fusion.1), channel_id=1, source_target_pairs={{0,448},{32,480},{64,0},{96,32},{128,64},{160,96},{192,128},{224,1... | collective-permute-start | bytes 2359304 | tf_op jit(solution)/shard_map/ppermute | solution.py:54
  234.3 22.1 %copy-start.24 = (s32[128,4]{0,1:T(4,128)S(1)}, s32[128,4]{0,1:T(4,128)}, u32[]{:S(2)}) copy-start(s32[128,4]{0,1:T(4,128)} %param.19) | copy-start | bytes 6148
  234.4 22.1 %copy-start.26 = (f32[128,4]{0,1:T(4,128)S(1)}, f32[128,4]{0,1:T(4,128)}, u32[]{:S(2)}) copy-start(f32[128,4]{0,1:T(4,128)} %param.20) | copy-start | bytes 6148
  248.0 13.7 %copy-start.19 = (f32[8,8,384]{2,1,0:T(8,128)S(1)}, f32[8,8,384]{2,1,0:T(8,128)}, u32[]{:S(2)}) copy-start(f32[8,8,384]{2,1,0:T(8,128)} %get-tuple-element.38) | copy-start | bytes 294916
  248.0 30.8 %all-to-all-start.4 = ((bf16[32,32,384]{2,1,0:T(8,128)(2,1)}), bf16[32,32,384]{2,1,0:T(8,128)(2,1)S(1)}, u32[]{:S(2)}, u32[]{:S(2)}) async-start(bf16[32,32,384]{2,1,0:T(8,128)(2,1)} %bitcast.32), calls=%async_computation.4 | async-start | bytes 1572864 | tf_op jit(solution)/shard_map/all_to_all | solution.py:66
  257.2 22.0 %collective-permute-start.15 = (f32[128,384]{1,0:T(8,128)S(1)}, f32[128,384]{1,0:T(8,128)S(1)}, u32[]{:S(2)}, u32[]{:S(2)}) collective-permute-start(f32[128,384]{1,0:T(8,128)S(1)} %fusion.8), channel_id=1, source_target_pairs={{0,256},{32,288},{64,320},{96,352},{128,384},{160,416},{192,448},{... | collective-permute-start | bytes 589832 | tf_op jit(solution)/shard_map/ppermute | solution.py:54
  (4 other events, 5.1 us)

commit v7 on v6

--- a/solution.py
+++ b/solution.py
@@ -1,6 +1,8 @@
 import jax
 import jax.numpy as jnp
 from jax import lax
+from jax.experimental import pallas as pl
+from jax.experimental.pallas import tpu as pltpu
 from jax.sharding import PartitionSpec as P
 
 HEAD_SIZE = 64
@@ -17,34 +19,65 @@
 LANES = 384
 FF_LANES = 256
 FAR = BLOCKS // 2
+PAIR_TILE = 16
 F32 = jnp.float32
 BF16 = jnp.bfloat16
 
 Z_GROUPS = [[z * HALVES + half for z in range(BLOCKS)] for half in range(HALVES)]
 
 
+def attention_kernel(queries_ref, cache_ref, new_ref, sink_ref, out_ref):
+    queries = queries_ref[...]
+    cache = cache_ref[...]
+    new = new_ref[...].astype(F32)
+    sink = sink_ref[...]
+    scale = HEAD_SIZE ** (-0.5)
+    over_lanes = (((2,), (2,)), ((0,), (0,)))
+    scores = lax.dot_general(queries, cache, over_lanes, preferred_element_type=F32) * scale
+    new_score = jnp.sum(queries.astype(F32) * new, axis=2, keepdims=True) * scale
+    top = jnp.maximum(jnp.maximum(jnp.max(scores, axis=2, keepdims=True), new_score), sink)
+    raised = jnp.exp(scores - top)
+    new_raised = jnp.exp(new_score - top)
+    total = jnp.sum(raised, axis=2, keepdims=True) + new_raised + jnp.exp(sink - top)
+    weights = (raised / total).astype(BF16)
+    new_weight = (new_raised / total).astype(BF16).astype(F32)
+    over_keys = (((2,), (1,)), ((0,), (0,)))
+    combined = lax.dot_general(weights, cache, over_keys, preferred_element_type=F32)
+    out_ref[...] = (combined + new_weight * new).astype(BF16)
+
+
 def attend(queries, window_key_value_cache, new_key_value, head_sink_logits):
-    count_of_rows = queries.shape[0]
-    query_groups = QUERY_HEADS // KEY_VALUE_HEADS
-    grouped_queries = queries.reshape(count_of_rows, KEY_VALUE_HEADS, query_groups, HEAD_SIZE)
-    all_keys = jnp.concatenate(
-        [window_key_value_cache[:, :, :, :HEAD_SIZE], new_key_value[:, :, None, :HEAD_SIZE]], axis=2
+    rows = queries.shape[0]
+    groups = QUERY_HEADS // KEY_VALUE_HEADS
+    pairs = rows * KEY_VALUE_HEADS
+    window, lanes = window_key_value_cache.shape[2:]
+    queries = queries.reshape(pairs, groups, HEAD_SIZE)
+    queries = jnp.pad(queries, ((0, 0), (0, 0), (0, lanes - HEAD_SIZE)))
+    sink = head_sink_logits.reshape(1, KEY_VALUE_HEADS, groups, 1)
+    sink = jnp.broadcast_to(sink, (rows, KEY_VALUE_HEADS, groups, 1)).reshape(pairs, groups, 1)
+
+    def block(*shape):
+        return pl.BlockSpec((PAIR_TILE, *shape), lambda i: (i, 0, 0))
+
+    combined = pl.pallas_call(
+        attention_kernel,
+        grid=(pairs // PAIR_TILE,),
+        in_specs=[block(groups, lanes), block(window, lanes), block(1, lanes), block(groups, 1)],
+        out_specs=block(groups, lanes),
+        out_shape=jax.ShapeDtypeStruct((pairs, groups, lanes), BF16),
+        compiler_params=pltpu.CompilerParams(vmem_limit_bytes=32 * 2**20),
+        cost_estimate=pl.CostEstimate(
+            flops=4 * pairs * groups * window * lanes,
+            bytes_accessed=2 * pairs * window * lanes,
+            transcendentals=pairs * groups * window,
+        ),
+    )(
+        queries,
+        window_key_value_cache.reshape(pairs, window, lanes),
+        new_key_value.reshape(pairs, 1, lanes),
+        sink,
     )
-    all_values = jnp.concatenate(
-        [window_key_value_cache[:, :, :, HEAD_SIZE:], new_key_value[:, :, None, HEAD_SIZE:]], axis=2
-    )
-    scores = jnp.einsum(
-        "rkgd,rkjd->rkgj", grouped_queries, all_keys, preferred_element_type=jnp.float32
-    ) * HEAD_SIZE ** (-0.5)
-    sink_portion = head_sink_logits.reshape(1, KEY_VALUE_HEADS, query_groups, 1)
-    highest = jnp.maximum(jnp.max(scores, axis=3, keepdims=True), sink_portion)
-    raised = jnp.exp(scores - highest)
-    denominator = jnp.sum(raised, axis=3, keepdims=True) + jnp.exp(sink_portion - highest)
-    weights = (raised / denominator).astype(jnp.bfloat16)
-    combined = jnp.einsum(
-        "rkgj,rkjd->rkgd", weights, all_values, preferred_element_type=jnp.float32
-    )
-    return combined.reshape(count_of_rows, QUERY_HEADS * HEAD_SIZE).astype(jnp.bfloat16)
+    return combined[:, :, HEAD_SIZE:].reshape(rows, QUERY_HEADS * HEAD_SIZE)
 
 
 def shift_over_z(array, step):
@@ -147,6 +180,7 @@
         w = w.reshape(BLOCKS, BLOCK, FF_LOCAL)
         return jnp.pad(w, ((0, 0), (0, LANES - BLOCK), (0, FF_LANES - FF_LOCAL)))
 
+    scaled, w_gate, w_up, w_down = lax.optimization_barrier((scaled, w_gate, w_up, w_down))
     w_in = jnp.concatenate([padded_in(w_gate), padded_in(w_up)], axis=2)
     in_row = lax.broadcasted_iota(jnp.int32, w_in.shape, 1)
     in_column = lax.broadcasted_iota(jnp.int32, w_in.shape, 2)

time: 302 us -> 290 us (0.960)
  blocking collectives: 16.8 us -> 37 us
  waiting for transfers between devices: 107 us -> 91.8 us
  starting transfers between devices: 106 us -> 95.4 us
  matrix products: 33.8 us -> 29.7 us
    all_to_all x0 -> x1, blocking collectives: none -> 18.7 us  [over_z(): lax.all_to_all(array, 'attn', 0, 0, tiled=True, axis_index_groups=Z_GROUPS)]
    all_to_all x2 -> x1, starting transfers between devices: 17.4 us -> 3.69 us  [over_z(): lax.all_to_all(array, 'attn', 0, 0, tiled=True, axis_index_groups=Z_GROUPS)]
    ppermute x2, waiting for transfers between devices: 11.8 us -> 3.73 us  [swap_halves(): return lax.ppermute(array, 'attn', [(i, i ^ 1) for i in range(N_ATTN)])]
    ppermute x14, waiting for transfers between devices: 64.4 us -> 58.9 us  [shift_over_z(): return lax.ppermute(array, 'attn', pairs)]
    all_to_all x4, waiting for transfers between devices: 19.2 us -> 15.6 us  [over_experts(): return lax.all_to_all(array, 'exp', 0, 0, tiled=True)]
    optimization_barrier x0 -> x2, local copies, waits for them, and re-layouts: none -> 3.32 us  [local(): lax.optimization_barrier((scaled, w_gate, w_up, w_down))]
    all_to_all x2 -> x1, waiting for transfers between devices: 11.4 us -> 13.6 us  [over_z(): lax.all_to_all(array, 'attn', 0, 0, tiled=True, axis_index_groups=Z_GROUPS)]
    unnamed x70 -> x50, local copies, waits for them, and re-layouts: 7.6 us -> 7.65 us
  transfers between devices with their start and end apart: 22 -> 21, of which waited for: 14 -> 13; matrix products, arithmetic and copies ran while one was open for 16% -> 16% of each run, Pallas kernels for 0% -> 1%
where the time goes in v7:
time: 290 us; the launch traced here: 285 us
  starting transfers between devices  95.4 us (33%)
  waiting for transfers between devices  91.8 us (32%)
  blocking collectives  37 us (13%)
  matrix products  29.7 us (10%)
  local copies, waits for them, and re-layouts  22 us (8%)
  other arithmetic  6.43 us (2%)
    ppermute x14, waiting for transfers between devices, shift_over_z(): return lax.ppermute(array, 'attn', pairs)  58.9 us
    ppermute x14, starting transfers between devices, shift_over_z(): return lax.ppermute(array, 'attn', pairs)  51.1 us
    all_to_all x4, starting transfers between devices, over_experts(): return lax.all_to_all(array, 'exp', 0, 0, tiled=True)  33.9 us
    all_to_all x1, blocking collectives, over_z(): lax.all_to_all(array, 'attn', 0, 0, tiled=True, axis_index_groups=Z_GROUPS)  18.7 us
    all_to_all x1, blocking collectives, local(): lax.all_to_all(mixed.reshape(N_ATTN, own_rows, LANES), 'attn', 0, 0, tile...  18.4 us
    dot_general x8, matrix products, input_term(): return jnp.dot(rows, at_offset(w_in, offset), preferred_element_type=F32)  16.8 us
    all_to_all x4, waiting for transfers between devices, over_experts(): return lax.all_to_all(array, 'exp', 0, 0, tiled=True)  15.6 us
    all_to_all x1, waiting for transfers between devices, over_z(): lax.all_to_all(array, 'attn', 0, 0, tiled=True, axis_index_groups=Z_GROUPS)  13.6 us
  transfers between devices with their start and end apart: 21, of which 13 were waited for; matrix products, arithmetic and copies ran while one was open for 16% of the time, Pallas kernels for 1%

profile of v7, /device:TPU:6, one launch (start us, length us, event | category | flops | bytes accessed | tf_op | source)
XLA Modules:
  0.0 284.9 jit_solution(7262926692249842599)
XLA Ops:
  0.0 3.4 %collective-permute-start = (bf16[128,2880]{0,1:T(8,128)(2,1)}, bf16[128,2880]{0,1:T(8,128)(2,1)S(1)}, u32[]{:S(2)}, u32[]{:S(2)}) collective-permute-start(bf16[128,2880]{0,1:T(8,128)(2,1)} %param.17), channel_id=1, source_target_pairs={{0,32},{32,0},{64,96},{96,64},{128,160},{160,128},{192,224},{224,1... | collective-permute-start | bytes 2211848 | tf_op jit(solution)/shard_map/ppermute | solution.py:91
  7.3 1.7 shard_map.118
  9.5 18.7 %all_to_all.35 = bf16[8,8,640]{2,1,0:T(8,128)(2,1)S(1)} all-to-all(bf16[8,8,640]{2,1,0:T(8,128)(2,1)S(1)} %copy.72), channel_id=1, replica_groups={{0,64,128,192,256,320,384,448},{32,96,160,224,288,352,416,480},{1,65,12..., dimensions={0} | all-to-all | bytes 163840 | tf_op jit(solution)/shard_map/all_to_all | solution.py:95
  30.4 3.7 %all-to-all-start.1 = ((bf16[8,64,384]{2,1,0:T(8,128)(2,1)}), bf16[8,64,384]{2,1,0:T(8,128)(2,1)S(1)}, u32[]{:S(2)}, u32[]{:S(2)}) async-start(bf16[8,64,384]{2,1,0:T(8,128)(2,1)} %pad_bitcast_fusion.1), calls=%async_computation.1 | async-start | bytes 786432 | tf_op jit(solution)/shard_map/all_to_all | solution.py:95
  34.2 13.6 %all-to-all-done.1 = bf16[8,64,384]{2,1,0:T(8,128)(2,1)S(1)} async-done(((bf16[8,64,384]{2,1,0:T(8,128)(2,1)}), bf16[8,64,384]{2,1,0:T(8,128)(2,1)S(1)}, u32[]{:S(2)}, u32[]{:S(2)}) %all-to-all-start.1) | async-done | bytes 393248 | tf_op jit(solution)/shard_map/all_to_all | solution.py:95
  48.8 3.3 %collective-permute-start.1 = (bf16[64,384]{1,0:T(8,128)(2,1)S(1)}, bf16[64,384]{1,0:T(8,128)(2,1)S(1)}, u32[]{:S(2)}, u32[]{:S(2)}) collective-permute-start(bf16[64,384]{1,0:T(8,128)(2,1)S(1)} %select_convert_fusion), channel_id=1, source_target_pairs={{0,32},{32,0},{64,96},{96,64},{128,160},{160,128},{192,224},{224,1... | collective-permute-start | bytes 147464 | tf_op jit(solution)/shard_map/ppermute | solution.py:91
  52.6 3.7 %collective-permute-done.1 = bf16[64,384]{1,0:T(8,128)(2,1)S(1)} collective-permute-done((bf16[64,384]{1,0:T(8,128)(2,1)S(1)}, bf16[64,384]{1,0:T(8,128)(2,1)S(1)}, u32[]{:S(2)}, u32[]{:S(2)}) %collective-permute-start.1) | collective-permute-done | bytes 49184 | tf_op jit(solution)/shard_map/ppermute | solution.py:91
  57.0 2.1 convolution_convert_fusion.4
  59.1 8.9 %all-to-all-start.2 = ((bf16[32,32,384]{2,1,0:T(8,128)(2,1)}), bf16[32,32,384]{2,1,0:T(8,128)(2,1)}, u32[]{:S(2)}, u32[]{:S(2)}) async-start(bf16[32,32,384]{2,1,0:T(8,128)(2,1)} %bitcast.16), calls=%async_computation.2 | async-start | bytes 1572864 | tf_op jit(solution)/shard_map/all_to_all | solution.py:99
  68.1 2.6 collective-permute-start.2
  70.7 1.7 copy.76
  72.4 1.7 copy.77
  74.0 1.5 reshape_squeeze.3
  76.9 2.1 and_select_fusion
  79.0 4.0 %pad_dynamic-slice_fusion = (bf16[1,256,384]{2,0,1:T(2,128)(2,1)S(1)}, bf16[1,256,384]{2,0,1:T(2,128)(2,1)S(1)}, bf16[1,256,384]{2,0,1:T(2,128)(2,1)S(1)}, bf16[...) fusion(s32[]{:T(128)S(6)} %select_n.145, ...), kind=kLoop, calls=%fused_computation.10 | loop fusion | bytes 2678816 | tf_op jit(solution)/shard_map/jit(dynamic_index_in_dim)/dynamic_slice | solution.py:192
  88.0 2.1 convolution_convert_fusion.3
  90.4 8.1 %all-to-all-start.3 = ((bf16[32,32,384]{2,1,0:T(8,128)(2,1)}), bf16[32,32,384]{2,1,0:T(8,128)(2,1)}, u32[]{:S(2)}, u32[]{:S(2)}) async-start(bf16[32,32,384]{2,1,0:T(8,128)(2,1)} %bitcast.155), calls=%async_computation.3 | async-start | bytes 1572864 | tf_op jit(solution)/shard_map/all_to_all | solution.py:99
  98.5 3.2 %collective-permute-start.3 = (bf16[1024,384]{1,0:T(8,128)(2,1)}, bf16[1024,384]{1,0:T(8,128)(2,1)}, u32[]{:S(2)}, u32[]{:S(2)}) collective-permute-start(bf16[1024,384]{1,0:T(8,128)(2,1)} %bitcast.17), channel_id=1, source_target_pairs={{0,64},{32,96},{64,128},{96,160},{128,192},{160,224},{192,256},{22... | collective-permute-start | bytes 2359304 | tf_op jit(solution)/shard_map/ppermute | solution.py:87
  101.7 3.9 %collective-permute-start.4 = (bf16[1024,384]{1,0:T(8,128)(2,1)}, bf16[1024,384]{1,0:T(8,128)(2,1)}, u32[]{:S(2)}, u32[]{:S(2)}) collective-permute-start(bf16[1024,384]{1,0:T(8,128)(2,1)} %bitcast.17), channel_id=1, source_target_pairs={{0,448},{32,480},{64,0},{96,32},{128,64},{160,96},{192,128},{224,1... | collective-permute-start | bytes 2359304 | tf_op jit(solution)/shard_map/ppermute | solution.py:87
  105.6 3.2 %fusion.35 = f32[1024,512]{1,0:T(8,128)} fusion(bf16[1024,384]{1,0:T(8,128)(2,1)} %bitcast.17, bf16[8,384,512]{2,1,0:T(8,128)(2,1)S(1)} %and_select_fusion, s32[]{:T(128)S(6)} %select_n.138), kind=kOutput, calls=%fused_computation.69 | convolution fusion | flops 402653184 | bytes 3276804 | tf_op jit(solution)/shard_map/dot_general | solution.py:195
  108.8 12.7 %collective-permute-done.3 = bf16[1024,384]{1,0:T(8,128)(2,1)} collective-permute-done((bf16[1024,384]{1,0:T(8,128)(2,1)}, bf16[1024,384]{1,0:T(8,128)(2,1)}, u32[]{:S(2)}, u32[]{:S(2)}) %collective-permute-start.3) | collective-permute-done | bytes 786464 | tf_op jit(solution)/shard_map/ppermute | solution.py:87
  121.5 2.0 collective-permute-start.5
  123.5 5.2 %collective-permute-start.6 = (bf16[1024,384]{1,0:T(8,128)(2,1)}, bf16[1024,384]{1,0:T(8,128)(2,1)}, u32[]{:S(2)}, u32[]{:S(2)}) collective-permute-start(bf16[1024,384]{1,0:T(8,128)(2,1)} %collective-permute-done.4), channel_id=1, source_target_pairs={{0,448},{32,480},{64,0},{96,32},{128,64},{160,96},{192,128},{224,1... | collective-permute-start | bytes 2359304 | tf_op jit(solution)/shard_map/ppermute | solution.py:87
  128.8 3.2 %fusion.33 = f32[1024,512]{1,0:T(8,128)} fusion(bf16[1024,384]{1,0:T(8,128)(2,1)} %collective-permute-done.3, bf16[8,384,512]{2,1,0:T(8,128)(2,1)S(1)} %and_select_fusion, s32[]{:T(128)S(6)} %select_n.145), kind=kOutput, calls=%fused_computation.67 | convolution fusion | flops 402653184 | bytes 3276804 | tf_op jit(solution)/shard_map/dot_general | solution.py:195
  132.0 3.2 %fusion.31 = f32[1024,512]{1,0:T(8,128)} fusion(bf16[1024,384]{1,0:T(8,128)(2,1)} %collective-permute-done.4, bf16[8,384,512]{2,1,0:T(8,128)(2,1)S(1)} %and_select_fusion, s32[]{:T(128)S(6)} %select_n.139), kind=kOutput, calls=%fused_computation.65 | convolution fusion | flops 402653184 | bytes 3276804 | tf_op jit(solution)/shard_map/dot_general | solution.py:195
  135.2 2.0 fusion.17
  137.2 6.5 %collective-permute-done.5 = bf16[1024,384]{1,0:T(8,128)(2,1)} collective-permute-done((bf16[1024,384]{1,0:T(8,128)(2,1)}, bf16[1024,384]{1,0:T(8,128)(2,1)}, u32[]{:S(2)}, u32[]{:S(2)}) %collective-permute-start.5) | collective-permute-done | bytes 786464 | tf_op jit(solution)/shard_map/ppermute | solution.py:87
  143.7 1.9 collective-permute-start.7
  145.7 5.1 %collective-permute-start.8 = (bf16[1024,384]{1,0:T(8,128)(2,1)}, bf16[1024,384]{1,0:T(8,128)(2,1)S(1)}, u32[]{:S(2)}, u32[]{:S(2)}) collective-permute-start(bf16[1024,384]{1,0:T(8,128)(2,1)} %collective-permute-done.6), channel_id=1, source_target_pairs={{0,448},{32,480},{64,0},{96,32},{128,64},{160,96},{192,128},{224,1... | collective-permute-start | bytes 2359304 | tf_op jit(solution)/shard_map/ppermute | solution.py:87
  150.8 1.8 fusion.29
  152.7 1.9 add_add_fusion.1
  154.6 10.3 %collective-permute-done.7 = bf16[1024,384]{1,0:T(8,128)(2,1)S(1)} collective-permute-done((bf16[1024,384]{1,0:T(8,128)(2,1)}, bf16[1024,384]{1,0:T(8,128)(2,1)S(1)}, u32[]{:S(2)}, u32[]{:S(2)}) %collective-permute-start.7) | collective-permute-done | bytes 786464 | tf_op jit(solution)/shard_map/ppermute | solution.py:87
  169.2 3.6 %collective-permute-start.9 = (bf16[1024,384]{1,0:T(8,128)(2,1)}, bf16[1024,384]{1,0:T(8,128)(2,1)}, u32[]{:S(2)}, u32[]{:S(2)}) collective-permute-start(bf16[1024,384]{1,0:T(8,128)(2,1)} %convolution_convert_fusion.2), channel_id=1, source_target_pairs={{0,64},{32,96},{64,128},{96,160},{128,192},{160,224},{192,256},{22... | collective-permute-start | bytes 2359304 | tf_op jit(solution)/shard_map/ppermute | solution.py:87
  173.2 4.0 %collective-permute-start.12 = (bf16[1024,384]{1,0:T(8,128)(2,1)S(1)}, bf16[1024,384]{1,0:T(8,128)(2,1)S(1)}, u32[]{:S(2)}, u32[]{:S(2)}) collective-permute-start(bf16[1024,384]{1,0:T(8,128)(2,1)S(1)} %convolution_convert_fusion.1), channel_id=1, source_target_pairs={{0,448},{32,480},{64,0},{96,32},{128,64},{160,96},{192,128},{224,1... | collective-permute-start | bytes 2359304 | tf_op jit(solution)/shard_map/ppermute | solution.py:87
  178.5 8.4 %all-to-all-start.5 = ((bf16[32,32,384]{2,1,0:T(8,128)(2,1)}), bf16[32,32,384]{2,1,0:T(8,128)(2,1)S(1)}, u32[]{:S(2)}, u32[]{:S(2)}) async-start(bf16[32,32,384]{2,1,0:T(8,128)(2,1)} %bitcast.34), calls=%async_computation.5 | async-start | bytes 1572864 | tf_op jit(solution)/shard_map/all_to_all | solution.py:99
  186.9 3.0 %collective-permute-done.9 = bf16[1024,384]{1,0:T(8,128)(2,1)} collective-permute-done((bf16[1024,384]{1,0:T(8,128)(2,1)}, bf16[1024,384]{1,0:T(8,128)(2,1)}, u32[]{:S(2)}, u32[]{:S(2)}) %collective-permute-start.9) | collective-permute-done | bytes 786464 | tf_op jit(solution)/shard_map/ppermute | solution.py:87
  190.0 1.6 add_convert_fusion.4
  191.6 2.5 collective-permute-start.10
  194.5 4.7 %collective-permute-start.13 = (bf16[1024,384]{1,0:T(8,128)(2,1)S(1)}, bf16[1024,384]{1,0:T(8,128)(2,1)S(1)}, u32[]{:S(2)}, u32[]{:S(2)}) collective-permute-start(bf16[1024,384]{1,0:T(8,128)(2,1)S(1)} %add_convert_fusion.2), channel_id=1, source_target_pairs={{0,448},{32,480},{64,0},{96,32},{128,64},{160,96},{192,128},{224,1... | collective-permute-start | bytes 2359304 | tf_op jit(solution)/shard_map/ppermute | solution.py:87
  200.1 11.3 %collective-permute-done.10 = bf16[1024,384]{1,0:T(8,128)(2,1)S(1)} collective-permute-done((bf16[1024,384]{1,0:T(8,128)(2,1)S(1)}, bf16[1024,384]{1,0:T(8,128)(2,1)S(1)}, u32[]{:S(2)}, u32[]{:S(2)}) %collective-permute-start.10) | collective-permute-done | bytes 786464 | tf_op jit(solution)/shard_map/ppermute | solution.py:87
  211.6 2.1 collective-permute-start.11
  214.6 4.3 %collective-permute-start.14 = (bf16[1024,384]{1,0:T(8,128)(2,1)S(1)}, bf16[1024,384]{1,0:T(8,128)(2,1)S(1)}, u32[]{:S(2)}, u32[]{:S(2)}) collective-permute-start(bf16[1024,384]{1,0:T(8,128)(2,1)S(1)} %add_convert_fusion.1), channel_id=1, source_target_pairs={{0,448},{32,480},{64,0},{96,32},{128,64},{160,96},{192,128},{224,1... | collective-permute-start | bytes 2359304 | tf_op jit(solution)/shard_map/ppermute | solution.py:87
  219.3 11.1 %collective-permute-done.11 = bf16[1024,384]{1,0:T(8,128)(2,1)S(1)} collective-permute-done((bf16[1024,384]{1,0:T(8,128)(2,1)S(1)}, bf16[1024,384]{1,0:T(8,128)(2,1)S(1)}, u32[]{:S(2)}, u32[]{:S(2)}) %collective-permute-start.11) | collective-permute-done | bytes 786464 | tf_op jit(solution)/shard_map/ppermute | solution.py:87
  230.4 2.5 collective-permute-done.14
  234.2 8.4 %all-to-all-start.4 = ((bf16[32,32,384]{2,1,0:T(8,128)(2,1)}), bf16[32,32,384]{2,1,0:T(8,128)(2,1)S(1)}, u32[]{:S(2)}, u32[]{:S(2)}) async-start(bf16[32,32,384]{2,1,0:T(8,128)(2,1)} %bitcast.31), calls=%async_computation.4 | async-start | bytes 1572864 | tf_op jit(solution)/shard_map/all_to_all | solution.py:99
  243.3 6.1 %collective-permute-start.15 = (f32[128,384]{1,0:T(8,128)S(1)}, f32[128,384]{1,0:T(8,128)S(1)}, u32[]{:S(2)}, u32[]{:S(2)}) collective-permute-start(f32[128,384]{1,0:T(8,128)S(1)} %fusion.7), channel_id=1, source_target_pairs={{0,256},{32,288},{64,320},{96,352},{128,384},{160,416},{192,448},{... | collective-permute-start | bytes 589832 | tf_op jit(solution)/shard_map/ppermute | solution.py:87
  249.7 15.3 %all-to-all-done.4 = bf16[32,32,384]{2,1,0:T(8,128)(2,1)S(1)} async-done(((bf16[32,32,384]{2,1,0:T(8,128)(2,1)}), bf16[32,32,384]{2,1,0:T(8,128)(2,1)S(1)}, u32[]{:S(2)}, u32[]{:S(2)}) %all-to-all-start.4) | async-done | bytes 786464 | tf_op jit(solution)/shard_map/all_to_all | solution.py:99
  265.7 18.4 %all_to_all.36 = f32[16,8,384]{2,1,0:T(8,128)S(1)} all-to-all(f32[16,8,384]{2,1,0:T(8,128)S(1)} %fusion.8), channel_id=1, replica_groups=mesh['attn'=16,'exp'=32] {'attn'}, dimensions={0} | all-to-all | bytes 393216 | tf_op jit(solution)/shard_map/all_to_all | solution.py:232
  (123 shorter events, 27.7 us)
Async XLA Ops:
  0.0 9.3 %copy-start.17 = (bf16[8,2880]{1,0:T(8,128)(2,1)S(1)}, bf16[8,2880]{1,0:T(8,128)(2,1)}, u32[]{:S(2)}) copy-start(bf16[8,2880]{1,0:T(8,128)(2,1)} %param.12) | copy-start | bytes 138244
  0.0 28.6 %collective-permute-start = (bf16[128,2880]{0,1:T(8,128)(2,1)}, bf16[128,2880]{0,1:T(8,128)(2,1)S(1)}, u32[]{:S(2)}, u32[]{:S(2)}) collective-permute-start(bf16[128,2880]{0,1:T(8,128)(2,1)} %param.17), channel_id=1, source_target_pairs={{0,32},{32,0},{64,96},{96,64},{128,160},{160,128},{192,224},{224,1... | collective-permute-start | bytes 2211848 | tf_op jit(solution)/shard_map/ppermute | solution.py:91
  6.1 1.2 copy-start
  7.3 20.8 %copy-start.15 = (bf16[128,2880]{0,1:T(8,128)(2,1)S(1)}, bf16[128,2880]{0,1:T(8,128)(2,1)}, u32[]{:S(2)}) copy-start(bf16[128,2880]{0,1:T(8,128)(2,1)} %param.17) | copy-start | bytes 2211844
  28.5 5.5 %copy-start.18 = (f32[2880]{0:T(1024)S(1)}, f32[2880]{0:T(1024)}, u32[]{:S(2)}) copy-start(f32[2880]{0:T(1024)} %param.18) | copy-start | bytes 34564
  28.6 5.6 %copy-start.19 = (s32[128,4]{0,1:T(4,128)S(1)}, s32[128,4]{0,1:T(4,128)}, u32[]{:S(2)}) copy-start(s32[128,4]{0,1:T(4,128)} %param.19) | copy-start | bytes 6148
  30.4 17.5 %all-to-all-start.1 = ((bf16[8,64,384]{2,1,0:T(8,128)(2,1)}), bf16[8,64,384]{2,1,0:T(8,128)(2,1)S(1)}, u32[]{:S(2)}, u32[]{:S(2)}) async-start(bf16[8,64,384]{2,1,0:T(8,128)(2,1)} %pad_bitcast_fusion.1), calls=%async_computation.1 | async-start | bytes 786432 | tf_op jit(solution)/shard_map/all_to_all | solution.py:95
  34.2 36.5 %copy-start.5 = (bf16[1,2880,180]{1,2,0:T(8,128)(2,1)S(1)}, bf16[1,2880,180]{1,2,0:T(8,128)(2,1)}, u32[]{:S(2)}) copy-start(bf16[1,2880,180]{1,2,0:T(8,128)(2,1)} %param.21) | copy-start | bytes 3110404
  48.8 7.5 %collective-permute-start.1 = (bf16[64,384]{1,0:T(8,128)(2,1)S(1)}, bf16[64,384]{1,0:T(8,128)(2,1)S(1)}, u32[]{:S(2)}, u32[]{:S(2)}) collective-permute-start(bf16[64,384]{1,0:T(8,128)(2,1)S(1)} %select_convert_fusion), channel_id=1, source_target_pairs={{0,32},{32,0},{64,96},{96,64},{128,160},{160,128},{192,224},{224,1... | collective-permute-start | bytes 147464 | tf_op jit(solution)/shard_map/ppermute | solution.py:91
  59.1 13.2 %copy-start.6 = (bf16[1,2880,180]{1,2,0:T(8,128)(2,1)S(1)}, bf16[1,2880,180]{1,2,0:T(8,128)(2,1)}, u32[]{:S(2)}) copy-start(bf16[1,2880,180]{1,2,0:T(8,128)(2,1)} %param.22) | copy-start | bytes 3110404
  59.1 31.3 %all-to-all-start.2 = ((bf16[32,32,384]{2,1,0:T(8,128)(2,1)}), bf16[32,32,384]{2,1,0:T(8,128)(2,1)}, u32[]{:S(2)}, u32[]{:S(2)}) async-start(bf16[32,32,384]{2,1,0:T(8,128)(2,1)} %bitcast.16), calls=%async_computation.2 | async-start | bytes 1572864 | tf_op jit(solution)/shard_map/all_to_all | solution.py:99
  68.1 6.0 %copy-start.7 = (bf16[1,180,2880]{2,1,0:T(8,128)(2,1)S(1)}, bf16[1,180,2880]{2,1,0:T(8,128)(2,1)}, u32[]{:S(2)}) copy-start(bf16[1,180,2880]{2,1,0:T(8,128)(2,1)} %param.23) | copy-start | bytes 3110404
  68.1 19.9 %collective-permute-start.2 = (bf16[128,384]{1,0:T(8,128)(2,1)}, bf16[128,384]{1,0:T(8,128)(2,1)}, u32[]{:S(2)}, u32[]{:S(2)}) collective-permute-start(bf16[128,384]{1,0:T(8,128)(2,1)} %bitcast.15), channel_id=1, source_target_pairs={{0,256},{32,288},{64,320},{96,352},{128,384},{160,416},{192,448},{... | collective-permute-start | bytes 294920 | tf_op jit(solution)/shard_map/ppermute | solution.py:87
  75.5 1.4 copy-start.4
  90.4 44.7 %all-to-all-start.3 = ((bf16[32,32,384]{2,1,0:T(8,128)(2,1)}), bf16[32,32,384]{2,1,0:T(8,128)(2,1)}, u32[]{:S(2)}, u32[]{:S(2)}) async-start(bf16[32,32,384]{2,1,0:T(8,128)(2,1)} %bitcast.155), calls=%async_computation.3 | async-start | bytes 1572864 | tf_op jit(solution)/shard_map/all_to_all | solution.py:99
  98.5 23.0 %collective-permute-start.3 = (bf16[1024,384]{1,0:T(8,128)(2,1)}, bf16[1024,384]{1,0:T(8,128)(2,1)}, u32[]{:S(2)}, u32[]{:S(2)}) collective-permute-start(bf16[1024,384]{1,0:T(8,128)(2,1)} %bitcast.17), channel_id=1, source_target_pairs={{0,64},{32,96},{64,128},{96,160},{128,192},{160,224},{192,256},{22... | collective-permute-start | bytes 2359304 | tf_op jit(solution)/shard_map/ppermute | solution.py:87
  101.7 21.8 %collective-permute-start.4 = (bf16[1024,384]{1,0:T(8,128)(2,1)}, bf16[1024,384]{1,0:T(8,128)(2,1)}, u32[]{:S(2)}, u32[]{:S(2)}) collective-permute-start(bf16[1024,384]{1,0:T(8,128)(2,1)} %bitcast.17), channel_id=1, source_target_pairs={{0,448},{32,480},{64,0},{96,32},{128,64},{160,96},{192,128},{224,1... | collective-permute-start | bytes 2359304 | tf_op jit(solution)/shard_map/ppermute | solution.py:87
  121.5 22.2 %collective-permute-start.5 = (bf16[1024,384]{1,0:T(8,128)(2,1)}, bf16[1024,384]{1,0:T(8,128)(2,1)}, u32[]{:S(2)}, u32[]{:S(2)}) collective-permute-start(bf16[1024,384]{1,0:T(8,128)(2,1)} %collective-permute-done.3), channel_id=1, source_target_pairs={{0,64},{32,96},{64,128},{96,160},{128,192},{160,224},{192,256},{22... | collective-permute-start | bytes 2359304 | tf_op jit(solution)/shard_map/ppermute | solution.py:87
  123.5 22.1 %collective-permute-start.6 = (bf16[1024,384]{1,0:T(8,128)(2,1)}, bf16[1024,384]{1,0:T(8,128)(2,1)}, u32[]{:S(2)}, u32[]{:S(2)}) collective-permute-start(bf16[1024,384]{1,0:T(8,128)(2,1)} %collective-permute-done.4), channel_id=1, source_target_pairs={{0,448},{32,480},{64,0},{96,32},{128,64},{160,96},{192,128},{224,1... | collective-permute-start | bytes 2359304 | tf_op jit(solution)/shard_map/ppermute | solution.py:87
  135.2 17.5 %copy-start.2 = (f32[1024,512]{1,0:T(8,128)S(1)}, f32[1024,512]{1,0:T(8,128)}, u32[]{:S(2)}) copy-start(f32[1024,512]{1,0:T(8,128)} %fusion.33) | copy-start | bytes 6291460
  135.2 17.5 %copy-start.3 = (f32[1024,512]{1,0:T(8,128)S(1)}, f32[1024,512]{1,0:T(8,128)}, u32[]{:S(2)}) copy-start(f32[1024,512]{1,0:T(8,128)} %fusion.31) | copy-start | bytes 6291460
  137.2 15.5 %copy-start.1 = (f32[1024,512]{1,0:T(8,128)S(1)}, f32[1024,512]{1,0:T(8,128)}, u32[]{:S(2)}) copy-start(f32[1024,512]{1,0:T(8,128)} %fusion.35) | copy-start | bytes 6291460
  143.7 21.1 %collective-permute-start.7 = (bf16[1024,384]{1,0:T(8,128)(2,1)}, bf16[1024,384]{1,0:T(8,128)(2,1)S(1)}, u32[]{:S(2)}, u32[]{:S(2)}) collective-permute-start(bf16[1024,384]{1,0:T(8,128)(2,1)} %collective-permute-done.5), channel_id=1, source_target_pairs={{0,64},{32,96},{64,128},{96,160},{128,192},{160,224},{192,256},{22... | collective-permute-start | bytes 2359304 | tf_op jit(solution)/shard_map/ppermute | solution.py:87
  145.7 20.5 %collective-permute-start.8 = (bf16[1024,384]{1,0:T(8,128)(2,1)}, bf16[1024,384]{1,0:T(8,128)(2,1)S(1)}, u32[]{:S(2)}, u32[]{:S(2)}) collective-permute-start(bf16[1024,384]{1,0:T(8,128)(2,1)} %collective-permute-done.6), channel_id=1, source_target_pairs={{0,448},{32,480},{64,0},{96,32},{128,64},{160,96},{192,128},{224,1... | collective-permute-start | bytes 2359304 | tf_op jit(solution)/shard_map/ppermute | solution.py:87
  166.9 0.9 copy-start.14
  167.3 5.5 %copy-start.13 = (bf16[1,256,384]{2,1,0:T(8,128)(2,1)S(1)}, bf16[1,256,384]{2,1,0:T(8,128)(2,1)}, u32[]{:S(2)}) copy-start(bf16[1,256,384]{2,1,0:T(8,128)(2,1)} %copy.109) | copy-start | bytes 589828
  167.8 9.3 %copy-start.12 = (bf16[1,256,384]{2,1,0:T(8,128)(2,1)S(1)}, bf16[1,256,384]{2,1,0:T(8,128)(2,1)}, u32[]{:S(2)}) copy-start(bf16[1,256,384]{2,1,0:T(8,128)(2,1)} %copy.110) | copy-start | bytes 589828
  169.2 20.8 %copy-start.11 = (bf16[1,256,384]{2,1,0:T(8,128)(2,1)S(1)}, bf16[1,256,384]{2,1,0:T(8,128)(2,1)}, u32[]{:S(2)}) copy-start(bf16[1,256,384]{2,1,0:T(8,128)(2,1)} %copy.112) | copy-start | bytes 589828
  169.2 20.8 %collective-permute-start.9 = (bf16[1024,384]{1,0:T(8,128)(2,1)}, bf16[1024,384]{1,0:T(8,128)(2,1)}, u32[]{:S(2)}, u32[]{:S(2)}) collective-permute-start(bf16[1024,384]{1,0:T(8,128)(2,1)} %convolution_convert_fusion.2), channel_id=1, source_target_pairs={{0,64},{32,96},{64,128},{96,160},{128,192},{160,224},{192,256},{22... | collective-permute-start | bytes 2359304 | tf_op jit(solution)/shard_map/ppermute | solution.py:87
  173.2 20.9 %collective-permute-start.12 = (bf16[1024,384]{1,0:T(8,128)(2,1)S(1)}, bf16[1024,384]{1,0:T(8,128)(2,1)S(1)}, u32[]{:S(2)}, u32[]{:S(2)}) collective-permute-start(bf16[1024,384]{1,0:T(8,128)(2,1)S(1)} %convolution_convert_fusion.1), channel_id=1, source_target_pairs={{0,448},{32,480},{64,0},{96,32},{128,64},{160,96},{192,128},{224,1... | collective-permute-start | bytes 2359304 | tf_op jit(solution)/shard_map/ppermute | solution.py:87
  178.5 15.6 %copy-start.9 = (bf16[1,256,384]{2,1,0:T(8,128)(2,1)S(1)}, bf16[1,256,384]{2,1,0:T(8,128)(2,1)}, u32[]{:S(2)}) copy-start(bf16[1,256,384]{2,1,0:T(8,128)(2,1)} %copy.108) | copy-start | bytes 589828
  178.5 55.7 %all-to-all-start.5 = ((bf16[32,32,384]{2,1,0:T(8,128)(2,1)}), bf16[32,32,384]{2,1,0:T(8,128)(2,1)S(1)}, u32[]{:S(2)}, u32[]{:S(2)}) async-start(bf16[32,32,384]{2,1,0:T(8,128)(2,1)} %bitcast.34), calls=%async_computation.5 | async-start | bytes 1572864 | tf_op jit(solution)/shard_map/all_to_all | solution.py:99
  186.9 12.3 %copy-start.10 = (bf16[1,256,384]{2,1,0:T(8,128)(2,1)S(1)}, bf16[1,256,384]{2,1,0:T(8,128)(2,1)}, u32[]{:S(2)}) copy-start(bf16[1,256,384]{2,1,0:T(8,128)(2,1)} %copy.113) | copy-start | bytes 589828
  191.5 8.1 %copy-start.8 = (bf16[1,256,384]{2,1,0:T(8,128)(2,1)S(1)}, bf16[1,256,384]{2,1,0:T(8,128)(2,1)}, u32[]{:S(2)}) copy-start(bf16[1,256,384]{2,1,0:T(8,128)(2,1)} %copy.107) | copy-start | bytes 589828
  191.6 19.9 %collective-permute-start.10 = (bf16[1024,384]{1,0:T(8,128)(2,1)S(1)}, bf16[1024,384]{1,0:T(8,128)(2,1)S(1)}, u32[]{:S(2)}, u32[]{:S(2)}) collective-permute-start(bf16[1024,384]{1,0:T(8,128)(2,1)S(1)} %add_convert_fusion.4), channel_id=1, source_target_pairs={{0,64},{32,96},{64,128},{96,160},{128,192},{160,224},{192,256},{22... | collective-permute-start | bytes 2359304 | tf_op jit(solution)/shard_map/ppermute | solution.py:87
  194.5 19.9 %collective-permute-start.13 = (bf16[1024,384]{1,0:T(8,128)(2,1)S(1)}, bf16[1024,384]{1,0:T(8,128)(2,1)S(1)}, u32[]{:S(2)}, u32[]{:S(2)}) collective-permute-start(bf16[1024,384]{1,0:T(8,128)(2,1)S(1)} %add_convert_fusion.2), channel_id=1, source_target_pairs={{0,448},{32,480},{64,0},{96,32},{128,64},{160,96},{192,128},{224,1... | collective-permute-start | bytes 2359304 | tf_op jit(solution)/shard_map/ppermute | solution.py:87
  211.6 18.8 %collective-permute-start.11 = (bf16[1024,384]{1,0:T(8,128)(2,1)S(1)}, bf16[1024,384]{1,0:T(8,128)(2,1)S(1)}, u32[]{:S(2)}, u32[]{:S(2)}) collective-permute-start(bf16[1024,384]{1,0:T(8,128)(2,1)S(1)} %add_convert_fusion.3), channel_id=1, source_target_pairs={{0,64},{32,96},{64,128},{96,160},{128,192},{160,224},{192,256},{22... | collective-permute-start | bytes 2359304 | tf_op jit(solution)/shard_map/ppermute | solution.py:87
  214.6 18.3 %collective-permute-start.14 = (bf16[1024,384]{1,0:T(8,128)(2,1)S(1)}, bf16[1024,384]{1,0:T(8,128)(2,1)S(1)}, u32[]{:S(2)}, u32[]{:S(2)}) collective-permute-start(bf16[1024,384]{1,0:T(8,128)(2,1)S(1)} %add_convert_fusion.1), channel_id=1, source_target_pairs={{0,448},{32,480},{64,0},{96,32},{128,64},{160,96},{192,128},{224,1... | collective-permute-start | bytes 2359304 | tf_op jit(solution)/shard_map/ppermute | solution.py:87
  219.3 23.3 %copy-start.20 = (f32[128,4]{0,1:T(4,128)S(1)}, f32[128,4]{0,1:T(4,128)}, u32[]{:S(2)}) copy-start(f32[128,4]{0,1:T(4,128)} %param.20) | copy-start | bytes 6148
  234.2 15.4 %copy-start.16 = (f32[8,8,384]{2,1,0:T(8,128)S(1)}, f32[8,8,384]{2,1,0:T(8,128)}, u32[]{:S(2)}) copy-start(f32[8,8,384]{2,1,0:T(8,128)} %get-tuple-element.44) | copy-start | bytes 294916
  234.2 30.8 %all-to-all-start.4 = ((bf16[32,32,384]{2,1,0:T(8,128)(2,1)}), bf16[32,32,384]{2,1,0:T(8,128)(2,1)S(1)}, u32[]{:S(2)}, u32[]{:S(2)}) async-start(bf16[32,32,384]{2,1,0:T(8,128)(2,1)} %bitcast.31), calls=%async_computation.4 | async-start | bytes 1572864 | tf_op jit(solution)/shard_map/all_to_all | solution.py:99
  243.3 22.0 %collective-permute-start.15 = (f32[128,384]{1,0:T(8,128)S(1)}, f32[128,384]{1,0:T(8,128)S(1)}, u32[]{:S(2)}, u32[]{:S(2)}) collective-permute-start(f32[128,384]{1,0:T(8,128)S(1)} %fusion.7), channel_id=1, source_target_pairs={{0,256},{32,288},{64,320},{96,352},{128,384},{160,416},{192,448},{... | collective-permute-start | bytes 589832 | tf_op jit(solution)/shard_map/ppermute | solution.py:87

commit v8 on v7

--- a/solution.py
+++ b/solution.py
@@ -180,26 +180,23 @@
         w = w.reshape(BLOCKS, BLOCK, FF_LOCAL)
         return jnp.pad(w, ((0, 0), (0, LANES - BLOCK), (0, FF_LANES - FF_LOCAL)))
 
-    scaled, w_gate, w_up, w_down = lax.optimization_barrier((scaled, w_gate, w_up, w_down))
+    def at_offset(blocks, offset):
+        index = lax.bitwise_and(z_index + offset % BLOCKS, BLOCKS - 1)
+        return lax.dynamic_index_in_dim(blocks, index, 0, keepdims=False)
+
+    def input_term(rows, offset):
+        return jnp.dot(rows, at_offset(w_in, offset), preferred_element_type=F32)
+
+    far_outgoing = picked(shift_over_z(scaled, FAR))
+    own = over_experts(picked(scaled)).reshape(N_EXP * CAP, LANES)
+    own, far_outgoing, w_gate, w_up = lax.optimization_barrier((own, far_outgoing, w_gate, w_up))
     w_in = jnp.concatenate([padded_in(w_gate), padded_in(w_up)], axis=2)
     in_row = lax.broadcasted_iota(jnp.int32, w_in.shape, 1)
     in_column = lax.broadcasted_iota(jnp.int32, w_in.shape, 2)
     w_in = jnp.where((in_column == FF_LOCAL) & (in_row >= BLOCK) & (in_row < BLOCK + 2), jnp.ones((), BF16), w_in)
+    up_block, down_block = shift_over_z(own, 1), shift_over_z(own, -1)
+    up_block, w_down = lax.optimization_barrier((up_block, w_down))
     w_out = jnp.pad(to_blocks(w_down[0]).transpose(1, 0, 2), ((0, 0), (0, FF_LANES - FF_LOCAL), (0, 0)))
-
-    def at_offset(blocks, offset):
-        index = lax.bitwise_and(z_index + offset % BLOCKS, BLOCKS - 1)
-        return lax.dynamic_index_in_dim(blocks, index, 0, keepdims=False)
-
-    def input_term(rows, offset):
-        return jnp.dot(rows, at_offset(w_in, offset), preferred_element_type=F32)
-
-    w_out = [at_offset(w_out, offset) for offset in range(BLOCKS)]
-
-    far_outgoing = picked(shift_over_z(scaled, FAR))
-    own = over_experts(picked(scaled)).reshape(N_EXP * CAP, LANES)
-    own, w_in, far_outgoing, *w_out = lax.optimization_barrier((own, w_in, far_outgoing, *w_out))
-    up_block, down_block = shift_over_z(own, 1), shift_over_z(own, -1)
     far = over_experts(far_outgoing).reshape(N_EXP * CAP, LANES)
     both = input_term(own, 0) + input_term(up_block, -1) + input_term(down_block, 1)
     for step in range(2, FAR):
@@ -215,7 +212,7 @@
     expert_hidden = (gate * jax.nn.sigmoid(1.702 * gate) * (up + 1.0)).astype(BF16)
 
     def output_block(offset):
-        return jnp.dot(expert_hidden, w_out[offset % BLOCKS], preferred_element_type=F32)
+        return jnp.dot(expert_hidden, at_offset(w_out, offset), preferred_element_type=F32)
 
     up_sum = shift_over_z(output_block(FAR - 1).astype(BF16), 1)
     down_sum = shift_over_z(output_block(1 - FAR).astype(BF16), -1)

time: 290 us -> 283 us (0.976)
  starting transfers between devices: 95.4 us -> 91.2 us
    all_to_all x4, waiting for transfers between devices: 15.6 us -> 28.5 us  [over_experts(): return lax.all_to_all(array, 'exp', 0, 0, tiled=True)]
    ppermute x14, waiting for transfers between devices: 58.9 us -> 47.2 us  [shift_over_z(): return lax.ppermute(array, 'attn', pairs)]
    unnamed x50 -> x42, local copies, waits for them, and re-layouts: 7.65 us -> 1.47 us
  transfers between devices with their start and end apart: 21 -> 21, of which waited for: 13 -> 14; matrix products, arithmetic and copies ran while one was open for 16% -> 17% of each run, Pallas kernels for 1% -> 1%
where the time goes in v8:
time: 283 us; the launch traced here: 278 us
  waiting for transfers between devices  93.3 us (33%)
  starting transfers between devices  91.2 us (32%)
  blocking collectives  35.5 us (13%)
  matrix products  30.2 us (11%)
  local copies, waits for them, and re-layouts  19.4 us (7%)
  other arithmetic  6.1 us (2%)
    ppermute x14, starting transfers between devices, shift_over_z(): return lax.ppermute(array, 'attn', pairs)  49.2 us
    ppermute x14, waiting for transfers between devices, shift_over_z(): return lax.ppermute(array, 'attn', pairs)  47.2 us
    all_to_all x4, starting transfers between devices, over_experts(): return lax.all_to_all(array, 'exp', 0, 0, tiled=True)  31.5 us
    all_to_all x4, waiting for transfers between devices, over_experts(): return lax.all_to_all(array, 'exp', 0, 0, tiled=True)  28.5 us
    all_to_all x1, blocking collectives, over_z(): lax.all_to_all(array, 'attn', 0, 0, tiled=True, axis_index_groups=Z_GROUPS)  18.7 us
    dot_general x8, matrix products, input_term(): return jnp.dot(rows, at_offset(w_in, offset), preferred_element_type=F32)  16.8 us
    all_to_all x1, blocking collectives, local(): lax.all_to_all(mixed.reshape(N_ATTN, own_rows, LANES), 'attn', 0, 0, tile...  16.8 us
    all_to_all x1, waiting for transfers between devices, over_z(): lax.all_to_all(array, 'attn', 0, 0, tiled=True, axis_index_groups=Z_GROUPS)  13.5 us
  transfers between devices with their start and end apart: 21, of which 14 were waited for; matrix products, arithmetic and copies ran while one was open for 17% of the time, Pallas kernels for 1%

profile of v8, /device:TPU:6, one launch (start us, length us, event | category | flops | bytes accessed | tf_op | source)
XLA Modules:
  0.0 278.1 jit_solution(503585423034091341)
XLA Ops:
  0.0 3.4 %collective-permute-start = (bf16[128,2880]{0,1:T(8,128)(2,1)}, bf16[128,2880]{0,1:T(8,128)(2,1)S(1)}, u32[]{:S(2)}, u32[]{:S(2)}) collective-permute-start(bf16[128,2880]{0,1:T(8,128)(2,1)} %param.17), channel_id=1, source_target_pairs={{0,32},{32,0},{64,96},{96,64},{128,160},{160,128},{192,224},{224,1... | collective-permute-start | bytes 2211848 | tf_op jit(solution)/shard_map/ppermute | solution.py:91
  7.3 1.7 shard_map.118
  9.5 18.7 %all_to_all.35 = bf16[8,8,640]{2,1,0:T(8,128)(2,1)S(1)} all-to-all(bf16[8,8,640]{2,1,0:T(8,128)(2,1)S(1)} %copy.72), channel_id=1, replica_groups={{0,64,128,192,256,320,384,448},{32,96,160,224,288,352,416,480},{1,65,12..., dimensions={0} | all-to-all | bytes 163840 | tf_op jit(solution)/shard_map/all_to_all | solution.py:95
  30.4 3.7 %all-to-all-start.1 = ((bf16[8,64,384]{2,1,0:T(8,128)(2,1)}), bf16[8,64,384]{2,1,0:T(8,128)(2,1)S(1)}, u32[]{:S(2)}, u32[]{:S(2)}) async-start(bf16[8,64,384]{2,1,0:T(8,128)(2,1)} %pad_bitcast_fusion.1), calls=%async_computation.1 | async-start | bytes 786432 | tf_op jit(solution)/shard_map/all_to_all | solution.py:95
  34.4 13.5 %all-to-all-done.1 = bf16[8,64,384]{2,1,0:T(8,128)(2,1)S(1)} async-done(((bf16[8,64,384]{2,1,0:T(8,128)(2,1)}), bf16[8,64,384]{2,1,0:T(8,128)(2,1)S(1)}, u32[]{:S(2)}, u32[]{:S(2)}) %all-to-all-start.1) | async-done | bytes 393248 | tf_op jit(solution)/shard_map/all_to_all | solution.py:95
  48.8 3.3 %collective-permute-start.1 = (bf16[64,384]{1,0:T(8,128)(2,1)S(1)}, bf16[64,384]{1,0:T(8,128)(2,1)S(1)}, u32[]{:S(2)}, u32[]{:S(2)}) collective-permute-start(bf16[64,384]{1,0:T(8,128)(2,1)S(1)} %select_convert_fusion), channel_id=1, source_target_pairs={{0,32},{32,0},{64,96},{96,64},{128,160},{160,128},{192,224},{224,1... | collective-permute-start | bytes 147464 | tf_op jit(solution)/shard_map/ppermute | solution.py:91
  52.2 4.1 %collective-permute-done.1 = bf16[64,384]{1,0:T(8,128)(2,1)S(1)} collective-permute-done((bf16[64,384]{1,0:T(8,128)(2,1)S(1)}, bf16[64,384]{1,0:T(8,128)(2,1)S(1)}, u32[]{:S(2)}, u32[]{:S(2)}) %collective-permute-start.1) | collective-permute-done | bytes 49184 | tf_op jit(solution)/shard_map/ppermute | solution.py:91
  57.6 8.8 %all-to-all-start.2 = ((bf16[32,32,384]{2,1,0:T(8,128)(2,1)}), bf16[32,32,384]{2,1,0:T(8,128)(2,1)}, u32[]{:S(2)}, u32[]{:S(2)}) async-start(bf16[32,32,384]{2,1,0:T(8,128)(2,1)} %bitcast.16), calls=%async_computation.2 | async-start | bytes 1572864 | tf_op jit(solution)/shard_map/all_to_all | solution.py:99
  66.7 2.5 collective-permute-start.2
  69.2 8.3 %collective-permute-done.2 = bf16[128,384]{1,0:T(8,128)(2,1)S(1)} collective-permute-done((bf16[128,384]{1,0:T(8,128)(2,1)S(1)}, bf16[128,384]{1,0:T(8,128)(2,1)S(1)}, u32[]{:S(2)}, u32[]{:S(2)}) %collective-permute-start.2) | collective-permute-done | bytes 98336 | tf_op jit(solution)/shard_map/ppermute | solution.py:87
  78.8 10.0 %all-to-all-done.2 = bf16[32,32,384]{2,1,0:T(8,128)(2,1)} async-done(((bf16[32,32,384]{2,1,0:T(8,128)(2,1)}), bf16[32,32,384]{2,1,0:T(8,128)(2,1)}, u32[]{:S(2)}, u32[]{:S(2)}) %all-to-all-start.2) | async-done | bytes 786464 | tf_op jit(solution)/shard_map/all_to_all | solution.py:99
  88.8 2.5 collective-permute-start.3
  91.3 4.6 %collective-permute-start.4 = (bf16[1024,384]{1,0:T(8,128)(2,1)}, bf16[1024,384]{1,0:T(8,128)(2,1)}, u32[]{:S(2)}, u32[]{:S(2)}) collective-permute-start(bf16[1024,384]{1,0:T(8,128)(2,1)} %bitcast.17), channel_id=1, source_target_pairs={{0,448},{32,480},{64,0},{96,32},{128,64},{160,96},{192,128},{224,1... | collective-permute-start | bytes 2359304 | tf_op jit(solution)/shard_map/ppermute | solution.py:87
  95.9 1.7 copy.76
  97.5 1.7 copy.77
  99.2 5.5 %all-to-all-start.3 = ((bf16[32,32,384]{2,1,0:T(8,128)(2,1)}), bf16[32,32,384]{2,1,0:T(8,128)(2,1)}, u32[]{:S(2)}, u32[]{:S(2)}) async-start(bf16[32,32,384]{2,1,0:T(8,128)(2,1)} %bitcast.19), calls=%async_computation.3 | async-start | bytes 1572864 | tf_op jit(solution)/shard_map/all_to_all | solution.py:99
  104.7 2.3 and_select_fusion
  107.0 3.2 %fusion.29 = f32[1024,512]{1,0:T(8,128)} fusion(bf16[1024,384]{1,0:T(8,128)(2,1)} %bitcast.17, bf16[8,384,512]{2,1,0:T(8,128)(2,1)S(1)} %and_select_fusion, s32[]{:T(128)S(6)} %select_n.138), kind=kOutput, calls=%fused_computation.67 | convolution fusion | flops 402653184 | bytes 3276804 | tf_op jit(solution)/shard_map/dot_general | solution.py:188
  110.5 1.9 collective-permute-start.5
  112.4 3.4 %reshape_squeeze.3 = bf16[180,8,360]{2,1,0:T(8,128)(2,1)} reshape(bf16[1,180,2880]{2,1,0:T(8,128)(2,1)} %param.23) | data formatting | bytes 2073600 | tf_op jit(solution)/shard_map/reshape;squeeze | solution.py:103
  115.8 5.1 %collective-permute-start.6 = (bf16[1024,384]{1,0:T(8,128)(2,1)}, bf16[1024,384]{1,0:T(8,128)(2,1)}, u32[]{:S(2)}, u32[]{:S(2)}) collective-permute-start(bf16[1024,384]{1,0:T(8,128)(2,1)} %collective-permute-done.4), channel_id=1, source_target_pairs={{0,448},{32,480},{64,0},{96,32},{128,64},{160,96},{192,128},{224,1... | collective-permute-start | bytes 2359304 | tf_op jit(solution)/shard_map/ppermute | solution.py:87
  121.0 3.2 %fusion.27 = f32[1024,512]{1,0:T(8,128)} fusion(bf16[1024,384]{1,0:T(8,128)(2,1)} %collective-permute-done.3, bf16[8,384,512]{2,1,0:T(8,128)(2,1)S(1)} %and_select_fusion, s32[]{:T(128)S(6)} %select_n.139), kind=kOutput, calls=%fused_computation.65 | convolution fusion | flops 402653184 | bytes 3276804 | tf_op jit(solution)/shard_map/dot_general | solution.py:188
  124.2 3.3 %fusion.25 = f32[1024,512]{1,0:T(8,128)} fusion(bf16[1024,384]{1,0:T(8,128)(2,1)} %collective-permute-done.4, bf16[8,384,512]{2,1,0:T(8,128)(2,1)S(1)} %and_select_fusion, s32[]{:T(128)S(6)} %select_n.140), kind=kOutput, calls=%fused_computation.63 | convolution fusion | flops 402653184 | bytes 3276804 | tf_op jit(solution)/shard_map/dot_general | solution.py:188
  127.6 5.6 %pad_dynamic-slice_fusion.5 = (bf16[1,256,384]{2,0,1:T(2,128)(2,1)}, bf16[1,256,384]{2,0,1:T(2,128)(2,1)}, bf16[1,256,384]{2,0,1:T(2,128)(2,1)}, bf16[1,256,384]...) fusion(s32[]{:T(128)S(6)} %select_n.142, ...), kind=kLoop, calls=%fused_computation.15 | loop fusion | bytes 2678816 | tf_op jit(solution)/shard_map/jit(dynamic_index_in_dim)/dynamic_slice | solution.py:185
  133.2 2.0 fusion.17
  135.3 2.1 collective-permute-start.7
  137.8 5.8 %collective-permute-start.8 = (bf16[1024,384]{1,0:T(8,128)(2,1)}, bf16[1024,384]{1,0:T(8,128)(2,1)S(1)}, u32[]{:S(2)}, u32[]{:S(2)}) collective-permute-start(bf16[1024,384]{1,0:T(8,128)(2,1)} %collective-permute-done.6), channel_id=1, source_target_pairs={{0,448},{32,480},{64,0},{96,32},{128,64},{160,96},{192,128},{224,1... | collective-permute-start | bytes 2359304 | tf_op jit(solution)/shard_map/ppermute | solution.py:87
  143.6 1.8 fusion.23
  145.5 1.9 add_add_fusion.1
  147.4 10.1 %collective-permute-done.7 = bf16[1024,384]{1,0:T(8,128)(2,1)S(1)} collective-permute-done((bf16[1024,384]{1,0:T(8,128)(2,1)}, bf16[1024,384]{1,0:T(8,128)(2,1)S(1)}, u32[]{:S(2)}, u32[]{:S(2)}) %collective-permute-start.7) | collective-permute-done | bytes 786464 | tf_op jit(solution)/shard_map/ppermute | solution.py:87
  162.5 1.9 collective-permute-start.9
  165.7 5.5 %collective-permute-start.12 = (bf16[1024,384]{1,0:T(8,128)(2,1)}, bf16[1024,384]{1,0:T(8,128)(2,1)}, u32[]{:S(2)}, u32[]{:S(2)}) collective-permute-start(bf16[1024,384]{1,0:T(8,128)(2,1)} %convolution_convert_fusion.1), channel_id=1, source_target_pairs={{0,448},{32,480},{64,0},{96,32},{128,64},{160,96},{192,128},{224,1... | collective-permute-start | bytes 2359304 | tf_op jit(solution)/shard_map/ppermute | solution.py:87
  171.2 1.3 convolution_convert_fusion
  172.6 8.7 %all-to-all-start.5 = ((bf16[32,32,384]{2,1,0:T(8,128)(2,1)}), bf16[32,32,384]{2,1,0:T(8,128)(2,1)S(1)}, u32[]{:S(2)}, u32[]{:S(2)}) async-start(bf16[32,32,384]{2,1,0:T(8,128)(2,1)} %bitcast.35), calls=%async_computation.5 | async-start | bytes 1572864 | tf_op jit(solution)/shard_map/all_to_all | solution.py:99
  181.3 2.5 collective-permute-done.9
  183.8 1.6 add_convert_fusion.4
  185.4 1.9 collective-permute-start.10
  187.4 1.6 add_convert_fusion.2
  189.0 5.1 %collective-permute-start.13 = (bf16[1024,384]{1,0:T(8,128)(2,1)S(1)}, bf16[1024,384]{1,0:T(8,128)(2,1)S(1)}, u32[]{:S(2)}, u32[]{:S(2)}) collective-permute-start(bf16[1024,384]{1,0:T(8,128)(2,1)S(1)} %add_convert_fusion.2), channel_id=1, source_target_pairs={{0,448},{32,480},{64,0},{96,32},{128,64},{160,96},{192,128},{224,1... | collective-permute-start | bytes 2359304 | tf_op jit(solution)/shard_map/ppermute | solution.py:87
  195.0 10.6 %collective-permute-done.10 = bf16[1024,384]{1,0:T(8,128)(2,1)S(1)} collective-permute-done((bf16[1024,384]{1,0:T(8,128)(2,1)S(1)}, bf16[1024,384]{1,0:T(8,128)(2,1)S(1)}, u32[]{:S(2)}, u32[]{:S(2)}) %collective-permute-start.10) | collective-permute-done | bytes 786464 | tf_op jit(solution)/shard_map/ppermute | solution.py:87
  205.8 1.9 collective-permute-start.11
  208.7 5.6 %collective-permute-start.14 = (bf16[1024,384]{1,0:T(8,128)(2,1)S(1)}, bf16[1024,384]{1,0:T(8,128)(2,1)S(1)}, u32[]{:S(2)}, u32[]{:S(2)}) collective-permute-start(bf16[1024,384]{1,0:T(8,128)(2,1)S(1)} %add_convert_fusion.1), channel_id=1, source_target_pairs={{0,448},{32,480},{64,0},{96,32},{128,64},{160,96},{192,128},{224,1... | collective-permute-start | bytes 2359304 | tf_op jit(solution)/shard_map/ppermute | solution.py:87
  214.8 10.4 %collective-permute-done.11 = bf16[1024,384]{1,0:T(8,128)(2,1)S(1)} collective-permute-done((bf16[1024,384]{1,0:T(8,128)(2,1)S(1)}, bf16[1024,384]{1,0:T(8,128)(2,1)S(1)}, u32[]{:S(2)}, u32[]{:S(2)}) %collective-permute-start.11) | collective-permute-done | bytes 786464 | tf_op jit(solution)/shard_map/ppermute | solution.py:87
  225.2 2.6 collective-permute-done.14
  229.0 8.5 %all-to-all-start.4 = ((bf16[32,32,384]{2,1,0:T(8,128)(2,1)}), bf16[32,32,384]{2,1,0:T(8,128)(2,1)S(1)}, u32[]{:S(2)}, u32[]{:S(2)}) async-start(bf16[32,32,384]{2,1,0:T(8,128)(2,1)} %bitcast.32), calls=%async_computation.4 | async-start | bytes 1572864 | tf_op jit(solution)/shard_map/all_to_all | solution.py:99
  238.2 2.9 %collective-permute-start.15 = (f32[128,384]{1,0:T(8,128)S(1)}, f32[128,384]{1,0:T(8,128)S(1)}, u32[]{:S(2)}, u32[]{:S(2)}) collective-permute-start(f32[128,384]{1,0:T(8,128)S(1)} %fusion.7), channel_id=1, source_target_pairs={{0,256},{32,288},{64,320},{96,352},{128,384},{160,416},{192,448},{... | collective-permute-start | bytes 589832 | tf_op jit(solution)/shard_map/ppermute | solution.py:87
  241.3 18.5 %all-to-all-done.4 = bf16[32,32,384]{2,1,0:T(8,128)(2,1)S(1)} async-done(((bf16[32,32,384]{2,1,0:T(8,128)(2,1)}), bf16[32,32,384]{2,1,0:T(8,128)(2,1)S(1)}, u32[]{:S(2)}, u32[]{:S(2)}) %all-to-all-start.4) | async-done | bytes 786464 | tf_op jit(solution)/shard_map/all_to_all | solution.py:99
  260.5 16.8 %all_to_all.36 = f32[16,8,384]{2,1,0:T(8,128)S(1)} all-to-all(f32[16,8,384]{2,1,0:T(8,128)S(1)} %fusion.8), channel_id=1, replica_groups=mesh['attn'=16,'exp'=32] {'attn'}, dimensions={0} | all-to-all | bytes 393216 | tf_op jit(solution)/shard_map/all_to_all | solution.py:229
  (116 shorter events, 23.7 us)
Async XLA Ops:
  0.0 9.3 %copy-start.16 = (bf16[8,2880]{1,0:T(8,128)(2,1)S(1)}, bf16[8,2880]{1,0:T(8,128)(2,1)}, u32[]{:S(2)}) copy-start(bf16[8,2880]{1,0:T(8,128)(2,1)} %param.12) | copy-start | bytes 138244
  0.0 28.6 %collective-permute-start = (bf16[128,2880]{0,1:T(8,128)(2,1)}, bf16[128,2880]{0,1:T(8,128)(2,1)S(1)}, u32[]{:S(2)}, u32[]{:S(2)}) collective-permute-start(bf16[128,2880]{0,1:T(8,128)(2,1)} %param.17), channel_id=1, source_target_pairs={{0,32},{32,0},{64,96},{96,64},{128,160},{160,128},{192,224},{224,1... | collective-permute-start | bytes 2211848 | tf_op jit(solution)/shard_map/ppermute | solution.py:91
  6.1 1.2 copy-start
  7.3 20.8 %copy-start.14 = (bf16[128,2880]{0,1:T(8,128)(2,1)S(1)}, bf16[128,2880]{0,1:T(8,128)(2,1)}, u32[]{:S(2)}) copy-start(bf16[128,2880]{0,1:T(8,128)(2,1)} %param.17) | copy-start | bytes 2211844
  28.5 5.5 %copy-start.17 = (f32[2880]{0:T(1024)S(1)}, f32[2880]{0:T(1024)}, u32[]{:S(2)}) copy-start(f32[2880]{0:T(1024)} %param.18) | copy-start | bytes 34564
  28.6 5.6 %copy-start.18 = (s32[128,4]{0,1:T(4,128)S(1)}, s32[128,4]{0,1:T(4,128)}, u32[]{:S(2)}) copy-start(s32[128,4]{0,1:T(4,128)} %param.19) | copy-start | bytes 6148
  30.4 17.5 %all-to-all-start.1 = ((bf16[8,64,384]{2,1,0:T(8,128)(2,1)}), bf16[8,64,384]{2,1,0:T(8,128)(2,1)S(1)}, u32[]{:S(2)}, u32[]{:S(2)}) async-start(bf16[8,64,384]{2,1,0:T(8,128)(2,1)} %pad_bitcast_fusion.1), calls=%async_computation.1 | async-start | bytes 786432 | tf_op jit(solution)/shard_map/all_to_all | solution.py:95
  48.8 7.5 %collective-permute-start.1 = (bf16[64,384]{1,0:T(8,128)(2,1)S(1)}, bf16[64,384]{1,0:T(8,128)(2,1)S(1)}, u32[]{:S(2)}, u32[]{:S(2)}) collective-permute-start(bf16[64,384]{1,0:T(8,128)(2,1)S(1)} %select_convert_fusion), channel_id=1, source_target_pairs={{0,32},{32,0},{64,96},{96,64},{128,160},{160,128},{192,224},{224,1... | collective-permute-start | bytes 147464 | tf_op jit(solution)/shard_map/ppermute | solution.py:91
  52.2 43.6 %copy-start.5 = (bf16[1,2880,180]{1,2,0:T(8,128)(2,1)S(1)}, bf16[1,2880,180]{1,2,0:T(8,128)(2,1)}, u32[]{:S(2)}) copy-start(bf16[1,2880,180]{1,2,0:T(8,128)(2,1)} %param.21) | copy-start | bytes 3110404
  57.6 31.2 %all-to-all-start.2 = ((bf16[32,32,384]{2,1,0:T(8,128)(2,1)}), bf16[32,32,384]{2,1,0:T(8,128)(2,1)}, u32[]{:S(2)}, u32[]{:S(2)}) async-start(bf16[32,32,384]{2,1,0:T(8,128)(2,1)} %bitcast.16), calls=%async_computation.2 | async-start | bytes 1572864 | tf_op jit(solution)/shard_map/all_to_all | solution.py:99
  66.4 31.1 %copy-start.6 = (bf16[1,2880,180]{1,2,0:T(8,128)(2,1)S(1)}, bf16[1,2880,180]{1,2,0:T(8,128)(2,1)}, u32[]{:S(2)}) copy-start(bf16[1,2880,180]{1,2,0:T(8,128)(2,1)} %param.22) | copy-start | bytes 3110404
  66.7 10.7 %collective-permute-start.2 = (bf16[128,384]{1,0:T(8,128)(2,1)S(1)}, bf16[128,384]{1,0:T(8,128)(2,1)S(1)}, u32[]{:S(2)}, u32[]{:S(2)}) collective-permute-start(bf16[128,384]{1,0:T(8,128)(2,1)S(1)} %bitcast.154), channel_id=1, source_target_pairs={{0,256},{32,288},{64,320},{96,352},{128,384},{160,416},{192,448},{... | collective-permute-start | bytes 294920 | tf_op jit(solution)/shard_map/ppermute | solution.py:87
  88.8 21.7 %collective-permute-start.3 = (bf16[1024,384]{1,0:T(8,128)(2,1)}, bf16[1024,384]{1,0:T(8,128)(2,1)}, u32[]{:S(2)}, u32[]{:S(2)}) collective-permute-start(bf16[1024,384]{1,0:T(8,128)(2,1)} %bitcast.17), channel_id=1, source_target_pairs={{0,64},{32,96},{64,128},{96,160},{128,192},{160,224},{192,256},{22... | collective-permute-start | bytes 2359304 | tf_op jit(solution)/shard_map/ppermute | solution.py:87
  91.3 24.6 %collective-permute-start.4 = (bf16[1024,384]{1,0:T(8,128)(2,1)}, bf16[1024,384]{1,0:T(8,128)(2,1)}, u32[]{:S(2)}, u32[]{:S(2)}) collective-permute-start(bf16[1024,384]{1,0:T(8,128)(2,1)} %bitcast.17), channel_id=1, source_target_pairs={{0,448},{32,480},{64,0},{96,32},{128,64},{160,96},{192,128},{224,1... | collective-permute-start | bytes 2359304 | tf_op jit(solution)/shard_map/ppermute | solution.py:87
  99.2 34.0 %all-to-all-start.3 = ((bf16[32,32,384]{2,1,0:T(8,128)(2,1)}), bf16[32,32,384]{2,1,0:T(8,128)(2,1)}, u32[]{:S(2)}, u32[]{:S(2)}) async-start(bf16[32,32,384]{2,1,0:T(8,128)(2,1)} %bitcast.19), calls=%async_computation.3 | async-start | bytes 1572864 | tf_op jit(solution)/shard_map/all_to_all | solution.py:99
  110.5 24.8 %collective-permute-start.5 = (bf16[1024,384]{1,0:T(8,128)(2,1)}, bf16[1024,384]{1,0:T(8,128)(2,1)}, u32[]{:S(2)}, u32[]{:S(2)}) collective-permute-start(bf16[1024,384]{1,0:T(8,128)(2,1)} %collective-permute-done.3), channel_id=1, source_target_pairs={{0,64},{32,96},{64,128},{96,160},{128,192},{160,224},{192,256},{22... | collective-permute-start | bytes 2359304 | tf_op jit(solution)/shard_map/ppermute | solution.py:87
  115.8 22.0 %collective-permute-start.6 = (bf16[1024,384]{1,0:T(8,128)(2,1)}, bf16[1024,384]{1,0:T(8,128)(2,1)}, u32[]{:S(2)}, u32[]{:S(2)}) collective-permute-start(bf16[1024,384]{1,0:T(8,128)(2,1)} %collective-permute-done.4), channel_id=1, source_target_pairs={{0,448},{32,480},{64,0},{96,32},{128,64},{160,96},{192,128},{224,1... | collective-permute-start | bytes 2359304 | tf_op jit(solution)/shard_map/ppermute | solution.py:87
  124.2 3.3 %copy-start.4 = (bf16[180,8,360]{2,1,0:T(8,128)(2,1)S(1)}, bf16[180,8,360]{2,1,0:T(8,128)(2,1)}, u32[]{:S(2)}) copy-start(bf16[180,8,360]{2,1,0:T(8,128)(2,1)} %reshape_squeeze.3) | copy-start | bytes 3110404
  133.2 12.2 %copy-start.2 = (f32[1024,512]{1,0:T(8,128)S(1)}, f32[1024,512]{1,0:T(8,128)}, u32[]{:S(2)}) copy-start(f32[1024,512]{1,0:T(8,128)} %fusion.27) | copy-start | bytes 6291460
  133.2 12.2 %copy-start.3 = (f32[1024,512]{1,0:T(8,128)S(1)}, f32[1024,512]{1,0:T(8,128)}, u32[]{:S(2)}) copy-start(f32[1024,512]{1,0:T(8,128)} %fusion.25) | copy-start | bytes 6291460
  135.2 10.3 %copy-start.1 = (f32[1024,512]{1,0:T(8,128)S(1)}, f32[1024,512]{1,0:T(8,128)}, u32[]{:S(2)}) copy-start(f32[1024,512]{1,0:T(8,128)} %fusion.29) | copy-start | bytes 6291460
  135.3 22.2 %collective-permute-start.7 = (bf16[1024,384]{1,0:T(8,128)(2,1)}, bf16[1024,384]{1,0:T(8,128)(2,1)S(1)}, u32[]{:S(2)}, u32[]{:S(2)}) collective-permute-start(bf16[1024,384]{1,0:T(8,128)(2,1)} %collective-permute-done.5), channel_id=1, source_target_pairs={{0,64},{32,96},{64,128},{96,160},{128,192},{160,224},{192,256},{22... | collective-permute-start | bytes 2359304 | tf_op jit(solution)/shard_map/ppermute | solution.py:87
  137.8 21.6 %collective-permute-start.8 = (bf16[1024,384]{1,0:T(8,128)(2,1)}, bf16[1024,384]{1,0:T(8,128)(2,1)S(1)}, u32[]{:S(2)}, u32[]{:S(2)}) collective-permute-start(bf16[1024,384]{1,0:T(8,128)(2,1)} %collective-permute-done.6), channel_id=1, source_target_pairs={{0,448},{32,480},{64,0},{96,32},{128,64},{160,96},{192,128},{224,1... | collective-permute-start | bytes 2359304 | tf_op jit(solution)/shard_map/ppermute | solution.py:87
  160.1 1.0 copy-start.13
  160.5 3.9 %copy-start.12 = (bf16[1,256,384]{2,0,1:T(2,128)(2,1)S(1)}, bf16[1,256,384]{2,0,1:T(2,128)(2,1)}, u32[]{:S(2)}) copy-start(bf16[1,256,384]{2,0,1:T(2,128)(2,1)} %get-tuple-element.22) | copy-start | bytes 589828
  161.0 10.2 %copy-start.11 = (bf16[1,256,384]{2,0,1:T(2,128)(2,1)S(1)}, bf16[1,256,384]{2,0,1:T(2,128)(2,1)}, u32[]{:S(2)}) copy-start(bf16[1,256,384]{2,0,1:T(2,128)(2,1)} %get-tuple-element.23) | copy-start | bytes 589828
  162.5 21.3 %collective-permute-start.9 = (bf16[1024,384]{1,0:T(8,128)(2,1)}, bf16[1024,384]{1,0:T(8,128)(2,1)}, u32[]{:S(2)}, u32[]{:S(2)}) collective-permute-start(bf16[1024,384]{1,0:T(8,128)(2,1)} %convolution_convert_fusion.2), channel_id=1, source_target_pairs={{0,64},{32,96},{64,128},{96,160},{128,192},{160,224},{192,256},{22... | collective-permute-start | bytes 2359304 | tf_op jit(solution)/shard_map/ppermute | solution.py:87
  164.4 19.4 %copy-start.10 = (bf16[1,256,384]{2,0,1:T(2,128)(2,1)S(1)}, bf16[1,256,384]{2,0,1:T(2,128)(2,1)}, u32[]{:S(2)}) copy-start(bf16[1,256,384]{2,0,1:T(2,128)(2,1)} %get-tuple-element.17) | copy-start | bytes 589828
  165.7 21.6 %collective-permute-start.12 = (bf16[1024,384]{1,0:T(8,128)(2,1)}, bf16[1024,384]{1,0:T(8,128)(2,1)}, u32[]{:S(2)}, u32[]{:S(2)}) collective-permute-start(bf16[1024,384]{1,0:T(8,128)(2,1)} %convolution_convert_fusion.1), channel_id=1, source_target_pairs={{0,448},{32,480},{64,0},{96,32},{128,64},{160,96},{192,128},{224,1... | collective-permute-start | bytes 2359304 | tf_op jit(solution)/shard_map/ppermute | solution.py:87
  172.6 14.8 %copy-start.9 = (bf16[1,256,384]{2,0,1:T(2,128)(2,1)S(1)}, bf16[1,256,384]{2,0,1:T(2,128)(2,1)}, u32[]{:S(2)}) copy-start(bf16[1,256,384]{2,0,1:T(2,128)(2,1)} %get-tuple-element.21) | copy-start | bytes 589828
  172.6 56.4 %all-to-all-start.5 = ((bf16[32,32,384]{2,1,0:T(8,128)(2,1)}), bf16[32,32,384]{2,1,0:T(8,128)(2,1)S(1)}, u32[]{:S(2)}, u32[]{:S(2)}) async-start(bf16[32,32,384]{2,1,0:T(8,128)(2,1)} %bitcast.35), calls=%async_computation.5 | async-start | bytes 1572864 | tf_op jit(solution)/shard_map/all_to_all | solution.py:99
  183.8 10.4 %copy-start.8 = (bf16[1,256,384]{2,0,1:T(2,128)(2,1)S(1)}, bf16[1,256,384]{2,0,1:T(2,128)(2,1)}, u32[]{:S(2)}) copy-start(bf16[1,256,384]{2,0,1:T(2,128)(2,1)} %get-tuple-element.18) | copy-start | bytes 589828
  185.4 20.3 %collective-permute-start.10 = (bf16[1024,384]{1,0:T(8,128)(2,1)S(1)}, bf16[1024,384]{1,0:T(8,128)(2,1)S(1)}, u32[]{:S(2)}, u32[]{:S(2)}) collective-permute-start(bf16[1024,384]{1,0:T(8,128)(2,1)S(1)} %add_convert_fusion.4), channel_id=1, source_target_pairs={{0,64},{32,96},{64,128},{96,160},{128,192},{160,224},{192,256},{22... | collective-permute-start | bytes 2359304 | tf_op jit(solution)/shard_map/ppermute | solution.py:87
  187.3 7.2 %copy-start.7 = (bf16[1,256,384]{2,0,1:T(2,128)(2,1)S(1)}, bf16[1,256,384]{2,0,1:T(2,128)(2,1)}, u32[]{:S(2)}) copy-start(bf16[1,256,384]{2,0,1:T(2,128)(2,1)} %get-tuple-element.20) | copy-start | bytes 589828
  189.0 19.5 %collective-permute-start.13 = (bf16[1024,384]{1,0:T(8,128)(2,1)S(1)}, bf16[1024,384]{1,0:T(8,128)(2,1)S(1)}, u32[]{:S(2)}, u32[]{:S(2)}) collective-permute-start(bf16[1024,384]{1,0:T(8,128)(2,1)S(1)} %add_convert_fusion.2), channel_id=1, source_target_pairs={{0,448},{32,480},{64,0},{96,32},{128,64},{160,96},{192,128},{224,1... | collective-permute-start | bytes 2359304 | tf_op jit(solution)/shard_map/ppermute | solution.py:87
  205.8 19.3 %collective-permute-start.11 = (bf16[1024,384]{1,0:T(8,128)(2,1)S(1)}, bf16[1024,384]{1,0:T(8,128)(2,1)S(1)}, u32[]{:S(2)}, u32[]{:S(2)}) collective-permute-start(bf16[1024,384]{1,0:T(8,128)(2,1)S(1)} %add_convert_fusion.3), channel_id=1, source_target_pairs={{0,64},{32,96},{64,128},{96,160},{128,192},{160,224},{192,256},{22... | collective-permute-start | bytes 2359304 | tf_op jit(solution)/shard_map/ppermute | solution.py:87
  208.7 19.0 %collective-permute-start.14 = (bf16[1024,384]{1,0:T(8,128)(2,1)S(1)}, bf16[1024,384]{1,0:T(8,128)(2,1)S(1)}, u32[]{:S(2)}, u32[]{:S(2)}) collective-permute-start(bf16[1024,384]{1,0:T(8,128)(2,1)S(1)} %add_convert_fusion.1), channel_id=1, source_target_pairs={{0,448},{32,480},{64,0},{96,32},{128,64},{160,96},{192,128},{224,1... | collective-permute-start | bytes 2359304 | tf_op jit(solution)/shard_map/ppermute | solution.py:87
  214.7 22.7 %copy-start.19 = (s32[128,4]{0,1:T(4,128)S(1)}, s32[128,4]{0,1:T(4,128)}, u32[]{:S(2)}) copy-start(s32[128,4]{0,1:T(4,128)} %param.19) | copy-start | bytes 6148
  214.7 22.7 %copy-start.20 = (f32[128,4]{0,1:T(4,128)S(1)}, f32[128,4]{0,1:T(4,128)}, u32[]{:S(2)}) copy-start(f32[128,4]{0,1:T(4,128)} %param.20) | copy-start | bytes 6148
  229.0 12.2 %copy-start.15 = (f32[8,8,384]{2,1,0:T(8,128)S(1)}, f32[8,8,384]{2,1,0:T(8,128)}, u32[]{:S(2)}) copy-start(f32[8,8,384]{2,1,0:T(8,128)} %get-tuple-element.26) | copy-start | bytes 294916
  229.0 30.9 %all-to-all-start.4 = ((bf16[32,32,384]{2,1,0:T(8,128)(2,1)}), bf16[32,32,384]{2,1,0:T(8,128)(2,1)S(1)}, u32[]{:S(2)}, u32[]{:S(2)}) async-start(bf16[32,32,384]{2,1,0:T(8,128)(2,1)} %bitcast.32), calls=%async_computation.4 | async-start | bytes 1572864 | tf_op jit(solution)/shard_map/all_to_all | solution.py:99
  238.2 22.0 %collective-permute-start.15 = (f32[128,384]{1,0:T(8,128)S(1)}, f32[128,384]{1,0:T(8,128)S(1)}, u32[]{:S(2)}, u32[]{:S(2)}) collective-permute-start(f32[128,384]{1,0:T(8,128)S(1)} %fusion.7), channel_id=1, source_target_pairs={{0,256},{32,288},{64,320},{96,352},{128,384},{160,416},{192,448},{... | collective-permute-start | bytes 589832 | tf_op jit(solution)/shard_map/ppermute | solution.py:87

commit v9 on v8

--- a/solution.py
+++ b/solution.py
@@ -226,7 +226,8 @@
     mixed = mixed.reshape(BLOCKS, HALVES, own_rows, LANES)
     halves = jnp.arange(HALVES, dtype=jnp.int32)[None, :, None, None]
     mixed = mixed + jnp.where(halves == half, hidden_state.reshape(BLOCKS, 1, own_rows, LANES), 0.0)
-    last = lax.all_to_all(mixed.reshape(N_ATTN, own_rows, LANES), "attn", 0, 0, tiled=True)
+    mixed = mixed.reshape(N_ATTN, own_rows, LANES).astype(BF16)
+    last = lax.all_to_all(mixed, "attn", 0, 0, tiled=True).astype(F32)
     last = jnp.sum(last.reshape(BLOCKS, HALVES, own_rows, LANES), axis=1)
     return last[:, :, :BLOCK].transpose(1, 0, 2).reshape(own_rows, D).astype(BF16)
 

time: 283 us -> 282 us (level)
  no operation moved by 1% of the time
where the time goes in v9:
time: 282 us; the launch traced here: 277 us
  waiting for transfers between devices  93.3 us (33%)
  starting transfers between devices  91.2 us (32%)
  blocking collectives  34.5 us (12%)
  matrix products  30.2 us (11%)
  local copies, waits for them, and re-layouts  19.4 us (7%)
  other arithmetic  6.1 us (2%)
    ppermute x14, starting transfers between devices, shift_over_z(): return lax.ppermute(array, 'attn', pairs)  49.2 us
    ppermute x14, waiting for transfers between devices, shift_over_z(): return lax.ppermute(array, 'attn', pairs)  47.2 us
    all_to_all x4, starting transfers between devices, over_experts(): return lax.all_to_all(array, 'exp', 0, 0, tiled=True)  31.5 us
    all_to_all x4, waiting for transfers between devices, over_experts(): return lax.all_to_all(array, 'exp', 0, 0, tiled=True)  28.5 us
    all_to_all x1, blocking collectives, over_z(): lax.all_to_all(array, 'attn', 0, 0, tiled=True, axis_index_groups=Z_GROUPS)  18.7 us
    dot_general x8, matrix products, input_term(): return jnp.dot(rows, at_offset(w_in, offset), preferred_element_type=F32)  16.8 us
    all_to_all x1, blocking collectives, local(): last = lax.all_to_all(mixed, 'attn', 0, 0, tiled=True).astype(F32)  15.8 us
    all_to_all x1, waiting for transfers between devices, over_z(): lax.all_to_all(array, 'attn', 0, 0, tiled=True, axis_index_groups=Z_GROUPS)  13.5 us
  transfers between devices with their start and end apart: 21, of which 14 were waited for; matrix products, arithmetic and copies ran while one was open for 17% of the time, Pallas kernels for 1%

profile of v9, /device:TPU:6, one launch (start us, length us, event | category | flops | bytes accessed | tf_op | source)
XLA Modules:
  0.0 277.2 jit_solution(1128786900824132928)
XLA Ops:
  0.0 3.4 %collective-permute-start = (bf16[128,2880]{0,1:T(8,128)(2,1)}, bf16[128,2880]{0,1:T(8,128)(2,1)S(1)}, u32[]{:S(2)}, u32[]{:S(2)}) collective-permute-start(bf16[128,2880]{0,1:T(8,128)(2,1)} %param.17), channel_id=1, source_target_pairs={{0,32},{32,0},{64,96},{96,64},{128,160},{160,128},{192,224},{224,1... | collective-permute-start | bytes 2211848 | tf_op jit(solution)/shard_map/ppermute | solution.py:91
  7.3 1.7 shard_map.118
  9.5 18.7 %all_to_all.35 = bf16[8,8,640]{2,1,0:T(8,128)(2,1)S(1)} all-to-all(bf16[8,8,640]{2,1,0:T(8,128)(2,1)S(1)} %copy.72), channel_id=1, replica_groups={{0,64,128,192,256,320,384,448},{32,96,160,224,288,352,416,480},{1,65,12..., dimensions={0} | all-to-all | bytes 163840 | tf_op jit(solution)/shard_map/all_to_all | solution.py:95
  30.4 3.7 %all-to-all-start.1 = ((bf16[8,64,384]{2,1,0:T(8,128)(2,1)}), bf16[8,64,384]{2,1,0:T(8,128)(2,1)S(1)}, u32[]{:S(2)}, u32[]{:S(2)}) async-start(bf16[8,64,384]{2,1,0:T(8,128)(2,1)} %pad_bitcast_fusion.1), calls=%async_computation.1 | async-start | bytes 786432 | tf_op jit(solution)/shard_map/all_to_all | solution.py:95
  34.4 13.5 %all-to-all-done.1 = bf16[8,64,384]{2,1,0:T(8,128)(2,1)S(1)} async-done(((bf16[8,64,384]{2,1,0:T(8,128)(2,1)}), bf16[8,64,384]{2,1,0:T(8,128)(2,1)S(1)}, u32[]{:S(2)}, u32[]{:S(2)}) %all-to-all-start.1) | async-done | bytes 393248 | tf_op jit(solution)/shard_map/all_to_all | solution.py:95
  48.8 3.3 %collective-permute-start.1 = (bf16[64,384]{1,0:T(8,128)(2,1)S(1)}, bf16[64,384]{1,0:T(8,128)(2,1)S(1)}, u32[]{:S(2)}, u32[]{:S(2)}) collective-permute-start(bf16[64,384]{1,0:T(8,128)(2,1)S(1)} %select_convert_fusion), channel_id=1, source_target_pairs={{0,32},{32,0},{64,96},{96,64},{128,160},{160,128},{192,224},{224,1... | collective-permute-start | bytes 147464 | tf_op jit(solution)/shard_map/ppermute | solution.py:91
  52.2 4.1 %collective-permute-done.1 = bf16[64,384]{1,0:T(8,128)(2,1)S(1)} collective-permute-done((bf16[64,384]{1,0:T(8,128)(2,1)S(1)}, bf16[64,384]{1,0:T(8,128)(2,1)S(1)}, u32[]{:S(2)}, u32[]{:S(2)}) %collective-permute-start.1) | collective-permute-done | bytes 49184 | tf_op jit(solution)/shard_map/ppermute | solution.py:91
  57.6 8.8 %all-to-all-start.2 = ((bf16[32,32,384]{2,1,0:T(8,128)(2,1)}), bf16[32,32,384]{2,1,0:T(8,128)(2,1)}, u32[]{:S(2)}, u32[]{:S(2)}) async-start(bf16[32,32,384]{2,1,0:T(8,128)(2,1)} %bitcast.16), calls=%async_computation.2 | async-start | bytes 1572864 | tf_op jit(solution)/shard_map/all_to_all | solution.py:99
  66.7 2.5 collective-permute-start.2
  69.2 8.3 %collective-permute-done.2 = bf16[128,384]{1,0:T(8,128)(2,1)S(1)} collective-permute-done((bf16[128,384]{1,0:T(8,128)(2,1)S(1)}, bf16[128,384]{1,0:T(8,128)(2,1)S(1)}, u32[]{:S(2)}, u32[]{:S(2)}) %collective-permute-start.2) | collective-permute-done | bytes 98336 | tf_op jit(solution)/shard_map/ppermute | solution.py:87
  78.8 10.0 %all-to-all-done.2 = bf16[32,32,384]{2,1,0:T(8,128)(2,1)} async-done(((bf16[32,32,384]{2,1,0:T(8,128)(2,1)}), bf16[32,32,384]{2,1,0:T(8,128)(2,1)}, u32[]{:S(2)}, u32[]{:S(2)}) %all-to-all-start.2) | async-done | bytes 786464 | tf_op jit(solution)/shard_map/all_to_all | solution.py:99
  88.8 2.5 collective-permute-start.3
  91.3 4.6 %collective-permute-start.4 = (bf16[1024,384]{1,0:T(8,128)(2,1)}, bf16[1024,384]{1,0:T(8,128)(2,1)}, u32[]{:S(2)}, u32[]{:S(2)}) collective-permute-start(bf16[1024,384]{1,0:T(8,128)(2,1)} %bitcast.17), channel_id=1, source_target_pairs={{0,448},{32,480},{64,0},{96,32},{128,64},{160,96},{192,128},{224,1... | collective-permute-start | bytes 2359304 | tf_op jit(solution)/shard_map/ppermute | solution.py:87
  95.9 1.7 copy.76
  97.5 1.7 copy.77
  99.2 5.5 %all-to-all-start.3 = ((bf16[32,32,384]{2,1,0:T(8,128)(2,1)}), bf16[32,32,384]{2,1,0:T(8,128)(2,1)}, u32[]{:S(2)}, u32[]{:S(2)}) async-start(bf16[32,32,384]{2,1,0:T(8,128)(2,1)} %bitcast.19), calls=%async_computation.3 | async-start | bytes 1572864 | tf_op jit(solution)/shard_map/all_to_all | solution.py:99
  104.7 2.3 and_select_fusion
  107.0 3.2 %fusion.30 = f32[1024,512]{1,0:T(8,128)} fusion(bf16[1024,384]{1,0:T(8,128)(2,1)} %bitcast.17, bf16[8,384,512]{2,1,0:T(8,128)(2,1)S(1)} %and_select_fusion, s32[]{:T(128)S(6)} %select_n.138), kind=kOutput, calls=%fused_computation.68 | convolution fusion | flops 402653184 | bytes 3276804 | tf_op jit(solution)/shard_map/dot_general | solution.py:188
  110.5 1.9 collective-permute-start.5
  112.4 3.4 %reshape_squeeze.3 = bf16[180,8,360]{2,1,0:T(8,128)(2,1)} reshape(bf16[1,180,2880]{2,1,0:T(8,128)(2,1)} %param.23) | data formatting | bytes 2073600 | tf_op jit(solution)/shard_map/reshape;squeeze | solution.py:103
  115.8 5.1 %collective-permute-start.6 = (bf16[1024,384]{1,0:T(8,128)(2,1)}, bf16[1024,384]{1,0:T(8,128)(2,1)}, u32[]{:S(2)}, u32[]{:S(2)}) collective-permute-start(bf16[1024,384]{1,0:T(8,128)(2,1)} %collective-permute-done.4), channel_id=1, source_target_pairs={{0,448},{32,480},{64,0},{96,32},{128,64},{160,96},{192,128},{224,1... | collective-permute-start | bytes 2359304 | tf_op jit(solution)/shard_map/ppermute | solution.py:87
  121.0 3.2 %fusion.28 = f32[1024,512]{1,0:T(8,128)} fusion(bf16[1024,384]{1,0:T(8,128)(2,1)} %collective-permute-done.3, bf16[8,384,512]{2,1,0:T(8,128)(2,1)S(1)} %and_select_fusion, s32[]{:T(128)S(6)} %select_n.139), kind=kOutput, calls=%fused_computation.66 | convolution fusion | flops 402653184 | bytes 3276804 | tf_op jit(solution)/shard_map/dot_general | solution.py:188
  124.2 3.3 %fusion.26 = f32[1024,512]{1,0:T(8,128)} fusion(bf16[1024,384]{1,0:T(8,128)(2,1)} %collective-permute-done.4, bf16[8,384,512]{2,1,0:T(8,128)(2,1)S(1)} %and_select_fusion, s32[]{:T(128)S(6)} %select_n.140), kind=kOutput, calls=%fused_computation.64 | convolution fusion | flops 402653184 | bytes 3276804 | tf_op jit(solution)/shard_map/dot_general | solution.py:188
  127.6 5.6 %pad_dynamic-slice_fusion.5 = (bf16[1,256,384]{2,0,1:T(2,128)(2,1)}, bf16[1,256,384]{2,0,1:T(2,128)(2,1)}, bf16[1,256,384]{2,0,1:T(2,128)(2,1)}, bf16[1,256,384]...) fusion(s32[]{:T(128)S(6)} %select_n.142, ...), kind=kLoop, calls=%fused_computation.15 | loop fusion | bytes 2678816 | tf_op jit(solution)/shard_map/jit(dynamic_index_in_dim)/dynamic_slice | solution.py:185
  133.2 2.0 fusion.18
  135.3 2.1 collective-permute-start.7
  137.8 5.8 %collective-permute-start.8 = (bf16[1024,384]{1,0:T(8,128)(2,1)}, bf16[1024,384]{1,0:T(8,128)(2,1)S(1)}, u32[]{:S(2)}, u32[]{:S(2)}) collective-permute-start(bf16[1024,384]{1,0:T(8,128)(2,1)} %collective-permute-done.6), channel_id=1, source_target_pairs={{0,448},{32,480},{64,0},{96,32},{128,64},{160,96},{192,128},{224,1... | collective-permute-start | bytes 2359304 | tf_op jit(solution)/shard_map/ppermute | solution.py:87
  143.6 1.8 fusion.24
  145.5 1.9 add_add_fusion.1
  147.4 10.1 %collective-permute-done.7 = bf16[1024,384]{1,0:T(8,128)(2,1)S(1)} collective-permute-done((bf16[1024,384]{1,0:T(8,128)(2,1)}, bf16[1024,384]{1,0:T(8,128)(2,1)S(1)}, u32[]{:S(2)}, u32[]{:S(2)}) %collective-permute-start.7) | collective-permute-done | bytes 786464 | tf_op jit(solution)/shard_map/ppermute | solution.py:87
  162.5 1.9 collective-permute-start.9
  165.7 5.5 %collective-permute-start.12 = (bf16[1024,384]{1,0:T(8,128)(2,1)}, bf16[1024,384]{1,0:T(8,128)(2,1)}, u32[]{:S(2)}, u32[]{:S(2)}) collective-permute-start(bf16[1024,384]{1,0:T(8,128)(2,1)} %convolution_convert_fusion.1), channel_id=1, source_target_pairs={{0,448},{32,480},{64,0},{96,32},{128,64},{160,96},{192,128},{224,1... | collective-permute-start | bytes 2359304 | tf_op jit(solution)/shard_map/ppermute | solution.py:87
  171.2 1.3 convolution_convert_fusion
  172.6 8.7 %all-to-all-start.5 = ((bf16[32,32,384]{2,1,0:T(8,128)(2,1)}), bf16[32,32,384]{2,1,0:T(8,128)(2,1)S(1)}, u32[]{:S(2)}, u32[]{:S(2)}) async-start(bf16[32,32,384]{2,1,0:T(8,128)(2,1)} %bitcast.35), calls=%async_computation.5 | async-start | bytes 1572864 | tf_op jit(solution)/shard_map/all_to_all | solution.py:99
  181.3 2.5 collective-permute-done.9
  183.8 1.6 add_convert_fusion.4
  185.4 1.9 collective-permute-start.10
  187.4 1.6 add_convert_fusion.2
  189.0 5.1 %collective-permute-start.13 = (bf16[1024,384]{1,0:T(8,128)(2,1)S(1)}, bf16[1024,384]{1,0:T(8,128)(2,1)S(1)}, u32[]{:S(2)}, u32[]{:S(2)}) collective-permute-start(bf16[1024,384]{1,0:T(8,128)(2,1)S(1)} %add_convert_fusion.2), channel_id=1, source_target_pairs={{0,448},{32,480},{64,0},{96,32},{128,64},{160,96},{192,128},{224,1... | collective-permute-start | bytes 2359304 | tf_op jit(solution)/shard_map/ppermute | solution.py:87
  195.0 10.6 %collective-permute-done.10 = bf16[1024,384]{1,0:T(8,128)(2,1)S(1)} collective-permute-done((bf16[1024,384]{1,0:T(8,128)(2,1)S(1)}, bf16[1024,384]{1,0:T(8,128)(2,1)S(1)}, u32[]{:S(2)}, u32[]{:S(2)}) %collective-permute-start.10) | collective-permute-done | bytes 786464 | tf_op jit(solution)/shard_map/ppermute | solution.py:87
  205.8 1.9 collective-permute-start.11
  208.7 5.6 %collective-permute-start.14 = (bf16[1024,384]{1,0:T(8,128)(2,1)S(1)}, bf16[1024,384]{1,0:T(8,128)(2,1)S(1)}, u32[]{:S(2)}, u32[]{:S(2)}) collective-permute-start(bf16[1024,384]{1,0:T(8,128)(2,1)S(1)} %add_convert_fusion.1), channel_id=1, source_target_pairs={{0,448},{32,480},{64,0},{96,32},{128,64},{160,96},{192,128},{224,1... | collective-permute-start | bytes 2359304 | tf_op jit(solution)/shard_map/ppermute | solution.py:87
  214.8 10.4 %collective-permute-done.11 = bf16[1024,384]{1,0:T(8,128)(2,1)S(1)} collective-permute-done((bf16[1024,384]{1,0:T(8,128)(2,1)S(1)}, bf16[1024,384]{1,0:T(8,128)(2,1)S(1)}, u32[]{:S(2)}, u32[]{:S(2)}) %collective-permute-start.11) | collective-permute-done | bytes 786464 | tf_op jit(solution)/shard_map/ppermute | solution.py:87
  225.2 2.6 collective-permute-done.14
  229.0 8.5 %all-to-all-start.4 = ((bf16[32,32,384]{2,1,0:T(8,128)(2,1)}), bf16[32,32,384]{2,1,0:T(8,128)(2,1)S(1)}, u32[]{:S(2)}, u32[]{:S(2)}) async-start(bf16[32,32,384]{2,1,0:T(8,128)(2,1)} %bitcast.32), calls=%async_computation.4 | async-start | bytes 1572864 | tf_op jit(solution)/shard_map/all_to_all | solution.py:99
  238.2 2.9 %collective-permute-start.15 = (f32[128,384]{1,0:T(8,128)S(1)}, f32[128,384]{1,0:T(8,128)S(1)}, u32[]{:S(2)}, u32[]{:S(2)}) collective-permute-start(f32[128,384]{1,0:T(8,128)S(1)} %fusion.7), channel_id=1, source_target_pairs={{0,256},{32,288},{64,320},{96,352},{128,384},{160,416},{192,448},{... | collective-permute-start | bytes 589832 | tf_op jit(solution)/shard_map/ppermute | solution.py:87
  241.3 18.5 %all-to-all-done.4 = bf16[32,32,384]{2,1,0:T(8,128)(2,1)S(1)} async-done(((bf16[32,32,384]{2,1,0:T(8,128)(2,1)}), bf16[32,32,384]{2,1,0:T(8,128)(2,1)S(1)}, u32[]{:S(2)}, u32[]{:S(2)}) %all-to-all-start.4) | async-done | bytes 786464 | tf_op jit(solution)/shard_map/all_to_all | solution.py:99
  260.5 15.8 %all_to_all.36 = bf16[16,8,384]{2,1,0:T(8,128)(2,1)S(1)} all-to-all(bf16[16,8,384]{2,1,0:T(8,128)(2,1)S(1)} %fusion.9), channel_id=1, replica_groups=mesh['attn'=16,'exp'=32] {'attn'}, dimensions={0} | all-to-all | bytes 196608 | tf_op jit(solution)/shard_map/all_to_all | solution.py:230
  (116 shorter events, 23.7 us)
Async XLA Ops:
  0.0 9.3 %copy-start.16 = (bf16[8,2880]{1,0:T(8,128)(2,1)S(1)}, bf16[8,2880]{1,0:T(8,128)(2,1)}, u32[]{:S(2)}) copy-start(bf16[8,2880]{1,0:T(8,128)(2,1)} %param.12) | copy-start | bytes 138244
  0.0 28.6 %collective-permute-start = (bf16[128,2880]{0,1:T(8,128)(2,1)}, bf16[128,2880]{0,1:T(8,128)(2,1)S(1)}, u32[]{:S(2)}, u32[]{:S(2)}) collective-permute-start(bf16[128,2880]{0,1:T(8,128)(2,1)} %param.17), channel_id=1, source_target_pairs={{0,32},{32,0},{64,96},{96,64},{128,160},{160,128},{192,224},{224,1... | collective-permute-start | bytes 2211848 | tf_op jit(solution)/shard_map/ppermute | solution.py:91
  6.1 1.2 copy-start
  7.3 20.8 %copy-start.14 = (bf16[128,2880]{0,1:T(8,128)(2,1)S(1)}, bf16[128,2880]{0,1:T(8,128)(2,1)}, u32[]{:S(2)}) copy-start(bf16[128,2880]{0,1:T(8,128)(2,1)} %param.17) | copy-start | bytes 2211844
  28.5 5.5 %copy-start.17 = (f32[2880]{0:T(1024)S(1)}, f32[2880]{0:T(1024)}, u32[]{:S(2)}) copy-start(f32[2880]{0:T(1024)} %param.18) | copy-start | bytes 34564
  28.6 5.6 %copy-start.18 = (s32[128,4]{0,1:T(4,128)S(1)}, s32[128,4]{0,1:T(4,128)}, u32[]{:S(2)}) copy-start(s32[128,4]{0,1:T(4,128)} %param.19) | copy-start | bytes 6148
  30.4 17.5 %all-to-all-start.1 = ((bf16[8,64,384]{2,1,0:T(8,128)(2,1)}), bf16[8,64,384]{2,1,0:T(8,128)(2,1)S(1)}, u32[]{:S(2)}, u32[]{:S(2)}) async-start(bf16[8,64,384]{2,1,0:T(8,128)(2,1)} %pad_bitcast_fusion.1), calls=%async_computation.1 | async-start | bytes 786432 | tf_op jit(solution)/shard_map/all_to_all | solution.py:95
  48.8 7.5 %collective-permute-start.1 = (bf16[64,384]{1,0:T(8,128)(2,1)S(1)}, bf16[64,384]{1,0:T(8,128)(2,1)S(1)}, u32[]{:S(2)}, u32[]{:S(2)}) collective-permute-start(bf16[64,384]{1,0:T(8,128)(2,1)S(1)} %select_convert_fusion), channel_id=1, source_target_pairs={{0,32},{32,0},{64,96},{96,64},{128,160},{160,128},{192,224},{224,1... | collective-permute-start | bytes 147464 | tf_op jit(solution)/shard_map/ppermute | solution.py:91
  52.2 43.6 %copy-start.5 = (bf16[1,2880,180]{1,2,0:T(8,128)(2,1)S(1)}, bf16[1,2880,180]{1,2,0:T(8,128)(2,1)}, u32[]{:S(2)}) copy-start(bf16[1,2880,180]{1,2,0:T(8,128)(2,1)} %param.21) | copy-start | bytes 3110404
  57.6 31.2 %all-to-all-start.2 = ((bf16[32,32,384]{2,1,0:T(8,128)(2,1)}), bf16[32,32,384]{2,1,0:T(8,128)(2,1)}, u32[]{:S(2)}, u32[]{:S(2)}) async-start(bf16[32,32,384]{2,1,0:T(8,128)(2,1)} %bitcast.16), calls=%async_computation.2 | async-start | bytes 1572864 | tf_op jit(solution)/shard_map/all_to_all | solution.py:99
  66.4 31.1 %copy-start.6 = (bf16[1,2880,180]{1,2,0:T(8,128)(2,1)S(1)}, bf16[1,2880,180]{1,2,0:T(8,128)(2,1)}, u32[]{:S(2)}) copy-start(bf16[1,2880,180]{1,2,0:T(8,128)(2,1)} %param.22) | copy-start | bytes 3110404
  66.7 10.7 %collective-permute-start.2 = (bf16[128,384]{1,0:T(8,128)(2,1)S(1)}, bf16[128,384]{1,0:T(8,128)(2,1)S(1)}, u32[]{:S(2)}, u32[]{:S(2)}) collective-permute-start(bf16[128,384]{1,0:T(8,128)(2,1)S(1)} %bitcast.158), channel_id=1, source_target_pairs={{0,256},{32,288},{64,320},{96,352},{128,384},{160,416},{192,448},{... | collective-permute-start | bytes 294920 | tf_op jit(solution)/shard_map/ppermute | solution.py:87
  88.8 21.7 %collective-permute-start.3 = (bf16[1024,384]{1,0:T(8,128)(2,1)}, bf16[1024,384]{1,0:T(8,128)(2,1)}, u32[]{:S(2)}, u32[]{:S(2)}) collective-permute-start(bf16[1024,384]{1,0:T(8,128)(2,1)} %bitcast.17), channel_id=1, source_target_pairs={{0,64},{32,96},{64,128},{96,160},{128,192},{160,224},{192,256},{22... | collective-permute-start | bytes 2359304 | tf_op jit(solution)/shard_map/ppermute | solution.py:87
  91.3 24.6 %collective-permute-start.4 = (bf16[1024,384]{1,0:T(8,128)(2,1)}, bf16[1024,384]{1,0:T(8,128)(2,1)}, u32[]{:S(2)}, u32[]{:S(2)}) collective-permute-start(bf16[1024,384]{1,0:T(8,128)(2,1)} %bitcast.17), channel_id=1, source_target_pairs={{0,448},{32,480},{64,0},{96,32},{128,64},{160,96},{192,128},{224,1... | collective-permute-start | bytes 2359304 | tf_op jit(solution)/shard_map/ppermute | solution.py:87
  99.2 34.0 %all-to-all-start.3 = ((bf16[32,32,384]{2,1,0:T(8,128)(2,1)}), bf16[32,32,384]{2,1,0:T(8,128)(2,1)}, u32[]{:S(2)}, u32[]{:S(2)}) async-start(bf16[32,32,384]{2,1,0:T(8,128)(2,1)} %bitcast.19), calls=%async_computation.3 | async-start | bytes 1572864 | tf_op jit(solution)/shard_map/all_to_all | solution.py:99
  110.5 24.8 %collective-permute-start.5 = (bf16[1024,384]{1,0:T(8,128)(2,1)}, bf16[1024,384]{1,0:T(8,128)(2,1)}, u32[]{:S(2)}, u32[]{:S(2)}) collective-permute-start(bf16[1024,384]{1,0:T(8,128)(2,1)} %collective-permute-done.3), channel_id=1, source_target_pairs={{0,64},{32,96},{64,128},{96,160},{128,192},{160,224},{192,256},{22... | collective-permute-start | bytes 2359304 | tf_op jit(solution)/shard_map/ppermute | solution.py:87
  115.8 22.0 %collective-permute-start.6 = (bf16[1024,384]{1,0:T(8,128)(2,1)}, bf16[1024,384]{1,0:T(8,128)(2,1)}, u32[]{:S(2)}, u32[]{:S(2)}) collective-permute-start(bf16[1024,384]{1,0:T(8,128)(2,1)} %collective-permute-done.4), channel_id=1, source_target_pairs={{0,448},{32,480},{64,0},{96,32},{128,64},{160,96},{192,128},{224,1... | collective-permute-start | bytes 2359304 | tf_op jit(solution)/shard_map/ppermute | solution.py:87
  124.2 3.3 %copy-start.4 = (bf16[180,8,360]{2,1,0:T(8,128)(2,1)S(1)}, bf16[180,8,360]{2,1,0:T(8,128)(2,1)}, u32[]{:S(2)}) copy-start(bf16[180,8,360]{2,1,0:T(8,128)(2,1)} %reshape_squeeze.3) | copy-start | bytes 3110404
  133.2 12.2 %copy-start.2 = (f32[1024,512]{1,0:T(8,128)S(1)}, f32[1024,512]{1,0:T(8,128)}, u32[]{:S(2)}) copy-start(f32[1024,512]{1,0:T(8,128)} %fusion.28) | copy-start | bytes 6291460
  133.2 12.2 %copy-start.3 = (f32[1024,512]{1,0:T(8,128)S(1)}, f32[1024,512]{1,0:T(8,128)}, u32[]{:S(2)}) copy-start(f32[1024,512]{1,0:T(8,128)} %fusion.26) | copy-start | bytes 6291460
  135.2 10.3 %copy-start.1 = (f32[1024,512]{1,0:T(8,128)S(1)}, f32[1024,512]{1,0:T(8,128)}, u32[]{:S(2)}) copy-start(f32[1024,512]{1,0:T(8,128)} %fusion.30) | copy-start | bytes 6291460
  135.3 22.2 %collective-permute-start.7 = (bf16[1024,384]{1,0:T(8,128)(2,1)}, bf16[1024,384]{1,0:T(8,128)(2,1)S(1)}, u32[]{:S(2)}, u32[]{:S(2)}) collective-permute-start(bf16[1024,384]{1,0:T(8,128)(2,1)} %collective-permute-done.5), channel_id=1, source_target_pairs={{0,64},{32,96},{64,128},{96,160},{128,192},{160,224},{192,256},{22... | collective-permute-start | bytes 2359304 | tf_op jit(solution)/shard_map/ppermute | solution.py:87
  137.8 21.6 %collective-permute-start.8 = (bf16[1024,384]{1,0:T(8,128)(2,1)}, bf16[1024,384]{1,0:T(8,128)(2,1)S(1)}, u32[]{:S(2)}, u32[]{:S(2)}) collective-permute-start(bf16[1024,384]{1,0:T(8,128)(2,1)} %collective-permute-done.6), channel_id=1, source_target_pairs={{0,448},{32,480},{64,0},{96,32},{128,64},{160,96},{192,128},{224,1... | collective-permute-start | bytes 2359304 | tf_op jit(solution)/shard_map/ppermute | solution.py:87
  160.1 1.0 copy-start.13
  160.5 3.9 %copy-start.12 = (bf16[1,256,384]{2,0,1:T(2,128)(2,1)S(1)}, bf16[1,256,384]{2,0,1:T(2,128)(2,1)}, u32[]{:S(2)}) copy-start(bf16[1,256,384]{2,0,1:T(2,128)(2,1)} %get-tuple-element.22) | copy-start | bytes 589828
  161.0 10.2 %copy-start.11 = (bf16[1,256,384]{2,0,1:T(2,128)(2,1)S(1)}, bf16[1,256,384]{2,0,1:T(2,128)(2,1)}, u32[]{:S(2)}) copy-start(bf16[1,256,384]{2,0,1:T(2,128)(2,1)} %get-tuple-element.23) | copy-start | bytes 589828
  162.5 21.3 %collective-permute-start.9 = (bf16[1024,384]{1,0:T(8,128)(2,1)}, bf16[1024,384]{1,0:T(8,128)(2,1)}, u32[]{:S(2)}, u32[]{:S(2)}) collective-permute-start(bf16[1024,384]{1,0:T(8,128)(2,1)} %convolution_convert_fusion.2), channel_id=1, source_target_pairs={{0,64},{32,96},{64,128},{96,160},{128,192},{160,224},{192,256},{22... | collective-permute-start | bytes 2359304 | tf_op jit(solution)/shard_map/ppermute | solution.py:87
  164.4 19.4 %copy-start.10 = (bf16[1,256,384]{2,0,1:T(2,128)(2,1)S(1)}, bf16[1,256,384]{2,0,1:T(2,128)(2,1)}, u32[]{:S(2)}) copy-start(bf16[1,256,384]{2,0,1:T(2,128)(2,1)} %get-tuple-element.17) | copy-start | bytes 589828
  165.7 21.6 %collective-permute-start.12 = (bf16[1024,384]{1,0:T(8,128)(2,1)}, bf16[1024,384]{1,0:T(8,128)(2,1)}, u32[]{:S(2)}, u32[]{:S(2)}) collective-permute-start(bf16[1024,384]{1,0:T(8,128)(2,1)} %convolution_convert_fusion.1), channel_id=1, source_target_pairs={{0,448},{32,480},{64,0},{96,32},{128,64},{160,96},{192,128},{224,1... | collective-permute-start | bytes 2359304 | tf_op jit(solution)/shard_map/ppermute | solution.py:87
  172.6 14.8 %copy-start.9 = (bf16[1,256,384]{2,0,1:T(2,128)(2,1)S(1)}, bf16[1,256,384]{2,0,1:T(2,128)(2,1)}, u32[]{:S(2)}) copy-start(bf16[1,256,384]{2,0,1:T(2,128)(2,1)} %get-tuple-element.21) | copy-start | bytes 589828
  172.6 56.4 %all-to-all-start.5 = ((bf16[32,32,384]{2,1,0:T(8,128)(2,1)}), bf16[32,32,384]{2,1,0:T(8,128)(2,1)S(1)}, u32[]{:S(2)}, u32[]{:S(2)}) async-start(bf16[32,32,384]{2,1,0:T(8,128)(2,1)} %bitcast.35), calls=%async_computation.5 | async-start | bytes 1572864 | tf_op jit(solution)/shard_map/all_to_all | solution.py:99
  183.8 10.4 %copy-start.8 = (bf16[1,256,384]{2,0,1:T(2,128)(2,1)S(1)}, bf16[1,256,384]{2,0,1:T(2,128)(2,1)}, u32[]{:S(2)}) copy-start(bf16[1,256,384]{2,0,1:T(2,128)(2,1)} %get-tuple-element.18) | copy-start | bytes 589828
  185.4 20.3 %collective-permute-start.10 = (bf16[1024,384]{1,0:T(8,128)(2,1)S(1)}, bf16[1024,384]{1,0:T(8,128)(2,1)S(1)}, u32[]{:S(2)}, u32[]{:S(2)}) collective-permute-start(bf16[1024,384]{1,0:T(8,128)(2,1)S(1)} %add_convert_fusion.4), channel_id=1, source_target_pairs={{0,64},{32,96},{64,128},{96,160},{128,192},{160,224},{192,256},{22... | collective-permute-start | bytes 2359304 | tf_op jit(solution)/shard_map/ppermute | solution.py:87
  187.3 7.2 %copy-start.7 = (bf16[1,256,384]{2,0,1:T(2,128)(2,1)S(1)}, bf16[1,256,384]{2,0,1:T(2,128)(2,1)}, u32[]{:S(2)}) copy-start(bf16[1,256,384]{2,0,1:T(2,128)(2,1)} %get-tuple-element.20) | copy-start | bytes 589828
  189.0 19.5 %collective-permute-start.13 = (bf16[1024,384]{1,0:T(8,128)(2,1)S(1)}, bf16[1024,384]{1,0:T(8,128)(2,1)S(1)}, u32[]{:S(2)}, u32[]{:S(2)}) collective-permute-start(bf16[1024,384]{1,0:T(8,128)(2,1)S(1)} %add_convert_fusion.2), channel_id=1, source_target_pairs={{0,448},{32,480},{64,0},{96,32},{128,64},{160,96},{192,128},{224,1... | collective-permute-start | bytes 2359304 | tf_op jit(solution)/shard_map/ppermute | solution.py:87
  205.8 19.3 %collective-permute-start.11 = (bf16[1024,384]{1,0:T(8,128)(2,1)S(1)}, bf16[1024,384]{1,0:T(8,128)(2,1)S(1)}, u32[]{:S(2)}, u32[]{:S(2)}) collective-permute-start(bf16[1024,384]{1,0:T(8,128)(2,1)S(1)} %add_convert_fusion.3), channel_id=1, source_target_pairs={{0,64},{32,96},{64,128},{96,160},{128,192},{160,224},{192,256},{22... | collective-permute-start | bytes 2359304 | tf_op jit(solution)/shard_map/ppermute | solution.py:87
  208.7 19.0 %collective-permute-start.14 = (bf16[1024,384]{1,0:T(8,128)(2,1)S(1)}, bf16[1024,384]{1,0:T(8,128)(2,1)S(1)}, u32[]{:S(2)}, u32[]{:S(2)}) collective-permute-start(bf16[1024,384]{1,0:T(8,128)(2,1)S(1)} %add_convert_fusion.1), channel_id=1, source_target_pairs={{0,448},{32,480},{64,0},{96,32},{128,64},{160,96},{192,128},{224,1... | collective-permute-start | bytes 2359304 | tf_op jit(solution)/shard_map/ppermute | solution.py:87
  214.7 22.7 %copy-start.19 = (s32[128,4]{0,1:T(4,128)S(1)}, s32[128,4]{0,1:T(4,128)}, u32[]{:S(2)}) copy-start(s32[128,4]{0,1:T(4,128)} %param.19) | copy-start | bytes 6148
  214.7 22.7 %copy-start.20 = (f32[128,4]{0,1:T(4,128)S(1)}, f32[128,4]{0,1:T(4,128)}, u32[]{:S(2)}) copy-start(f32[128,4]{0,1:T(4,128)} %param.20) | copy-start | bytes 6148
  229.0 12.2 %copy-start.15 = (f32[8,8,384]{2,1,0:T(8,128)S(1)}, f32[8,8,384]{2,1,0:T(8,128)}, u32[]{:S(2)}) copy-start(f32[8,8,384]{2,1,0:T(8,128)} %get-tuple-element.26) | copy-start | bytes 294916
  229.0 30.9 %all-to-all-start.4 = ((bf16[32,32,384]{2,1,0:T(8,128)(2,1)}), bf16[32,32,384]{2,1,0:T(8,128)(2,1)S(1)}, u32[]{:S(2)}, u32[]{:S(2)}) async-start(bf16[32,32,384]{2,1,0:T(8,128)(2,1)} %bitcast.32), calls=%async_computation.4 | async-start | bytes 1572864 | tf_op jit(solution)/shard_map/all_to_all | solution.py:99
  238.2 22.0 %collective-permute-start.15 = (f32[128,384]{1,0:T(8,128)S(1)}, f32[128,384]{1,0:T(8,128)S(1)}, u32[]{:S(2)}, u32[]{:S(2)}) collective-permute-start(f32[128,384]{1,0:T(8,128)S(1)} %fusion.7), channel_id=1, source_target_pairs={{0,256},{32,288},{64,320},{96,352},{128,384},{160,416},{192,448},{... | collective-permute-start | bytes 589832 | tf_op jit(solution)/shard_map/ppermute | solution.py:87
